TPU v7x, 32 devices: a whole 2x2x4 slice. The times are simulated.
32 devices in a mesh: section: 2 (over core), ctx: 4 (over z), dp: 4 (over y, x).
Axes of the slice: x: 2, y: 2, z: 4, core: 2. Of those that a mesh axis runs over, the one named last changes fastest.
Arguments:
- tokens: bfloat16 [3, 4, 1024, 896], P(None, 'dp', 'ctx'), may hold values from -6 to 6
- doc_starts: int32 [3, 4, 4], P(None, 'dp'), may hold values from 0 to 1023, as said below
- cotangent: bfloat16 [3, 4, 1024, 896], P(None, 'dp', 'ctx'), may hold values from -6 to 6
- norm_one: bfloat16 [2, 896], P('section', 'dp'), may hold values from 0.25 to 1.75
- w_query: bfloat16 [2, 896, 896], P('section', 'dp'), may hold values from -0.1875 to 0.1875
- b_query: bfloat16 [2, 896], P('section', 'dp'), may hold values from -3 to 3
- w_key: bfloat16 [2, 896, 128], P('section', 'dp'), may hold values from -0.1875 to 0.1875
- b_key: bfloat16 [2, 128], P('section', 'dp'), may hold values from -3 to 3
- w_value: bfloat16 [2, 896, 128], P('section', 'dp'), may hold values from -0.1875 to 0.1875
- b_value: bfloat16 [2, 128], P('section', 'dp'), may hold values from -3 to 3
- w_out: bfloat16 [2, 896, 896], P('section', 'dp'), may hold values from -0.75 to 0.75
- norm_two: bfloat16 [2, 896], P('section', 'dp'), may hold values from 0.25 to 1.75
- w_gate: bfloat16 [2, 896, 4864], P('section', 'dp'), may hold values from -0.1875 to 0.1875
- w_up: bfloat16 [2, 896, 4864], P('section', 'dp'), may hold values from -0.1875 to 0.1875
- w_down: bfloat16 [2, 4864, 896], P('section', 'dp'), may hold values from -0.078125 to 0.078125
Outputs:
- section_out: bfloat16 [2, 3, 4, 1024, 896], P('section', None, 'dp', 'ctx')
- section_grad: float32 [2, 3, 4, 1024, 896], P('section', None, 'dp', 'ctx')
- grad_norm_one: float32 [2, 896], P('section', 'dp')
- grad_w_query: float32 [2, 896, 896], P('section', 'dp')
- grad_b_query: float32 [2, 896], P('section', 'dp')
- grad_w_key: float32 [2, 896, 128], P('section', 'dp')
- grad_b_key: float32 [2, 128], P('section', 'dp')
- grad_w_value: float32 [2, 896, 128], P('section', 'dp')
- grad_b_value: float32 [2, 128], P('section', 'dp')
- grad_w_out: float32 [2, 896, 896], P('section', 'dp')
- grad_norm_two: float32 [2, 896], P('section', 'dp')
- grad_w_gate: float32 [2, 896, 4864], P('section', 'dp')
- grad_w_up: float32 [2, 896, 4864], P('section', 'dp')
- grad_w_down: float32 [2, 4864, 896], P('section', 'dp')
Inputs may be any that keep to these rules, and one draw needn't show every extreme that they name: `doc_starts`: each stream's starts rise strictly from 0; its second document begins within the first 256 tokens and its third within the last 256 tokens, so the second document spans tokens held by every index of ctx. In some stream the last document is its final token alone.
All inputs are finite; a program needn't handle non-finite values.
Results may differ from a plain program's by a relative error of at most 0.03.
Values may be sent and summed in bfloat16 or wider, within the bound.
No kernel may reach another device: no remote copies, remote signals or barrier semaphores. Data moves between devices by JAX's collectives and lax.ppermute only.
A program may use at most 320 MiB of HBM per device.

v0:
```python
import math

import jax
import jax.numpy as jnp
from jax import lax
from jax.sharding import PartitionSpec as P

KV_HEADS = 2
HEAD = 64


rope_base = 1000000.0
norm_eps = 1e-06
masked = -1e30


def from_behind(block, axis, distance):
    devices = range(lax.axis_size(axis))
    route = [(i - distance, i) for i in devices if i - distance in devices]
    return lax.ppermute(block, axis, route)


def for_sending(shard):
    return jax.tree.map(lambda a: a.astype(jnp.bfloat16) if a.dtype == jnp.float32 else a, shard)


def matmul(left, right):
    return jnp.dot(left, right, preferred_element_type=jnp.float32)


def norm_scale(values, gain):
    inverse = lax.rsqrt(jnp.mean(values * values, axis=-1, keepdims=True) + norm_eps)
    return values * inverse * gain


def rotate(values, cos_table, sin_table, head_size):
    row_count = values.shape[0]
    by_head = values.reshape(row_count, -1, head_size)
    half_size = head_size // 2
    turned = jnp.concatenate([-by_head[..., half_size:], by_head[..., :half_size]], axis=-1)
    return (by_head * cos_table[:, None, :] + turned * sin_table[:, None, :]).reshape(row_count, -1)


def tables(starts, places, head_size):
    begins = jnp.max(jnp.where(starts[None, :] <= places[:, None], starts[None, :], 0), axis=1)
    offsets = (places - begins).astype(jnp.float32)
    frequency = rope_base ** (-jnp.arange(0, head_size, 2, dtype=jnp.float32) / head_size)
    angles = offsets[:, None] * frequency[None, :]
    angles = jnp.concatenate([angles, angles], axis=-1)
    return (begins, jnp.cos(angles), jnp.sin(angles))


def to_heads(values, kv_heads, head_size):
    row_count = values.shape[0]
    group_size = values.shape[1] // (kv_heads * head_size)
    by_head = values.reshape(row_count, kv_heads, group_size, head_size)
    return by_head.transpose(1, 2, 0, 3).reshape(kv_heads, group_size * row_count, head_size)


def from_heads(values, row_count):
    kv_heads, merged, head_size = values.shape
    group_size = merged // row_count
    return (
        values.reshape(kv_heads, group_size, row_count, head_size)
        .transpose(2, 0, 1, 3)
        .reshape(row_count, -1)
    )


def attend(queries, key_rows, value_rows, places, begins, kv_heads, head_size):
    row_count = queries.shape[0]
    query_mat = to_heads(queries, kv_heads, head_size)
    merged = query_mat.shape[1]
    group_size = merged // row_count
    query_pos = jnp.tile(places, group_size)
    query_begin = jnp.tile(begins, group_size)
    scaling = head_size ** (-0.5)
    key_all, value_all = (
        lax.all_gather(key_rows, "ctx", axis=0, tiled=True),
        lax.all_gather(value_rows, "ctx", axis=0, tiled=True),
    )
    total_len = key_all.shape[0]
    block_len = math.gcd(total_len, 1024)

    def block_scores(block_no):
        key_block = key_all.reshape(block_len, kv_heads, head_size)
        key_pos = block_no * block_len + jnp.arange(block_len, dtype=jnp.int32)
        scores = (
            jnp.einsum("hrd,khd->hrk", query_mat, key_block, preferred_element_type=jnp.float32)
            * scaling
        )
        visible = (key_pos[None, :] <= query_pos[:, None]) & (
            key_pos[None, :] >= query_begin[:, None]
        )
        return (jnp.where(visible[None], scores, masked), visible)

    def stats(block_no, running):
        run_max, run_sum = running
        scores, visible = block_scores(block_no)
        new_max = jnp.maximum(run_max, jnp.max(scores, axis=-1))
        exp_terms = jnp.where(visible[None], jnp.exp(scores - new_max[..., None]), 0.0)
        run_sum = run_sum * jnp.exp(run_max - new_max) + jnp.sum(exp_terms, axis=-1)
        return (new_max, run_sum)

    start_stats = (
        jnp.full((kv_heads, merged), masked, jnp.float32),
        jnp.zeros((kv_heads, merged), jnp.float32),
    )
    run_max, run_sum = lax.fori_loop(0, total_len // block_len, stats, start_stats)
    log_sum = run_max + jnp.log(run_sum)

    def accumulate(block_no, run_acc):
        scores, visible = block_scores(block_no)
        value_block = value_all.reshape(block_len, kv_heads, head_size)
        probs = jnp.where(visible[None], jnp.exp(scores - log_sum[..., None]), 0.0).astype(
            jnp.bfloat16
        )
        return run_acc + jnp.einsum(
            "hrk,khd->hrd", probs, value_block, preferred_element_type=jnp.float32
        )

    run_acc = lax.fori_loop(
        0, total_len // block_len, accumulate, jnp.zeros((kv_heads, merged, head_size), jnp.float32)
    )
    return (from_heads(run_acc, row_count), log_sum)


def attend_back(
    queries, key_rows, value_rows, log_sum, grad_output, places, begins, kv_heads, head_size
):
    row_count = queries.shape[0]
    query_mat = to_heads(queries, kv_heads, head_size)
    grad_mat = to_heads(grad_output, kv_heads, head_size)
    merged = query_mat.shape[1]
    group_size = merged // row_count
    query_pos = jnp.tile(places, group_size)
    query_begin = jnp.tile(begins, group_size)
    scaling = head_size ** (-0.5)
    key_all, value_all = (
        lax.all_gather(key_rows, "ctx", axis=0, tiled=True),
        lax.all_gather(value_rows, "ctx", axis=0, tiled=True),
    )
    total_len = key_all.shape[0]
    block_len = math.gcd(total_len, 1024)
    width = key_rows.shape[1]

    def block_terms(block_no):
        key_block = key_all.reshape(block_len, kv_heads, head_size)
        value_block = value_all.reshape(block_len, kv_heads, head_size)
        key_pos = block_no * block_len + jnp.arange(block_len, dtype=jnp.int32)
        scores = (
            jnp.einsum("hrd,khd->hrk", query_mat, key_block, preferred_element_type=jnp.float32)
            * scaling
        )
        visible = (key_pos[None, :] <= query_pos[:, None]) & (
            key_pos[None, :] >= query_begin[:, None]
        )
        probs = jnp.where(
            visible[None],
            jnp.exp(jnp.where(visible[None], scores, masked) - log_sum[..., None]),
            0.0,
        )
        grad_prob = jnp.einsum(
            "hrd,khd->hrk", grad_mat, value_block, preferred_element_type=jnp.float32
        )
        return (key_block, probs, grad_prob)

    def correction(block_no, delta_rows):
        unused, probs, grad_prob = block_terms(block_no)
        return delta_rows + jnp.sum(probs * grad_prob, axis=-1)

    delta_rows = lax.fori_loop(
        0, total_len // block_len, correction, jnp.zeros((kv_heads, merged), jnp.float32)
    )

    def visit(grad_query, block_no):
        key_block, probs, grad_prob = block_terms(block_no)
        grad_score = (probs * (grad_prob - delta_rows[..., None])).astype(jnp.bfloat16)
        grad_value = jnp.einsum(
            "hrk,hrd->khd", probs.astype(jnp.bfloat16), grad_mat, preferred_element_type=jnp.float32
        )
        grad_key = (
            jnp.einsum("hrk,hrd->khd", grad_score, query_mat, preferred_element_type=jnp.float32)
            * scaling
        )
        grad_query = (
            grad_query
            + jnp.einsum("hrk,khd->hrd", grad_score, key_block, preferred_element_type=jnp.float32)
            * scaling
        )
        return (
            grad_query,
            (grad_key.reshape(block_len, width), grad_value.reshape(block_len, width)),
        )

    start_grad = jnp.zeros(query_mat.shape, jnp.float32)
    grad_query, (key_parts, value_parts) = lax.scan(
        visit, start_grad, jnp.arange(total_len // block_len, dtype=jnp.int32)
    )
    grad_keys, grad_values = (
        lax.psum_scatter(
            key_parts.reshape(total_len, width).astype(jnp.bfloat16),
            "ctx",
            scatter_dimension=0,
            tiled=True,
        ).astype(jnp.float32),
        lax.psum_scatter(
            value_parts.reshape(total_len, width).astype(jnp.bfloat16),
            "ctx",
            scatter_dimension=0,
            tiled=True,
        ).astype(jnp.float32),
    )
    return (from_heads(grad_query, row_count), grad_keys, grad_values)


def layer_fwd(layer_in, params, cos_table, sin_table, places, begins):
    (
        gain_one,
        w_query,
        b_query,
        w_key,
        b_key,
        w_value,
        b_value,
        w_out,
        gain_two,
        w_gate,
        w_up,
        w_down,
    ) = params
    normed = norm_scale(layer_in, gain_one.astype(jnp.float32)).astype(jnp.bfloat16)
    queries = rotate(
        matmul(normed, w_query) + b_query.astype(jnp.float32), cos_table, sin_table, HEAD
    ).astype(jnp.bfloat16)
    key_rows = rotate(
        matmul(normed, w_key) + b_key.astype(jnp.float32), cos_table, sin_table, HEAD
    ).astype(jnp.bfloat16)
    value_rows = (matmul(normed, w_value) + b_value.astype(jnp.float32)).astype(jnp.bfloat16)
    output, log_sum = attend(queries, key_rows, value_rows, places, begins, KV_HEADS, HEAD)
    attended = output.astype(jnp.bfloat16)
    residual = layer_in + matmul(attended, w_out)
    mixing = norm_scale(residual, gain_two.astype(jnp.float32)).astype(jnp.bfloat16)
    gate_rows = matmul(mixing, w_gate)
    up_rows = matmul(mixing, w_up)
    hidden = (jax.nn.silu(gate_rows) * up_rows).astype(jnp.bfloat16)
    result = (residual + matmul(hidden, w_down)).astype(jnp.bfloat16)
    return (
        result,
        (
            layer_in,
            normed,
            queries,
            key_rows,
            value_rows,
            output,
            log_sum,
            attended,
            residual,
            mixing,
            gate_rows,
            up_rows,
            hidden,
        ),
    )


def swiglu(gate_val, up_val):
    return jax.nn.silu(gate_val) * up_val


def layer_back(upstream, kept, params, cos_table, sin_table, places, begins):
    (
        layer_in,
        normed,
        queries,
        key_rows,
        value_rows,
        output,
        log_sum,
        attended,
        residual,
        mixing,
        gate_rows,
        up_rows,
        hidden,
    ) = kept
    (
        gain_one,
        w_query,
        b_query,
        w_key,
        b_key,
        w_value,
        b_value,
        w_out,
        gain_two,
        w_gate,
        w_up,
        w_down,
    ) = params
    grad_ffn = upstream.astype(jnp.bfloat16)
    grad_wdown = matmul(hidden.T, grad_ffn)
    grad_hidden = matmul(grad_ffn, w_down.T)
    unused, pull_mlp = jax.vjp(swiglu, gate_rows, up_rows)
    grad_gate, grad_up = pull_mlp(grad_hidden)
    grad_gate = grad_gate.astype(jnp.bfloat16)
    grad_up = grad_up.astype(jnp.bfloat16)
    grad_wgate = matmul(mixing.T, grad_gate)
    grad_wup = matmul(mixing.T, grad_up)
    grad_mixing = matmul(grad_gate, w_gate.T) + matmul(grad_up, w_up.T)
    unused, pull_two = jax.vjp(norm_scale, residual, gain_two.astype(jnp.float32))
    grad_res_norm, grad_gain_two = pull_two(grad_mixing)
    grad_residual = upstream + grad_res_norm
    grad_attended = grad_residual.astype(jnp.bfloat16)
    grad_wout = matmul(attended.T, grad_attended)
    grad_output = matmul(grad_attended, w_out.T).astype(jnp.bfloat16)
    grad_rot_q, grad_rot_k, grad_values = attend_back(
        queries, key_rows, value_rows, log_sum, grad_output, places, begins, KV_HEADS, HEAD
    )
    grad_q = rotate(grad_rot_q, cos_table, -sin_table, HEAD).astype(jnp.bfloat16)
    grad_k = rotate(grad_rot_k, cos_table, -sin_table, HEAD).astype(jnp.bfloat16)
    grad_v = grad_values.astype(jnp.bfloat16)
    grad_wquery = matmul(normed.T, grad_q)
    grad_wkey = matmul(normed.T, grad_k)
    grad_wvalue = matmul(normed.T, grad_v)
    grad_bquery = jnp.sum(grad_q.astype(jnp.float32), axis=0)
    grad_bkey = jnp.sum(grad_k.astype(jnp.float32), axis=0)
    grad_bvalue = jnp.sum(grad_v.astype(jnp.float32), axis=0)
    grad_normed = matmul(grad_q, w_query.T) + matmul(grad_k, w_key.T) + matmul(grad_v, w_value.T)
    unused, pull_one = jax.vjp(norm_scale, layer_in, gain_one.astype(jnp.float32))
    grad_in_norm, grad_gain_one = pull_one(grad_normed)
    terms = (
        grad_gain_one,
        grad_wquery,
        grad_bquery,
        grad_wkey,
        grad_bkey,
        grad_wvalue,
        grad_bvalue,
        grad_wout,
        grad_gain_two,
        grad_wgate,
        grad_wup,
        grad_wdown,
    )
    return (grad_residual + grad_in_norm, terms)


def local(
    tokens,
    doc_starts,
    cotangent,
    norm_one,
    w_query,
    b_query,
    w_key,
    b_key,
    w_value,
    b_value,
    w_out,
    norm_two,
    w_gate,
    w_up,
    w_down,
):
    section_no = lax.axis_index("section")
    shards = (
        norm_one,
        w_query,
        b_query,
        w_key,
        b_key,
        w_value,
        b_value,
        w_out,
        norm_two,
        w_gate,
        w_up,
        w_down,
    )
    gathered = (
        lax.all_gather(shards[0], "dp", axis=1, tiled=True),
        lax.all_gather(shards[1], "dp", axis=1, tiled=True),
        lax.all_gather(shards[2], "dp", axis=1, tiled=True),
        lax.all_gather(shards[3], "dp", axis=1, tiled=True),
        lax.all_gather(shards[4], "dp", axis=1, tiled=True),
        lax.all_gather(shards[5], "dp", axis=1, tiled=True),
        lax.all_gather(shards[6], "dp", axis=1, tiled=True),
        lax.all_gather(shards[7], "dp", axis=1, tiled=True),
        lax.all_gather(shards[8], "dp", axis=1, tiled=True),
        lax.all_gather(shards[9], "dp", axis=1, tiled=True),
        lax.all_gather(shards[10], "dp", axis=1, tiled=True),
        lax.all_gather(shards[11], "dp", axis=1, tiled=True),
    )
    params = tuple((whole[0] for whole in gathered))
    micro_count = tokens.shape[0]
    row_count = tokens.shape[2]
    width = tokens.shape[3]
    places = lax.axis_index("ctx") * row_count + jnp.arange(row_count, dtype=jnp.int32)
    stream_starts = doc_starts[:, 0]

    def context(micro_no):
        starts = lax.dynamic_index_in_dim(stream_starts, micro_no, 0, keepdims=False)
        return tables(starts, places, HEAD)

    received = jnp.zeros((row_count, width), jnp.bfloat16)
    outputs = []
    saved = []
    for tick_no in range(micro_count + 1):
        micro_no = jnp.clip(tick_no - section_no, 0, micro_count - 1)
        fresh = tokens[min(tick_no, micro_count - 1), 0]
        layer_in = jnp.where(section_no == 0, fresh, received).astype(jnp.float32)
        begins, cos_table, sin_table = context(micro_no)
        result, kept = layer_fwd(layer_in, params, cos_table, sin_table, places, begins)
        outputs.append(result)
        saved.append(kept)
        if tick_no < micro_count:
            received = from_behind(result, "section", 1)
    section_out = jnp.where(
        section_no == 0, jnp.stack(outputs[:micro_count]), jnp.stack(outputs[1:])
    )
    regathered = (
        lax.all_gather(shards[0], "dp", axis=1, tiled=True),
        lax.all_gather(shards[1], "dp", axis=1, tiled=True),
        lax.all_gather(shards[2], "dp", axis=1, tiled=True),
        lax.all_gather(shards[3], "dp", axis=1, tiled=True),
        lax.all_gather(shards[4], "dp", axis=1, tiled=True),
        lax.all_gather(shards[5], "dp", axis=1, tiled=True),
        lax.all_gather(shards[6], "dp", axis=1, tiled=True),
        lax.all_gather(shards[7], "dp", axis=1, tiled=True),
        lax.all_gather(shards[8], "dp", axis=1, tiled=True),
        lax.all_gather(shards[9], "dp", axis=1, tiled=True),
        lax.all_gather(shards[10], "dp", axis=1, tiled=True),
        lax.all_gather(shards[11], "dp", axis=1, tiled=True),
    )
    back_params = tuple((whole[0] for whole in regathered))

    def pick(earlier, later):
        return jnp.where(section_no == 0, earlier, later)

    totals = tuple((jnp.zeros(param.shape, jnp.float32) for param in back_params))
    returned = jnp.zeros((row_count, width), jnp.float32)
    grads_in = []
    for tick_no in range(micro_count + 1):
        micro_no = jnp.clip(tick_no - 1 + section_no, 0, micro_count - 1)
        valid = jnp.where(section_no == 0, tick_no >= 1, tick_no < micro_count)
        from_loss = cotangent[min(tick_no, micro_count - 1), 0].astype(jnp.float32)
        upstream = jnp.where(valid, jnp.where(section_no == 1, from_loss, returned), 0.0)
        kept = jax.tree.map(pick, saved[max(tick_no - 1, 0)], saved[min(tick_no + 1, micro_count)])
        begins, cos_table, sin_table = context(micro_no)
        grad_in, terms = layer_back(
            upstream, kept, back_params, cos_table, sin_table, places, begins
        )
        totals = tuple((total + term for total, term in zip(totals, terms)))
        grads_in.append(grad_in)
        if tick_no < micro_count:
            returned = from_behind(grad_in.astype(jnp.bfloat16), "section", -1).astype(
                grad_in.dtype
            )
    section_grad = jnp.where(
        section_no == 0, jnp.stack(grads_in[1:]), jnp.stack(grads_in[:micro_count])
    )
    shares = jax.tree.map(
        lambda part: part.astype(jnp.float32),
        lax.psum_scatter(
            for_sending(tuple((total[None] for total in totals))),
            "dp",
            scatter_dimension=1,
            tiled=True,
        ),
    )
    shares = jax.tree.map(
        lambda part: part.astype(jnp.float32), lax.psum(for_sending(tuple(shares)), "ctx")
    )
    return (section_out[None, :, None], section_grad[None, :, None]) + tuple(shares)


def solution(mesh):
    return jax.shard_map(
        local,
        mesh=mesh,
        in_specs=(
            P(None, "dp", "ctx", None),
            P(None, "dp", None),
            P(None, "dp", "ctx", None),
            P("section", "dp"),
            P("section", "dp", None),
            P("section", "dp"),
            P("section", "dp", None),
            P("section", "dp"),
            P("section", "dp", None),
            P("section", "dp"),
            P("section", "dp", None),
            P("section", "dp"),
            P("section", "dp", None),
            P("section", "dp", None),
            P("section", "dp", None),
        ),
        out_specs=(
            P("section", None, "dp", "ctx", None),
            P("section", None, "dp", "ctx", None),
            P("section", "dp"),
            P("section", "dp", None),
            P("section", "dp"),
            P("section", "dp", None),
            P("section", "dp"),
            P("section", "dp", None),
            P("section", "dp"),
            P("section", "dp", None),
            P("section", "dp"),
            P("section", "dp", None),
            P("section", "dp", None),
            P("section", "dp", None),
        ),
        check_vma=False,
    )
```

profile of v0, /device:TPU:1, one launch (start us, length us, event | category | flops | bytes accessed | tf_op | source)
XLA Modules:
  0.0 2043.1 jit_solution(5989162597002005568)
XLA Ops:
  13.9 8.9 all-reduce.5
  30.9 8.4 all_gather.96
  54.1 11.8 all_gather.101
  66.0 11.8 all_gather.98
  77.8 16.5 fusion.63
  130.3 40.8 %all-gather.10.cloned.1.call-done = bf16[1,896,4864]{2,1,0:T(8,128)(2,1)} async-done(((bf16[1,224,4864]{2,1,0:T(8,128)(2,1)}), bf16[1,896,4864]{2,1,0:T(8,128)(2,1)}) %all-gather.10.cloned.1.call-update) | async-done | bytes 8716304 | tf_op jit(solution)/shard_map/all_gather | solution.py:392
  179.2 83.9 %all-gather.12.cloned.1.call-done = bf16[1,896,4864]{2,1,0:T(8,128)(2,1)} async-done(((bf16[1,224,4864]{2,1,0:T(8,128)(2,1)}), bf16[1,896,4864]{2,1,0:T(8,128)(2,1)}) %all-gather.12.cloned.1.call-update) | async-done | bytes 8716304 | tf_op jit(solution)/shard_map/all_gather | solution.py:393
  263.2 9.5 multiply_convert_fusion.11
  272.7 82.5 %all-gather.14.cloned.1.call-done = bf16[1,4864,896]{2,1,0:T(8,128)(2,1)} async-done(((bf16[1,1216,896]{2,1,0:T(8,128)(2,1)}), bf16[1,4864,896]{2,1,0:T(8,128)(2,1)}) %all-gather.14.cloned.1.call-update) | async-done | bytes 8716304 | tf_op jit(solution)/shard_map/all_gather | solution.py:394
  369.4 12.8 all_gather.108
  393.3 10.9 all_gather.107
  424.3 8.9 fusion.33
  437.6 10.9 fusion.81
  458.0 11.8 all_gather.114
  480.7 11.7 all_gather.113
  499.8 11.8 all_gather.110
  528.4 11.0 all_gather.109
  572.3 8.9 multiply_reduce_fusion.3
  581.2 12.3 multiply_convert_fusion.3
  628.6 11.8 all_gather.115
  642.8 8.3 fusion.243
  662.9 32.3 %reduce-scatter.33.cloned.1.call-done = bf16[256,128]{0,1:T(8,128)(2,1)} async-done(((bf16[1024,128]{0,1:T(8,128)(2,1)}), bf16[256,128]{0,1:T(8,128)(2,1)}) %reduce-scatter.33.cloned.1.call-update) | async-done | bytes 65552 | tf_op jit(solution)/shard_map/reduce_scatter | solution.py:207
  721.2 11.1 all_gather.111
  735.0 11.9 all_gather.112
  768.6 9.6 collective-permute-start.3
  781.3 12.4 all_gather.116
  794.8 11.6 all_gather.118
  806.5 11.6 all_gather.117
  819.3 12.9 all_gather.120
  846.5 11.6 all_gather.119
  860.8 10.4 fusion.84
  891.7 9.0 multiply_reduce_fusion.2
  900.7 11.8 multiply_convert_fusion.2
  935.1 12.2 reduce-scatter.35.cloned.1.call-done
  954.0 14.1 reduce-scatter.37.cloned.1.call-done
  981.5 10.6 fusion.87
  1012.8 8.8 multiply_reduce_fusion.1
  1021.6 11.8 multiply_convert_fusion.1
  1044.4 8.3 fusion.249
  1059.0 16.5 reduce-scatter.41.cloned.1.call-done
  1088.6 12.5 fusion.90
  1118.1 8.4 fusion.456
  1126.6 9.2 multiply_reduce_fusion
  1135.8 11.8 multiply_convert_fusion
  1155.8 8.3 fusion.252
  1178.5 10.6 reduce-scatter.45.cloned.1.call-done
  1213.7 10.2 fusion.352
  1236.5 10.4 fusion.354
  1246.9 8.5 fusion.356
  1255.4 21.8 %fusion.53 = bf16[1,896,4864]{2,1,0:T(8,128)(2,1)} fusion(bf16[256,4864]{1,0:T(8,128)(2,1)} %get-tuple-element.537, f32[896,4864]{1,0:T(8,128)} %fusion.356, f32[896,4864]{1,0:T(8,128)} %fusion.352, f32[896,4864]{1,0:T(8,128)} %fusion.354, bf16[256,896]{1,0:T(8,128)(2,1)S(1)} %copy-done.21, bf16[256,896]{1,0:T(8,128)(2,1)S(1)} %copy-done.11, pred[]{:T(512)S(6)} %eq.4), kind=kOutput, calls=%fused_computation.80 | convolution fusion | flops 2249031680 | bytes 64421888 | tf_op jit(solution)/shard_map/dot_general | solution.py:28
  1277.5 10.3 fusion.351
  1287.8 8.6 fusion.353
  1296.4 8.5 fusion.355
  1304.9 21.9 %fusion.54 = bf16[1,896,4864]{2,1,0:T(8,128)(2,1)} fusion(bf16[256,4864]{1,0:T(8,128)(2,1)} %get-tuple-element.538, f32[896,4864]{1,0:T(8,128)} %fusion.355, f32[896,4864]{1,0:T(8,128)} %fusion.351, f32[896,4864]{1,0:T(8,128)} %fusion.353, bf16[256,896]{1,0:T(8,128)(2,1)S(1)} %copy-done.21, bf16[256,896]{1,0:T(8,128)(2,1)S(1)} %copy-done.11, pred[]{:T(512)S(6)} %eq.4), kind=kOutput, calls=%fused_computation.81 | convolution fusion | flops 2249031680 | bytes 64421888 | tf_op jit(solution)/shard_map/dot_general | solution.py:28
  1328.1 10.6 fusion.99
  1346.4 8.6 fusion.95
  1355.0 21.9 %fusion.4 = bf16[1,4864,896]{2,1,0:T(8,128)(2,1)} fusion(f32[4864,896]{1,0:T(8,128)} %fusion.95, f32[4864,896]{1,0:T(8,128)} %fusion.99, f32[4864,896]{1,0:T(8,128)} %fusion.97, bf16[256,4864]{1,0:T(8,128)(2,1)} %copy-done.41, bf16[256,4864]{1,0:T(8,128)(2,1)} %get-tuple-element.545, pred[]{:T(512)S(6)} %eq.4, bf16[256,896]{1,0:T(8,128)(2,1)S(1)} %copy-done.107, ...), kind=kOutput, calls=%fused_computation.31 | convolution fusion | flops 2251194368 | bytes 66913792 | tf_op jit(solution)/shard_map/dot_general | solution.py:28
  1384.4 26.1 %reduce-scatter.47.cloned.1.call-done = bf16[1,224,896]{2,1,0:T(8,128)(2,1)} async-done(((bf16[1,896,896]{2,1,0:T(8,128)(2,1)}), bf16[1,224,896]{2,1,0:T(8,128)(2,1)}) %reduce-scatter.47.cloned.1.call-update) | async-done | bytes 401424 | tf_op jit(solution)/shard_map/reduce_scatter | solution.py:466
  1410.6 35.0 %reduce-scatter.53.cloned.1.call-done = bf16[1,224,896]{2,1,0:T(8,128)(2,1)} async-done(((bf16[1,896,896]{2,1,0:T(8,128)(2,1)}), bf16[1,224,896]{2,1,0:T(8,128)(2,1)}) %reduce-scatter.53.cloned.1.call-update) | async-done | bytes 401424 | tf_op jit(solution)/shard_map/reduce_scatter | solution.py:466
  1445.6 92.6 %reduce-scatter.55.cloned.1.call-done = bf16[1,224,4864]{2,1,0:T(8,128)(2,1)} async-done(((bf16[1,896,4864]{2,1,0:T(8,128)(2,1)}), bf16[1,224,4864]{2,1,0:T(8,128)(2,1)}) %reduce-scatter.55.cloned.1.call-update) | async-done | bytes 2179088 | tf_op jit(solution)/shard_map/reduce_scatter | solution.py:466
  1538.1 92.4 %reduce-scatter.57.cloned.1.call-done = bf16[1,224,4864]{2,1,0:T(8,128)(2,1)} async-done(((bf16[1,896,4864]{2,1,0:T(8,128)(2,1)}), bf16[1,224,4864]{2,1,0:T(8,128)(2,1)}) %reduce-scatter.57.cloned.1.call-update) | async-done | bytes 2179088 | tf_op jit(solution)/shard_map/reduce_scatter | solution.py:466
  1630.6 92.6 %reduce-scatter.59.cloned.1.call-done = bf16[1,1216,896]{2,1,0:T(8,128)(2,1)} async-done(((bf16[1,4864,896]{2,1,0:T(8,128)(2,1)}), bf16[1,1216,896]{2,1,0:T(8,128)(2,1)}) %reduce-scatter.59.cloned.1.call-update) | async-done | bytes 2179088 | tf_op jit(solution)/shard_map/reduce_scatter | solution.py:466
  1735.5 24.9 %all-reduce.11.cloned.1.call-done = (bf16[1,224]{1,0:T(2,128)(2,1)}, bf16[1,224]{1,0:T(2,128)(2,1)}, bf16[1,224,128]{2,1,0:T(8,128)(2,1)}, bf16[1,32]{1,0:T(2,12...) async-done(((bf16[1,224]{1,0:T(2,128)(2,1)}, bf16[1,224]{1,0:T(2,128)(2,1)}, bf16[1,224,128]{2,1,0:T(8,128)(2,1)}, ...) | async-done | bytes 116176 | tf_op jit(solution)/shard_map/psum | solution.py:474
  1769.3 253.8 %all-reduce.13.cloned.1.call-done = (bf16[1,224,896]{2,1,0:T(8,128)(2,1)}, bf16[1,224,896]{2,1,0:T(8,128)(2,1)}, bf16[1,224,4864]{2,1,0:T(8,128)(2,1)}, bf16[1,2...) async-done(((bf16[1,224,896]{2,1,0:T(8,128)(2,1)}, bf16[1,224,896]{2,1,0:T(8,128)(2,1)}, bf16[1,224,4864]{2,1,0:T(8,128)(2,1)}, bf16[1,224,4864]{2,1,0:T(8,128)(2,1)}, ...) | async-done | bytes 7340048 | tf_op jit(solution)/shard_map/psum | solution.py:474
  (1041 shorter events, 559.6 us)
Async XLA Ops:
  7.3 87.1 %all-gather.6.cloned.1.call-start = ((), (), s32[]{:S(2)}) async-start(), calls=%async_computation.20 | async-start | bytes 2007040 | tf_op jit(solution)/shard_map/all_gather | solution.py:384
  8.0 119.8 %all-gather.8.cloned.1.call-start = ((), (), s32[]{:S(2)}) async-start(), calls=%async_computation.21 | async-start | bytes 2007040 | tf_op jit(solution)/shard_map/all_gather | solution.py:390
  8.8 162.3 %all-gather.10.cloned.1.call-start = ((), (), s32[]{:S(2)}) async-start(), calls=%async_computation.22 | async-start | bytes 10895360 | tf_op jit(solution)/shard_map/all_gather | solution.py:392
  9.5 253.7 %all-gather.12.cloned.1.call-start = ((), (), s32[]{:S(2)}) async-start(), calls=%async_computation.23 | async-start | bytes 10895360 | tf_op jit(solution)/shard_map/all_gather | solution.py:393
  10.1 345.1 %all-gather.14.cloned.1.call-start = ((), (), s32[]{:S(2)}) async-start(), calls=%async_computation.24 | async-start | bytes 10895360 | tf_op jit(solution)/shard_map/all_gather | solution.py:394
  10.7 647.0 %reduce-scatter.31.cloned.1.call-start = ((), (), s32[]{:S(2)}) async-start(), calls=%async_computation.25 | async-start | bytes 327680 | tf_op jit(solution)/shard_map/reduce_scatter | solution.py:201
  40.5 435.7 %copy-start.178 = (f32[896]{0:T(1024)}, f32[896]{0:T(1024)S(1)}, u32[]{:S(2)}) copy-start(f32[896]{0:T(1024)S(1)} %mul.1752) | copy-start | bytes 10756
  53.7 313.6 %copy-start.62 = (bf16[1,896,128]{2,1,0:T(8,128)(2,1)}, bf16[1,896,128]{2,1,0:T(8,128)(2,1)S(1)}, u32[]{:S(2)}) copy-start(bf16[1,896,128]{2,1,0:T(8,128)(2,1)S(1)} %all_gather.99) | copy-start | bytes 688132
  130.1 293.7 %copy-start.31 = (f32[256,896]{1,0:T(8,128)}, f32[256,896]{1,0:T(8,128)S(1)}, u32[]{:S(2)}) copy-start(f32[256,896]{1,0:T(8,128)S(1)} %get-tuple-element.684) | copy-start | bytes 2752516
  130.3 132.8 %copy-start.18 = (bf16[256,896]{1,0:T(8,128)(2,1)}, bf16[256,896]{1,0:T(8,128)(2,1)S(1)}, u32[]{:S(2)}) copy-start(bf16[256,896]{1,0:T(8,128)(2,1)S(1)} %multiply_convert_fusion.15) | copy-start | bytes 1376260
  362.4 4.5 collective-permute-start
  367.3 128.0 %copy-start.220 = (f32[256]{0:T(256)}, f32[256]{0:T(256)S(1)}, u32[]{:S(2)}) copy-start(f32[256]{0:T(256)S(1)} %get-tuple-element.380) | copy-start | bytes 3076
  367.3 397.8 %copy-start.12 = (bf16[256,896]{1,0:T(8,128)(2,1)}, bf16[256,896]{1,0:T(8,128)(2,1)S(1)}, u32[]{:S(2)}) copy-start(bf16[256,896]{1,0:T(8,128)(2,1)S(1)} %get-tuple-element.536) | copy-start | bytes 1376260
  424.2 52.0 %copy-start.93 = (f32[256,896]{1,0:T(8,128)}, f32[256,896]{1,0:T(8,128)S(1)}, u32[]{:S(2)}) copy-start(f32[256,896]{1,0:T(8,128)S(1)} %get-tuple-element.521) | copy-start | bytes 2752516
  456.7 39.2 %collective-permute-start.1 = (bf16[256,896]{1,0:T(8,128)(2,1)}, bf16[256,896]{1,0:T(8,128)(2,1)}, u32[]{:S(2)}, u32[]{:S(2)}) collective-permute-start(bf16[256,896]{1,0:T(8,128)(2,1)} %fusion.218), channel_id=1, source_target_pairs={{0,16},{1,17},{2,18},{3,19},{4,20},{5,21},{6,22},{7,23},{8,24},{9,... | collective-permute-start | bytes 1376264 | tf_op jit(solution)/shard_map/ppermute | solution.py:20
  497.3 695.4 %copy-start.14 = (bf16[256,896]{1,0:T(8,128)(2,1)}, bf16[256,896]{1,0:T(8,128)(2,1)S(1)}, u32[]{:S(2)}) copy-start(bf16[256,896]{1,0:T(8,128)(2,1)S(1)} %get-tuple-element.523) | copy-start | bytes 1376260
  559.4 42.2 %copy-start.20 = (bf16[256,896]{1,0:T(8,128)(2,1)}, bf16[256,896]{1,0:T(8,128)(2,1)S(1)}, u32[]{:S(2)}) copy-start(bf16[256,896]{1,0:T(8,128)(2,1)S(1)} %get-tuple-element.664) | copy-start | bytes 1376260
  614.9 81.6 %collective-permute-start.2 = (bf16[256,896]{1,0:T(8,128)(2,1)}, bf16[256,896]{1,0:T(8,128)(2,1)}, u32[]{:S(2)}, u32[]{:S(2)}) collective-permute-start(bf16[256,896]{1,0:T(8,128)(2,1)} %fusion.215), channel_id=1, source_target_pairs={{0,16},{1,17},{2,18},{3,19},{4,20},{5,21},{6,22},{7,23},{8,24},{9,... | collective-permute-start | bytes 1376264 | tf_op jit(solution)/shard_map/ppermute | solution.py:20
  616.3 79.0 %reduce-scatter.33.cloned.1.call-start = ((), (), s32[]{:S(2)}) async-start(), calls=%async_computation.26 | async-start | bytes 327680 | tf_op jit(solution)/shard_map/reduce_scatter | solution.py:207
  642.8 53.7 %copy-start.234 = (f32[256]{0:T(256)S(1)}, f32[256]{0:T(256)}, u32[]{:S(2)}) copy-start(f32[256]{0:T(256)} %fusion.392) | copy-start | bytes 3076
  651.1 296.1 %reduce-scatter.35.cloned.1.call-start = ((), (), s32[]{:S(2)}) async-start(), calls=%async_computation.27 | async-start | bytes 327680 | tf_op jit(solution)/shard_map/reduce_scatter | solution.py:201
  701.7 62.5 %copy-start.16 = (bf16[256,896]{1,0:T(8,128)(2,1)}, bf16[256,896]{1,0:T(8,128)(2,1)S(1)}, u32[]{:S(2)}) copy-start(bf16[256,896]{1,0:T(8,128)(2,1)S(1)} %get-tuple-element.513) | copy-start | bytes 1376260
  764.2 71.5 %slice-start.21 = ((s8[8716288]{0:T(1024)(128)(4,1)}), s8[4194304]{0:T(1024)(128)(4,1)S(1)}, s32[]{:S(2)}) async-start(s8[8716288]{0:T(1024)(128)(4,1)} %bitcast.806), calls=%async_computation.68 | async-start | bytes 8388608
  765.2 70.5 %slice-start.22 = ((s8[8716288]{0:T(1024)(128)(4,1)}), s8[4194304]{0:T(1024)(128)(4,1)S(1)}, s32[]{:S(2)}) async-start(s8[8716288]{0:T(1024)(128)(4,1)} %bitcast.806), calls=%async_computation.69 | async-start | bytes 8388608
  768.5 50.2 %copy-start.240 = (f32[256]{0:T(256)S(1)}, f32[256]{0:T(256)}, u32[]{:S(2)}) copy-start(f32[256]{0:T(256)} %get-tuple-element.367) | copy-start | bytes 3076
  768.5 50.7 %copy-start.194 = (bf16[256,128]{0,1:T(8,128)(2,1)S(1)}, bf16[256,128]{0,1:T(8,128)(2,1)}, u32[]{:S(2)}) copy-start(bf16[256,128]{0,1:T(8,128)(2,1)} %get-tuple-element.636) | copy-start | bytes 196612
  768.5 63.6 %copy-start.61 = (bf16[256,896]{1,0:T(8,128)(2,1)S(1)}, bf16[256,896]{1,0:T(8,128)(2,1)}, u32[]{:S(2)}) copy-start(bf16[256,896]{1,0:T(8,128)(2,1)} %get-tuple-element.558) | copy-start | bytes 1376260
  768.5 63.6 %copy-start.146 = (bf16[256,128]{0,1:T(8,128)(2,1)S(1)}, bf16[256,128]{0,1:T(8,128)(2,1)}, u32[]{:S(2)}) copy-start(bf16[256,128]{0,1:T(8,128)(2,1)} %copy-done.145) | copy-start | bytes 196612
  768.6 64.7 %copy-start.115 = (bf16[256,896]{0,1:T(8,128)(2,1)S(1)}, bf16[256,896]{0,1:T(8,128)(2,1)}, u32[]{:S(2)}) copy-start(bf16[256,896]{0,1:T(8,128)(2,1)} %fusion.300) | copy-start | bytes 1376260
  768.6 92.2 %collective-permute-start.3 = (bf16[256,896]{1,0:T(8,128)(2,1)}, bf16[256,896]{1,0:T(8,128)(2,1)S(1)}, u32[]{:S(2)}, u32[]{:S(2)}) collective-permute-start(bf16[256,896]{1,0:T(8,128)(2,1)} %get-tuple-element.499), channel_id=1, source_target_pairs={{16,0},{17,1},{18,2},{19,3},{20,4},{21,5},{22,6},{23,7},{24,8},{25... | collective-permute-start | bytes 1376264 | tf_op jit(solution)/shard_map/ppermute | solution.py:20
  778.2 57.5 %slice-start.23 = ((s8[8716288]{0:T(1024)(128)(4,1)}), s8[327680]{0:T(1024)(128)(4,1)S(1)}, s32[]{:S(2)}) async-start(s8[8716288]{0:T(1024)(128)(4,1)} %bitcast.806), calls=%async_computation.70 | async-start | bytes 655360
  780.1 55.6 %copy-start.223 = (f32[256]{0:T(256)}, f32[256]{0:T(256)S(1)}, u32[]{:S(2)}) copy-start(f32[256]{0:T(256)S(1)} %get-tuple-element.583) | copy-start | bytes 3076
  780.1 55.6 %copy-start.225 = (f32[256]{0:T(256)}, f32[256]{0:T(256)S(1)}, u32[]{:S(2)}) copy-start(f32[256]{0:T(256)S(1)} %get-tuple-element.585) | copy-start | bytes 3076
  780.1 55.6 %copy-start.227 = (f32[256]{0:T(256)}, f32[256]{0:T(256)S(1)}, u32[]{:S(2)}) copy-start(f32[256]{0:T(256)S(1)} %get-tuple-element.497) | copy-start | bytes 3076
  780.1 60.1 %copy-start.10 = (bf16[256,896]{1,0:T(8,128)(2,1)}, bf16[256,896]{1,0:T(8,128)(2,1)S(1)}, u32[]{:S(2)}) copy-start(bf16[256,896]{1,0:T(8,128)(2,1)S(1)} %get-tuple-element.587) | copy-start | bytes 1376260
  840.2 38.2 %slice-start.12 = ((s8[8716288]{0:T(1024)(128)(4,1)}), s8[327680]{0:T(1024)(128)(4,1)S(1)}, s32[]{:S(2)}) async-start(s8[8716288]{0:T(1024)(128)(4,1)} %bitcast.800), calls=%async_computation.59 | async-start | bytes 655360
  883.4 89.4 %copy-start.24 = (f32[256,896]{1,0:T(8,128)}, f32[256,896]{1,0:T(8,128)S(1)}, u32[]{:S(2)}) copy-start(f32[256,896]{1,0:T(8,128)S(1)} %fusion.281) | copy-start | bytes 2752516
  917.9 50.2 %reduce-scatter.37.cloned.1.call-start = ((), (), s32[]{:S(2)}) async-start(), calls=%async_computation.28 | async-start | bytes 327680 | tf_op jit(solution)/shard_map/reduce_scatter | solution.py:207
  931.5 36.6 %copy-start.64 = (bf16[1,896,128]{2,1,0:T(8,128)(2,1)S(1)}, bf16[1,896,128]{2,1,0:T(8,128)(2,1)}, u32[]{:S(2)}) copy-start(bf16[1,896,128]{2,1,0:T(8,128)(2,1)} %copy-done.62) | copy-start | bytes 688132
  931.5 37.8 %copy-start.40 = (bf16[3,1,256,896]{3,2,1,0:T(8,128)(2,1)S(1)}, bf16[3,1,256,896]{3,2,1,0:T(8,128)(2,1)}, u32[]{:S(2)}) copy-start(bf16[3,1,256,896]{3,2,1,0:T(8,128)(2,1)} %param.15) | copy-start | bytes 4128772
  931.5 37.8 %copy-start.219 = (f32[256]{0:T(256)S(1)}, f32[256]{0:T(256)}, u32[]{:S(2)}) copy-start(f32[256]{0:T(256)} %fusion.394) | copy-start | bytes 3076
  931.5 123.1 %reduce-scatter.39.cloned.1.call-start = ((), (), s32[]{:S(2)}) async-start(), calls=%async_computation.29 | async-start | bytes 327680 | tf_op jit(solution)/shard_map/reduce_scatter | solution.py:201
  935.1 37.7 %copy-start.245 = (f32[256]{0:T(256)S(1)}, f32[256]{0:T(256)}, u32[]{:S(2)}) copy-start(f32[256]{0:T(256)} %get-tuple-element.366) | copy-start | bytes 3076
  974.1 7.4 collective-permute-start.4
  1004.5 75.1 %copy-start.22 = (f32[256,896]{1,0:T(8,128)}, f32[256,896]{1,0:T(8,128)S(1)}, u32[]{:S(2)}) copy-start(f32[256,896]{1,0:T(8,128)S(1)} %fusion.283) | copy-start | bytes 2752516
  1038.7 36.8 %reduce-scatter.41.cloned.1.call-start = ((), (), s32[]{:S(2)}) async-start(), calls=%async_computation.30 | async-start | bytes 327680 | tf_op jit(solution)/shard_map/reduce_scatter | solution.py:207
  1052.7 121.0 %reduce-scatter.43.cloned.1.call-start = ((), (), s32[]{:S(2)}) async-start(), calls=%async_computation.31 | async-start | bytes 327680 | tf_op jit(solution)/shard_map/reduce_scatter | solution.py:201
  1080.9 7.7 collective-permute-start.5
  1152.1 37.0 %reduce-scatter.45.cloned.1.call-start = ((), (), s32[]{:S(2)}) async-start(), calls=%async_computation.32 | async-start | bytes 327680 | tf_op jit(solution)/shard_map/reduce_scatter | solution.py:207
  1164.2 212.8 %reduce-scatter.63.cloned.1.call-start = ((), (), s32[]{:S(2)}) async-start(), calls=%async_computation.41 | async-start | bytes 286720
  1170.8 207.8 %reduce-scatter.69.cloned.1.call-start = ((), (), s32[]{:S(2)}) async-start(), calls=%async_computation.44 | async-start | bytes 286720
  1173.7 206.3 %reduce-scatter.65.cloned.1.call-start = ((), (), s32[]{:S(2)}) async-start(), calls=%async_computation.42 | async-start | bytes 40960
  1178.5 202.8 %reduce-scatter.67.cloned.1.call-start = ((), (), s32[]{:S(2)}) async-start(), calls=%async_computation.43 | async-start | bytes 40960
  1191.5 191.1 %reduce-scatter.61.cloned.1.call-start = ((), (), s32[]{:S(2)}) async-start(), calls=%async_computation.40 | async-start | bytes 286720
  1197.9 186.1 %reduce-scatter.49.cloned.1.call-start = ((), (), s32[]{:S(2)}) async-start(), calls=%async_computation.34 | async-start | bytes 286720 | tf_op jit(solution)/shard_map/reduce_scatter | solution.py:466
  1200.1 183.9 %reduce-scatter.51.cloned.1.call-start = ((), (), s32[]{:S(2)}) async-start(), calls=%async_computation.35 | async-start | bytes 286720 | tf_op jit(solution)/shard_map/reduce_scatter | solution.py:466
  1207.6 202.9 %reduce-scatter.47.cloned.1.call-start = ((), (), s32[]{:S(2)}) async-start(), calls=%async_computation.33 | async-start | bytes 2007040 | tf_op jit(solution)/shard_map/reduce_scatter | solution.py:466
  1213.6 231.9 %reduce-scatter.53.cloned.1.call-start = ((), (), s32[]{:S(2)}) async-start(), calls=%async_computation.36 | async-start | bytes 2007040 | tf_op jit(solution)/shard_map/reduce_scatter | solution.py:466
  1236.2 301.9 %reduce-scatter.55.cloned.1.call-start = ((), (), s32[]{:S(2)}) async-start(), calls=%async_computation.37 | async-start | bytes 10895360 | tf_op jit(solution)/shard_map/reduce_scatter | solution.py:466
  1277.2 353.4 %reduce-scatter.57.cloned.1.call-start = ((), (), s32[]{:S(2)}) async-start(), calls=%async_computation.38 | async-start | bytes 10895360 | tf_op jit(solution)/shard_map/reduce_scatter | solution.py:466
  1326.8 396.4 %reduce-scatter.59.cloned.1.call-start = ((), (), s32[]{:S(2)}) async-start(), calls=%async_computation.39 | async-start | bytes 10895360 | tf_op jit(solution)/shard_map/reduce_scatter | solution.py:466
  1376.9 346.2 %copy-start.89 = (f32[256,896]{1,0:T(8,128)S(1)}, f32[256,896]{1,0:T(8,128)}, u32[]{:S(2)}) copy-start(f32[256,896]{1,0:T(8,128)} %copy-done.88) | copy-start | bytes 2752516
  1376.9 383.5 %all-reduce.11.cloned.1.call-start = ((), (), s32[]{:S(2)}) async-start(), calls=%async_computation.45 | async-start | bytes 237568 | tf_op jit(solution)/shard_map/psum | solution.py:474
  1384.1 639.0 %all-reduce.13.cloned.1.call-start = ((), (), s32[]{:S(2)}) async-start(), calls=%async_computation.46 | async-start | bytes 14680064 | tf_op jit(solution)/shard_map/psum | solution.py:474
  (268 other events, 2951.2 us)
Sparse Core Ops, SparseCore 0:
  9.9 35.2 all-gather.5
  47.1 31.7 all-gather.7
  80.7 90.3 all-gather.9
  172.8 90.3 all-gather.11
  264.8 90.3 all-gather.13
  616.4 41.1 reduce-scatter.30
  660.6 34.6 reduce-scatter.32
  918.0 29.1 reduce-scatter.34
  950.2 17.8 reduce-scatter.36
  1038.9 15.7 reduce-scatter.38
  1057.6 17.9 reduce-scatter.40
  1152.2 16.5 reduce-scatter.42
  1171.1 17.9 reduce-scatter.44
  1191.7 23.4 reduce-scatter.62
  1218.0 23.9 reduce-scatter.68
  1245.2 23.5 reduce-scatter.64
  1271.6 23.5 reduce-scatter.66
  1297.8 24.0 reduce-scatter.60
  1324.9 24.0 reduce-scatter.48
  1351.5 24.0 reduce-scatter.50
  1378.9 31.5 reduce-scatter.46
  1414.4 31.1 reduce-scatter.52
  1449.0 89.0 reduce-scatter.54
  1541.4 89.0 reduce-scatter.56
  1634.0 89.0 reduce-scatter.58
  1727.3 33.1 all-reduce.10
  1763.0 260.0 all-reduce.12
where the time goes:
time: 2050 us; the launch traced here: 2040 us
  waiting for transfers between devices  922 us (45%)
  matrix products  559 us (27%)
  blocking collectives  213 us (10%)
  other arithmetic  199 us (10%)
  local copies, waits for them, and re-layouts  104 us (5%)
  starting transfers between devices  25.5 us (1%)
    dot_general x84, matrix products, matmul(): return jnp.dot(left, right, preferred_element_type=jnp.float32)  401 us
    reduce_scatter x7, waiting for transfers between devices, local(): lax.psum_scatter(for_sending(tuple((total[None] for total in totals))), '...  339 us
    psum x2, waiting for transfers between devices, local(): lax.psum(for_sending(tuple(shares)), 'ctx')  279 us
    all_gather x1, waiting for transfers between devices, local(): lax.all_gather(shards[10], 'dp', axis=1, tiled=True)  83.9 us
    all_gather x1, waiting for transfers between devices, local(): lax.all_gather(shards[11], 'dp', axis=1, tiled=True)  82.5 us
    reduce_scatter x4, waiting for transfers between devices, attend_back(): lax.psum_scatter(value_parts.reshape(total_len, width).astype(jnp.bfloat1...  73.5 us
    all_gather x4, blocking collectives, attend_back(): lax.all_gather(value_rows, 'ctx', axis=0, tiled=True)  48.6 us
    all_gather x4, blocking collectives, attend(): lax.all_gather(value_rows, 'ctx', axis=0, tiled=True)  48.3 us
  transfers between devices with their start and end apart: 33, of which 17 were waited for; matrix products, arithmetic and copies ran while one was open for 21% of the time, Pallas kernels for 0%

commit v1 on v0

v1 whole, which is shorter than its diff:
```python
import functools

import jax
import jax.numpy as jnp
from jax import lax
from jax.experimental import pallas as pl
from jax.experimental.pallas import tpu as pltpu
from jax.sharding import PartitionSpec as P

HEAD = 64
rope_base = 1000000.0
norm_eps = 1e-06
masked = -1e30
bf16 = jnp.bfloat16
f32 = jnp.float32


def matmul(left, right):
    return jnp.dot(left, right, preferred_element_type=f32)


def matmul_nt(left, right):
    return lax.dot_general(left, right, (((1,), (1,)), ((), ())), preferred_element_type=f32)


def inverse_rms(values):
    return lax.rsqrt(jnp.mean(values * values, axis=-1, keepdims=True) + norm_eps)


def step_masks(axis):
    size = lax.axis_size(axis)
    assert size & (size - 1) == 0
    ahead = [1 << n for n in range(size.bit_length() - 1)]
    return list(zip(ahead, ahead[::-1] if axis == "dp" else ahead))


def step(block, axis, masks):
    size = lax.axis_size(axis)
    route = [
        (core * size + i, core * size + (i ^ mask))
        for core, mask in enumerate(masks)
        for i in range(size)
    ]
    return lax.ppermute(block, ("section", axis), route)


def gather_parts(rows, axis):
    for masks in step_masks(axis)[:-1]:
        rows = jnp.concatenate([rows, step(rows, axis, masks)])
    return rows, step(rows, axis, step_masks(axis)[-1])


def gather_blocks(rows, axis):
    return jnp.concatenate(gather_parts(rows, axis)).reshape((-1,) + rows.shape)


def scatter_parts(lower, upper, axis):
    masks = step_masks(axis)
    for pair in masks[:0:-1]:
        total = lower.astype(f32) + step(upper.astype(bf16), axis, pair).astype(f32)
        half = total.shape[0] // 2
        lower, upper = total[:half], total[half:]
    return lower.astype(f32), step(upper.astype(bf16), axis, masks[0])


def reorder(blocks, axis, back=False):
    me = lax.axis_index(axis)
    masks = step_masks(axis)

    def moved(i, core):
        if back:
            return sum(pair[core] for n, pair in enumerate(masks) if i & (1 << n)) ^ me
        return sum(
            jnp.where(((me ^ i) & pair[core]) != 0, 1 << n, 0) for n, pair in enumerate(masks)
        )

    places = [by_section(moved(i, 0), moved(i, 1)) for i in range(blocks.shape[0])]
    return jnp.stack([lax.dynamic_index_in_dim(blocks, place, 0, False) for place in places])


def exchange(blocks, axis):
    blocks = reorder(blocks, axis, back=True)
    count = blocks.shape[0]
    for n, masks in enumerate(step_masks(axis)):
        cut = blocks.reshape((count >> (n + 1), 2, 1 << n) + blocks.shape[1:])
        got = step(cut[:, 1], axis, masks)
        blocks = jnp.stack([cut[:, 0], got], axis=1).reshape(blocks.shape)
    return reorder(blocks, axis)


def other(block):
    return lax.ppermute(block, "section", [(0, 1), (1, 0)])


def by_section(first, second):
    return jnp.where(lax.axis_index("section") == 0, first, second)


def both(mine, axis):
    theirs = other(mine)
    return by_section(jnp.stack([mine, theirs], axis), jnp.stack([theirs, mine], axis))


def after(value, first):
    return lax.optimization_barrier((value, first))[0]


def tables(starts, places):
    begins = jnp.max(jnp.where(starts[None, :] <= places[:, None], starts[None, :], 0), axis=1)
    offsets = (places - begins).astype(f32)
    frequency = rope_base ** (-jnp.arange(0, HEAD, 2, dtype=f32) / HEAD)
    angles = offsets[:, None] * frequency[None, :]
    sines = jnp.sin(angles)
    cos_table = jnp.tile(jnp.cos(angles), (1, lanes * 2 // HEAD))
    sin_table = jnp.tile(jnp.concatenate([-sines, sines], axis=1), (1, lanes // HEAD))
    return (begins, cos_table, sin_table)


vmem_bytes = 56 * 1024 * 1024
lanes = 128


def call(kernel, outs, args, scratch=(), flops=0, grid=None, in_specs=None, out_specs=None):
    moved = sum(a.size * a.dtype.itemsize for a in args)
    moved += sum(o.size * o.dtype.itemsize for o in outs)
    whole = pl.BlockSpec(memory_space=pltpu.VMEM)
    return pl.pallas_call(
        kernel,
        out_shape=outs,
        grid=grid or (),
        in_specs=in_specs or [whole] * len(args),
        out_specs=out_specs or [whole] * len(outs),
        scratch_shapes=scratch,
        cost_estimate=pl.CostEstimate(flops=int(flops), bytes_accessed=int(moved), transcendentals=0),
        compiler_params=pltpu.CompilerParams(vmem_limit_bytes=vmem_bytes),
    )(*args)


def shape(rows, columns, kind):
    return jax.ShapeDtypeStruct((rows, columns), kind)


def lane_of(block):
    return lax.broadcasted_iota(jnp.int32, block.shape, 1)


def turn(block, cos_table, sin_table):
    quarter = HEAD // 2
    first = lax.rem(lane_of(block), HEAD) < quarter
    turned = jnp.where(first, pltpu.roll(block, lanes - quarter, 1), pltpu.roll(block, quarter, 1))
    return block * cos_table + turned * sin_table


def qkv_kernel(x_ref, gain_ref, w_ref, bias_ref, cos_ref, sin_ref, normed_ref, q_ref, kv_ref):
    x = x_ref[...].astype(f32)
    normed = (x * inverse_rms(x) * gain_ref[...]).astype(bf16)
    normed_ref[...] = normed
    cos_table, sin_table = cos_ref[...], sin_ref[...]
    rows = matmul(normed, w_ref[...]) + bias_ref[...]
    query_width = q_ref.shape[1]
    key_end = query_width + kv_ref.shape[1] // 2
    for start in range(0, rows.shape[1], lanes):
        block = rows[:, start : start + lanes]
        if start < key_end:
            block = turn(block, cos_table, sin_table)
        if start < query_width:
            q_ref[:, start : start + lanes] = block.astype(bf16)
        else:
            kv_ref[:, start - query_width : start - query_width + lanes] = block.astype(bf16)


def qkv_rows(x, p, cos_table, sin_table, kv_width):
    rows, width = x.shape
    total = p["qkv"].shape[1]
    query_width = total - 2 * kv_width
    return call(
        qkv_kernel,
        [shape(rows, width, bf16), shape(rows, query_width, bf16), shape(rows, 2 * kv_width, bf16)],
        [x, p["gain_one"], p["qkv"], p["bias"], cos_table, sin_table],
        flops=2 * rows * width * total,
    )


def variants(block):
    swapped = pltpu.roll(block, HEAD, 1)
    low = lane_of(block) < HEAD
    return jnp.where(low, block, swapped), block, jnp.where(low, swapped, block)


def pair_rows(block):
    low = lane_of(block) < HEAD
    return jnp.concatenate([jnp.where(low, block, 0.0), jnp.where(low, 0.0, block)]).astype(bf16)


def pair_columns(block):
    count = block.shape[1] // 2
    return jnp.concatenate([block[:HEAD, :count], block[HEAD:, count:]]).T


def head_kind(pair, group):
    return lax.div(2 * pair, group) + lax.div(2 * pair + 1, group)


def pair_probs(keys, query_pair, bias):
    scores = matmul_nt(keys, query_pair) + jnp.concatenate([bias, bias], axis=1)
    terms = jnp.exp(scores - jnp.max(scores, axis=0, keepdims=True))
    return terms * (1.0 / jnp.sum(terms, axis=0, keepdims=True))


def attend_kernel(
    group,
    q_ref,
    kva_ref,
    kvb_ref,
    bias_ref,
    x_ref,
    wo_ref,
    gain_ref,
    att_ref,
    res_ref,
    mix_ref,
    keys,
    values,
):
    count = kva_ref.shape[0]
    for i, ref in enumerate((kva_ref, kvb_ref)):
        part = slice(i * count, (i + 1) * count)
        for kind, block in enumerate(variants(ref[:, :lanes].astype(f32))):
            keys[kind, part, :] = block.astype(bf16)
        turned = ref[:, lanes:].astype(f32).T.astype(bf16)
        low, high = turned[:HEAD], turned[HEAD:]
        for kind, (one, two) in enumerate(((low, low), (low, high), (high, high))):
            values[kind, :HEAD, part] = one
            values[kind, HEAD:, part] = two

    @pl.loop(0, q_ref.shape[1] // lanes)
    def _(pair):
        place = pl.ds(pl.multiple_of(pair * lanes, lanes), lanes)
        kind = head_kind(pair, group)
        query_pair = pair_rows(q_ref[:, place].astype(f32) * HEAD**-0.5)
        probs = pair_probs(keys[kind], query_pair, bias_ref[...]).astype(bf16)
        att_ref[:, place] = pair_columns(matmul(values[kind], probs)).astype(bf16)

    residual = x_ref[...].astype(f32) + matmul(att_ref[...], wo_ref[...])
    res_ref[...] = residual
    mix_ref[...] = (residual * inverse_rms(residual) * gain_ref[...]).astype(bf16)


def attend(queries, kva, kvb, bias, x, p):
    rows, width = queries.shape
    total = bias.shape[0]
    kv_width = kva.shape[1] // 2
    group = width // kv_width
    flops = 4 * rows * total * width * 4 + 2 * rows * width * x.shape[1]
    return call(
        functools.partial(attend_kernel, group),
        [shape(rows, width, bf16), shape(*x.shape, f32), shape(*x.shape, bf16)],
        [queries, kva, kvb, bias, x, p["out"], p["gain_two"]],
        scratch=[pltpu.VMEM((3, total, lanes), bf16), pltpu.VMEM((3, lanes, total), bf16)],
        flops=flops,
    )


def norm_back(values, gain, grad):
    inverse = inverse_rms(values)
    unit = values * inverse
    scaled = grad * gain
    back = inverse * (scaled - unit * jnp.mean(scaled * unit, axis=-1, keepdims=True))
    return back, jnp.sum(grad * unit, axis=0, keepdims=True)


def attend_back_kernel(
    group,
    q_ref,
    kva_ref,
    kvb_ref,
    bias_ref,
    mix_low_ref,
    mix_got_ref,
    res_ref,
    gain_ref,
    up_ref,
    wo_ref,
    cos_ref,
    sin_ref,
    dq_ref,
    dkva_ref,
    dkvb_ref,
    gres_ref,
    gatt_ref,
    gain_two_ref,
    keys,
    values,
    keys_turned,
    grad_keys,
    grad_values,
    grad_out,
):
    count = kva_ref.shape[0]
    for i, ref in enumerate((kva_ref, kvb_ref)):
        part = slice(i * count, (i + 1) * count)
        key_block = ref[:, :lanes].astype(f32)
        for kind, block in enumerate(variants(key_block)):
            keys[kind, part, :] = block.astype(bf16)
        for kind, block in enumerate(variants(ref[:, lanes:].astype(f32))):
            values[kind, part, :] = block.astype(bf16)
        turned = key_block.T.astype(bf16)
        low, high = turned[:HEAD], turned[HEAD:]
        for kind, (one, two) in enumerate(((low, low), (low, high), (high, high))):
            keys_turned[kind, :HEAD, part] = one
            keys_turned[kind, HEAD:, part] = two

    grad_mixing = mix_low_ref[...] + mix_got_ref[...].astype(f32)
    back, gain_two = norm_back(res_ref[...], gain_ref[...], grad_mixing)
    gain_two_ref[...] = gain_two
    grad_residual = up_ref[...] + back
    gres_ref[...] = grad_residual
    grad_attended = grad_residual.astype(bf16)
    gatt_ref[...] = grad_attended
    grad_out[...] = matmul_nt(grad_attended, wo_ref[...]).astype(bf16)
    grad_keys[...] = jnp.zeros_like(grad_keys)
    grad_values[...] = jnp.zeros_like(grad_values)

    @pl.loop(0, q_ref.shape[1] // lanes)
    def _(pair):
        place = pl.ds(pl.multiple_of(pair * lanes, lanes), lanes)
        kind = head_kind(pair, group)
        query_pair = pair_rows(q_ref[:, place].astype(f32) * HEAD**-0.5)
        out_pair = pair_rows(grad_out[:, place].astype(f32))
        probs = pair_probs(keys[kind], query_pair, bias_ref[...])
        grad_values[kind] += matmul(probs.astype(bf16), out_pair)
        grad_probs = matmul_nt(values[kind], out_pair)
        delta = jnp.sum(probs * grad_probs, axis=0, keepdims=True)
        grad_scores = (probs * (grad_probs - delta)).astype(bf16)
        grad_keys[kind] += matmul(grad_scores, query_pair)
        grad_query = pair_columns(matmul(keys_turned[kind], grad_scores)) * HEAD**-0.5
        dq_ref[:, place] = turn(grad_query, cos_ref[...], -sin_ref[...]).astype(bf16)

    for i, ref in enumerate((dkva_ref, dkvb_ref)):
        part = slice(i * count, (i + 1) * count)
        for n, sums in enumerate((grad_keys, grad_values)):
            first, mixed, second = sums[0, part, :], sums[1, part, :], sums[2, part, :]
            first = first + pltpu.roll(first, HEAD, 1)
            second = second + pltpu.roll(second, HEAD, 1)
            folded = mixed + jnp.where(lane_of(mixed) < HEAD, first, second)
            ref[:, n * lanes : (n + 1) * lanes] = folded.astype(bf16)


def attend_back(
    queries, kva, kvb, bias, mix_low, mix_got, residual, upstream, p, cos_table, sin_table
):
    rows, width = queries.shape
    total = bias.shape[0]
    kv_width = kva.shape[1] // 2
    group = width // kv_width
    flops = 10 * rows * total * width * 3 + 2 * rows * width * residual.shape[1]
    return call(
        functools.partial(attend_back_kernel, group),
        [
            shape(rows, width, bf16),
            shape(*kva.shape, bf16),
            shape(*kvb.shape, bf16),
            shape(*residual.shape, f32),
            shape(*residual.shape, bf16),
            shape(1, residual.shape[1], f32),
        ],
        [
            queries,
            kva,
            kvb,
            bias,
            mix_low,
            mix_got,
            residual,
            p["gain_two"],
            upstream,
            p["out"],
            cos_table,
            sin_table,
        ],
        scratch=[
            pltpu.VMEM((3, total, lanes), bf16),
            pltpu.VMEM((3, total, lanes), bf16),
            pltpu.VMEM((3, lanes, total), bf16),
            pltpu.VMEM((3, total, lanes), f32),
            pltpu.VMEM((3, total, lanes), f32),
            pltpu.VMEM((rows, width), bf16),
        ],
        flops=flops,
    )


def qkv_back_kernel(
    dq_ref,
    low_ref,
    got_ref,
    cos_ref,
    sin_ref,
    w_ref,
    x_ref,
    gain_ref,
    gres_ref,
    dqkv_ref,
    gin_ref,
    gin_low_ref,
    gain_one_ref,
    bias_ref,
):
    query_width = dq_ref.shape[1]
    grad_kv = low_ref[...] + got_ref[...].astype(f32)
    dqkv_ref[:, :query_width] = dq_ref[...]
    grad_key = turn(grad_kv[:, :lanes], cos_ref[...], -sin_ref[...])
    dqkv_ref[:, query_width : query_width + lanes] = grad_key.astype(bf16)
    dqkv_ref[:, query_width + lanes :] = grad_kv[:, lanes:].astype(bf16)
    dqkv = dqkv_ref[...]
    bias_ref[...] = jnp.sum(dqkv.astype(f32), axis=0, keepdims=True)
    grad_normed = matmul_nt(dqkv, w_ref[...])
    back, gain_one = norm_back(x_ref[...].astype(f32), gain_ref[...], grad_normed)
    gain_one_ref[...] = gain_one
    grad_in = gres_ref[...] + back
    gin_ref[...] = grad_in
    gin_low_ref[...] = grad_in.astype(bf16)


def qkv_back(dq, low, got, x, grad_residual, p, cos_table, sin_table):
    rows, width = x.shape
    total = p["qkv"].shape[1]
    return call(
        qkv_back_kernel,
        [
            shape(rows, total, bf16),
            shape(rows, width, f32),
            shape(rows, width, bf16),
            shape(1, width, f32),
            shape(1, total, f32),
        ],
        [dq, low, got, cos_table, sin_table, p["qkv"], x, p["gain_one"], grad_residual],
        flops=2 * rows * width * total,
    )


def chunk_of(size):
    return 256 if size % 256 == 0 else 128


def ffn_kernel(lower_ref, upper_ref, wg_ref, wu_ref, wd_ref, low_ref, up_ref, hid_ref, g_ref, u_ref, rows, total):
    n = pl.program_id(0)
    half = lower_ref.shape[0]

    @pl.when(n == 0)
    def _():
        rows[:half] = lower_ref[...]
        rows[half:] = upper_ref[...]
        total[...] = jnp.zeros_like(total)

    gate = matmul(rows[...], wg_ref[...])
    up = matmul(rows[...], wu_ref[...])
    hidden = (gate * (1.0 / (1.0 + jnp.exp(-gate))) * up).astype(bf16)
    hid_ref[...] = hidden
    g_ref[...] = gate.astype(bf16)
    u_ref[...] = up.astype(bf16)
    total[...] += matmul(hidden, wd_ref[...])

    @pl.when(n == pl.num_programs(0) - 1)
    def _():
        low_ref[...] = total[:half].astype(bf16)
        up_ref[...] = total[half:].astype(bf16)


def ffn(lower, upper, p):
    half, width = lower.shape
    wide = p["gate"].shape[1]
    chunk = chunk_of(wide)
    rows = half + upper.shape[0]
    whole = pl.BlockSpec((half, width), lambda n: (0, 0))
    columns = pl.BlockSpec((width, chunk), lambda n: (0, n))
    return call(
        ffn_kernel,
        [shape(half, width, bf16), shape(rows - half, width, bf16)] + [shape(rows, wide, bf16)] * 3,
        [lower, upper, p["gate"], p["up"], p["down"]],
        scratch=[pltpu.VMEM((rows, width), bf16), pltpu.VMEM((rows, width), f32)],
        flops=6 * rows * width * wide,
        grid=(wide // chunk,),
        in_specs=[whole, whole, columns, columns, pl.BlockSpec((chunk, width), lambda n: (n, 0))],
        out_specs=[whole, whole] + [pl.BlockSpec((rows, chunk), lambda n: (0, n))] * 3,
    )


def ffn_back_kernel(
    lower_ref, upper_ref, g_ref, u_ref, wg_ref, wu_ref, wd_ref, low_ref, up_ref, gg_ref, gu_ref, rows, total
):
    n = pl.program_id(0)
    half = lower_ref.shape[0]

    @pl.when(n == 0)
    def _():
        rows[:half] = lower_ref[...]
        rows[half:] = upper_ref[...]
        total[...] = jnp.zeros_like(total)

    grad_hidden = matmul_nt(rows[...], wd_ref[...])
    gate = g_ref[...].astype(f32)
    up = u_ref[...].astype(f32)
    sigmoid = 1.0 / (1.0 + jnp.exp(-gate))
    grad_up = (grad_hidden * gate * sigmoid).astype(bf16)
    grad_gate = (grad_hidden * up * sigmoid * (1.0 + gate * (1.0 - sigmoid))).astype(bf16)
    gg_ref[...] = grad_gate
    gu_ref[...] = grad_up
    total[...] += matmul_nt(grad_gate, wg_ref[...]) + matmul_nt(grad_up, wu_ref[...])

    @pl.when(n == pl.num_programs(0) - 1)
    def _():
        low_ref[...] = total[:half].astype(bf16)
        up_ref[...] = total[half:].astype(bf16)


def ffn_back(lower, upper, gate, up, p):
    half, width = lower.shape
    wide = p["gate"].shape[1]
    chunk = chunk_of(wide)
    rows = half + upper.shape[0]
    whole = pl.BlockSpec((half, width), lambda n: (0, 0))
    columns = pl.BlockSpec((width, chunk), lambda n: (0, n))
    inner = pl.BlockSpec((rows, chunk), lambda n: (0, n))
    return call(
        ffn_back_kernel,
        [shape(half, width, bf16), shape(rows - half, width, bf16)] + [shape(rows, wide, bf16)] * 2,
        [lower, upper, gate, up, p["gate"], p["up"], p["down"]],
        scratch=[pltpu.VMEM((rows, width), bf16), pltpu.VMEM((rows, width), f32)],
        flops=6 * rows * width * wide,
        grid=(wide // chunk,),
        in_specs=[
            whole,
            whole,
            inner,
            inner,
            columns,
            columns,
            pl.BlockSpec((chunk, width), lambda n: (n, 0)),
        ],
        out_specs=[whole, whole, inner, inner],
    )


def product_kernel(count, turn_once, *refs):
    lefts, rights = refs[:count], refs[count:-2]
    out_ref, turned = refs[-2:]

    def fill():
        start = 0
        for ref in lefts:
            turned[:, start : start + ref.shape[0]] = ref[...].T
            start += ref.shape[0]

    if turn_once:
        pl.when(pl.program_id(0) == 0)(fill)
    else:
        fill()
    right = jnp.concatenate([ref[...] for ref in rights])
    out_ref[...] = matmul(turned[...], right).astype(out_ref.dtype)


def product_over_rows(lefts, rights):
    depth = sum(left.shape[0] for left in lefts)
    height, width = lefts[0].shape[1], rights[0].shape[1]
    by_columns = width % 256 == 0 or height % 256 != 0
    if by_columns:
        chunk = 256 if width % 256 == 0 else (384 if width % 384 == 0 else width)
        grid = (width // chunk,)
        left_specs = [pl.BlockSpec(left.shape, lambda n: (0, 0)) for left in lefts]
        right_specs = [pl.BlockSpec((r.shape[0], chunk), lambda n: (0, n)) for r in rights]
        out_spec = pl.BlockSpec((height, chunk), lambda n: (0, n))
        turned = pltpu.VMEM((height, depth), bf16)
    else:
        chunk = 256
        grid = (height // chunk,)
        left_specs = [pl.BlockSpec((left.shape[0], chunk), lambda n: (0, n)) for left in lefts]
        right_specs = [pl.BlockSpec(r.shape, lambda n: (0, 0)) for r in rights]
        out_spec = pl.BlockSpec((chunk, width), lambda n: (n, 0))
        turned = pltpu.VMEM((chunk, depth), bf16)
    return call(
        functools.partial(product_kernel, len(lefts), by_columns),
        [shape(height, width, bf16)],
        list(lefts) + list(rights),
        scratch=[turned],
        flops=2 * depth * height * width,
        grid=grid,
        in_specs=left_specs + right_specs,
        out_specs=[out_spec],
    )[0]


def local(
    tokens,
    doc_starts,
    cotangent,
    norm_one,
    w_query,
    b_query,
    w_key,
    b_key,
    w_value,
    b_value,
    w_out,
    norm_two,
    w_gate,
    w_up,
    w_down,
):
    core = lax.axis_index("section")
    cores = lax.axis_size("section")
    spread = lax.axis_size("dp")
    micro_count, _, row_count, width = tokens.shape
    layers = range(2)
    share = row_count // cores
    shard = w_query.shape[1]
    half = shard // 2
    query_width = w_query.shape[2]
    kv_width = w_key.shape[2]
    ff = w_gate.shape[2]
    slice_ff = ff // spread

    def column(vector):
        return jnp.pad(vector, (0, shard - vector.shape[0]))

    vectors = jnp.stack(
        [norm_one[0], norm_two[0], b_query[0], column(b_key[0]), column(b_value[0])], axis=1
    )
    vectors = jnp.pad(vectors, ((0, 0), (0, lanes - vectors.shape[1])))
    attn_own = jnp.concatenate([w_query[0], w_key[0], w_value[0], w_out[0], vectors], axis=1)

    def halves(own):
        middle = own.shape[0] // 2
        low, high = own[:middle], own[middle:]
        got = other(by_section(high, low))
        return by_section(low, got), by_section(got, high)

    def whole(part):
        return both(part, 1).reshape(-1, part.shape[-1])

    def columns_of(part):
        return part.reshape(half, spread, slice_ff).transpose(1, 0, 2)

    wide = -(-slice_ff // lanes) * lanes

    def widen(full, axis):
        pads = [(0, 0), (0, 0)]
        pads[axis] = (0, wide - slice_ff)
        return jnp.pad(full, pads)

    attn_halves = halves(attn_own)
    gate_halves = halves(w_gate[0])
    up_halves = halves(w_up[0])
    attn_full, gate_full, up_full = [], [], []
    for layer in layers:
        part = attn_halves[layer]
        if layer:
            part = after(part, gate_full[layer - 1])
        attn_full.append(whole(reorder(gather_blocks(part, "dp"), "dp")))
        parts = [columns_of(halves_of[layer]) for halves_of in (gate_halves, up_halves)]
        parts = after(jnp.concatenate(parts, axis=1), attn_full[layer])
        parts = exchange(parts, "dp")
        gate_full.append(whole(parts[:, :half]))
        up_full.append(whole(parts[:, half:]))
    down_other = other(w_down[0])
    down_full = [by_section(w_down[0], down_other), by_section(down_other, w_down[0])]

    params = []
    for layer in layers:
        full = attn_full[layer]
        edge = query_width + 2 * kv_width
        small = full[:, edge + width :].astype(f32).reshape(spread, shard, lanes)
        per = kv_width // spread
        bias = jnp.concatenate(
            [
                small[:, :, 2].reshape(-1),
                small[:, :per, 3].reshape(-1),
                small[:, :per, 4].reshape(-1),
            ]
        )
        params.append(
            dict(
                qkv=full[:, :edge],
                out=full[:, edge : edge + width],
                gain_one=small[:, :, 0].reshape(1, -1),
                gain_two=small[:, :, 1].reshape(1, -1),
                bias=bias[None],
                gate=widen(gate_full[layer], 1),
                up=widen(up_full[layer], 1),
                down=widen(down_full[layer], 0),
            )
        )

    first = core * share
    place = lax.axis_index("ctx")
    places = place * row_count + first + jnp.arange(share, dtype=jnp.int32)
    my_tokens = lax.dynamic_slice_in_dim(tokens[:, 0], first, share, 1)
    my_cotangent = lax.dynamic_slice_in_dim(cotangent[:, 0], first, share, 1)
    key_places = jnp.concatenate(
        [
            (place ^ block) * row_count + whose * share + jnp.arange(share, dtype=jnp.int32)
            for whose in (core, 1 - core)
            for block in range(lax.axis_size("ctx"))
        ]
    )

    context = []
    for micro in range(micro_count):
        begins, cos_table, sin_table = tables(doc_starts[micro, 0], places)
        visible = (key_places[:, None] <= places[None, :]) & (
            key_places[:, None] >= begins[None, :]
        )
        context.append((jnp.where(visible, 0.0, masked).astype(f32), cos_table, sin_table))

    kept = [[None] * micro_count for _ in layers]
    rows_in = [my_tokens[micro] for micro in range(micro_count)]
    outputs = []
    for layer in layers:
        p = params[layer]
        results = []
        for micro in range(micro_count):
            bias, cos_table, sin_table = context[micro]
            x = rows_in[micro]
            normed, queries, kv = qkv_rows(x, p, cos_table, sin_table, kv_width)
            kva = jnp.concatenate(gather_parts(kv, "ctx"))
            kvb = other(kva)
            attended, residual, mixing = attend(queries, kva, kvb, bias, x, p)
            lower, upper = gather_parts(mixing, "dp")
            part_low, part_up, hidden, gate, up = ffn(lower, upper, p)
            low, got = scatter_parts(part_low, part_up, "dp")
            results.append((residual + low + got.astype(f32)).astype(bf16))
            kept[layer][micro] = dict(
                x=x,
                normed=normed,
                queries=queries,
                kva=kva,
                kvb=kvb,
                attended=attended,
                residual=residual,
                mixing=(lower, upper),
                hidden=hidden,
                gate=gate,
                up=up,
            )
        outputs.append(jnp.stack(results))
        rows_in = results

    section_out = both_rows(outputs)

    upstream = [(my_cotangent[n].astype(f32), my_cotangent[n]) for n in range(micro_count)]
    grads_in = [None, None]
    final = [None, None]
    for layer in reversed(layers):
        p = params[layer]
        results = []
        for micro in range(micro_count):
            bias, cos_table, sin_table = context[micro]
            k = kept[layer][micro]
            above, above_low = upstream[micro]
            k["grad_ffn"] = gather_parts(above_low, "dp")
            part_low, part_up, k["grad_gate"], k["grad_up"] = ffn_back(
                *k["grad_ffn"], k["gate"], k["up"], p
            )
            low, got = scatter_parts(part_low, part_up, "dp")
            dq, dkva, dkvb, grad_residual, k["grad_attended"], k["gain_two"] = attend_back(
                k["queries"],
                k["kva"],
                k["kvb"],
                bias,
                low,
                got,
                k["residual"],
                above,
                p,
                cos_table,
                sin_table,
            )
            pair = dkva.astype(f32) + other(dkvb).astype(f32)
            middle = pair.shape[0] // 2
            low, got = scatter_parts(pair[:middle], pair[middle:], "ctx")
            k["grad_qkv"], grad_in, grad_low, k["gain_one"], k["bias"] = qkv_back(
                dq, low, got, k["x"], grad_residual, p, cos_table, sin_table
            )
            results.append((grad_in, grad_low))
        upstream = results
        grads_in[layer] = jnp.stack([grad_in for grad_in, _ in results])
        parts = weight_grads(kept[layer], spread, shard, kv_width, query_width, width, slice_ff)
        if final[1] is not None:
            parts = after(parts, final[1])
        final[layer] = lax.psum(parts, "ctx")

    section_grad = both_rows(grads_in)

    from_zero = [lax.ppermute(part, "section", [(0, 1)]) for part in final[1]]
    from_one = [lax.ppermute(part, "section", [(1, 0)]) for part in final[0]]
    attn, gate, up, down = [
        jnp.concatenate([by_section(a0, r1), by_section(r0, a1)], axis=0).astype(f32)
        for a0, a1, r0, r1 in zip(final[0], final[1], from_one, from_zero)
    ]
    edge = query_width + 2 * kv_width
    per = kv_width // spread
    small = attn[:, edge + width :]
    return (
        section_out,
        section_grad,
        small[None, :, 0],
        attn[None, :, :query_width],
        small[None, :, 2],
        attn[None, :, query_width : query_width + kv_width],
        small[None, :per, 3],
        attn[None, :, query_width + kv_width : edge],
        small[None, :per, 4],
        attn[None, :, edge : edge + width],
        small[None, :, 1],
        gate[None],
        up[None],
        down[None],
    )


def both_rows(per_layer):
    first, second = per_layer
    got = other(by_section(second, first))
    return by_section(
        jnp.concatenate([first, got], axis=1), jnp.concatenate([got, second], axis=1)
    )[None, :, None]


def weight_grads(kept, spread, shard, kv_width, query_width, width, slice_ff):
    def column_of(name):
        return [k[name] for k in kept]

    def parts_of(name):
        return [part for k in kept for part in k[name]]

    half = shard // 2

    def split(part):
        mine = by_section(part[:, :half], part[:, half:])
        theirs = by_section(part[:, half:], part[:, :half])
        return (mine.astype(f32) + other(theirs).astype(f32)).astype(bf16)

    down = product_over_rows(column_of("hidden"), parts_of("grad_ffn"))[:slice_ff]
    middle = slice_ff // 2
    mine = by_section(down[:middle], down[middle:])
    theirs = by_section(down[middle:], down[:middle])
    down = (mine.astype(f32) + other(theirs).astype(f32)).astype(bf16)

    def columns(name):
        part = product_over_rows(parts_of("mixing"), column_of(name))[:, :slice_ff]
        return split(part.reshape(spread, shard, slice_ff))

    part = exchange(jnp.concatenate([columns("grad_gate"), columns("grad_up")], axis=1), "dp")
    part = part.reshape(spread, 2, half, slice_ff).transpose(1, 2, 0, 3)
    gate, up = part.reshape(2, half, spread * slice_ff)

    qkv = product_over_rows(column_of("normed"), column_of("grad_qkv"))
    out = product_over_rows(column_of("attended"), column_of("grad_attended"))
    bias = sum(column_of("bias"))[0]
    per = kv_width // spread

    def column(vector):
        return jnp.pad(vector.reshape(spread, -1), ((0, 0), (0, shard - per))).reshape(-1)

    vectors = jnp.stack(
        [
            sum(column_of("gain_one"))[0],
            sum(column_of("gain_two"))[0],
            bias[:query_width],
            column(bias[query_width : query_width + kv_width]),
            column(bias[query_width + kv_width :]),
        ],
        axis=1,
    )
    vectors = jnp.pad(vectors, ((0, 0), (0, lanes - vectors.shape[1])))
    attn = jnp.concatenate([qkv, out, vectors.astype(bf16)], axis=1)
    attn = split(attn.reshape(spread, shard, -1))
    attn = reorder(attn, "dp", back=True).reshape(spread * half, -1)
    low, got = scatter_parts(*jnp.split(attn, 2), "dp")
    attn = (low + got.astype(f32)).astype(bf16)
    return attn, gate, up, down


def solution(mesh):
    return jax.shard_map(
        local,
        mesh=mesh,
        in_specs=(
            P(None, "dp", "ctx", None),
            P(None, "dp", None),
            P(None, "dp", "ctx", None),
            P("section", "dp"),
            P("section", "dp", None),
            P("section", "dp"),
            P("section", "dp", None),
            P("section", "dp"),
            P("section", "dp", None),
            P("section", "dp"),
            P("section", "dp", None),
            P("section", "dp"),
            P("section", "dp", None),
            P("section", "dp", None),
            P("section", "dp", None),
        ),
        out_specs=(
            P("section", None, "dp", "ctx", None),
            P("section", None, "dp", "ctx", None),
            P("section", "dp"),
            P("section", "dp", None),
            P("section", "dp"),
            P("section", "dp", None),
            P("section", "dp"),
            P("section", "dp", None),
            P("section", "dp"),
            P("section", "dp", None),
            P("section", "dp"),
            P("section", "dp", None),
            P("section", "dp", None),
            P("section", "dp", None),
        ),
        check_vma=False,
    )
```

time: 2050 us -> 1200 us (0.59)
  waiting for transfers between devices: 922 us -> 359 us
  matrix products: 559 us -> 0 us
  Pallas kernels: 0 us -> 389 us
  blocking collectives: 213 us -> 0 us
  starting transfers between devices: 25.5 us -> 132 us
  other arithmetic: 199 us -> 149 us
  local copies, waits for them, and re-layouts: 104 us -> 151 us
    dot_general x112 -> x0, matrix products: 559 us -> none  [the longest x84 401 us: matmul(): return jnp.dot(left, right, preferred_element_type=jnp.float32)]
    reduce_scatter x15 -> x0, waiting for transfers between devices: 433 us -> none  [the longest x7 339 us: local(): lax.psum_scatter(for_sending(tuple((total[None] for total in totals))), '...]
    pallas_call x0 -> x46, Pallas kernels: none -> 389 us  [call(): pl.pallas_call(kernel, out_shape=outs, grid=grid or (), in_specs=in_specs...]
    all_gather x5 -> x0, waiting for transfers between devices: 207 us -> none  [the longest x1 83.9 us: local(): lax.all_gather(shards[10], 'dp', axis=1, tiled=True)]
    all_gather x18 -> x0, blocking collectives: 204 us -> none  [the longest x4 48.6 us: attend_back(): lax.all_gather(value_rows, 'ctx', axis=0, tiled=True)]
    ppermute x6 -> x128, waiting for transfers between devices: 0.02 us -> 139 us  [the longest x88 136 us: step(): return lax.ppermute(block, ('section', axis), route)]
    ppermute x6 -> x128, starting transfers between devices: 22.9 us -> 131 us  [the longest x88 75.8 us: step(): return lax.ppermute(block, ('section', axis), route)]
    psum x2, waiting for transfers between devices: 279 us -> 220 us  [local(): final[layer] = lax.psum(parts, 'ctx')]
  transfers between devices with their start and end apart: 33 -> 130, of which waited for: 17 -> 30; matrix products, arithmetic and copies ran while one was open for 21% -> 23% of each run, Pallas kernels for 0% -> 33%
where the time goes in v1:
time: 1200 us
  Pallas kernels  389 us (32%)
  waiting for transfers between devices  359 us (30%)
  local copies, waits for them, and re-layouts  151 us (13%)
  other arithmetic  149 us (12%)
  starting transfers between devices  132 us (11%)
  between operations  16.9 us (1%)
    pallas_call x46, Pallas kernels, call(): pl.pallas_call(kernel, out_shape=outs, grid=grid or (), in_specs=in_specs...  389 us
    psum x2, waiting for transfers between devices, local(): final[layer] = lax.psum(parts, 'ctx')  220 us
    ppermute x88, waiting for transfers between devices, step(): return lax.ppermute(block, ('section', axis), route)  136 us
    ppermute x88, starting transfers between devices, step(): return lax.ppermute(block, ('section', axis), route)  75.8 us
    unnamed x330, local copies, waits for them, and re-layouts  45.3 us
    ppermute x32, starting transfers between devices, other(): return lax.ppermute(block, 'section', [(0, 1), (1, 0)])  43.4 us
    select_n x23, other arithmetic, by_section(): return jnp.where(lax.axis_index('section') == 0, first, second)  41.7 us
    another operation x12, other arithmetic, reorder(): jnp.stack([lax.dynamic_index_in_dim(blocks, place, 0, False) for place in...  25.6 us
  transfers between devices with their start and end apart: 130, of which 30 were waited for; matrix products, arithmetic and copies ran while one was open for 23% of the time, Pallas kernels for 33%

profile of v1, /device:TPU:1, one launch (start us, length us, event | category | flops | bytes accessed | tf_op | source)
XLA Modules:
  0.0 1196.5 jit_solution(16060630608704756665)
XLA Ops:
  27.9 6.2 collective-permute-done.1
  38.5 11.2 collective-permute-done.2
  69.7 4.4 maximum_select_fusion
  74.2 4.8 constant_dynamic-slice_fusion.35
  78.9 6.5 pad_maximum_fusion.1
  85.4 4.8 reshape.546
  90.2 4.2 fusion.52
  157.9 8.2 collective-permute-done.5
  169.6 10.5 shard_map.255
  180.9 10.2 shard_map.258
  199.1 10.2 shard_map.261
  222.5 14.8 %collective-permute-done.29.upper_ref.refs_5_ = bf16[256,896]{1,0:T(8,128)(2,1)S(1)} collective-permute-done((bf16[256,896]{1,0:T(8,128)(2,1)S(1)}, bf16[256,896]{1,0:T(8,128)(2,1)S(1)}, u32[]{:S(2)}, u32[]{:S(2)}) %collective-permute-start.29) | collective-permute-done | bytes 458784 | tf_op jit(solution)/shard_map/ppermute | solution.py:44
  238.2 9.5 shard_map.262
  252.5 9.5 shard_map.259
  262.9 9.6 shard_map.256
  275.1 8.6 collective-permute-done.16
  286.5 4.4 maximum_select_fusion.1
  290.9 5.2 constant_dynamic-slice_fusion.23
  296.1 6.6 pad_maximum_fusion.5
  302.6 4.8 reshape.553
  307.4 4.3 fusion.50
  341.1 9.4 collective-permute-start.55
  356.4 10.2 shard_map.270
  369.6 10.2 shard_map.267
  381.0 10.5 shard_map.264
  409.3 7.6 collective-permute-done.57.upper_ref.refs_5_
  417.6 9.5 shard_map.271
  427.1 11.7 shard_map.284
  440.4 9.6 shard_map.268
  450.0 11.6 shard_map.278
  463.2 9.5 shard_map.265
  472.7 11.7 shard_map.272
  485.2 8.9 shard_map.299
  499.4 8.8 shard_map.297
  510.0 8.9 shard_map.298
  529.3 14.7 %shard_map.285 = (bf16[128,896]{1,0:T(8,128)(2,1)}, bf16[512,256]{1,0:T(8,128)(2,1)}, bf16[512,256]{1,0:T(8,128)(2,1)}, f32[128,896]{1,0:T(8,128)}, bf16[128,896]{1,0:T(8,128)(2,1)}, /*index=5*/f32[1,896]{1,0:T(1,128)}) custom-call(bf16[128,896]{1,0:T(8,128)(2,1)} %get-tuple-element.207.q_ref, bf16[512,256]{1,0:T(8,128)(2,1)} %copy-done.97, ...), custom_call_target="tpu_custom_call" | custom-call | flops 3728736256 | bytes 6069248 | tf_op jit(solution)/shard_map/pallas_call | solution.py:127
  545.2 14.7 %shard_map.279 = (bf16[128,896]{1,0:T(8,128)(2,1)}, bf16[512,256]{1,0:T(8,128)(2,1)}, bf16[512,256]{1,0:T(8,128)(2,1)}, f32[128,896]{1,0:T(8,128)}, bf16[128,896]{1,0:T(8,128)(2,1)}, /*index=5*/f32[1,896]{1,0:T(1,128)}) custom-call(bf16[128,896]{1,0:T(8,128)(2,1)} %get-tuple-element.201.q_ref, bf16[512,256]{1,0:T(8,128)(2,1)} %copy-done.96, ...), custom_call_target="tpu_custom_call" | custom-call | flops 3728736256 | bytes 6069248 | tf_op jit(solution)/shard_map/pallas_call | solution.py:127
  560.6 14.9 %shard_map.273 = (bf16[128,896]{1,0:T(8,128)(2,1)}, bf16[512,256]{1,0:T(8,128)(2,1)}, bf16[512,256]{1,0:T(8,128)(2,1)}, f32[128,896]{1,0:T(8,128)}, bf16[128,896]{1,0:T(8,128)(2,1)}, /*index=5*/f32[1,896]{1,0:T(1,128)}) custom-call(bf16[128,896]{1,0:T(8,128)(2,1)} %get-tuple-element.194.q_ref, bf16[512,256]{1,0:T(8,128)(2,1)} %copy-done.95, ...), custom_call_target="tpu_custom_call" | custom-call | flops 3728736256 | bytes 6069248 | tf_op jit(solution)/shard_map/pallas_call | solution.py:127
  583.4 8.9 collective-permute-done.94
  593.0 4.9 collective-permute-done.80
  627.0 4.9 shard_map.295
  635.3 11.7 shard_map.287
  648.5 12.0 %shard_map.281 = (bf16[256,896]{1,0:T(8,128)(2,1)}, bf16[256,896]{1,0:T(8,128)(2,1)}, bf16[512,1280]{1,0:T(8,128)(2,1)}, bf16[512,1280]{1,0:T(8,128)(2,1)}) custom-call(bf16[256,896]{1,0:T(8,128)(2,1)} %copy-done.81, bf16[256,896]{1,0:T(8,128)(2,1)} %copy-done.129, bf16[512,1280]{1,0:T(8,128)(2,1)} %get-tuple-element.241.g_ref, ...), custom_call_target="tpu_custom_call" | custom-call | flops 3523215360 | bytes 13959168 | tf_op jit(solution)/shard_map/pallas_call | solution.py:127
  662.1 11.7 shard_map.275
  674.5 8.5 shard_map.294
  687.4 8.8 shard_map.293
  696.3 8.9 shard_map.292
  720.8 14.9 %shard_map.288 = (bf16[128,896]{1,0:T(8,128)(2,1)}, bf16[512,256]{1,0:T(8,128)(2,1)}, bf16[512,256]{1,0:T(8,128)(2,1)}, f32[128,896]{1,0:T(8,128)}, bf16[128,896]{1,0:T(8,128)(2,1)}, /*index=5*/f32[1,896]{1,0:T(1,128)}) custom-call(bf16[128,896]{1,0:T(8,128)(2,1)} %get-tuple-element.187.q_ref, bf16[512,256]{1,0:T(8,128)(2,1)} %constant_dynamic-update-slice_fusion.14.kva_ref, ...), custom_call_target="tpu_custom_call" | custom-call | flops 3728736256 | bytes 6069248 | tf_op jit(solution)/shard_map/pallas_call | solution.py:127
  737.0 14.7 %shard_map.282 = (bf16[128,896]{1,0:T(8,128)(2,1)}, bf16[512,256]{1,0:T(8,128)(2,1)}, bf16[512,256]{1,0:T(8,128)(2,1)}, f32[128,896]{1,0:T(8,128)}, bf16[128,896]{1,0:T(8,128)(2,1)}, /*index=5*/f32[1,896]{1,0:T(1,128)}) custom-call(bf16[128,896]{1,0:T(8,128)(2,1)} %get-tuple-element.181.q_ref, bf16[512,256]{1,0:T(8,128)(2,1)} %copy-done.93, ...), custom_call_target="tpu_custom_call" | custom-call | flops 3728736256 | bytes 6069248 | tf_op jit(solution)/shard_map/pallas_call | solution.py:127
  752.4 14.7 %shard_map.276 = (bf16[128,896]{1,0:T(8,128)(2,1)}, bf16[512,256]{1,0:T(8,128)(2,1)}, bf16[512,256]{1,0:T(8,128)(2,1)}, f32[128,896]{1,0:T(8,128)}, bf16[128,896]{1,0:T(8,128)(2,1)}, /*index=5*/f32[1,896]{1,0:T(1,128)}) custom-call(bf16[128,896]{1,0:T(8,128)(2,1)} %get-tuple-element.174.q_ref, bf16[512,256]{1,0:T(8,128)(2,1)} %copy-done.94, ...), custom_call_target="tpu_custom_call" | custom-call | flops 3728736256 | bytes 6069248 | tf_op jit(solution)/shard_map/pallas_call | solution.py:127
  775.6 6.2 collective-permute-done.101
  782.5 7.7 collective-permute-done.87
  790.9 7.7 collective-permute-done.73
  816.7 3.8 shard_map.277
  828.2 4.8 shard_map.290
  843.7 10.1 collective-permute-done.110
  859.1 5.5 pad_maximum_fusion.13
  882.4 5.5 pad_maximum_fusion.10
  902.5 117.7 %all-reduce.22.cloned.1.call-done = (bf16[112,2176]{1,0:T(8,128)(2,1)}, bf16[112,4864]{1,0:T(8,128)(2,1)}, bf16[112,4864]{1,0:T(8,128)(2,1)}, bf16[608,896]{1,0:T(8,128)(2,1)}) async-done(((bf16[112,2176]{1,0:T(8,128)(2,1)}, bf16[112,4864]{1,0:T(8,128)(2,1)}, bf16[112,4864]{1,0:T(8,128)(2,1)}, bf16[608,896]{1,0:T(8,128)(2,1)}), (bf16[112,2176]{1,0:T(8,128)(2,1)}, bf16[112,4864]{1,0:T(8,128)(2,1)}, ...) | async-done | bytes 3756048 | tf_op jit(solution)/shard_map/psum | solution.py:790
  1023.0 5.0 collective-permute-done.58
  1034.4 5.9 collective-permute-done.44
  1042.3 4.8 collective-permute-start.103
  1049.0 4.8 collective-permute-start.60
  1062.8 102.2 %all-reduce.20.cloned.1.call-done = (bf16[112,2176]{1,0:T(8,128)(2,1)}, bf16[112,4864]{1,0:T(8,128)(2,1)}, bf16[112,4864]{1,0:T(8,128)(2,1)}, bf16[608,896]{1,0:T(8,128)(2,1)}) async-done(((bf16[112,2176]{1,0:T(8,128)(2,1)}, bf16[112,4864]{1,0:T(8,128)(2,1)}, bf16[112,4864]{1,0:T(8,128)(2,1)}, bf16[608,896]{1,0:T(8,128)(2,1)}), (bf16[112,2176]{1,0:T(8,128)(2,1)}, bf16[112,4864]{1,0:T(8,128)(2,1)}, ...) | async-done | bytes 3756048 | tf_op jit(solution)/shard_map/psum | solution.py:790
  (879 shorter events, 422.8 us)
Async XLA Ops:
  7.2 1013.1 %all-reduce.22.cloned.1.call-start = ((), (), s32[]{:S(2)}) async-start(), calls=%async_computation.1 | async-start | bytes 7512064 | tf_op jit(solution)/shard_map/psum | solution.py:790
  15.4 47.5 %collective-permute-start.10 = (bf16[112,4864]{1,0:T(8,128)(2,1)}, bf16[112,4864]{1,0:T(8,128)(2,1)}, u32[]{:S(2)}, u32[]{:S(2)}) collective-permute-start(bf16[112,4864]{1,0:T(8,128)(2,1)} %bitcast_select_fusion.1), channel_id=1, source_target_pairs={{0,16},{16,0},{1,17},{17,1},{2,18},{18,2},{3,19},{19,3},{4,20},{20... | collective-permute-start | bytes 3268616 | tf_op jit(solution)/shard_map/ppermute | solution.py:92
  17.4 37.7 %collective-permute-start.9 = (bf16[112,4864]{1,0:T(8,128)(2,1)}, bf16[112,4864]{1,0:T(8,128)(2,1)}, u32[]{:S(2)}, u32[]{:S(2)}) collective-permute-start(bf16[112,4864]{1,0:T(8,128)(2,1)} %bitcast_select_fusion.4), channel_id=1, source_target_pairs={{0,16},{16,0},{1,17},{17,1},{2,18},{18,2},{3,19},{19,3},{4,20},{20... | collective-permute-start | bytes 3268616 | tf_op jit(solution)/shard_map/ppermute | solution.py:92
  19.8 85.9 %collective-permute-start.61 = (bf16[128,896]{1,0:T(8,128)(2,1)}, bf16[128,896]{1,0:T(8,128)(2,1)}, u32[]{:S(2)}, u32[]{:S(2)}) collective-permute-start(bf16[128,896]{1,0:T(8,128)(2,1)} %get-tuple-element.421), channel_id=1, source_target_pairs={{0,1},{1,0},{2,3},{3,2},{16,18},{17,19},{18,16},{19,17},{4,5},{5,4... | collective-permute-start | bytes 688136 | tf_op jit(solution)/shard_map/ppermute | solution.py:44
  22.5 85.1 %collective-permute-start.75 = (bf16[128,896]{1,0:T(8,128)(2,1)S(1)}, bf16[128,896]{1,0:T(8,128)(2,1)}, u32[]{:S(2)}, u32[]{:S(2)}) collective-permute-start(bf16[128,896]{1,0:T(8,128)(2,1)S(1)} %get-tuple-element.520), channel_id=1, source_target_pairs={{0,1},{1,0},{2,3},{3,2},{16,18},{17,19},{18,16},{19,17},{4,5},{5,4... | collective-permute-start | bytes 688136 | tf_op jit(solution)/shard_map/ppermute | solution.py:44
  49.7 53.8 %collective-permute-start.89 = (bf16[128,896]{1,0:T(8,128)(2,1)}, bf16[128,896]{1,0:T(8,128)(2,1)}, u32[]{:S(2)}, u32[]{:S(2)}) collective-permute-start(bf16[128,896]{1,0:T(8,128)(2,1)} %get-tuple-element.522), channel_id=1, source_target_pairs={{0,1},{1,0},{2,3},{3,2},{16,18},{17,19},{18,16},{19,17},{4,5},{5,4... | collective-permute-start | bytes 688136 | tf_op jit(solution)/shard_map/ppermute | solution.py:44
  62.9 57.2 %collective-permute-start.15 = (bf16[1216,896]{1,0:T(8,128)(2,1)}, bf16[1216,896]{1,0:T(8,128)(2,1)}, u32[]{:S(2)}, u32[]{:S(2)}) collective-permute-start(bf16[1216,896]{1,0:T(8,128)(2,1)} %bitcast.270), channel_id=1, source_target_pairs={{0,16},{16,0},{1,17},{17,1},{2,18},{18,2},{3,19},{19,3},{4,20},{20... | collective-permute-start | bytes 6537224 | tf_op jit(solution)/shard_map/ppermute | solution.py:92
  95.6 20.3 %collective-permute-start.11 = (bf16[2,1,224,1216]{3,2,0,1:T(8,128)(2,1)}, bf16[2,1,224,1216]{3,2,0,1:T(8,128)(2,1)}, u32[]{:S(2)}, u32[]{:S(2)}) collective-permute-start(bf16[2,1,224,1216]{3,2,0,1:T(8,128)(2,1)} %bitcast.226), channel_id=1, source_target_pairs={{0,1},{1,0},{2,3},{3,2},{16,18},{17,19},{18,16},{19,17},{4,5},{5,4... | collective-permute-start | bytes 3268616 | tf_op jit(solution)/shard_map/ppermute | solution.py:44
  105.4 321.8 %collective-permute-start.90 = (bf16[256,896]{1,0:T(8,128)(2,1)}, bf16[256,896]{1,0:T(8,128)(2,1)}, u32[]{:S(2)}, u32[]{:S(2)}) collective-permute-start(bf16[256,896]{1,0:T(8,128)(2,1)} %pad_maximum_fusion.30.lower_ref.refs_7_), channel_id=1, source_target_pairs={{0,2},{1,3},{2,0},{3,1},{16,17},{17,16},{18,19},{19,18},{4,6},{5,7... | collective-permute-start | bytes 1376264 | tf_op jit(solution)/shard_map/ppermute | solution.py:44
  119.0 30.1 %collective-permute-start.12 = (bf16[1,2,224,1216]{3,2,1,0:T(8,128)(2,1)}, bf16[1,2,224,1216]{3,2,1,0:T(8,128)(2,1)}, u32[]{:S(2)}, u32[]{:S(2)}) collective-permute-start(bf16[1,2,224,1216]{3,2,1,0:T(8,128)(2,1)} %get-tuple-element.485), channel_id=1, source_target_pairs={{0,2},{1,3},{2,0},{3,1},{16,17},{17,16},{18,19},{19,18},{4,6},{5,7... | collective-permute-start | bytes 3268616 | tf_op jit(solution)/shard_map/ppermute | solution.py:44
  146.6 21.1 %collective-permute-start.26 = (bf16[256,256]{1,0:T(8,128)(2,1)S(1)}, bf16[256,256]{1,0:T(8,128)(2,1)S(1)}, u32[]{:S(2)}, u32[]{:S(2)}) collective-permute-start(bf16[256,256]{1,0:T(8,128)(2,1)S(1)} %pad_maximum_fusion.33), channel_id=1, source_target_pairs={{0,8},{4,12},{8,0},{12,4},{16,24},{20,28},{24,16},{28,20},{1,9},{5... | collective-permute-start | bytes 393224 | tf_op jit(solution)/shard_map/ppermute | solution.py:44
  149.0 18.6 %collective-permute-start.19 = (bf16[256,256]{1,0:T(8,128)(2,1)S(1)}, bf16[256,256]{1,0:T(8,128)(2,1)S(1)}, u32[]{:S(2)}, u32[]{:S(2)}) collective-permute-start(bf16[256,256]{1,0:T(8,128)(2,1)S(1)} %pad_maximum_fusion.32), channel_id=1, source_target_pairs={{0,8},{4,12},{8,0},{12,4},{16,24},{20,28},{24,16},{28,20},{1,9},{5... | collective-permute-start | bytes 393224 | tf_op jit(solution)/shard_map/ppermute | solution.py:44
  152.4 38.7 %collective-permute-start.13 = (bf16[4,112,1216]{2,1,0:T(8,128)(2,1)S(1)}, bf16[4,112,1216]{2,1,0:T(8,128)(2,1)S(1)}, u32[]{:S(2)}, u32[]{:S(2)}) collective-permute-start(bf16[4,112,1216]{2,1,0:T(8,128)(2,1)S(1)} %get-tuple-element.479), channel_id=1, source_target_pairs={{0,16},{16,0},{1,17},{17,1},{2,18},{18,2},{3,19},{19,3},{4,20},{20... | collective-permute-start | bytes 3268616 | tf_op jit(solution)/shard_map/ppermute | solution.py:92
  168.4 30.5 %collective-permute-start.27 = (bf16[512,256]{1,0:T(8,128)(2,1)}, bf16[512,256]{1,0:T(8,128)(2,1)}, u32[]{:S(2)}, u32[]{:S(2)}) collective-permute-start(bf16[512,256]{1,0:T(8,128)(2,1)} %constant_dynamic-update-slice_fusion.14.kva_ref), channel_id=1, source_target_pairs={{0,16},{16,0},{1,17},{17,1},{2,18},{18,2},{3,19},{19,3},{4,20},{20... | collective-permute-start | bytes 786440 | tf_op jit(solution)/shard_map/ppermute | solution.py:92
  180.0 33.6 %collective-permute-start.7 = (bf16[128,896]{1,0:T(8,128)(2,1)}, bf16[128,896]{1,0:T(8,128)(2,1)}, u32[]{:S(2)}, u32[]{:S(2)}) collective-permute-start(bf16[128,896]{1,0:T(8,128)(2,1)} %get-tuple-element.177), channel_id=1, source_target_pairs={{0,1},{1,0},{2,3},{3,2},{16,18},{17,19},{18,16},{19,17},{4,5},{5,4... | collective-permute-start | bytes 688136 | tf_op jit(solution)/shard_map/ppermute | solution.py:44
  196.4 23.6 %collective-permute-start.14 = (bf16[4,112,1216]{2,1,0:T(8,128)(2,1)}, bf16[4,112,1216]{2,1,0:T(8,128)(2,1)S(1)}, u32[]{:S(2)}, u32[]{:S(2)}) collective-permute-start(bf16[4,112,1216]{2,1,0:T(8,128)(2,1)} %get-tuple-element.478), channel_id=1, source_target_pairs={{0,16},{16,0},{1,17},{17,1},{2,18},{18,2},{3,19},{19,3},{4,20},{20... | collective-permute-start | bytes 3268616 | tf_op jit(solution)/shard_map/ppermute | solution.py:92
  213.6 34.7 %collective-permute-start.33 = (bf16[224,2176]{1,0:T(8,128)(2,1)}, bf16[224,2176]{1,0:T(8,128)(2,1)}, u32[]{:S(2)}, u32[]{:S(2)}) collective-permute-start(bf16[224,2176]{1,0:T(8,128)(2,1)} %pad_maximum_fusion.21), channel_id=1, source_target_pairs={{0,2},{1,3},{2,0},{3,1},{16,17},{17,16},{18,19},{19,18},{4,6},{5,7... | collective-permute-start | bytes 2924552 | tf_op jit(solution)/shard_map/ppermute | solution.py:44
  216.1 46.8 %collective-permute-start.8 = (bf16[256,896]{1,0:T(8,128)(2,1)}, bf16[256,896]{1,0:T(8,128)(2,1)}, u32[]{:S(2)}, u32[]{:S(2)}) collective-permute-start(bf16[256,896]{1,0:T(8,128)(2,1)} %constant_dynamic-update-slice_fusion.7.lower_ref.refs_0_), channel_id=1, source_target_pairs={{0,2},{1,3},{2,0},{3,1},{16,17},{17,16},{18,19},{19,18},{4,6},{5,7... | collective-permute-start | bytes 1376264 | tf_op jit(solution)/shard_map/ppermute | solution.py:44
  216.7 20.6 %collective-permute-start.29 = (bf16[256,896]{1,0:T(8,128)(2,1)S(1)}, bf16[256,896]{1,0:T(8,128)(2,1)S(1)}, u32[]{:S(2)}, u32[]{:S(2)}) collective-permute-start(bf16[256,896]{1,0:T(8,128)(2,1)S(1)} %constant_dynamic-update-slice_fusion.17.lower_ref.refs_4_), channel_id=1, source_target_pairs={{0,2},{1,3},{2,0},{3,1},{16,17},{17,16},{18,19},{19,18},{4,6},{5,7... | collective-permute-start | bytes 1376264 | tf_op jit(solution)/shard_map/ppermute | solution.py:44
  220.0 32.4 %collective-permute-start.22 = (bf16[256,896]{1,0:T(8,128)(2,1)}, bf16[256,896]{1,0:T(8,128)(2,1)}, u32[]{:S(2)}, u32[]{:S(2)}) collective-permute-start(bf16[256,896]{1,0:T(8,128)(2,1)} %constant_dynamic-update-slice_fusion.12.lower_ref.refs_2_), channel_id=1, source_target_pairs={{0,2},{1,3},{2,0},{3,1},{16,17},{17,16},{18,19},{19,18},{4,6},{5,7... | collective-permute-start | bytes 1376264 | tf_op jit(solution)/shard_map/ppermute | solution.py:44
  247.7 25.5 %collective-permute-start.30 = (bf16[256,896]{1,0:T(8,128)(2,1)}, bf16[256,896]{1,0:T(8,128)(2,1)S(1)}, u32[]{:S(2)}, u32[]{:S(2)}) collective-permute-start(bf16[256,896]{1,0:T(8,128)(2,1)} %get-tuple-element.192), channel_id=1, source_target_pairs={{0,2},{1,3},{2,0},{3,1},{16,17},{17,16},{18,19},{19,18},{4,6},{5,7... | collective-permute-start | bytes 1376264 | tf_op jit(solution)/shard_map/ppermute | solution.py:44
  251.5 35.0 %collective-permute-start.34 = (bf16[4,112,2176]{2,1,0:T(8,128)(2,1)}, bf16[4,112,2176]{2,1,0:T(8,128)(2,1)}, u32[]{:S(2)}, u32[]{:S(2)}) collective-permute-start(bf16[4,112,2176]{2,1,0:T(8,128)(2,1)} %get-tuple-element.503), channel_id=1, source_target_pairs={{0,16},{16,0},{1,17},{17,1},{2,18},{18,2},{3,19},{19,3},{4,20},{20... | collective-permute-start | bytes 5849096 | tf_op jit(solution)/shard_map/ppermute | solution.py:92
  283.8 29.7 %collective-permute-start.17 = (bf16[128,896]{1,0:T(8,128)(2,1)S(1)}, bf16[128,896]{1,0:T(8,128)(2,1)}, u32[]{:S(2)}, u32[]{:S(2)}) collective-permute-start(bf16[128,896]{1,0:T(8,128)(2,1)S(1)} %slice.939), channel_id=1, source_target_pairs={{0,1},{1,0},{2,3},{3,2},{16,18},{17,19},{18,16},{19,17},{4,5},{5,4... | collective-permute-start | bytes 688136 | tf_op jit(solution)/shard_map/ppermute | solution.py:44
  312.8 23.2 %collective-permute-start.40 = (bf16[2,1,224,1216]{3,2,0,1:T(8,128)(2,1)}, bf16[2,1,224,1216]{3,2,0,1:T(8,128)(2,1)}, u32[]{:S(2)}, u32[]{:S(2)}) collective-permute-start(bf16[2,1,224,1216]{3,2,0,1:T(8,128)(2,1)} %bitcast.225), channel_id=1, source_target_pairs={{0,1},{1,0},{2,3},{3,2},{16,18},{17,19},{18,16},{19,17},{4,5},{5,4... | collective-permute-start | bytes 3268616 | tf_op jit(solution)/shard_map/ppermute | solution.py:44
  337.6 29.5 %collective-permute-start.41 = (bf16[1,2,224,1216]{3,2,1,0:T(8,128)(2,1)S(1)}, bf16[1,2,224,1216]{3,2,1,0:T(8,128)(2,1)S(1)}, u32[]{:S(2)}, u32[]{:S(2)}) collective-permute-start(bf16[1,2,224,1216]{3,2,1,0:T(8,128)(2,1)S(1)} %get-tuple-element.469), channel_id=1, source_target_pairs={{0,2},{1,3},{2,0},{3,1},{16,17},{17,16},{18,19},{19,18},{4,6},{5,7... | collective-permute-start | bytes 3268616 | tf_op jit(solution)/shard_map/ppermute | solution.py:44
  354.8 25.5 %collective-permute-start.37 = (bf16[512,256]{1,0:T(8,128)(2,1)S(1)}, bf16[512,256]{1,0:T(8,128)(2,1)S(1)}, u32[]{:S(2)}, u32[]{:S(2)}) collective-permute-start(bf16[512,256]{1,0:T(8,128)(2,1)S(1)} %constant_dynamic-update-slice_fusion.19.kva_ref), channel_id=1, source_target_pairs={{0,16},{16,0},{1,17},{17,1},{2,18},{18,2},{3,19},{19,3},{4,20},{20... | collective-permute-start | bytes 786440 | tf_op jit(solution)/shard_map/ppermute | solution.py:92
  366.6 29.2 %collective-permute-start.56 = (bf16[128,896]{1,0:T(8,128)(2,1)}, bf16[128,896]{1,0:T(8,128)(2,1)S(1)}, u32[]{:S(2)}, u32[]{:S(2)}) collective-permute-start(bf16[128,896]{1,0:T(8,128)(2,1)} %get-tuple-element.210), channel_id=1, source_target_pairs={{0,1},{1,0},{2,3},{3,2},{16,18},{17,19},{18,16},{19,17},{4,5},{5,4... | collective-permute-start | bytes 688136 | tf_op jit(solution)/shard_map/ppermute | solution.py:44
  368.1 35.1 %collective-permute-start.43 = (bf16[4,112,1216]{2,1,0:T(8,128)(2,1)S(1)}, bf16[4,112,1216]{2,1,0:T(8,128)(2,1)S(1)}, u32[]{:S(2)}, u32[]{:S(2)}) collective-permute-start(bf16[4,112,1216]{2,1,0:T(8,128)(2,1)S(1)} %get-tuple-element.462), channel_id=1, source_target_pairs={{0,16},{16,0},{1,17},{17,1},{2,18},{18,2},{3,19},{19,3},{4,20},{20... | collective-permute-start | bytes 3268616 | tf_op jit(solution)/shard_map/ppermute | solution.py:92
  380.3 24.0 %collective-permute-start.42 = (bf16[4,112,1216]{2,1,0:T(8,128)(2,1)S(1)}, bf16[4,112,1216]{2,1,0:T(8,128)(2,1)S(1)}, u32[]{:S(2)}, u32[]{:S(2)}) collective-permute-start(bf16[4,112,1216]{2,1,0:T(8,128)(2,1)S(1)} %get-tuple-element.463), channel_id=1, source_target_pairs={{0,16},{16,0},{1,17},{17,1},{2,18},{18,2},{3,19},{19,3},{4,20},{20... | collective-permute-start | bytes 3268616 | tf_op jit(solution)/shard_map/ppermute | solution.py:92
  396.9 53.1 %collective-permute-start.76 = (bf16[256,896]{1,0:T(8,128)(2,1)S(1)}, bf16[256,896]{1,0:T(8,128)(2,1)}, u32[]{:S(2)}, u32[]{:S(2)}) collective-permute-start(bf16[256,896]{1,0:T(8,128)(2,1)S(1)} %copy-done.49), channel_id=1, source_target_pairs={{0,2},{1,3},{2,0},{3,1},{16,17},{17,16},{18,19},{19,18},{4,6},{5,7... | collective-permute-start | bytes 1376264 | tf_op jit(solution)/shard_map/ppermute | solution.py:44
  401.7 71.1 %collective-permute-start.62 = (bf16[256,896]{1,0:T(8,128)(2,1)S(1)}, bf16[256,896]{1,0:T(8,128)(2,1)}, u32[]{:S(2)}, u32[]{:S(2)}) collective-permute-start(bf16[256,896]{1,0:T(8,128)(2,1)S(1)} %copy-done.48), channel_id=1, source_target_pairs={{0,2},{1,3},{2,0},{3,1},{16,17},{17,16},{18,19},{19,18},{4,6},{5,7... | collective-permute-start | bytes 1376264 | tf_op jit(solution)/shard_map/ppermute | solution.py:44
  404.3 35.3 %collective-permute-start.50 = (bf16[256,896]{1,0:T(8,128)(2,1)}, bf16[256,896]{1,0:T(8,128)(2,1)S(1)}, u32[]{:S(2)}, u32[]{:S(2)}) collective-permute-start(bf16[256,896]{1,0:T(8,128)(2,1)} %constant_dynamic-update-slice_fusion.27.lower_ref.refs_2_), channel_id=1, source_target_pairs={{0,2},{1,3},{2,0},{3,1},{16,17},{17,16},{18,19},{19,18},{4,6},{5,7... | collective-permute-start | bytes 1376264 | tf_op jit(solution)/shard_map/ppermute | solution.py:44
  416.9 45.5 %collective-permute-start.39 = (bf16[256,896]{1,0:T(8,128)(2,1)}, bf16[256,896]{1,0:T(8,128)(2,1)S(1)}, u32[]{:S(2)}, u32[]{:S(2)}) collective-permute-start(bf16[256,896]{1,0:T(8,128)(2,1)} %constant_dynamic-update-slice_fusion.22.lower_ref.refs_0_), channel_id=1, source_target_pairs={{0,2},{1,3},{2,0},{3,1},{16,17},{17,16},{18,19},{19,18},{4,6},{5,7... | collective-permute-start | bytes 1376264 | tf_op jit(solution)/shard_map/ppermute | solution.py:44
  438.9 81.9 %collective-permute-start.91 = (bf16[256,896]{1,0:T(8,128)(2,1)}, bf16[256,896]{1,0:T(8,128)(2,1)S(1)}, u32[]{:S(2)}, u32[]{:S(2)}) collective-permute-start(bf16[256,896]{1,0:T(8,128)(2,1)} %get-tuple-element.254), channel_id=1, source_target_pairs={{0,2},{1,3},{2,0},{3,1},{16,17},{17,16},{18,19},{19,18},{4,6},{5,7... | collective-permute-start | bytes 1376264 | tf_op jit(solution)/shard_map/ppermute | solution.py:44
  461.6 60.6 %collective-permute-start.77 = (bf16[256,896]{1,0:T(8,128)(2,1)}, bf16[256,896]{1,0:T(8,128)(2,1)S(1)}, u32[]{:S(2)}, u32[]{:S(2)}) collective-permute-start(bf16[256,896]{1,0:T(8,128)(2,1)} %get-tuple-element.235), channel_id=1, source_target_pairs={{0,2},{1,3},{2,0},{3,1},{16,17},{17,16},{18,19},{19,18},{4,6},{5,7... | collective-permute-start | bytes 1376264 | tf_op jit(solution)/shard_map/ppermute | solution.py:44
  484.4 39.7 %collective-permute-start.63 = (bf16[256,896]{1,0:T(8,128)(2,1)}, bf16[256,896]{1,0:T(8,128)(2,1)S(1)}, u32[]{:S(2)}, u32[]{:S(2)}) collective-permute-start(bf16[256,896]{1,0:T(8,128)(2,1)} %get-tuple-element.216), channel_id=1, source_target_pairs={{0,2},{1,3},{2,0},{3,1},{16,17},{17,16},{18,19},{19,18},{4,6},{5,7... | collective-permute-start | bytes 1376264 | tf_op jit(solution)/shard_map/ppermute | solution.py:44
  496.8 108.6 %collective-permute-start.119 = (bf16[608,896]{1,0:T(8,128)(2,1)}, bf16[608,896]{1,0:T(8,128)(2,1)S(1)}, u32[]{:S(2)}, u32[]{:S(2)}) collective-permute-start(bf16[608,896]{1,0:T(8,128)(2,1)} %broadcast_select_fusion.8), channel_id=1, source_target_pairs={{0,16},{16,0},{1,17},{17,1},{2,18},{18,2},{3,19},{19,3},{4,20},{20... | collective-permute-start | bytes 3268616 | tf_op jit(solution)/shard_map/ppermute | solution.py:92
  520.6 82.2 %collective-permute-start.116 = (bf16[4,112,1216]{2,1,0:T(8,128)(2,1)S(1)}, bf16[4,112,1216]{2,1,0:T(8,128)(2,1)S(1)}, u32[]{:S(2)}, u32[]{:S(2)}) collective-permute-start(bf16[4,112,1216]{2,1,0:T(8,128)(2,1)S(1)} %broadcast_select_fusion.4), channel_id=1, source_target_pairs={{0,16},{16,0},{1,17},{17,1},{2,18},{18,2},{3,19},{19,3},{4,20},{20... | collective-permute-start | bytes 3268616 | tf_op jit(solution)/shard_map/ppermute | solution.py:92
  520.7 82.6 %collective-permute-start.115 = (bf16[4,112,1216]{2,1,0:T(8,128)(2,1)S(1)}, bf16[4,112,1216]{2,1,0:T(8,128)(2,1)S(1)}, u32[]{:S(2)}, u32[]{:S(2)}) collective-permute-start(bf16[4,112,1216]{2,1,0:T(8,128)(2,1)S(1)} %broadcast_select_fusion.5), channel_id=1, source_target_pairs={{0,16},{16,0},{1,17},{17,1},{2,18},{18,2},{3,19},{19,3},{4,20},{20... | collective-permute-start | bytes 3268616 | tf_op jit(solution)/shard_map/ppermute | solution.py:92
  525.1 18.9 %collective-permute-start.78 = (bf16[128,896]{1,0:T(8,128)(2,1)S(1)}, bf16[128,896]{1,0:T(8,128)(2,1)S(1)}, u32[]{:S(2)}, u32[]{:S(2)}) collective-permute-start(bf16[128,896]{1,0:T(8,128)(2,1)S(1)} %slice.931), channel_id=1, source_target_pairs={{0,1},{1,0},{2,3},{3,2},{16,18},{17,19},{18,16},{19,17},{4,5},{5,4... | collective-permute-start | bytes 688136 | tf_op jit(solution)/shard_map/ppermute | solution.py:44
  528.3 31.6 %collective-permute-start.64 = (bf16[128,896]{1,0:T(8,128)(2,1)S(1)}, bf16[128,896]{1,0:T(8,128)(2,1)S(1)}, u32[]{:S(2)}, u32[]{:S(2)}) collective-permute-start(bf16[128,896]{1,0:T(8,128)(2,1)S(1)} %slice.933), channel_id=1, source_target_pairs={{0,1},{1,0},{2,3},{3,2},{16,18},{17,19},{18,16},{19,17},{4,5},{5,4... | collective-permute-start | bytes 688136 | tf_op jit(solution)/shard_map/ppermute | solution.py:44
  544.0 36.0 %collective-permute-start.93 = (bf16[512,256]{1,0:T(8,128)(2,1)}, bf16[512,256]{1,0:T(8,128)(2,1)S(1)}, u32[]{:S(2)}, u32[]{:S(2)}) collective-permute-start(bf16[512,256]{1,0:T(8,128)(2,1)} %get-tuple-element.257), channel_id=1, source_target_pairs={{0,16},{16,0},{1,17},{17,1},{2,18},{18,2},{3,19},{19,3},{4,20},{20... | collective-permute-start | bytes 786440 | tf_op jit(solution)/shard_map/ppermute | solution.py:92
  559.9 20.8 %collective-permute-start.79 = (bf16[512,256]{1,0:T(8,128)(2,1)}, bf16[512,256]{1,0:T(8,128)(2,1)S(1)}, u32[]{:S(2)}, u32[]{:S(2)}) collective-permute-start(bf16[512,256]{1,0:T(8,128)(2,1)} %get-tuple-element.238), channel_id=1, source_target_pairs={{0,16},{16,0},{1,17},{17,1},{2,18},{18,2},{3,19},{19,3},{4,20},{20... | collective-permute-start | bytes 786440 | tf_op jit(solution)/shard_map/ppermute | solution.py:92
  604.5 104.7 %collective-permute-start.117 = (bf16[2,1,224,1216]{3,2,0,1:T(8,128)(2,1)S(1)}, bf16[2,1,224,1216]{3,2,0,1:T(8,128)(2,1)S(1)}, u32[]{:S(2)}, u32[]{:S(2)}) collective-permute-start(bf16[2,1,224,1216]{3,2,0,1:T(8,128)(2,1)S(1)} %get-tuple-element.441), channel_id=1, source_target_pairs={{0,1},{1,0},{2,3},{3,2},{16,18},{17,19},{18,16},{19,17},{4,5},{5,4... | collective-permute-start | bytes 3268616 | tf_op jit(solution)/shard_map/ppermute | solution.py:44
  626.2 21.6 %collective-permute-start.83 = (bf16[256,896]{1,0:T(8,128)(2,1)S(1)}, bf16[256,896]{1,0:T(8,128)(2,1)S(1)}, u32[]{:S(2)}, u32[]{:S(2)}) collective-permute-start(bf16[256,896]{1,0:T(8,128)(2,1)S(1)} %constant_dynamic-update-slice_fusion.36.lower_ref.refs_5_), channel_id=1, source_target_pairs={{0,2},{1,3},{2,0},{3,1},{16,17},{17,16},{18,19},{19,18},{4,6},{5,7... | collective-permute-start | bytes 1376264 | tf_op jit(solution)/shard_map/ppermute | solution.py:44
  631.9 29.4 %collective-permute-start.69 = (bf16[256,896]{1,0:T(8,128)(2,1)S(1)}, bf16[256,896]{1,0:T(8,128)(2,1)S(1)}, u32[]{:S(2)}, u32[]{:S(2)}) collective-permute-start(bf16[256,896]{1,0:T(8,128)(2,1)S(1)} %constant_dynamic-update-slice_fusion.34.lower_ref.refs_3_), channel_id=1, source_target_pairs={{0,2},{1,3},{2,0},{3,1},{16,17},{17,16},{18,19},{19,18},{4,6},{5,7... | collective-permute-start | bytes 1376264 | tf_op jit(solution)/shard_map/ppermute | solution.py:44
  646.9 63.6 %collective-permute-start.98 = (bf16[256,896]{1,0:T(8,128)(2,1)}, bf16[256,896]{1,0:T(8,128)(2,1)}, u32[]{:S(2)}, u32[]{:S(2)}) collective-permute-start(bf16[256,896]{1,0:T(8,128)(2,1)} %get-tuple-element.263), channel_id=1, source_target_pairs={{0,2},{1,3},{2,0},{3,1},{16,17},{17,16},{18,19},{19,18},{4,6},{5,7... | collective-permute-start | bytes 1376264 | tf_op jit(solution)/shard_map/ppermute | solution.py:44
  660.5 52.4 %collective-permute-start.84 = (bf16[256,896]{1,0:T(8,128)(2,1)}, bf16[256,896]{1,0:T(8,128)(2,1)}, u32[]{:S(2)}, u32[]{:S(2)}) collective-permute-start(bf16[256,896]{1,0:T(8,128)(2,1)} %get-tuple-element.244), channel_id=1, source_target_pairs={{0,2},{1,3},{2,0},{3,1},{16,17},{17,16},{18,19},{19,18},{4,6},{5,7... | collective-permute-start | bytes 1376264 | tf_op jit(solution)/shard_map/ppermute | solution.py:44
  673.8 41.9 %collective-permute-start.70 = (bf16[256,896]{1,0:T(8,128)(2,1)}, bf16[256,896]{1,0:T(8,128)(2,1)}, u32[]{:S(2)}, u32[]{:S(2)}) collective-permute-start(bf16[256,896]{1,0:T(8,128)(2,1)} %get-tuple-element.225), channel_id=1, source_target_pairs={{0,2},{1,3},{2,0},{3,1},{16,17},{17,16},{18,19},{19,18},{4,6},{5,7... | collective-permute-start | bytes 1376264 | tf_op jit(solution)/shard_map/ppermute | solution.py:44
  685.7 118.2 %collective-permute-start.111 = (bf16[608,896]{1,0:T(8,128)(2,1)}, bf16[608,896]{1,0:T(8,128)(2,1)}, u32[]{:S(2)}, u32[]{:S(2)}) collective-permute-start(bf16[608,896]{1,0:T(8,128)(2,1)} %broadcast_select_fusion.9), channel_id=1, source_target_pairs={{0,16},{16,0},{1,17},{17,1},{2,18},{18,2},{3,19},{19,3},{4,20},{20... | collective-permute-start | bytes 3268616 | tf_op jit(solution)/shard_map/ppermute | solution.py:92
  709.1 90.2 %collective-permute-start.108 = (bf16[4,112,1216]{2,1,0:T(8,128)(2,1)}, bf16[4,112,1216]{2,1,0:T(8,128)(2,1)S(1)}, u32[]{:S(2)}, u32[]{:S(2)}) collective-permute-start(bf16[4,112,1216]{2,1,0:T(8,128)(2,1)} %broadcast_select_fusion.6), channel_id=1, source_target_pairs={{0,16},{16,0},{1,17},{17,1},{2,18},{18,2},{3,19},{19,3},{4,20},{20... | collective-permute-start | bytes 3268616 | tf_op jit(solution)/shard_map/ppermute | solution.py:92
  710.5 90.7 %collective-permute-start.107 = (bf16[4,112,1216]{2,1,0:T(8,128)(2,1)}, bf16[4,112,1216]{2,1,0:T(8,128)(2,1)S(1)}, u32[]{:S(2)}, u32[]{:S(2)}) collective-permute-start(bf16[4,112,1216]{2,1,0:T(8,128)(2,1)} %broadcast_select_fusion.7), channel_id=1, source_target_pairs={{0,16},{16,0},{1,17},{17,1},{2,18},{18,2},{3,19},{19,3},{4,20},{20... | collective-permute-start | bytes 3268616 | tf_op jit(solution)/shard_map/ppermute | solution.py:92
  720.1 31.5 %collective-permute-start.71 = (bf16[128,896]{1,0:T(8,128)(2,1)S(1)}, bf16[128,896]{1,0:T(8,128)(2,1)S(1)}, u32[]{:S(2)}, u32[]{:S(2)}) collective-permute-start(bf16[128,896]{1,0:T(8,128)(2,1)S(1)} %slice.932), channel_id=1, source_target_pairs={{0,1},{1,0},{2,3},{3,2},{16,18},{17,19},{18,16},{19,17},{4,5},{5,4... | collective-permute-start | bytes 688136 | tf_op jit(solution)/shard_map/ppermute | solution.py:44
  735.7 35.8 %collective-permute-start.100 = (bf16[512,256]{1,0:T(8,128)(2,1)}, bf16[512,256]{1,0:T(8,128)(2,1)S(1)}, u32[]{:S(2)}, u32[]{:S(2)}) collective-permute-start(bf16[512,256]{1,0:T(8,128)(2,1)} %get-tuple-element.267), channel_id=1, source_target_pairs={{0,16},{16,0},{1,17},{17,1},{2,18},{18,2},{3,19},{19,3},{4,20},{20... | collective-permute-start | bytes 786440 | tf_op jit(solution)/shard_map/ppermute | solution.py:92
  751.7 20.6 %collective-permute-start.86 = (bf16[512,256]{1,0:T(8,128)(2,1)}, bf16[512,256]{1,0:T(8,128)(2,1)S(1)}, u32[]{:S(2)}, u32[]{:S(2)}) collective-permute-start(bf16[512,256]{1,0:T(8,128)(2,1)} %get-tuple-element.248), channel_id=1, source_target_pairs={{0,16},{16,0},{1,17},{17,1},{2,18},{18,2},{3,19},{19,3},{4,20},{20... | collective-permute-start | bytes 786440 | tf_op jit(solution)/shard_map/ppermute | solution.py:92
  772.3 63.3 %collective-permute-start.118 = (bf16[1,2,224,1216]{3,2,1,0:T(8,128)(2,1)}, bf16[1,2,224,1216]{3,2,1,0:T(8,128)(2,1)}, u32[]{:S(2)}, u32[]{:S(2)}) collective-permute-start(bf16[1,2,224,1216]{3,2,1,0:T(8,128)(2,1)} %get-tuple-element.439), channel_id=1, source_target_pairs={{0,2},{1,3},{2,0},{3,1},{16,17},{17,16},{18,19},{19,18},{4,6},{5,7... | collective-permute-start | bytes 3268616 | tf_op jit(solution)/shard_map/ppermute | solution.py:44
  803.9 33.2 %collective-permute-start.109 = (bf16[2,1,224,1216]{3,2,0,1:T(8,128)(2,1)}, bf16[2,1,224,1216]{3,2,0,1:T(8,128)(2,1)}, u32[]{:S(2)}, u32[]{:S(2)}) collective-permute-start(bf16[2,1,224,1216]{3,2,0,1:T(8,128)(2,1)} %get-tuple-element.455), channel_id=1, source_target_pairs={{0,1},{1,0},{2,3},{3,2},{16,18},{17,19},{18,16},{19,17},{4,5},{5,4... | collective-permute-start | bytes 3268616 | tf_op jit(solution)/shard_map/ppermute | solution.py:44
  842.1 22.6 %collective-permute-start.113 = (bf16[224,2176]{1,0:T(8,128)(2,1)S(1)}, bf16[224,2176]{1,0:T(8,128)(2,1)S(1)}, u32[]{:S(2)}, u32[]{:S(2)}) collective-permute-start(bf16[224,2176]{1,0:T(8,128)(2,1)S(1)} %bitcast.279), channel_id=1, source_target_pairs={{0,2},{1,3},{2,0},{3,1},{16,17},{17,16},{18,19},{19,18},{4,6},{5,7... | collective-permute-start | bytes 2924552 | tf_op jit(solution)/shard_map/ppermute | solution.py:44
  877.6 287.4 %all-reduce.20.cloned.1.call-start = ((), (), s32[]{:S(2)}) async-start(), calls=%async_computation | async-start | bytes 7512064 | tf_op jit(solution)/shard_map/psum | solution.py:790
  1047.2 120.4 %collective-permute-start.122 = (bf16[112,4864]{1,0:T(8,128)(2,1)S(1)}, bf16[112,4864]{1,0:T(8,128)(2,1)}, u32[]{:S(2)}, u32[]{:S(2)}) collective-permute-start(bf16[112,4864]{1,0:T(8,128)(2,1)S(1)} %copy-done.30), channel_id=1, source_target_pairs={{0,16},{1,17},{2,18},{3,19},{4,20},{5,21},{6,22},{7,23},{8,24},{9,... | collective-permute-start | bytes 3268616 | tf_op jit(solution)/shard_map/ppermute | solution.py:794
  1058.9 114.5 %collective-permute-start.120 = (bf16[112,2176]{1,0:T(8,128)(2,1)}, bf16[112,2176]{1,0:T(8,128)(2,1)}, u32[]{:S(2)}, u32[]{:S(2)}) collective-permute-start(bf16[112,2176]{1,0:T(8,128)(2,1)} %get-tuple-element.416), channel_id=1, source_target_pairs={{0,16},{1,17},{2,18},{3,19},{4,20},{5,21},{6,22},{7,23},{8,24},{9,... | collective-permute-start | bytes 1462280 | tf_op jit(solution)/shard_map/ppermute | solution.py:794
  1060.2 110.3 %collective-permute-start.124 = (bf16[112,4864]{1,0:T(8,128)(2,1)S(1)}, bf16[112,4864]{1,0:T(8,128)(2,1)}, u32[]{:S(2)}, u32[]{:S(2)}) collective-permute-start(bf16[112,4864]{1,0:T(8,128)(2,1)S(1)} %copy-done.32), channel_id=1, source_target_pairs={{0,16},{1,17},{2,18},{3,19},{4,20},{5,21},{6,22},{7,23},{8,24},{9,... | collective-permute-start | bytes 3268616 | tf_op jit(solution)/shard_map/ppermute | solution.py:794
  1061.5 114.3 %collective-permute-start.126 = (bf16[608,896]{1,0:T(8,128)(2,1)S(1)}, bf16[608,896]{1,0:T(8,128)(2,1)}, u32[]{:S(2)}, u32[]{:S(2)}) collective-permute-start(bf16[608,896]{1,0:T(8,128)(2,1)S(1)} %copy-done.31), channel_id=1, source_target_pairs={{0,16},{1,17},{2,18},{3,19},{4,20},{5,21},{6,22},{7,23},{8,24},{9,... | collective-permute-start | bytes 3268616 | tf_op jit(solution)/shard_map/ppermute | solution.py:794
  1167.7 19.2 %collective-permute-start.123 = (bf16[112,4864]{1,0:T(8,128)(2,1)}, bf16[112,4864]{1,0:T(8,128)(2,1)S(1)}, u32[]{:S(2)}, u32[]{:S(2)}) collective-permute-start(bf16[112,4864]{1,0:T(8,128)(2,1)} %get-tuple-element.413), channel_id=1, source_target_pairs={{16,0},{17,1},{18,2},{19,3},{20,4},{21,5},{22,6},{23,7},{24,8},{25... | collective-permute-start | bytes 3268616 | tf_op jit(solution)/shard_map/ppermute | solution.py:795
  (210 other events, 1934.5 us)
Sparse Core Ops, SparseCore 0:
  877.7 142.5 all-reduce.21
  1024.0 140.8 all-reduce.19

commit v2 on v1

v2 whole, which is shorter than its diff:
```python
import functools

import jax
import jax.numpy as jnp
from jax import lax
from jax.experimental import pallas as pl
from jax.experimental.pallas import tpu as pltpu
from jax.sharding import PartitionSpec as P

HEAD = 64
rope_base = 1000000.0
norm_eps = 1e-06
masked = -1e30
bf16 = jnp.bfloat16
f32 = jnp.float32


def matmul(left, right):
    return jnp.dot(left, right, preferred_element_type=f32)


def matmul_nt(left, right):
    return lax.dot_general(left, right, (((1,), (1,)), ((), ())), preferred_element_type=f32)


def inverse_rms(values):
    return lax.rsqrt(jnp.mean(values * values, axis=-1, keepdims=True) + norm_eps)


def step_masks(axis):
    size = lax.axis_size(axis)
    assert size & (size - 1) == 0
    ahead = [1 << n for n in range(size.bit_length() - 1)]
    return list(zip(ahead, ahead[::-1] if axis == "dp" else ahead))


def step(block, axis, masks):
    size = lax.axis_size(axis)
    route = [
        (core * size + i, core * size + (i ^ mask))
        for core, mask in enumerate(masks)
        for i in range(size)
    ]
    return lax.ppermute(block, ("section", axis), route)


def gather_steps(rows, axis, give):
    masks = step_masks(axis)
    for pair in masks:
        got = step(rows, axis, pair)
        yield got
        if pair is not masks[-1]:
            rows = jnp.concatenate([rows, got])
    give(rows, got)


def scatter_steps(lower, upper, axis, give):
    masks = step_masks(axis)
    for pair in masks[::-1]:
        got = step(upper.astype(bf16), axis, pair)
        yield got
        if pair is not masks[0]:
            total = lower.astype(f32) + got.astype(f32)
            half = total.shape[0] // 2
            lower, upper = total[:half], total[half:]
    give(lower.astype(f32), got)


def distance(block, axis, core):
    return sum(pair[core] for n, pair in enumerate(step_masks(axis)) if block & (1 << n))


def direct(block, axis, mask):
    size = lax.axis_size(axis)
    return lax.ppermute(block, axis, [(i, i ^ mask) for i in range(size)])


def other(block):
    return lax.ppermute(block, "section", [(0, 1), (1, 0)])


def by_section(first, second):
    return jnp.where(lax.axis_index("section") == 0, first, second)


def after(value, first):
    return lax.optimization_barrier((value, first))[0]


def tables(begins, places):
    lane = jnp.arange(lanes, dtype=jnp.int32) % HEAD
    frequency = rope_base ** (-2.0 * (lane % (HEAD // 2)).astype(f32) / HEAD)
    angles = (places - begins).astype(f32)[:, None] * frequency[None, :]
    signs = jnp.where(lane < HEAD // 2, -1.0, 1.0)
    return jnp.cos(angles), jnp.sin(angles) * signs[None, :]


megabyte = 1024 * 1024
lanes = 128


class Part:
    def __init__(self, array, dim, index):
        self.array, self.dim, self.index = array, dim, index

    def spec(self):
        block = list(self.array.shape)
        block[self.dim] = None
        at = [0] * len(block)
        at[self.dim] = self.index
        return pl.BlockSpec(tuple(block), lambda *_: tuple(at))

    @property
    def shape(self):
        return self.array.shape[: self.dim] + self.array.shape[self.dim + 1 :]

    @property
    def size(self):
        return self.array.size // self.array.shape[self.dim]

    @property
    def dtype(self):
        return self.array.dtype


def call(
    kernel, outs, args, scratch=(), flops=0, grid=None, in_specs=None, out_specs=None, vmem=4
):
    moved = sum(a.size * a.dtype.itemsize for a in args)
    moved += sum(o.size * o.dtype.itemsize for o in outs)
    whole = pl.BlockSpec(memory_space=pltpu.VMEM)
    scalars = pl.BlockSpec(memory_space=pltpu.SMEM)
    specs = []
    for n, arg in enumerate(args):
        if isinstance(arg, Part):
            specs.append(arg.spec())
            grid = grid or (1,)
        elif arg.dtype == jnp.int32:
            specs.append(scalars)
        else:
            specs.append(in_specs[n] if in_specs else whole)
    return pl.pallas_call(
        kernel,
        out_shape=outs,
        grid=grid or (),
        in_specs=specs,
        out_specs=out_specs or [whole] * len(outs),
        scratch_shapes=scratch,
        cost_estimate=pl.CostEstimate(
            flops=int(flops), bytes_accessed=int(moved), transcendentals=0
        ),
        compiler_params=pltpu.CompilerParams(
            vmem_limit_bytes=min(56, vmem * lax.axis_size("dp")) * megabyte
        ),
    )(*[arg.array if isinstance(arg, Part) else arg for arg in args])


def shape(*dims):
    return jax.ShapeDtypeStruct(dims[:-1], dims[-1])


def lane_of(block):
    return lax.broadcasted_iota(jnp.int32, block.shape, 1)


def turn(block, cos_table, sin_table):
    quarter = HEAD // 2
    first = lax.rem(lane_of(block), HEAD) < quarter
    turned = jnp.where(first, pltpu.roll(block, lanes - quarter, 1), pltpu.roll(block, quarter, 1))
    return block * cos_table + turned * sin_table


def qkv_kernel(x_ref, gain_ref, w_ref, bias_ref, cos_ref, sin_ref, normed_ref, q_ref, kv_ref):
    x = x_ref[...].astype(f32)
    normed = (x * inverse_rms(x) * gain_ref[...].astype(f32)).astype(bf16)
    normed_ref[...] = normed
    cos_table, sin_table = cos_ref[...], sin_ref[...]
    rows = matmul(normed, w_ref[...]) + bias_ref[...].astype(f32)
    query_width = q_ref.shape[1]
    key_end = query_width + kv_ref.shape[1] // 2
    for start in range(0, rows.shape[1], lanes):
        block = rows[:, start : start + lanes]
        if start < key_end:
            block = turn(block, cos_table, sin_table)
        if start < query_width:
            q_ref[:, start : start + lanes] = block.astype(bf16)
        else:
            kv_ref[:, start - query_width : start - query_width + lanes] = block.astype(bf16)


def qkv_rows(x, p, cos_table, sin_table, kv_width):
    rows, width = x.shape
    total = p["qkv"].shape[1]
    query_width = total - 2 * kv_width
    return call(
        qkv_kernel,
        [shape(rows, width, bf16), shape(rows, query_width, bf16), shape(rows, 2 * kv_width, bf16)],
        [x, p["gain_one"], p["qkv"], p["bias"], cos_table, sin_table],
        flops=2 * rows * width * total,
    )


def pair_rows(block, pair, group):
    swapped = pltpu.roll(block, HEAD, 1)
    low = lane_of(block) < HEAD
    rows = []
    for side in range(2):
        key_head = (2 * pair + side) // group
        here = block if key_head == side else swapped
        rows.append(jnp.where(low == (key_head == 0), here, 0.0))
    return jnp.concatenate(rows).astype(bf16)


def pair_columns(block, pair, group):
    count = block.shape[1] // 2
    parts = []
    for side in range(2):
        start = (2 * pair + side) // group * HEAD
        parts.append(block[start : start + HEAD, side * count : (side + 1) * count])
    return jnp.concatenate(parts).T


def pair_terms(keys, query_pair, bias):
    scores = matmul_nt(keys, query_pair) + jnp.concatenate([bias, bias], axis=1)
    terms = jnp.exp(scores - jnp.max(scores, axis=0, keepdims=True))
    return terms, 1.0 / jnp.sum(terms, axis=0, keepdims=True)


def lay_keys(refs, keys, values):
    count = refs[0].shape[0] * refs[0].shape[1]
    for i, ref in enumerate(refs):
        rows = ref[...].reshape(count, ref.shape[2])
        keys[i * count : (i + 1) * count] = rows[:, :lanes]
        values[i * count : (i + 1) * count] = rows[:, lanes:]


def attend_kernel(
    group,
    q_ref,
    kva_ref,
    kvb_ref,
    bias_ref,
    x_ref,
    wo_ref,
    gain_ref,
    att_ref,
    res_ref,
    mix_ref,
    keys,
    values,
):
    lay_keys((kva_ref, kvb_ref), keys, values)
    values_turned = values[...].T
    bias = bias_ref[...]
    for pair in range(q_ref.shape[1] // lanes):
        place = slice(pair * lanes, (pair + 1) * lanes)
        query_pair = pair_rows(q_ref[:, place].astype(f32) * HEAD**-0.5, pair, group)
        terms, inverse = pair_terms(keys[...], query_pair, bias)
        output = matmul(values_turned, terms.astype(bf16)) * inverse
        att_ref[:, place] = pair_columns(output, pair, group).astype(bf16)

    residual = x_ref[...].astype(f32) + matmul(att_ref[...], wo_ref[...])
    res_ref[...] = residual
    mix_ref[...] = (residual * inverse_rms(residual) * gain_ref[...].astype(f32)).astype(bf16)


def attend(queries, kva, kvb, bias, x, p, turn_of):
    rows, width = queries.shape
    total = bias.shape[0]
    kv_width = kva.shape[-1] // 2
    group = width // kv_width
    flops = 4 * rows * total * width * 4 + 2 * rows * width * x.shape[1]
    return call(
        functools.partial(attend_kernel, group),
        [shape(rows, width, bf16), shape(*x.shape, f32), shape(*x.shape, bf16)],
        [queries, kva, kvb, bias, x, p["out"], turn_of(p["gain_two"])],
        scratch=[pltpu.VMEM((total, lanes), bf16)] * 2,
        flops=flops,
    )


def norm_back(values, gain, grad):
    inverse = inverse_rms(values)
    unit = values * inverse
    scaled = grad * gain
    back = inverse * (scaled - unit * jnp.mean(scaled * unit, axis=-1, keepdims=True))
    return back, jnp.sum(grad * unit, axis=0, keepdims=True)


def attend_back_kernel(
    group,
    q_ref,
    kva_ref,
    kvb_ref,
    bias_ref,
    mix_low_ref,
    mix_got_ref,
    res_ref,
    gain_ref,
    up_ref,
    wo_ref,
    cos_ref,
    sin_ref,
    dq_ref,
    dkva_ref,
    dkvb_ref,
    gres_ref,
    gatt_ref,
    gain_two_ref,
    keys,
    values,
    queries,
    grads,
    all_probs,
    all_scores,
):
    lay_keys((kva_ref, kvb_ref), keys, values)
    grad_mixing = mix_low_ref[...] + mix_got_ref[...].astype(f32)
    back, gain_two = norm_back(res_ref[...], gain_ref[...].astype(f32), grad_mixing)
    gain_two_ref[...] = gain_two
    grad_residual = up_ref[...].astype(f32) + back
    gres_ref[...] = grad_residual
    grad_attended = grad_residual.astype(bf16)
    gatt_ref[...] = grad_attended
    grad_out = matmul_nt(grad_attended, wo_ref[...]).astype(bf16).astype(f32)
    bias = bias_ref[...]
    pairs = q_ref.shape[1] // lanes
    both = 2 * q_ref.shape[0]
    for pair in range(pairs):
        place = slice(pair * lanes, (pair + 1) * lanes)
        rows = slice(pair * both, (pair + 1) * both)
        query_pair = pair_rows(q_ref[:, place].astype(f32) * HEAD**-0.5, pair, group)
        grad_pair = pair_rows(grad_out[:, place], pair, group)
        queries[rows] = query_pair
        grads[rows] = grad_pair
        terms, inverse = pair_terms(keys[...], query_pair, bias)
        probs = terms * inverse
        all_probs[:, rows] = probs.astype(bf16)
        grad_probs = matmul_nt(values[...], grad_pair)
        delta = jnp.sum(probs * grad_probs, axis=0, keepdims=True)
        all_scores[:, rows] = (probs * (grad_probs - delta)).astype(bf16)

    grad_values = matmul(all_probs[...], grads[...]).astype(bf16)
    grad_keys = matmul(all_scores[...], queries[...]).astype(bf16)
    count = dkva_ref.shape[0]
    for i, ref in enumerate((dkva_ref, dkvb_ref)):
        ref[:, :lanes] = grad_keys[i * count : (i + 1) * count]
        ref[:, lanes:] = grad_values[i * count : (i + 1) * count]
    keys_turned = keys[...].T
    cos_table, sin_table = cos_ref[...], -sin_ref[...]
    for pair in range(pairs):
        place = slice(pair * lanes, (pair + 1) * lanes)
        turned = matmul(keys_turned, all_scores[:, pair * both : (pair + 1) * both])
        grad_query = pair_columns(turned, pair, group) * HEAD**-0.5
        dq_ref[:, place] = turn(grad_query, cos_table, sin_table).astype(bf16)


def attend_back(
    queries, kva, kvb, bias, mix_low, mix_got, residual, upstream, p, cos_table, sin_table
):
    rows, width = queries.shape
    total = bias.shape[0]
    kv_width = kva.shape[-1] // 2
    group = width // kv_width
    flops = 10 * rows * total * width * 3 + 2 * rows * width * residual.shape[1]
    return call(
        functools.partial(attend_back_kernel, group),
        [
            shape(rows, width, bf16),
            shape(total // 2, 2 * kv_width, bf16),
            shape(total // 2, 2 * kv_width, bf16),
            shape(*residual.shape, f32),
            shape(*residual.shape, bf16),
            shape(1, residual.shape[1], f32),
        ],
        [
            queries,
            kva,
            kvb,
            bias,
            mix_low,
            mix_got,
            residual,
            p["gain_two"],
            upstream,
            p["out"],
            cos_table,
            sin_table,
        ],
        scratch=[
            pltpu.VMEM((total, lanes), bf16),
            pltpu.VMEM((total, lanes), bf16),
            pltpu.VMEM((rows * width // HEAD, lanes), bf16),
            pltpu.VMEM((rows * width // HEAD, lanes), bf16),
            pltpu.VMEM((total, rows * width // HEAD), bf16),
            pltpu.VMEM((total, rows * width // HEAD), bf16),
        ],
        flops=flops,
        vmem=6,
    )


def qkv_back_kernel(
    dq_ref,
    low_ref,
    got_ref,
    cos_ref,
    sin_ref,
    w_ref,
    x_ref,
    gain_ref,
    gres_ref,
    dqkv_ref,
    gin_ref,
    gin_low_ref,
    gain_one_ref,
    bias_ref,
):
    query_width = dq_ref.shape[1]
    grad_kv = low_ref[...] + got_ref[...].astype(f32)
    dqkv_ref[:, :query_width] = dq_ref[...]
    grad_key = turn(grad_kv[:, :lanes], cos_ref[...], -sin_ref[...])
    dqkv_ref[:, query_width : query_width + lanes] = grad_key.astype(bf16)
    dqkv_ref[:, query_width + lanes :] = grad_kv[:, lanes:].astype(bf16)
    dqkv = dqkv_ref[...]
    bias_ref[...] = jnp.sum(dqkv.astype(f32), axis=0, keepdims=True)
    grad_normed = matmul_nt(dqkv, w_ref[...])
    back, gain_one = norm_back(x_ref[...].astype(f32), gain_ref[...].astype(f32), grad_normed)
    gain_one_ref[...] = gain_one
    grad_in = gres_ref[...] + back
    gin_ref[...] = grad_in
    gin_low_ref[...] = grad_in.astype(bf16)


def qkv_back(dq, low, got, x, grad_residual, p, cos_table, sin_table):
    rows, width = x.shape
    total = p["qkv"].shape[1]
    return call(
        qkv_back_kernel,
        [
            shape(rows, total, bf16),
            shape(rows, width, f32),
            shape(rows, width, bf16),
            shape(1, width, f32),
            shape(1, total, f32),
        ],
        [dq, low, got, cos_table, sin_table, p["qkv"], x, p["gain_one"], grad_residual],
        flops=2 * rows * width * total,
    )


def chunk_of(size):
    return 256 if size % 256 == 0 else 128


def ffn_kernel(lower_ref, upper_ref, wg_ref, wu_ref, wd_ref, low_ref, up_ref, hid_ref, g_ref, u_ref, rows, total):
    n = pl.program_id(0)
    half = rows.shape[0] // 2

    @pl.when(n == 0)
    def _():
        rows[:half] = lower_ref[...].reshape(half, rows.shape[1])
        rows[half:] = upper_ref[...].reshape(half, rows.shape[1])
        total[...] = jnp.zeros_like(total)

    gate = matmul(rows[...], wg_ref[...])
    up = matmul(rows[...], wu_ref[...])
    hidden = (gate * (1.0 / (1.0 + jnp.exp(-gate))) * up).astype(bf16)
    hid_ref[...] = hidden
    g_ref[...] = gate.astype(bf16)
    u_ref[...] = up.astype(bf16)
    total[...] += matmul(hidden, wd_ref[...])

    @pl.when(n == pl.num_programs(0) - 1)
    def _():
        low_ref[...] = total[:half].astype(bf16)
        up_ref[...] = total[half:].astype(bf16)


def ffn(lower, upper, p):
    half, width = lower.shape
    wide = p["gate"].shape[1]
    chunk = chunk_of(wide)
    rows = half + upper.shape[0]
    whole = pl.BlockSpec((half, width), lambda n: (0, 0))
    columns = pl.BlockSpec((width, chunk), lambda n: (0, n))
    return call(
        ffn_kernel,
        [shape(half, width, bf16), shape(rows - half, width, bf16)] + [shape(rows, wide, bf16)] * 3,
        [lower, upper, p["gate"], p["up"], p["down"]],
        scratch=[pltpu.VMEM((rows, width), bf16), pltpu.VMEM((rows, width), f32)],
        flops=6 * rows * width * wide,
        grid=(wide // chunk,),
        in_specs=[whole, whole, columns, columns, pl.BlockSpec((chunk, width), lambda n: (n, 0))],
        out_specs=[whole, whole] + [pl.BlockSpec((rows, chunk), lambda n: (0, n))] * 3,
    )


def ffn_back_kernel(
    lower_ref, upper_ref, g_ref, u_ref, wg_ref, wu_ref, wd_ref, low_ref, up_ref, gg_ref, gu_ref, rows, total
):
    n = pl.program_id(0)
    half = rows.shape[0] // 2

    @pl.when(n == 0)
    def _():
        rows[:half] = lower_ref[...].reshape(half, rows.shape[1])
        rows[half:] = upper_ref[...].reshape(half, rows.shape[1])
        total[...] = jnp.zeros_like(total)

    grad_hidden = matmul_nt(rows[...], wd_ref[...])
    gate = g_ref[...].astype(f32)
    up = u_ref[...].astype(f32)
    sigmoid = 1.0 / (1.0 + jnp.exp(-gate))
    grad_up = (grad_hidden * gate * sigmoid).astype(bf16)
    grad_gate = (grad_hidden * up * sigmoid * (1.0 + gate * (1.0 - sigmoid))).astype(bf16)
    gg_ref[...] = grad_gate
    gu_ref[...] = grad_up
    total[...] += matmul_nt(grad_gate, wg_ref[...]) + matmul_nt(grad_up, wu_ref[...])

    @pl.when(n == pl.num_programs(0) - 1)
    def _():
        low_ref[...] = total[:half].astype(bf16)
        up_ref[...] = total[half:].astype(bf16)


def ffn_back(lower, upper, gate, up, p):
    half, width = gate.shape[0] // 2, lower.shape[-1]
    wide = p["gate"].shape[1]
    chunk = chunk_of(wide)
    rows = 2 * half
    whole = pl.BlockSpec((half, width), lambda n: (0, 0))
    columns = pl.BlockSpec((width, chunk), lambda n: (0, n))
    inner = pl.BlockSpec((rows, chunk), lambda n: (0, n))
    return call(
        ffn_back_kernel,
        [shape(half, width, bf16), shape(rows - half, width, bf16)] + [shape(rows, wide, bf16)] * 2,
        [lower, upper, gate, up, p["gate"], p["up"], p["down"]],
        scratch=[pltpu.VMEM((rows, width), bf16), pltpu.VMEM((rows, width), f32)],
        flops=6 * rows * width * wide,
        grid=(wide // chunk,),
        in_specs=[
            whole,
            whole,
            inner,
            inner,
            columns,
            columns,
            pl.BlockSpec((chunk, width), lambda n: (n, 0)),
        ],
        out_specs=[whole, whole, inner, inner],
    )


def rows_of(ref):
    return ref[...].reshape(-1, ref.shape[-1])


def turn_rows(refs, turned):
    start = 0
    for ref in refs:
        turned[:, start : start + ref.shape[0]] = ref[...].T
        start += ref.shape[0]


def stack_rows(refs):
    return jnp.concatenate([rows_of(ref) for ref in refs])


def split_halves(info_ref, spread, result, keep_at, send_at):
    half = result.shape[0] // (2 * spread)
    for core in range(2):

        @pl.when(info_ref[0] == core)
        def _(core=core):
            for j in range(spread):
                for ref_at, whose in ((keep_at, core), (send_at, 1 - core)):
                    start = (2 * j + whose) * half
                    ref_at(j, result[start : start + half].astype(bf16))


def gate_up_product_kernel(lefts, spread, info_ref, *refs):
    left_refs, refs = refs[:lefts], refs[lefts:]
    keep_ref, send_ref, turned = refs[-3:]
    rights = refs[:-3]
    turn_rows(left_refs, turned)
    me = info_ref[1]
    count = len(rights) // 2
    for n in range(2):
        right = stack_rows(rights[n * count : (n + 1) * count])
        width = right.shape[1]
        for start in range(0, width, 512):
            place = slice(start, min(start + 512, width))
            result = matmul(turned[...], right[:, place])

            def keep_at(j, block, n=n, place=place):
                keep_ref[j ^ me, n, :, place] = block

            def send_at(j, block, n=n, place=place):
                send_ref[j ^ me, n, :, place] = block

            split_halves(info_ref, spread, result, keep_at, send_at)


def gate_up_product(info, lefts, gates, ups, spread):
    depth = sum(left.size // left.shape[-1] for left in lefts)
    height, width = lefts[0].shape[-1], gates[0].shape[1]
    out = shape(spread, 2, height // (2 * spread), width, bf16)
    return call(
        functools.partial(gate_up_product_kernel, len(lefts), spread),
        [out, out],
        [info] + list(lefts) + list(gates) + list(ups),
        scratch=[pltpu.VMEM((height, depth), bf16)],
        flops=4 * depth * height * width,
        vmem=8,
    )


def down_product_kernel(lefts, info_ref, *refs):
    left_refs, rights = refs[:lefts], refs[lefts:-3]
    keep_ref, send_ref, turned = refs[-3:]
    turn_rows(left_refs, turned)
    middle = keep_ref.shape[0]
    result = matmul(turned[: 2 * middle], stack_rows(rights))
    for core in range(2):

        @pl.when(info_ref[0] == core)
        def _(core=core):
            keep_ref[...] = result[core * middle : (core + 1) * middle].astype(bf16)
            send_ref[...] = result[(1 - core) * middle : (2 - core) * middle].astype(bf16)


def down_product(info, lefts, rights, rows):
    depth = sum(left.size // left.shape[-1] for left in lefts)
    height, width = lefts[0].shape[-1], rights[0].shape[-1]
    return call(
        functools.partial(down_product_kernel, len(lefts)),
        [shape(rows // 2, width, bf16)] * 2,
        [info] + list(lefts) + list(rights),
        scratch=[pltpu.VMEM((height, depth), bf16)],
        flops=2 * depth * height * width,
    )


def attn_product_kernel(count, spread, info_ref, *refs):
    normed, grad_qkv, attended, grad_attended = [
        refs[n * count : (n + 1) * count] for n in range(4)
    ]
    vector_ref, keep_ref, send_ref, turned = refs[4 * count :]
    start = 0
    for lefts, rights in ((normed, grad_qkv), (attended, grad_attended), (None, None)):
        if lefts:
            turn_rows(lefts, turned)
            result = matmul(turned[...], stack_rows(rights))
        else:
            rows = vector_ref[...]
            fill = jnp.zeros((lanes - rows.shape[0], rows.shape[1]), f32)
            result = jnp.concatenate([rows, fill]).T
        place = slice(start, start + result.shape[1])
        start += result.shape[1]

        def keep_at(j, block, place=place):
            keep_ref[info_ref[2 + j], :, place] = block

        def send_at(j, block, place=place):
            send_ref[info_ref[2 + spread + j], :, place] = block

        split_halves(info_ref, spread, result, keep_at, send_at)


def attn_product(info, normed, grad_qkv, attended, grad_attended, vectors, spread):
    depth = sum(part.shape[0] for part in normed)
    width = normed[0].shape[1]
    total = grad_qkv[0].shape[1] + grad_attended[0].shape[1] + lanes
    out = shape(spread, width // (2 * spread), total, bf16)
    return call(
        functools.partial(attn_product_kernel, len(normed), spread),
        [out, out],
        [info] + list(normed) + list(grad_qkv) + list(attended) + list(grad_attended) + [vectors],
        scratch=[pltpu.VMEM((width, depth), bf16)],
        flops=2 * depth * width * total,
    )


def pack_attn_kernel(info_ref, *refs):
    keep_ref, send_ref = refs[-2:]
    half = keep_ref.shape[0]
    for core in range(2):

        @pl.when(info_ref[0] == core)
        def _(core=core):
            start = 0
            for ref in refs[:-2]:
                place = slice(start, start + ref.shape[1])
                start += ref.shape[1]
                keep_ref[:, place] = ref[core * half : (core + 1) * half]
                send_ref[:, place] = ref[(1 - core) * half : (2 - core) * half]


def pack_attn(info, parts):
    out = shape(parts[0].shape[0] // 2, sum(part.shape[1] for part in parts), bf16)
    return call(pack_attn_kernel, [out, out], [info] + parts)


def pack_gate_up_kernel(spread, info_ref, gate_ref, up_ref, keep_ref, send_ref):
    me = info_ref[1]
    half, columns = keep_ref.shape[2:]
    for core in range(2):

        @pl.when(info_ref[0] == core)
        def _(core=core):
            for n, ref in enumerate((gate_ref, up_ref)):
                for j in range(spread):
                    block = ref[:, j * columns : (j + 1) * columns]
                    keep_ref[j ^ me, n] = block[core * half : (core + 1) * half]
                    send_ref[j ^ me, n] = block[(1 - core) * half : (2 - core) * half]


def pack_gate_up(info, gate, up, spread):
    out = shape(spread, 2, gate.shape[0] // 2, gate.shape[1] // spread, bf16)
    return call(
        functools.partial(pack_gate_up_kernel, spread), [out, out], [info, gate, up]
    )


def lay_attn_kernel(edges, at_ref, *refs):
    parts, outs = refs[:4], refs[4:]
    half = outs[0].shape[1]
    n = 0
    for ref in parts:
        for start in range(0, ref.shape[0], half):
            block = ref[start : start + half]
            for out, (low, high) in zip(outs, edges):
                out[at_ref[n]] = block[:, low:high]
            n += 1


def lay_attn(at, parts, half, edges):
    count = at.shape[0]
    outs = [shape(count, half, high - low, bf16) for low, high in edges]
    got = call(functools.partial(lay_attn_kernel, edges), outs, [at] + parts)
    return [part.reshape(count * half, -1) for part in got]


def lay_gate_up_kernel(at_ref, *refs):
    parts, outs = refs[:-2], refs[-2:]
    for i, ref in enumerate(parts):
        for n, out in enumerate(outs):
            columns = ref.shape[2]
            out[at_ref[i], :, :columns] = ref[n]
            if columns < out.shape[2]:
                rest = (out.shape[1], out.shape[2] - columns)
                out[at_ref[i], :, columns:] = jnp.zeros(rest, bf16)


def lay_gate_up(at, parts, wide):
    half = parts[0].shape[1]
    outs = [shape(len(parts), half, wide, bf16)] * 2
    got = call(lay_gate_up_kernel, outs, [at] + parts)
    return [part.reshape(len(parts) * half, wide) for part in got]


def spread_kernel(spread, info_ref, *refs):
    gate_ref, up_ref = refs[-2:]
    count = (len(refs) - 2) // 2
    per = spread // count
    me = info_ref[1]
    half = refs[0].shape[2]
    columns = gate_ref.shape[1] // spread
    for core in range(2):

        @pl.when(info_ref[0] == core)
        def _(core=core):
            for i in range(spread):
                for parts, whose in ((refs[:count], core), (refs[count:-2], 1 - core)):
                    for n, out in enumerate((gate_ref, up_ref)):
                        block = parts[i // per][i % per, n][:, :columns].astype(f32)
                        for j in range(spread):

                            @pl.when((i ^ me) == j)
                            def _(j=j, block=block, whose=whose, out=out):
                                place = slice(j * columns, (j + 1) * columns)
                                out[whose * half : (whose + 1) * half, place] = block


def spread_gate_up(info, mine, theirs, columns, spread):
    half = mine[0].shape[2]
    out = shape(2 * half, spread * columns, f32)
    return call(
        functools.partial(spread_kernel, spread), [out, out], [info] + list(mine) + list(theirs)
    )


def local(
    tokens,
    doc_starts,
    cotangent,
    norm_one,
    w_query,
    b_query,
    w_key,
    b_key,
    w_value,
    b_value,
    w_out,
    norm_two,
    w_gate,
    w_up,
    w_down,
):
    core = lax.axis_index("section")
    cores = lax.axis_size("section")
    spread = lax.axis_size("dp")
    micro_count, _, row_count, width = tokens.shape
    layers = range(2)
    share = row_count // cores
    shard = w_query.shape[1]
    half = shard // 2
    query_width = w_query.shape[2]
    kv_width = w_key.shape[2]
    ff = w_gate.shape[2]
    slice_ff = ff // spread

    me = lax.axis_index("dp")
    wide = -(-slice_ff // lanes) * lanes
    edge = query_width + 2 * kv_width
    per = kv_width // spread

    def order_of(mine):
        masks = step_masks("dp")

        def place(j, core):
            return sum(
                jnp.where(((me ^ j) & pair[core]) != 0, 1 << n, 0) for n, pair in enumerate(masks)
            )

        first, second = (0, 1) if mine else (1, 0)
        return [by_section(place(j, first), place(j, second)) for j in range(spread)]

    def owner(block, mine):
        first, second = (0, 1) if mine else (1, 0)
        masks = [distance(block, "dp", first), distance(block, "dp", second)]
        return me ^ by_section(*masks)

    info = jnp.stack([core, me] + order_of(True) + order_of(False)).astype(jnp.int32)
    attn_at = jnp.stack(
        [
            2 * owner(block, mine) + (core if mine else 1 - core)
            for mine in (True, False)
            for block in range(spread)
        ]
    ).astype(jnp.int32)
    gate_up_at = jnp.stack(
        [2 * (me ^ mask) + whose for whose in (core, 1 - core) for mask in range(spread)]
    ).astype(jnp.int32)

    def column(vector):
        return jnp.pad(vector, (0, shard - vector.shape[0]))

    vectors = jnp.stack(
        [norm_one[0], norm_two[0], b_query[0], column(b_key[0]), column(b_value[0])], axis=1
    )
    vectors = jnp.pad(vectors, ((0, 0), (0, lanes - vectors.shape[1])))

    def per_layer(keep, send):
        got = other(send)
        return by_section(keep, got), by_section(got, keep)

    attn_halves = per_layer(
        *pack_attn(info, [w_query[0], w_key[0], w_value[0], w_out[0], vectors])
    )
    gate_up_halves = per_layer(*pack_gate_up(info, w_gate[0], w_up[0], spread))
    down_other = other(w_down[0])
    downs = by_section(w_down[0], down_other), by_section(down_other, w_down[0])

    params = [{}, {}]
    clock, flows, last, pins = [0], [], [], []

    class Flow:
        def __init__(self, steps, slack):
            self.steps, self.slack = steps, slack
            self.move()
            flows.append(self)

        def move(self):
            self.value = next(self.steps, None)
            self.due = clock[0] + self.slack

        def finish(self):
            while self.value is not None:
                self.move()

    def turn_of(value):
        clock[0] += 1
        for flow in list(flows):
            if flow.value is not None and flow.due <= clock[0]:
                pins.append(flow.value)
                flow.move()
            if flow.value is None:
                flows.remove(flow)
        wait = last + pins
        pins.clear()
        return after(value, wait) if wait else value

    def done(value):
        last[:] = [value]

    def weights_steps(layer, part, blocks):
        p = params[layer]
        parts = []
        yield from gather_steps(part, "dp", lambda *got: parts.extend(got))
        blocks = after(blocks, parts[1])
        qkv, out, small = lay_attn(
            attn_at,
            parts + [other(part) for part in parts],
            half,
            ((0, edge), (edge, edge + width), (edge + width, edge + width + lanes)),
        )
        rows = small.T
        p["qkv"], p["out"] = qkv, out
        p["gain_one"], p["gain_two"] = rows[0:1], rows[1:2]
        key_bias, value_bias = [
            rows[n].reshape(spread, shard)[:, :per].reshape(1, -1) for n in (3, 4)
        ]
        p["bias"] = jnp.concatenate([rows[2:3], key_bias, value_bias], axis=1)
        blocks = [blocks[0]] + [direct(blocks[mask], "dp", mask) for mask in range(1, spread)]
        yield blocks
        p["gate"], p["up"] = lay_gate_up(
            gate_up_at, blocks + [other(block) for block in blocks], wide
        )
        p["down"] = jnp.pad(downs[layer], ((0, wide - slice_ff), (0, 0)))

    first = core * share
    place = lax.axis_index("ctx")
    places = place * row_count + first + jnp.arange(share, dtype=jnp.int32)
    my_tokens = lax.dynamic_slice_in_dim(tokens[:, 0], first, share, 1)
    my_cotangent = lax.dynamic_slice_in_dim(cotangent[:, 0], first, share, 1)
    key_places = jnp.concatenate(
        [
            (place ^ block) * row_count + whose * share + jnp.arange(share, dtype=jnp.int32)
            for whose in (core, 1 - core)
            for block in range(lax.axis_size("ctx"))
        ]
    )
    starts = doc_starts[:, 0, None, :]
    begins = jnp.max(jnp.where(starts <= places[None, :, None], starts, 0), axis=2)
    places_all = jnp.tile(places, micro_count)
    cos_all, sin_all = tables(begins.reshape(-1), places_all)
    visible = (key_places[None, :, None] <= places[None, None, :]) & (
        key_places[None, :, None] >= begins[:, None, :]
    )
    bias_all = jnp.where(visible, 0.0, masked).astype(f32)
    context = [
        (
            Part(bias_all, 0, n),
            Part(cos_all.reshape(micro_count, share, lanes), 0, n),
            Part(sin_all.reshape(micro_count, share, lanes), 0, n),
        )
        for n in range(micro_count)
    ]

    kept = [[{} for _ in range(micro_count)] for _ in layers]
    for n in range(micro_count):
        kept[1][n]["above"] = Part(my_cotangent, 0, n)
    def kv_steps(ks, kv):
        def give(*parts):
            whole = jnp.concatenate(parts)
            theirs = other(whole)
            for n, k in enumerate(ks):
                k["kva"], k["kvb"] = [
                    Part(part.reshape(-1, len(ks), share, 2 * kv_width), 1, n)
                    for part in (whole, theirs)
                ]

        yield from gather_steps(kv[None], "ctx", give)

    def run_q_all():
        flow = Flow(weights_steps(0, attn_halves[0], gate_up_halves[0]), weight_slack)
        while "qkv" not in params[0]:
            flow.move()
        kept[0][0]["weights"] = flow
        tokens_in = turn_of(my_tokens.reshape(-1, width))
        rows = qkv_rows(tokens_in, params[0], cos_all, sin_all, kv_width)
        done(rows[0])
        normed, queries = [part.reshape(micro_count, share, -1) for part in rows[:2]]
        for n in range(micro_count):
            k = kept[0][n]
            k["x"], k["normed"], k["queries"] = [
                Part(part, 0, n) for part in (my_tokens, normed, queries)
            ]
        flow = Flow(kv_steps(kept[0], rows[2]), 1)
        for n in range(micro_count):
            kept[0][n]["kv"] = flow
        part, blocks = after((attn_halves[1], gate_up_halves[1]), kept[0][0]["weights"].value)
        kept[1][0]["weights"] = Flow(weights_steps(1, part, blocks), 2)

    def run_q(n):
        k = kept[1][n]
        kept[0][n]["scatter"].finish()
        while "qkv" not in params[1]:
            kept[1][0]["weights"].move()
        k["x"] = turn_of(kept[0][n]["result"])
        k["normed"], k["queries"], kv = qkv_rows(k["x"], params[1], *context[n][1:], kv_width)
        done(k["normed"])
        k["kv"] = Flow(kv_steps([k], kv), 2)

    def run_a(layer, n):
        k, p = kept[layer][n], params[layer]
        k["kv"].finish()
        k["attended"], k["residual"], mixing = attend(
            k["queries"], k["kva"], k["kvb"], context[n][0], k["x"], p, turn_of
        )
        done(mixing)
        k["gather"] = Flow(gather_steps(mixing, "dp", lambda *got: k.update(mixing=got)), 2)

    def run_f(layer, n):
        k, p = kept[layer][n], params[layer]
        k["gather"].finish()
        kept[layer][0]["weights"].finish()
        lower, upper = k["mixing"]
        part_low, part_up, k["hidden"], k["gate"], k["up"] = ffn(lower, turn_of(upper), p)
        done(k["gate"])

        def give(low, got):
            k["result"] = (k["residual"] + low + got.astype(f32)).astype(bf16)

        k["scatter"] = Flow(scatter_steps(part_low, part_up, "dp", give), 2 if layer == 0 else 6)
        if layer:
            k["after"] = k["scatter"]

    def run_c():
        def give(*parts):
            for n in range(micro_count):
                kept[1][n]["grad_ffn"] = [
                    Part(part.reshape(-1, micro_count, share, width), 1, n) for part in parts
                ]

        rows = after(my_cotangent[None], last)
        kept[1][0]["cotangent"] = Flow(gather_steps(rows, "dp", give), 4)

    def run_d(layer, n):
        k, p = kept[layer][n], params[layer]
        if layer:
            kept[1][0]["cotangent"].finish()
        else:
            k["gather"].finish()
        lower, upper = k["grad_ffn"]
        part_low, part_up, k["grad_gate"], k["grad_up"] = ffn_back(
            lower, upper, turn_of(k["gate"]), k["up"], p
        )
        done(k["grad_gate"])
        k["scatter"] = Flow(
            scatter_steps(part_low, part_up, "dp", lambda *got: k.update(scattered=got)), 2
        )

    def run_b(layer, n):
        k, p = kept[layer][n], params[layer]
        k["scatter"].finish()
        bias, cos_table, sin_table = context[n]
        low, got = k["scattered"]
        k["dq"], dkva, dkvb, k["grad_residual"], k["grad_attended"], k["gain_two"] = attend_back(
            k["queries"],
            k["kva"],
            k["kvb"],
            bias,
            low,
            turn_of(got),
            k["residual"],
            k["above"],
            p,
            cos_table,
            sin_table,
        )
        done(k["dq"])
        pair = dkva.astype(f32) + other(dkvb).astype(f32)
        middle = pair.shape[0] // 2
        k["scatter"] = Flow(
            scatter_steps(
                pair[:middle], pair[middle:], "ctx", lambda *got: k.update(grad_kv=got)
            ),
            2,
        )

    def run_k(layer, n):
        k, p = kept[layer][n], params[layer]
        k["scatter"].finish()
        low, got = k["grad_kv"]
        k["grad_qkv"], k["grad_in"], grad_low, k["gain_one"], k["bias"] = qkv_back(
            k["dq"], low, turn_of(got), k["x"], k["grad_residual"], p, *context[n][1:]
        )
        done(k["grad_qkv"])
        if layer:
            below = kept[0][n]
            below["above"] = k["grad_in"]
            below["gather"] = Flow(
                gather_steps(grad_low, "dp", lambda *got: below.update(grad_ffn=got)), 2
            )

    ends = (place == 0) | (place == 3)
    hops = [[(0, 1), (3, 2)], [(1, 2), (2, 1)], [(1, 0), (2, 3)]]
    sums = {}

    def ctx_steps(name, value):
        for hop, route in enumerate(hops):
            got = lax.ppermute(value, "ctx", route)
            yield got
            if hop == 2:
                sums[name] = jnp.where(ends, got, value)
            else:
                value = (value.astype(f32) + got.astype(f32)).astype(bf16)

    waiting, moving, exchanges = {}, [], {}

    def tick(*names):
        for flow in list(moving):
            pins.append(flow.value)
            flow.move()
            if flow.value is None:
                moving.remove(flow)
        for name in names:
            if name not in waiting:
                exchanges.pop(name).finish()
            moving.append(Flow(ctx_steps(name, waiting.pop(name)), 1000))

    def column_of(layer, name):
        return [k[name] for k in kept[layer]]

    def parts_of(layer, name):
        return [part for k in kept[layer] for part in k[name]]

    def over_cores(keep, send):
        return keep.astype(f32) + other(send).astype(f32)

    def run_pd(layer):
        hidden = column_of(layer, "hidden")
        hidden[0] = turn_of(hidden[0])
        keep, send = down_product(info, hidden, parts_of(layer, "grad_ffn"), slice_ff)
        done(keep)
        waiting["down", layer] = over_cores(keep, send).astype(bf16)

    def run_pg(layer):
        grads = column_of(layer, "grad_gate")
        grads[0] = turn_of(grads[0])
        keep, send = gate_up_product(
            info, parts_of(layer, "mixing"), grads, column_of(layer, "grad_up"), spread
        )
        done(keep)
        blocks = over_cores(keep, send).astype(bf16)
        before = kept[layer][micro_count - 1]["scatter"].value

        def steps():
            sent = after(blocks, before) if before is not None else blocks
            parts = [sent[0]] + [direct(sent[mask], "dp", mask) for mask in range(1, spread)]
            yield parts[1:]
            middle = spread // 2
            waiting["low", layer] = jnp.stack(parts[:middle])
            waiting["high", layer] = jnp.stack(parts[middle:])

        exchanges["low", layer] = Flow(steps(), 3)

    def run_pa(layer):
        bias = sum(column_of(layer, "bias"))[0]

        def column_sum(vector):
            return jnp.pad(vector.reshape(spread, -1), ((0, 0), (0, shard - per))).reshape(-1)

        vectors = jnp.stack(
            [
                sum(column_of(layer, "gain_one"))[0],
                sum(column_of(layer, "gain_two"))[0],
                bias[:query_width],
                column_sum(bias[query_width : query_width + kv_width]),
                column_sum(bias[query_width + kv_width :]),
            ]
            + [jnp.zeros((width,), f32)] * 3
        )
        keep, send = attn_product(
            info,
            column_of(layer, "normed"),
            column_of(layer, "grad_qkv"),
            column_of(layer, "attended"),
            column_of(layer, "grad_attended"),
            turn_of(vectors),
            spread,
        )
        done(keep)
        attn = over_cores(keep, send).reshape(spread * half, -1)


        def give(low, got):
            waiting["attn", layer] = (low + got.astype(f32)).astype(bf16)

        exchanges["attn", layer] = Flow(scatter_steps(*jnp.split(attn, 2), "dp", give), 2)

    steps = dict(
        q=run_q,
        a=run_a,
        f=run_f,
        c=run_c,
        d=run_d,
        b=run_b,
        k=run_k,
        D=run_pd,
        G=run_pg,
        P=run_pa,
    )
    run_q_all()
    names = dict(d="down", l="low", h="high", a="attn")
    for word in order.split():
        if word[0] == "z":
            tick(*[(names[word[n]], int(word[n + 1])) for n in range(1, len(word), 2)])
        else:
            steps[word[0]](*[int(digit) for digit in word[1:]])
    while moving:
        tick()
    for k in kept[1]:
        if "result" not in k:
            k["after"].finish()

    section_out = both_rows([jnp.stack(column_of(layer, "result")) for layer in layers])
    section_grad = both_rows([jnp.stack(column_of(layer, "grad_in")) for layer in layers])

    final = [[sums[name, layer] for name in ("attn", "low", "high", "down")] for layer in layers]
    mine = [by_section(*pair) for pair in zip(*final)]
    theirs = [other(by_section(*pair[::-1])) for pair in zip(*final)]
    gate, up = spread_gate_up(info, mine[1:3], theirs[1:3], slice_ff, spread)

    def in_order(mine, theirs):
        return by_section(
            jnp.concatenate([mine, theirs]), jnp.concatenate([theirs, mine])
        ).astype(f32)

    attn = in_order(mine[0], theirs[0])
    down = in_order(mine[3], theirs[3])
    small = attn[:, edge + width :]
    return (
        section_out,
        section_grad,
        small[None, :, 0],
        attn[None, :, :query_width],
        small[None, :, 2],
        attn[None, :, query_width : query_width + kv_width],
        small[None, :per, 3],
        attn[None, :, query_width + kv_width : edge],
        small[None, :per, 4],
        attn[None, :, edge : edge + width],
        small[None, :, 1],
        gate[None],
        up[None],
        down[None],
    )


weight_slack = 3
order = (
    "a00 a01 f00 a02 f01 q0 f02 q1 a10 q2 a11 c f10 a12 f11 "
    "d10 f12 d11 b10 d12 D1 G1 b11 zd1 k10 b12 zl1 k11 d00 zh1 k12 d01 z P1 d02 za1 G0 z D0 b00 zl0 b01 zh0 k00 b02 zd0 k01 k02 "
    "P0 za0"
)


def both_rows(per_layer):
    first, second = per_layer
    got = other(by_section(second, first))
    return by_section(
        jnp.concatenate([first, got], axis=1), jnp.concatenate([got, second], axis=1)
    )[None, :, None]


def solution(mesh):
    return jax.shard_map(
        local,
        mesh=mesh,
        in_specs=(
            P(None, "dp", "ctx", None),
            P(None, "dp", None),
            P(None, "dp", "ctx", None),
            P("section", "dp"),
            P("section", "dp", None),
            P("section", "dp"),
            P("section", "dp", None),
            P("section", "dp"),
            P("section", "dp", None),
            P("section", "dp"),
            P("section", "dp", None),
            P("section", "dp"),
            P("section", "dp", None),
            P("section", "dp", None),
            P("section", "dp", None),
        ),
        out_specs=(
            P("section", None, "dp", "ctx", None),
            P("section", None, "dp", "ctx", None),
            P("section", "dp"),
            P("section", "dp", None),
            P("section", "dp"),
            P("section", "dp", None),
            P("section", "dp"),
            P("section", "dp", None),
            P("section", "dp"),
            P("section", "dp", None),
            P("section", "dp"),
            P("section", "dp", None),
            P("section", "dp", None),
            P("section", "dp", None),
        ),
        check_vma=False,
    )
```

time: 1200 us -> 928 us (0.77); the launches traced: 1200 us -> 910 us
  Pallas kernels: 389 us -> 243 us
  other arithmetic: 149 us -> 53.9 us
  starting transfers between devices: 132 us -> 224 us
  waiting for transfers between devices: 359 us -> 293 us
  local copies, waits for them, and re-layouts: 151 us -> 90.7 us
    psum x2 -> x0, waiting for transfers between devices: 220 us -> none  [local(): final[layer] = lax.psum(parts, 'ctx')]
    pallas_call x46 -> x47, Pallas kernels: 389 us -> 243 us  [call(): pl.pallas_call(kernel, out_shape=outs, grid=grid or (), in_specs=specs, o...]
    ppermute x8 -> x36, waiting for transfers between devices: 0.02 us -> 121 us  [the longest x24 110 us: ctx_steps(): got = lax.ppermute(value, 'ctx', route)]
    ppermute x8 -> x36, starting transfers between devices: 12.3 us -> 57.7 us  [the longest x24 45.6 us: ctx_steps(): got = lax.ppermute(value, 'ctx', route)]
    another operation x31 -> x7, other arithmetic: 42 us -> 2.9 us  [the longest x2 2.43 us: steps(): waiting['high', layer] = jnp.stack(parts[middle:])]
    ppermute x32 -> x37, starting transfers between devices: 43.4 us -> 77.5 us  [other(): return lax.ppermute(block, 'section', [(0, 1), (1, 0)])]
    ppermute x88 -> x72, waiting for transfers between devices: 136 us -> 170 us  [step(): return lax.ppermute(block, ('section', axis), route)]
    select_n x23 -> x6, other arithmetic: 41.7 us -> 9.09 us  [by_section(): return jnp.where(lax.axis_index('section') == 0, first, second)]
  transfers between devices with their start and end apart: 130 -> 145, of which waited for: 30 -> 44; matrix products, arithmetic and copies ran while one was open for 23% -> 8% of each run, Pallas kernels for 33% -> 25%
where the time goes in v2:
time: 928 us; the launch traced here: 910 us
  waiting for transfers between devices  293 us (32%)
  Pallas kernels  243 us (26%)
  starting transfers between devices  224 us (24%)
  local copies, waits for them, and re-layouts  90.7 us (10%)
  other arithmetic  53.9 us (6%)
    pallas_call x47, Pallas kernels, call(): pl.pallas_call(kernel, out_shape=outs, grid=grid or (), in_specs=specs, o...  243 us
    ppermute x72, waiting for transfers between devices, step(): return lax.ppermute(block, ('section', axis), route)  170 us
    ppermute x24, waiting for transfers between devices, ctx_steps(): got = lax.ppermute(value, 'ctx', route)  110 us
    ppermute x72, starting transfers between devices, step(): return lax.ppermute(block, ('section', axis), route)  88.7 us
    ppermute x37, starting transfers between devices, other(): return lax.ppermute(block, 'section', [(0, 1), (1, 0)])  77.5 us
    unnamed x574, local copies, waits for them, and re-layouts  65.2 us
    ppermute x24, starting transfers between devices, ctx_steps(): got = lax.ppermute(value, 'ctx', route)  45.6 us
  transfers between devices with their start and end apart: 145, of which 44 were waited for; matrix products, arithmetic and copies ran while one was open for 8% of the time, Pallas kernels for 25%

profile of v2, /device:TPU:1, one launch (start us, length us, event | category | flops | bytes accessed | tf_op | source)
XLA Modules:
  0.0 909.7 jit_solution(15301294184793808042)
XLA Ops:
  20.1 5.4 collective-permute-done.1
  31.7 7.2 collective-permute-done.2.refs_1_
  63.9 10.7 %collective-permute-done.12.refs_2_ = bf16[2,112,1216]{2,1,0:T(8,128)(2,1)} collective-permute-done((bf16[2,112,1216]{2,1,0:T(8,128)(2,1)}, bf16[2,112,1216]{2,1,0:T(8,128)(2,1)}, u32[]{:S(2)}, u32[]{:S(2)}) %collective-permute-start.12) | collective-permute-done | bytes 544800 | tf_op jit(solution)/shard_map/ppermute | solution.py:75
  85.5 12.6 %collective-permute-done.6 = bf16[2,384,256]{2,1,0:T(8,128)(2,1)S(1)} collective-permute-done((bf16[2,384,256]{2,1,0:T(8,128)(2,1)S(1)}, bf16[2,384,256]{2,1,0:T(8,128)(2,1)S(1)}, u32[]{:S(2)}, u32[]{:S(2)}) %collective-permute-start.6) | collective-permute-done | bytes 393248 | tf_op jit(solution)/shard_map/ppermute | solution.py:44
  113.0 5.9 shard_map.257
  120.9 5.6 shard_map.259
  134.3 5.6 collective-permute-done.9.upper_ref.refs_1_
  140.4 6.8 shard_map.261
  147.2 5.6 shard_map.262
  173.7 7.1 shard_map.263
  188.9 5.6 collective-permute-done.25
  195.9 6.2 shard_map.266
  205.3 11.2 %collective-permute-start.38 = (bf16[4,128,256]{2,1,0:T(8,128)(2,1)S(1)}, bf16[4,128,256]{2,1,0:T(8,128)(2,1)S(1)}, u32[]{:S(2)}, u32[]{:S(2)}) collective-permute-start(bf16[4,128,256]{2,1,0:T(8,128)(2,1)S(1)} %get-tuple-element.571), channel_id=1, source_target_pairs={{0,16},{16,0},{1,17},{17,1},{2,18},{18,2},{3,19},{19,3},{4,20},{20... | collective-permute-start | bytes 786440 | tf_op jit(solution)/shard_map/ppermute | solution.py:79
  220.9 5.6 shard_map.268
  231.7 4.1 collective-permute-start.43
  237.0 5.8 shard_map.270
  250.8 4.5 collective-permute-start.53
  263.1 6.0 shard_map.272
  269.2 5.6 shard_map.273
  276.4 6.2 collective-permute-done.52.upper_ref.refs_3_
  283.9 6.0 shard_map.274
  290.0 9.2 %shard_map.275 = (bf16[256,896]{1,0:T(8,128)(2,1)S(1)}, bf16[256,896]{1,0:T(8,128)(2,1)S(1)}, bf16[512,1280]{1,0:T(8,128)(2,1)S(1)}, bf16[512,1280]{1,0:T(8,128)(2,1)S(1)}) custom-call(bf16[2,3,128,896]{3,2,1,0:T(8,128)(2,1)S(1)} %constant_dynamic-update-slice_fusion.15.lower_ref.refs_3_.refs_5_.refs_7_, ...), custom_call_target="tpu_custom_call" | custom-call | flops 3523215360 | bytes 13959168 | tf_op jit(solution)/shard_map/pallas_call | solution.py:142
  300.8 6.4 shard_map.276
  308.3 9.2 %shard_map.277 = (bf16[256,896]{1,0:T(8,128)(2,1)S(1)}, bf16[256,896]{1,0:T(8,128)(2,1)S(1)}, bf16[512,1280]{1,0:T(8,128)(2,1)S(1)}, bf16[512,1280]{1,0:T(8,128)(2,1)S(1)}) custom-call(bf16[2,3,128,896]{3,2,1,0:T(8,128)(2,1)S(1)} %constant_dynamic-update-slice_fusion.15.lower_ref.refs_3_.refs_5_.refs_7_, ...), custom_call_target="tpu_custom_call" | custom-call | flops 3523215360 | bytes 13959168 | tf_op jit(solution)/shard_map/pallas_call | solution.py:142
  319.1 7.7 shard_map.278
  330.3 9.4 %shard_map.279 = (bf16[256,896]{1,0:T(8,128)(2,1)S(1)}, bf16[256,896]{1,0:T(8,128)(2,1)S(1)}, bf16[512,1280]{1,0:T(8,128)(2,1)S(1)}, bf16[512,1280]{1,0:T(8,128)(2,1)S(1)}) custom-call(bf16[2,3,128,896]{3,2,1,0:T(8,128)(2,1)S(1)} %constant_dynamic-update-slice_fusion.15.lower_ref.refs_3_.refs_5_.refs_7_, ...), custom_call_target="tpu_custom_call" | custom-call | flops 3523215360 | bytes 13959168 | tf_op jit(solution)/shard_map/pallas_call | solution.py:142
  342.3 4.2 collective-permute-done.67
  346.5 4.8 shard_map.280
  356.2 11.0 %shard_map.281 = (bf16[4,2,112,1280]{3,2,1,0:T(8,128)(2,1)S(1)}, bf16[4,2,112,1280]{3,2,1,0:T(8,128)(2,1)S(1)}) custom-call(s32[10]{0:T(128)S(1)} %stack.193.info_ref, bf16[256,896]{1,0:T(8,128)(2,1)S(1)} %constant_dynamic-update-slice_fusion.9.lower_ref.refs_0_, bf16[256,896]{1,0:T(8,128)(2,1)S(1)} %copy-done.121, bf16[256,896]{1,0:T(8,128)(2,1)S(1)} %copy-done.84, ...), custom_call_target="tpu_custom_call" | custom-call | flops 7046430720 | bytes 15204392 | tf_op jit(solution)/shard_map/pallas_call | solution.py:142
  376.3 7.7 shard_map.282
  394.5 6.3 collective-permute-start.83
  405.8 16.6 %collective-permute-done.83 = bf16[608,896]{1,0:T(8,128)(2,1)S(1)} collective-permute-done((bf16[608,896]{1,0:T(8,128)(2,1)S(1)}, bf16[608,896]{1,0:T(8,128)(2,1)S(1)}, u32[]{:S(2)}, u32[]{:S(2)}) %collective-permute-start.83) | collective-permute-done | bytes 1089568 | tf_op jit(solution)/shard_map/ppermute | solution.py:1105
  424.4 8.0 collective-permute-done.50
  434.8 7.7 shard_map.284
  442.8 4.9 collective-permute-start.90
  451.4 10.8 %collective-permute-start.85 = (bf16[256,256]{1,0:T(8,128)(2,1)S(1)}, bf16[256,256]{1,0:T(8,128)(2,1)S(1)}, u32[]{:S(2)}, u32[]{:S(2)}) collective-permute-start(bf16[256,256]{1,0:T(8,128)(2,1)S(1)} %slice.635), channel_id=1, source_target_pairs={{0,8},{4,12},{8,0},{12,4},{16,24},{20,28},{24,16},{28,20},{1,9},{5... | collective-permute-start | bytes 393224 | tf_op jit(solution)/shard_map/ppermute | solution.py:44
  467.3 7.6 collective-permute-done.85
  476.3 4.9 collective-permute-start.88
  484.4 9.1 %shard_map.286 = (bf16[256,896]{1,0:T(8,128)(2,1)S(1)}, bf16[256,896]{1,0:T(8,128)(2,1)S(1)}, bf16[512,1280]{1,0:T(8,128)(2,1)S(1)}, bf16[512,1280]{1,0:T(8,128)(2,1)S(1)}) custom-call(bf16[256,896]{1,0:T(8,128)(2,1)S(1)} %constant_dynamic-update-slice_fusion.17.lower_ref.refs_3_, bf16[256,896]{1,0:T(8,128)(2,1)S(1)} %collective-permute-done.74.upper_ref.refs_4_, ...), custom_call_target="tpu_custom_call" | custom-call | flops 3523215360 | bytes 13959168 | tf_op jit(solution)/shard_map/pallas_call | solution.py:142
  493.6 11.3 %collective-permute-done.88.got_ref = bf16[128,256]{1,0:T(8,128)(2,1)S(1)} collective-permute-done((bf16[128,256]{1,0:T(8,128)(2,1)S(1)}, bf16[128,256]{1,0:T(8,128)(2,1)S(1)}, u32[]{:S(2)}, u32[]{:S(2)}) %collective-permute-start.88) | collective-permute-done | bytes 65568 | tf_op jit(solution)/shard_map/ppermute | solution.py:44
  525.1 10.2 %shard_map.288 = (bf16[256,896]{1,0:T(8,128)(2,1)S(1)}, bf16[256,896]{1,0:T(8,128)(2,1)S(1)}, bf16[512,1280]{1,0:T(8,128)(2,1)S(1)}, bf16[512,1280]{1,0:T(8,128)(2,1)S(1)}) custom-call(bf16[256,896]{1,0:T(8,128)(2,1)} %constant_dynamic-update-slice_fusion.21.lower_ref.refs_5_, bf16[256,896]{1,0:T(8,128)(2,1)S(1)} %collective-permute-done.94.upper_ref.refs_6_, ...), custom_call_target="tpu_custom_call" | custom-call | flops 3523215360 | bytes 13959168 | tf_op jit(solution)/shard_map/pallas_call | solution.py:142
  539.1 5.1 collective-permute-start.102
  549.9 5.1 collective-permute-done.98
  564.1 9.1 %shard_map.290 = (bf16[256,896]{1,0:T(8,128)(2,1)S(1)}, bf16[256,896]{1,0:T(8,128)(2,1)S(1)}, bf16[512,1280]{1,0:T(8,128)(2,1)S(1)}, bf16[512,1280]{1,0:T(8,128)(2,1)S(1)}) custom-call(bf16[256,896]{1,0:T(8,128)(2,1)S(1)} %constant_dynamic-update-slice_fusion.19.lower_ref.refs_7_, bf16[256,896]{1,0:T(8,128)(2,1)S(1)} %collective-permute-done.93.upper_ref.refs_8_, ...), custom_call_target="tpu_custom_call" | custom-call | flops 3523215360 | bytes 13959168 | tf_op jit(solution)/shard_map/pallas_call | solution.py:142
  574.0 13.3 %collective-permute-done.99 = bf16[2,2,112,1280]{3,2,1,0:T(8,128)(2,1)S(1)} collective-permute-done((bf16[2,2,112,1280]{3,2,1,0:T(8,128)(2,1)S(1)}, bf16[2,2,112,1280]{3,2,1,0:T(8,128)(2,1)S(1)}, u32[]{:S(2)}, u32[]{:S(2)}) %collective-permute-start.99) | collective-permute-done | bytes 1146912 | tf_op jit(solution)/shard_map/ppermute | solution.py:1105
  588.3 11.4 %shard_map.291 = (bf16[4,2,112,1280]{3,2,1,0:T(8,128)(2,1)S(1)}, bf16[4,2,112,1280]{3,2,1,0:T(8,128)(2,1)S(1)}) custom-call(s32[10]{0:T(128)S(1)} %stack.193.info_ref, bf16[256,896]{1,0:T(8,128)(2,1)S(1)} %copy-done.86, bf16[256,896]{1,0:T(8,128)(2,1)S(1)} %copy-done.115, bf16[256,896]{1,0:T(8,128)(2,1)} %constant_dynamic-update-slice_fusion.3.lower_ref.refs_2_, ...), custom_call_target="tpu_custom_call" | custom-call | flops 7046430720 | bytes 15204392 | tf_op jit(solution)/shard_map/pallas_call | solution.py:142
  614.9 18.1 %collective-permute-done.101 = bf16[2,2,112,1280]{3,2,1,0:T(8,128)(2,1)S(1)} collective-permute-done((bf16[2,2,112,1280]{3,2,1,0:T(8,128)(2,1)S(1)}, bf16[2,2,112,1280]{3,2,1,0:T(8,128)(2,1)S(1)}, u32[]{:S(2)}, u32[]{:S(2)}) %collective-permute-start.101) | collective-permute-done | bytes 1146912 | tf_op jit(solution)/shard_map/ppermute | solution.py:1105
  633.4 5.5 shard_map.292
  640.0 7.7 shard_map.293
  653.3 16.2 %collective-permute-done.109 = bf16[256,256]{1,0:T(8,128)(2,1)S(1)} collective-permute-done((bf16[256,256]{1,0:T(8,128)(2,1)S(1)}, bf16[256,256]{1,0:T(8,128)(2,1)S(1)}, u32[]{:S(2)}, u32[]{:S(2)}) %collective-permute-start.109) | collective-permute-done | bytes 131104 | tf_op jit(solution)/shard_map/ppermute | solution.py:44
  671.2 7.7 shard_map.294
  689.4 6.4 collective-permute-done.110.got_ref
  701.0 8.3 shard_map.296
  720.3 28.5 %collective-permute-done.125 = bf16[256,256]{1,0:T(8,128)(2,1)S(1)} collective-permute-done((bf16[256,256]{1,0:T(8,128)(2,1)S(1)}, bf16[256,256]{1,0:T(8,128)(2,1)S(1)}, u32[]{:S(2)}, u32[]{:S(2)}) %collective-permute-start.125) | collective-permute-done | bytes 131104 | tf_op jit(solution)/shard_map/ppermute | solution.py:44
  780.1 18.2 %collective-permute-done.141 = bf16[608,896]{1,0:T(8,128)(2,1)S(1)} collective-permute-done((bf16[608,896]{1,0:T(8,128)(2,1)S(1)}, bf16[608,896]{1,0:T(8,128)(2,1)S(1)}, u32[]{:S(2)}, u32[]{:S(2)}) %collective-permute-start.141) | collective-permute-done | bytes 1089568 | tf_op jit(solution)/shard_map/ppermute | solution.py:1105
  807.1 6.0 collective-permute-done.129
  822.8 8.8 collective-permute-done.137
  835.6 5.3 collective-permute-done.131
  840.9 5.7 collective-permute-start.139
  846.7 9.5 %collective-permute-done.135 = bf16[2,2,112,1280]{3,2,1,0:T(8,128)(2,1)S(1)} collective-permute-done((bf16[2,2,112,1280]{3,2,1,0:T(8,128)(2,1)S(1)}, bf16[2,2,112,1280]{3,2,1,0:T(8,128)(2,1)S(1)}, u32[]{:S(2)}, u32[]{:S(2)}) %collective-permute-start.135) | collective-permute-done | bytes 1146912 | tf_op jit(solution)/shard_map/ppermute | solution.py:1105
  857.2 7.3 collective-permute-start.138
  864.6 14.9 %collective-permute-done.143 = bf16[608,896]{1,0:T(8,128)(2,1)S(1)} collective-permute-done((bf16[608,896]{1,0:T(8,128)(2,1)S(1)}, bf16[608,896]{1,0:T(8,128)(2,1)S(1)}, u32[]{:S(2)}, u32[]{:S(2)}) %collective-permute-start.143) | collective-permute-done | bytes 1089568 | tf_op jit(solution)/shard_map/ppermute | solution.py:1105
  890.4 4.8 collective-permute-start.134
  897.0 6.3 shard_map.300
  (1067 shorter events, 369.0 us)
Async XLA Ops:
  7.6 91.8 %collective-permute-start.19 = (bf16[1216,896]{1,0:T(8,128)(2,1)}, bf16[1216,896]{1,0:T(8,128)(2,1)}, u32[]{:S(2)}, u32[]{:S(2)}) collective-permute-start(bf16[1216,896]{1,0:T(8,128)(2,1)} %bitcast.284), channel_id=1, source_target_pairs={{0,16},{16,0},{1,17},{17,1},{2,18},{18,2},{3,19},{19,3},{4,20},{20... | collective-permute-start | bytes 6537224 | tf_op jit(solution)/shard_map/ppermute | solution.py:79
  15.3 25.1 %collective-permute-start.10 = (bf16[4,2,112,1216]{3,2,1,0:T(8,128)(2,1)}, bf16[4,2,112,1216]{3,2,1,0:T(8,128)(2,1)}, u32[]{:S(2)}, u32[]{:S(2)}) collective-permute-start(bf16[4,2,112,1216]{3,2,1,0:T(8,128)(2,1)} %get-tuple-element.247), channel_id=1, source_target_pairs={{0,16},{16,0},{1,17},{17,1},{2,18},{18,2},{3,19},{19,3},{4,20},{20... | collective-permute-start | bytes 6537224 | tf_op jit(solution)/shard_map/ppermute | solution.py:79
  48.5 26.0 %collective-permute-start.12 = (bf16[2,112,1216]{2,1,0:T(8,128)(2,1)}, bf16[2,112,1216]{2,1,0:T(8,128)(2,1)}, u32[]{:S(2)}, u32[]{:S(2)}) collective-permute-start(bf16[2,112,1216]{2,1,0:T(8,128)(2,1)} %get-tuple-element.548), channel_id=1, source_target_pairs={{0,2},{1,3},{2,0},{3,1},{4,6},{5,7},{6,4},{7,5},{8,10},{9,11},{10,... | collective-permute-start | bytes 1634312 | tf_op jit(solution)/shard_map/ppermute | solution.py:75
  48.8 25.8 %collective-permute-start.11 = (bf16[2,112,1216]{2,1,0:T(8,128)(2,1)}, bf16[2,112,1216]{2,1,0:T(8,128)(2,1)}, u32[]{:S(2)}, u32[]{:S(2)}) collective-permute-start(bf16[2,112,1216]{2,1,0:T(8,128)(2,1)} %get-tuple-element.549), channel_id=1, source_target_pairs={{0,1},{1,0},{2,3},{3,2},{4,5},{5,4},{6,7},{7,6},{8,9},{9,8},{10,11... | collective-permute-start | bytes 1634312 | tf_op jit(solution)/shard_map/ppermute | solution.py:75
  76.2 24.6 %collective-permute-start.15 = (bf16[2,112,1216]{2,1,0:T(8,128)(2,1)S(1)}, bf16[2,112,1216]{2,1,0:T(8,128)(2,1)S(1)}, u32[]{:S(2)}, u32[]{:S(2)}) collective-permute-start(bf16[2,112,1216]{2,1,0:T(8,128)(2,1)S(1)} %copy-done.12), channel_id=1, source_target_pairs={{0,16},{16,0},{1,17},{17,1},{2,18},{18,2},{3,19},{19,3},{4,20},{20... | collective-permute-start | bytes 1634312 | tf_op jit(solution)/shard_map/ppermute | solution.py:79
  78.0 20.1 %collective-permute-start.6 = (bf16[2,384,256]{2,1,0:T(8,128)(2,1)S(1)}, bf16[2,384,256]{2,1,0:T(8,128)(2,1)S(1)}, u32[]{:S(2)}, u32[]{:S(2)}) collective-permute-start(bf16[2,384,256]{2,1,0:T(8,128)(2,1)S(1)} %pad_maximum_fusion.11), channel_id=1, source_target_pairs={{0,8},{4,12},{8,0},{12,4},{16,24},{20,28},{24,16},{28,20},{1,9},{5... | collective-permute-start | bytes 1179656 | tf_op jit(solution)/shard_map/ppermute | solution.py:44
  81.5 22.9 %collective-permute-start.18 = (bf16[2,112,1216]{2,1,0:T(8,128)(2,1)}, bf16[2,112,1216]{2,1,0:T(8,128)(2,1)S(1)}, u32[]{:S(2)}, u32[]{:S(2)}) collective-permute-start(bf16[2,112,1216]{2,1,0:T(8,128)(2,1)} %collective-permute-done.13.refs_3_), channel_id=1, source_target_pairs={{0,16},{16,0},{1,17},{17,1},{2,18},{18,2},{3,19},{19,3},{4,20},{20... | collective-permute-start | bytes 1634312 | tf_op jit(solution)/shard_map/ppermute | solution.py:79
  82.8 22.1 %collective-permute-start.17 = (bf16[2,112,1216]{2,1,0:T(8,128)(2,1)}, bf16[2,112,1216]{2,1,0:T(8,128)(2,1)S(1)}, u32[]{:S(2)}, u32[]{:S(2)}) collective-permute-start(bf16[2,112,1216]{2,1,0:T(8,128)(2,1)} %collective-permute-done.12.refs_2_), channel_id=1, source_target_pairs={{0,16},{16,0},{1,17},{17,1},{2,18},{18,2},{3,19},{19,3},{4,20},{20... | collective-permute-start | bytes 1634312 | tf_op jit(solution)/shard_map/ppermute | solution.py:79
  104.4 49.8 %collective-permute-start.32 = (bf16[224,2176]{1,0:T(8,128)(2,1)S(1)}, bf16[224,2176]{1,0:T(8,128)(2,1)S(1)}, u32[]{:S(2)}, u32[]{:S(2)}) collective-permute-start(bf16[224,2176]{1,0:T(8,128)(2,1)S(1)} %constant_dynamic-update-slice_fusion.5.refs_0_), channel_id=1, source_target_pairs={{0,16},{16,0},{1,17},{17,1},{2,18},{18,2},{3,19},{19,3},{4,20},{20... | collective-permute-start | bytes 2924552 | tf_op jit(solution)/shard_map/ppermute | solution.py:79
  111.3 44.3 %collective-permute-start.33 = (bf16[224,2176]{1,0:T(8,128)(2,1)S(1)}, bf16[224,2176]{1,0:T(8,128)(2,1)S(1)}, u32[]{:S(2)}, u32[]{:S(2)}) collective-permute-start(bf16[224,2176]{1,0:T(8,128)(2,1)S(1)} %collective-permute-done.24.refs_1_), channel_id=1, source_target_pairs={{0,16},{16,0},{1,17},{17,1},{2,18},{18,2},{3,19},{19,3},{4,20},{20... | collective-permute-start | bytes 2924552 | tf_op jit(solution)/shard_map/ppermute | solution.py:79
  129.5 53.0 %collective-permute-start.31 = (bf16[2,112,1216]{2,1,0:T(8,128)(2,1)}, bf16[2,112,1216]{2,1,0:T(8,128)(2,1)}, u32[]{:S(2)}, u32[]{:S(2)}) collective-permute-start(bf16[2,112,1216]{2,1,0:T(8,128)(2,1)} %get-tuple-element.543), channel_id=1, source_target_pairs={{0,3},{1,2},{2,1},{3,0},{4,7},{5,6},{6,5},{7,4},{8,11},{9,10},{10,... | collective-permute-start | bytes 1634312 | tf_op jit(solution)/shard_map/ppermute | solution.py:75
  131.9 50.6 %collective-permute-start.30 = (bf16[2,112,1216]{2,1,0:T(8,128)(2,1)}, bf16[2,112,1216]{2,1,0:T(8,128)(2,1)}, u32[]{:S(2)}, u32[]{:S(2)}) collective-permute-start(bf16[2,112,1216]{2,1,0:T(8,128)(2,1)} %get-tuple-element.544), channel_id=1, source_target_pairs={{0,2},{1,3},{2,0},{3,1},{4,6},{5,7},{6,4},{7,5},{8,10},{9,11},{10,... | collective-permute-start | bytes 1634312 | tf_op jit(solution)/shard_map/ppermute | solution.py:75
  139.9 29.4 %collective-permute-start.23 = (bf16[256,896]{1,0:T(8,128)(2,1)}, bf16[256,896]{1,0:T(8,128)(2,1)}, u32[]{:S(2)}, u32[]{:S(2)}) collective-permute-start(bf16[256,896]{1,0:T(8,128)(2,1)} %constant_dynamic-update-slice_fusion.3.lower_ref.refs_2_), channel_id=1, source_target_pairs={{0,2},{1,3},{2,0},{3,1},{16,17},{17,16},{18,19},{19,18},{4,6},{5,7... | collective-permute-start | bytes 1376264 | tf_op jit(solution)/shard_map/ppermute | solution.py:44
  167.5 28.3 %collective-permute-start.28 = (bf16[256,896]{1,0:T(8,128)(2,1)}, bf16[256,896]{1,0:T(8,128)(2,1)S(1)}, u32[]{:S(2)}, u32[]{:S(2)}) collective-permute-start(bf16[256,896]{1,0:T(8,128)(2,1)} %constant_dynamic-update-slice_fusion.7.lower_ref.refs_4_), channel_id=1, source_target_pairs={{0,2},{1,3},{2,0},{3,1},{16,17},{17,16},{18,19},{19,18},{4,6},{5,7... | collective-permute-start | bytes 1376264 | tf_op jit(solution)/shard_map/ppermute | solution.py:44
  256.1 33.8 %collective-permute-start.60 = (bf16[2,3,128,896]{3,2,1,0:T(8,128)(2,1)S(1)}, bf16[2,3,128,896]{3,2,1,0:T(8,128)(2,1)S(1)}, u32[]{:S(2)}, u32[]{:S(2)}) collective-permute-start(bf16[2,3,128,896]{3,2,1,0:T(8,128)(2,1)S(1)} %constant_dynamic-update-slice_fusion.15.lower_ref.refs_3_.refs_5_.refs_7_), channel_id=1, source_target_pairs={{0,2},{1,3},{2,0},{3,1},{16,17},{17,16},{18,19},{19,18},{4,6},{5,7... | collective-permute-start | bytes 4128776 | tf_op jit(solution)/shard_map/ppermute | solution.py:44
  262.8 19.8 %collective-permute-start.52 = (bf16[256,896]{1,0:T(8,128)(2,1)S(1)}, bf16[256,896]{1,0:T(8,128)(2,1)S(1)}, u32[]{:S(2)}, u32[]{:S(2)}) collective-permute-start(bf16[256,896]{1,0:T(8,128)(2,1)S(1)} %constant_dynamic-update-slice_fusion.11.lower_ref.refs_2_), channel_id=1, source_target_pairs={{0,2},{1,3},{2,0},{3,1},{16,17},{17,16},{18,19},{19,18},{4,6},{5,7... | collective-permute-start | bytes 1376264 | tf_op jit(solution)/shard_map/ppermute | solution.py:44
  299.6 19.5 %collective-permute-start.49 = (bf16[256,896]{1,0:T(8,128)(2,1)S(1)}, bf16[256,896]{1,0:T(8,128)(2,1)S(1)}, u32[]{:S(2)}, u32[]{:S(2)}) collective-permute-start(bf16[256,896]{1,0:T(8,128)(2,1)S(1)} %get-tuple-element.295), channel_id=1, source_target_pairs={{0,2},{1,3},{2,0},{3,1},{16,17},{17,16},{18,19},{19,18},{4,6},{5,7... | collective-permute-start | bytes 1376264 | tf_op jit(solution)/shard_map/ppermute | solution.py:44
  318.5 23.8 %collective-permute-start.55 = (bf16[256,896]{1,0:T(8,128)(2,1)S(1)}, bf16[256,896]{1,0:T(8,128)(2,1)S(1)}, u32[]{:S(2)}, u32[]{:S(2)}) collective-permute-start(bf16[256,896]{1,0:T(8,128)(2,1)S(1)} %get-tuple-element.303), channel_id=1, source_target_pairs={{0,2},{1,3},{2,0},{3,1},{16,17},{17,16},{18,19},{19,18},{4,6},{5,7... | collective-permute-start | bytes 1376264 | tf_op jit(solution)/shard_map/ppermute | solution.py:44
  367.1 33.7 %collective-permute-start.78 = (bf16[4,2,112,1280]{3,2,1,0:T(8,128)(2,1)S(1)}, bf16[4,2,112,1280]{3,2,1,0:T(8,128)(2,1)S(1)}, u32[]{:S(2)}, u32[]{:S(2)}) collective-permute-start(bf16[4,2,112,1280]{3,2,1,0:T(8,128)(2,1)S(1)} %get-tuple-element.348), channel_id=1, source_target_pairs={{0,16},{16,0},{1,17},{17,1},{2,18},{18,2},{3,19},{19,3},{4,20},{20... | collective-permute-start | bytes 6881288 | tf_op jit(solution)/shard_map/ppermute | solution.py:79
  373.5 20.7 %collective-permute-start.82 = (bf16[608,896]{1,0:T(8,128)(2,1)S(1)}, bf16[608,896]{1,0:T(8,128)(2,1)S(1)}, u32[]{:S(2)}, u32[]{:S(2)}) collective-permute-start(bf16[608,896]{1,0:T(8,128)(2,1)S(1)} %get-tuple-element.352), channel_id=1, source_target_pairs={{0,16},{16,0},{1,17},{17,1},{2,18},{18,2},{3,19},{19,3},{4,20},{20... | collective-permute-start | bytes 3268616 | tf_op jit(solution)/shard_map/ppermute | solution.py:79
  394.5 27.9 %collective-permute-start.83 = (bf16[608,896]{1,0:T(8,128)(2,1)S(1)}, bf16[608,896]{1,0:T(8,128)(2,1)S(1)}, u32[]{:S(2)}, u32[]{:S(2)}) collective-permute-start(bf16[608,896]{1,0:T(8,128)(2,1)S(1)} %add_convert_fusion.15), channel_id=1, source_target_pairs={{0,4},{12,8},{1,5},{13,9},{2,6},{14,10},{3,7},{15,11},{16,20},{28,... | collective-permute-start | bytes 3268616 | tf_op jit(solution)/shard_map/ppermute | solution.py:1105
  401.7 31.9 %collective-permute-start.81 = (bf16[2,112,1280]{2,1,0:T(8,128)(2,1)S(1)}, bf16[2,112,1280]{2,1,0:T(8,128)(2,1)S(1)}, u32[]{:S(2)}, u32[]{:S(2)}) collective-permute-start(bf16[2,112,1280]{2,1,0:T(8,128)(2,1)S(1)} %get-tuple-element.540), channel_id=1, source_target_pairs={{0,3},{1,2},{2,1},{3,0},{4,7},{5,6},{6,5},{7,4},{8,11},{9,10},{10,... | collective-permute-start | bytes 1720328 | tf_op jit(solution)/shard_map/ppermute | solution.py:75
  403.2 30.4 %collective-permute-start.80 = (bf16[2,112,1280]{2,1,0:T(8,128)(2,1)S(1)}, bf16[2,112,1280]{2,1,0:T(8,128)(2,1)S(1)}, u32[]{:S(2)}, u32[]{:S(2)}) collective-permute-start(bf16[2,112,1280]{2,1,0:T(8,128)(2,1)S(1)} %get-tuple-element.541), channel_id=1, source_target_pairs={{0,2},{1,3},{2,0},{3,1},{4,6},{5,7},{6,4},{7,5},{8,10},{9,11},{10,... | collective-permute-start | bytes 1720328 | tf_op jit(solution)/shard_map/ppermute | solution.py:75
  403.8 30.9 %collective-permute-start.79 = (bf16[2,112,1280]{2,1,0:T(8,128)(2,1)S(1)}, bf16[2,112,1280]{2,1,0:T(8,128)(2,1)S(1)}, u32[]{:S(2)}, u32[]{:S(2)}) collective-permute-start(bf16[2,112,1280]{2,1,0:T(8,128)(2,1)S(1)} %get-tuple-element.542), channel_id=1, source_target_pairs={{0,1},{1,0},{2,3},{3,2},{4,5},{5,4},{6,7},{7,6},{8,9},{9,8},{10,11... | collective-permute-start | bytes 1720328 | tf_op jit(solution)/shard_map/ppermute | solution.py:75
  404.5 27.9 %collective-permute-start.50 = (bf16[128,896]{1,0:T(8,128)(2,1)S(1)}, bf16[128,896]{1,0:T(8,128)(2,1)S(1)}, u32[]{:S(2)}, u32[]{:S(2)}) collective-permute-start(bf16[128,896]{1,0:T(8,128)(2,1)S(1)} %slice.628), channel_id=1, source_target_pairs={{0,1},{1,0},{2,3},{3,2},{16,18},{17,19},{18,16},{19,17},{4,5},{5,4... | collective-permute-start | bytes 688136 | tf_op jit(solution)/shard_map/ppermute | solution.py:44
  422.4 42.0 %collective-permute-start.56 = (bf16[128,896]{1,0:T(8,128)(2,1)S(1)}, bf16[128,896]{1,0:T(8,128)(2,1)S(1)}, u32[]{:S(2)}, u32[]{:S(2)}) collective-permute-start(bf16[128,896]{1,0:T(8,128)(2,1)S(1)} %slice.627), channel_id=1, source_target_pairs={{0,1},{1,0},{2,3},{3,2},{16,18},{17,19},{18,16},{19,17},{4,5},{5,4... | collective-permute-start | bytes 688136 | tf_op jit(solution)/shard_map/ppermute | solution.py:44
  432.4 76.5 %collective-permute-start.62 = (bf16[128,896]{1,0:T(8,128)(2,1)S(1)}, bf16[128,896]{1,0:T(8,128)(2,1)S(1)}, u32[]{:S(2)}, u32[]{:S(2)}) collective-permute-start(bf16[128,896]{1,0:T(8,128)(2,1)S(1)} %slice.626), channel_id=1, source_target_pairs={{0,1},{1,0},{2,3},{3,2},{16,18},{17,19},{18,16},{19,17},{4,5},{5,4... | collective-permute-start | bytes 688136 | tf_op jit(solution)/shard_map/ppermute | solution.py:44
  442.8 33.5 %collective-permute-start.90 = (bf16[2,2,112,1280]{3,2,1,0:T(8,128)(2,1)S(1)}, bf16[2,2,112,1280]{3,2,1,0:T(8,128)(2,1)S(1)}, u32[]{:S(2)}, u32[]{:S(2)}) collective-permute-start(bf16[2,2,112,1280]{3,2,1,0:T(8,128)(2,1)S(1)} %pad_maximum_fusion.2), channel_id=1, source_target_pairs={{0,4},{12,8},{1,5},{13,9},{2,6},{14,10},{3,7},{15,11},{16,20},{28,... | collective-permute-start | bytes 3440648 | tf_op jit(solution)/shard_map/ppermute | solution.py:1105
  451.4 23.5 %collective-permute-start.85 = (bf16[256,256]{1,0:T(8,128)(2,1)S(1)}, bf16[256,256]{1,0:T(8,128)(2,1)S(1)}, u32[]{:S(2)}, u32[]{:S(2)}) collective-permute-start(bf16[256,256]{1,0:T(8,128)(2,1)S(1)} %slice.635), channel_id=1, source_target_pairs={{0,8},{4,12},{8,0},{12,4},{16,24},{20,28},{24,16},{28,20},{1,9},{5... | collective-permute-start | bytes 393224 | tf_op jit(solution)/shard_map/ppermute | solution.py:44
  464.4 70.9 %collective-permute-start.97 = (bf16[2,2,112,1280]{3,2,1,0:T(8,128)(2,1)}, bf16[2,2,112,1280]{3,2,1,0:T(8,128)(2,1)}, u32[]{:S(2)}, u32[]{:S(2)}) collective-permute-start(bf16[2,2,112,1280]{3,2,1,0:T(8,128)(2,1)} %pad_maximum_fusion.3), channel_id=1, source_target_pairs={{0,4},{12,8},{1,5},{13,9},{2,6},{14,10},{3,7},{15,11},{16,20},{28,... | collective-permute-start | bytes 3440648 | tf_op jit(solution)/shard_map/ppermute | solution.py:1105
  474.9 60.4 %collective-permute-start.95 = (bf16[608,896]{1,0:T(8,128)(2,1)}, bf16[608,896]{1,0:T(8,128)(2,1)}, u32[]{:S(2)}, u32[]{:S(2)}) collective-permute-start(bf16[608,896]{1,0:T(8,128)(2,1)} %add_convert_fusion.13), channel_id=1, source_target_pairs={{4,0},{8,12},{5,1},{9,13},{6,2},{10,14},{7,3},{11,15},{20,16},{24,... | collective-permute-start | bytes 3268616 | tf_op jit(solution)/shard_map/ppermute | solution.py:1105
  476.3 28.6 %collective-permute-start.88 = (bf16[128,256]{1,0:T(8,128)(2,1)S(1)}, bf16[128,256]{1,0:T(8,128)(2,1)S(1)}, u32[]{:S(2)}, u32[]{:S(2)}) collective-permute-start(bf16[128,256]{1,0:T(8,128)(2,1)S(1)} %slice.641), channel_id=1, source_target_pairs={{0,4},{4,0},{8,12},{12,8},{16,20},{20,16},{24,28},{28,24},{1,5},{5... | collective-permute-start | bytes 196616 | tf_op jit(solution)/shard_map/ppermute | solution.py:44
  482.5 52.8 %collective-permute-start.96 = (bf16[2,2,112,1280]{3,2,1,0:T(8,128)(2,1)}, bf16[2,2,112,1280]{3,2,1,0:T(8,128)(2,1)}, u32[]{:S(2)}, u32[]{:S(2)}) collective-permute-start(bf16[2,2,112,1280]{3,2,1,0:T(8,128)(2,1)} %add_convert_fusion.9), channel_id=1, source_target_pairs={{4,8},{8,4},{5,9},{9,5},{6,10},{10,6},{7,11},{11,7},{20,24},{24,20... | collective-permute-start | bytes 3440648 | tf_op jit(solution)/shard_map/ppermute | solution.py:1105
  513.7 21.6 %collective-permute-start.92 = (bf16[128,896]{1,0:T(8,128)(2,1)}, bf16[128,896]{1,0:T(8,128)(2,1)}, u32[]{:S(2)}, u32[]{:S(2)}) collective-permute-start(bf16[128,896]{1,0:T(8,128)(2,1)} %copy-done.71), channel_id=1, source_target_pairs={{0,1},{1,0},{2,3},{3,2},{16,18},{17,19},{18,16},{19,17},{4,5},{5,4... | collective-permute-start | bytes 688136 | tf_op jit(solution)/shard_map/ppermute | solution.py:44
  539.1 20.8 %collective-permute-start.102 = (bf16[4,112,2176]{2,1,0:T(8,128)(2,1)S(1)}, bf16[4,112,2176]{2,1,0:T(8,128)(2,1)S(1)}, u32[]{:S(2)}, u32[]{:S(2)}) collective-permute-start(bf16[4,112,2176]{2,1,0:T(8,128)(2,1)S(1)} %get-tuple-element.398), channel_id=1, source_target_pairs={{0,16},{16,0},{1,17},{17,1},{2,18},{18,2},{3,19},{19,3},{4,20},{20... | collective-permute-start | bytes 5849096 | tf_op jit(solution)/shard_map/ppermute | solution.py:79
  547.2 26.8 %collective-permute-start.100 = (bf16[2,2,112,1280]{3,2,1,0:T(8,128)(2,1)S(1)}, bf16[2,2,112,1280]{3,2,1,0:T(8,128)(2,1)S(1)}, u32[]{:S(2)}, u32[]{:S(2)}) collective-permute-start(bf16[2,2,112,1280]{3,2,1,0:T(8,128)(2,1)S(1)} %add_convert_fusion.7), channel_id=1, source_target_pairs={{4,8},{8,4},{5,9},{9,5},{6,10},{10,6},{7,11},{11,7},{20,24},{24,20... | collective-permute-start | bytes 3440648 | tf_op jit(solution)/shard_map/ppermute | solution.py:1105
  555.2 58.4 %collective-permute-start.106 = (bf16[128,896]{1,0:T(8,128)(2,1)S(1)}, bf16[128,896]{1,0:T(8,128)(2,1)S(1)}, u32[]{:S(2)}, u32[]{:S(2)}) collective-permute-start(bf16[128,896]{1,0:T(8,128)(2,1)S(1)} %slice.621), channel_id=1, source_target_pairs={{0,1},{1,0},{2,3},{3,2},{16,18},{17,19},{18,16},{19,17},{4,5},{5,4... | collective-permute-start | bytes 688136 | tf_op jit(solution)/shard_map/ppermute | solution.py:44
  558.4 28.9 %collective-permute-start.99 = (bf16[2,2,112,1280]{3,2,1,0:T(8,128)(2,1)S(1)}, bf16[2,2,112,1280]{3,2,1,0:T(8,128)(2,1)S(1)}, u32[]{:S(2)}, u32[]{:S(2)}) collective-permute-start(bf16[2,2,112,1280]{3,2,1,0:T(8,128)(2,1)S(1)} %add_convert_fusion.8), channel_id=1, source_target_pairs={{4,0},{8,12},{5,1},{9,13},{6,2},{10,14},{7,3},{11,15},{20,16},{24,... | collective-permute-start | bytes 3440648 | tf_op jit(solution)/shard_map/ppermute | solution.py:1105
  561.4 39.2 %collective-permute-start.103 = (bf16[224,2176]{1,0:T(8,128)(2,1)}, bf16[224,2176]{1,0:T(8,128)(2,1)}, u32[]{:S(2)}, u32[]{:S(2)}) collective-permute-start(bf16[224,2176]{1,0:T(8,128)(2,1)} %bitcast.97), channel_id=1, source_target_pairs={{0,2},{1,3},{2,0},{3,1},{16,17},{17,16},{18,19},{19,18},{4,6},{5,7... | collective-permute-start | bytes 2924552 | tf_op jit(solution)/shard_map/ppermute | solution.py:44
  573.2 32.7 %collective-permute-start.107 = (bf16[256,896]{1,0:T(8,128)(2,1)S(1)}, bf16[256,896]{1,0:T(8,128)(2,1)S(1)}, u32[]{:S(2)}, u32[]{:S(2)}) collective-permute-start(bf16[256,896]{1,0:T(8,128)(2,1)S(1)} %get-tuple-element.400), channel_id=1, source_target_pairs={{0,2},{1,3},{2,0},{3,1},{16,17},{17,16},{18,19},{19,18},{4,6},{5,7... | collective-permute-start | bytes 1376264 | tf_op jit(solution)/shard_map/ppermute | solution.py:44
  604.7 28.4 %collective-permute-start.101 = (bf16[2,2,112,1280]{3,2,1,0:T(8,128)(2,1)S(1)}, bf16[2,2,112,1280]{3,2,1,0:T(8,128)(2,1)S(1)}, u32[]{:S(2)}, u32[]{:S(2)}) collective-permute-start(bf16[2,2,112,1280]{3,2,1,0:T(8,128)(2,1)S(1)} %add_convert_fusion.6), channel_id=1, source_target_pairs={{4,0},{8,12},{5,1},{9,13},{6,2},{10,14},{7,3},{11,15},{20,16},{24,... | collective-permute-start | bytes 3440648 | tf_op jit(solution)/shard_map/ppermute | solution.py:1105
  606.1 64.9 %collective-permute-start.112 = (bf16[128,896]{1,0:T(8,128)(2,1)S(1)}, bf16[128,896]{1,0:T(8,128)(2,1)S(1)}, u32[]{:S(2)}, u32[]{:S(2)}) collective-permute-start(bf16[128,896]{1,0:T(8,128)(2,1)S(1)} %slice.620), channel_id=1, source_target_pairs={{0,1},{1,0},{2,3},{3,2},{16,18},{17,19},{18,16},{19,17},{4,5},{5,4... | collective-permute-start | bytes 688136 | tf_op jit(solution)/shard_map/ppermute | solution.py:44
  610.4 23.0 %collective-permute-start.105 = (bf16[112,2176]{1,0:T(8,128)(2,1)S(1)}, bf16[112,2176]{1,0:T(8,128)(2,1)S(1)}, u32[]{:S(2)}, u32[]{:S(2)}) collective-permute-start(bf16[112,2176]{1,0:T(8,128)(2,1)S(1)} %fusion.4), channel_id=1, source_target_pairs={{0,4},{12,8},{1,5},{13,9},{2,6},{14,10},{3,7},{15,11},{16,20},{28,... | collective-permute-start | bytes 1462280 | tf_op jit(solution)/shard_map/ppermute | solution.py:1105
  612.9 69.8 %collective-permute-start.121 = (bf16[2,112,1280]{2,1,0:T(8,128)(2,1)S(1)}, bf16[2,112,1280]{2,1,0:T(8,128)(2,1)S(1)}, u32[]{:S(2)}, u32[]{:S(2)}) collective-permute-start(bf16[2,112,1280]{2,1,0:T(8,128)(2,1)S(1)} %get-tuple-element.535), channel_id=1, source_target_pairs={{0,2},{1,3},{2,0},{3,1},{4,6},{5,7},{6,4},{7,5},{8,10},{9,11},{10,... | collective-permute-start | bytes 1720328 | tf_op jit(solution)/shard_map/ppermute | solution.py:75
  613.6 71.5 %collective-permute-start.122 = (bf16[2,112,1280]{2,1,0:T(8,128)(2,1)S(1)}, bf16[2,112,1280]{2,1,0:T(8,128)(2,1)S(1)}, u32[]{:S(2)}, u32[]{:S(2)}) collective-permute-start(bf16[2,112,1280]{2,1,0:T(8,128)(2,1)S(1)} %get-tuple-element.536), channel_id=1, source_target_pairs={{0,3},{1,2},{2,1},{3,0},{4,7},{5,6},{6,5},{7,4},{8,11},{9,10},{10,... | collective-permute-start | bytes 1720328 | tf_op jit(solution)/shard_map/ppermute | solution.py:75
  650.7 20.5 %collective-permute-start.111 = (bf16[112,2176]{1,0:T(8,128)(2,1)S(1)}, bf16[112,2176]{1,0:T(8,128)(2,1)S(1)}, u32[]{:S(2)}, u32[]{:S(2)}) collective-permute-start(bf16[112,2176]{1,0:T(8,128)(2,1)S(1)} %add_convert_fusion.19), channel_id=1, source_target_pairs={{4,8},{8,4},{5,9},{9,5},{6,10},{10,6},{7,11},{11,7},{20,24},{24,20... | collective-permute-start | bytes 1462280 | tf_op jit(solution)/shard_map/ppermute | solution.py:1105
  669.5 29.1 %collective-permute-start.116 = (bf16[2,2,112,1280]{3,2,1,0:T(8,128)(2,1)S(1)}, bf16[2,2,112,1280]{3,2,1,0:T(8,128)(2,1)S(1)}, u32[]{:S(2)}, u32[]{:S(2)}) collective-permute-start(bf16[2,2,112,1280]{3,2,1,0:T(8,128)(2,1)S(1)} %pad_maximum_fusion.4), channel_id=1, source_target_pairs={{0,4},{12,8},{1,5},{13,9},{2,6},{14,10},{3,7},{15,11},{16,20},{28,... | collective-permute-start | bytes 3440648 | tf_op jit(solution)/shard_map/ppermute | solution.py:1105
  671.1 24.7 %collective-permute-start.110 = (bf16[128,256]{1,0:T(8,128)(2,1)S(1)}, bf16[128,256]{1,0:T(8,128)(2,1)S(1)}, u32[]{:S(2)}, u32[]{:S(2)}) collective-permute-start(bf16[128,256]{1,0:T(8,128)(2,1)S(1)} %slice.640), channel_id=1, source_target_pairs={{0,4},{4,0},{8,12},{12,8},{16,20},{20,16},{24,28},{28,24},{1,5},{5... | collective-permute-start | bytes 196616 | tf_op jit(solution)/shard_map/ppermute | solution.py:44
  686.3 62.7 %collective-permute-start.123 = (bf16[2,2,112,1280]{3,2,1,0:T(8,128)(2,1)}, bf16[2,2,112,1280]{3,2,1,0:T(8,128)(2,1)}, u32[]{:S(2)}, u32[]{:S(2)}) collective-permute-start(bf16[2,2,112,1280]{3,2,1,0:T(8,128)(2,1)} %pad_maximum_fusion.5), channel_id=1, source_target_pairs={{0,4},{12,8},{1,5},{13,9},{2,6},{14,10},{3,7},{15,11},{16,20},{28,... | collective-permute-start | bytes 3440648 | tf_op jit(solution)/shard_map/ppermute | solution.py:1105
  712.3 36.7 %collective-permute-start.120 = (bf16[2,2,112,1280]{3,2,1,0:T(8,128)(2,1)}, bf16[2,2,112,1280]{3,2,1,0:T(8,128)(2,1)}, u32[]{:S(2)}, u32[]{:S(2)}) collective-permute-start(bf16[2,2,112,1280]{3,2,1,0:T(8,128)(2,1)} %add_convert_fusion.5), channel_id=1, source_target_pairs={{4,8},{8,4},{5,9},{9,5},{6,10},{10,6},{7,11},{11,7},{20,24},{24,20... | collective-permute-start | bytes 3440648 | tf_op jit(solution)/shard_map/ppermute | solution.py:1105
  714.0 57.5 %collective-permute-start.140 = (bf16[608,896]{1,0:T(8,128)(2,1)}, bf16[608,896]{1,0:T(8,128)(2,1)}, u32[]{:S(2)}, u32[]{:S(2)}) collective-permute-start(bf16[608,896]{1,0:T(8,128)(2,1)} %copy-done.106), channel_id=1, source_target_pairs={{0,16},{16,0},{1,17},{17,1},{2,18},{18,2},{3,19},{19,3},{4,20},{20... | collective-permute-start | bytes 3268616 | tf_op jit(solution)/shard_map/ppermute | solution.py:79
  715.3 33.6 %collective-permute-start.125 = (bf16[256,256]{1,0:T(8,128)(2,1)S(1)}, bf16[256,256]{1,0:T(8,128)(2,1)S(1)}, u32[]{:S(2)}, u32[]{:S(2)}) collective-permute-start(bf16[256,256]{1,0:T(8,128)(2,1)S(1)} %slice.632), channel_id=1, source_target_pairs={{0,8},{4,12},{8,0},{12,4},{16,24},{20,28},{24,16},{28,20},{1,9},{5... | collective-permute-start | bytes 393224 | tf_op jit(solution)/shard_map/ppermute | solution.py:44
  720.2 28.8 %collective-permute-start.119 = (bf16[128,256]{1,0:T(8,128)(2,1)S(1)}, bf16[128,256]{1,0:T(8,128)(2,1)S(1)}, u32[]{:S(2)}, u32[]{:S(2)}) collective-permute-start(bf16[128,256]{1,0:T(8,128)(2,1)S(1)} %slice.639), channel_id=1, source_target_pairs={{0,4},{4,0},{8,12},{12,8},{16,20},{20,16},{24,28},{28,24},{1,5},{5... | collective-permute-start | bytes 196616 | tf_op jit(solution)/shard_map/ppermute | solution.py:44
  769.5 29.9 %collective-permute-start.128 = (bf16[4,112,2176]{2,1,0:T(8,128)(2,1)S(1)}, bf16[4,112,2176]{2,1,0:T(8,128)(2,1)S(1)}, u32[]{:S(2)}, u32[]{:S(2)}) collective-permute-start(bf16[4,112,2176]{2,1,0:T(8,128)(2,1)S(1)} %get-tuple-element.452), channel_id=1, source_target_pairs={{0,16},{16,0},{1,17},{17,1},{2,18},{18,2},{3,19},{19,3},{4,20},{20... | collective-permute-start | bytes 5849096 | tf_op jit(solution)/shard_map/ppermute | solution.py:79
  773.2 25.1 %collective-permute-start.141 = (bf16[608,896]{1,0:T(8,128)(2,1)S(1)}, bf16[608,896]{1,0:T(8,128)(2,1)S(1)}, u32[]{:S(2)}, u32[]{:S(2)}) collective-permute-start(bf16[608,896]{1,0:T(8,128)(2,1)S(1)} %add_convert_fusion.12), channel_id=1, source_target_pairs={{0,4},{12,8},{1,5},{13,9},{2,6},{14,10},{3,7},{15,11},{16,20},{28,... | collective-permute-start | bytes 3268616 | tf_op jit(solution)/shard_map/ppermute | solution.py:1105
  776.6 105.9 %collective-permute-start.63 = (bf16[3,128,896]{2,1,0:T(8,128)(2,1)S(1)}, bf16[3,128,896]{2,1,0:T(8,128)(2,1)S(1)}, u32[]{:S(2)}, u32[]{:S(2)}) collective-permute-start(bf16[3,128,896]{2,1,0:T(8,128)(2,1)S(1)} %get-tuple-element.565), channel_id=1, source_target_pairs={{0,16},{16,0},{1,17},{17,1},{2,18},{18,2},{3,19},{19,3},{4,20},{20... | collective-permute-start | bytes 2064392 | tf_op jit(solution)/shard_map/ppermute | solution.py:79
  779.4 21.5 %collective-permute-start.136 = (bf16[2,2,112,1280]{3,2,1,0:T(8,128)(2,1)S(1)}, bf16[2,2,112,1280]{3,2,1,0:T(8,128)(2,1)S(1)}, u32[]{:S(2)}, u32[]{:S(2)}) collective-permute-start(bf16[2,2,112,1280]{3,2,1,0:T(8,128)(2,1)S(1)} %add_convert_fusion.3), channel_id=1, source_target_pairs={{4,8},{8,4},{5,9},{9,5},{6,10},{10,6},{7,11},{11,7},{20,24},{24,20... | collective-permute-start | bytes 3440648 | tf_op jit(solution)/shard_map/ppermute | solution.py:1105
  802.6 29.0 %collective-permute-start.137 = (bf16[2,2,112,1280]{3,2,1,0:T(8,128)(2,1)S(1)}, bf16[2,2,112,1280]{3,2,1,0:T(8,128)(2,1)S(1)}, u32[]{:S(2)}, u32[]{:S(2)}) collective-permute-start(bf16[2,2,112,1280]{3,2,1,0:T(8,128)(2,1)S(1)} %add_convert_fusion.2), channel_id=1, source_target_pairs={{4,0},{8,12},{5,1},{9,13},{6,2},{10,14},{7,3},{11,15},{20,16},{24,... | collective-permute-start | bytes 3440648 | tf_op jit(solution)/shard_map/ppermute | solution.py:1105
  805.6 50.6 %collective-permute-start.135 = (bf16[2,2,112,1280]{3,2,1,0:T(8,128)(2,1)S(1)}, bf16[2,2,112,1280]{3,2,1,0:T(8,128)(2,1)S(1)}, u32[]{:S(2)}, u32[]{:S(2)}) collective-permute-start(bf16[2,2,112,1280]{3,2,1,0:T(8,128)(2,1)S(1)} %add_convert_fusion.4), channel_id=1, source_target_pairs={{4,0},{8,12},{5,1},{9,13},{6,2},{10,14},{7,3},{11,15},{20,16},{24,... | collective-permute-start | bytes 3440648 | tf_op jit(solution)/shard_map/ppermute | solution.py:1105
  814.8 80.4 %collective-permute-start.127 = (f32[3,128,896]{2,1,0:T(8,128)S(1)}, f32[3,128,896]{2,1,0:T(8,128)S(1)}, u32[]{:S(2)}, u32[]{:S(2)}) collective-permute-start(f32[3,128,896]{2,1,0:T(8,128)S(1)} %get-tuple-element.558), channel_id=1, source_target_pairs={{0,16},{16,0},{1,17},{17,1},{2,18},{18,2},{3,19},{19,3},{4,20},{20... | collective-permute-start | bytes 4128776 | tf_op jit(solution)/shard_map/ppermute | solution.py:79
  821.4 58.2 %collective-permute-start.143 = (bf16[608,896]{1,0:T(8,128)(2,1)S(1)}, bf16[608,896]{1,0:T(8,128)(2,1)S(1)}, u32[]{:S(2)}, u32[]{:S(2)}) collective-permute-start(bf16[608,896]{1,0:T(8,128)(2,1)S(1)} %add_convert_fusion.10), channel_id=1, source_target_pairs={{4,0},{8,12},{5,1},{9,13},{6,2},{10,14},{7,3},{11,15},{20,16},{24,... | collective-permute-start | bytes 3268616 | tf_op jit(solution)/shard_map/ppermute | solution.py:1105
  840.9 56.1 %collective-permute-start.139 = (bf16[2,2,112,1280]{3,2,1,0:T(8,128)(2,1)S(1)}, bf16[2,2,112,1280]{3,2,1,0:T(8,128)(2,1)S(1)}, u32[]{:S(2)}, u32[]{:S(2)}) collective-permute-start(bf16[2,2,112,1280]{3,2,1,0:T(8,128)(2,1)S(1)} %get-tuple-element.525), channel_id=1, source_target_pairs={{0,16},{16,0},{1,17},{17,1},{2,18},{18,2},{3,19},{19,3},{4,20},{20... | collective-permute-start | bytes 3440648 | tf_op jit(solution)/shard_map/ppermute | solution.py:79
  857.2 39.8 %collective-permute-start.138 = (bf16[2,2,112,1280]{3,2,1,0:T(8,128)(2,1)S(1)}, bf16[2,2,112,1280]{3,2,1,0:T(8,128)(2,1)S(1)}, u32[]{:S(2)}, u32[]{:S(2)}) collective-permute-start(bf16[2,2,112,1280]{3,2,1,0:T(8,128)(2,1)S(1)} %get-tuple-element.527), channel_id=1, source_target_pairs={{0,16},{16,0},{1,17},{17,1},{2,18},{18,2},{3,19},{19,3},{4,20},{20... | collective-permute-start | bytes 3440648 | tf_op jit(solution)/shard_map/ppermute | solution.py:79
  882.4 20.8 %collective-permute-start.144 = (bf16[608,896]{1,0:T(8,128)(2,1)S(1)}, bf16[608,896]{1,0:T(8,128)(2,1)S(1)}, u32[]{:S(2)}, u32[]{:S(2)}) collective-permute-start(bf16[608,896]{1,0:T(8,128)(2,1)S(1)} %get-tuple-element.532), channel_id=1, source_target_pairs={{0,16},{16,0},{1,17},{17,1},{2,18},{18,2},{3,19},{19,3},{4,20},{20... | collective-permute-start | bytes 3268616 | tf_op jit(solution)/shard_map/ppermute | solution.py:79
  (362 other events, 4264.5 us)

commit v3 on v2

--- a/solution.py
+++ b/solution.py
@@ -925,10 +925,11 @@
         p["bias"] = jnp.concatenate([rows[2:3], key_bias, value_bias], axis=1)
         blocks = [blocks[0]] + [direct(blocks[mask], "dp", mask) for mask in range(1, spread)]
         yield blocks
-        p["gate"], p["up"] = lay_gate_up(
-            gate_up_at, blocks + [other(block) for block in blocks], wide
-        )
-        p["down"] = jnp.pad(downs[layer], ((0, wide - slice_ff), (0, 0)))
+        yield blocks
+        blocks = blocks + [other(block) for block in blocks]
+        blocks, down = after((blocks, downs[layer]), list(last))
+        p["gate"], p["up"] = lay_gate_up(gate_up_at, blocks, wide)
+        p["down"] = jnp.pad(down, ((0, wide - slice_ff), (0, 0)))
 
     first = core * share
     place = lax.axis_index("ctx")
@@ -991,8 +992,8 @@
         flow = Flow(kv_steps(kept[0], rows[2]), 1)
         for n in range(micro_count):
             kept[0][n]["kv"] = flow
-        part, blocks = after((attn_halves[1], gate_up_halves[1]), kept[0][0]["weights"].value)
-        kept[1][0]["weights"] = Flow(weights_steps(1, part, blocks), 2)
+        halves = after((attn_halves[1], gate_up_halves[1]), list(last))
+        kept[1][0]["weights"] = Flow(weights_steps(1, *halves), 1)
 
     def run_q(n):
         k = kept[1][n]
@@ -1206,7 +1207,7 @@
     )
     run_q_all()
     names = dict(d="down", l="low", h="high", a="attn")
-    for word in order.split():
+    for word in order:
         if word[0] == "z":
             tick(*[(names[word[n]], int(word[n + 1])) for n in range(1, len(word), 2)])
         else:
@@ -1230,7 +1231,7 @@
             jnp.concatenate([mine, theirs]), jnp.concatenate([theirs, mine])
         ).astype(f32)
 
-    attn = in_order(mine[0], theirs[0])
+    attn = in_order(*after((mine[0], theirs[0]), gate))
     down = in_order(mine[3], theirs[3])
     small = attn[:, edge + width :]
     return (
@@ -1251,11 +1252,12 @@
     )
 
 
-weight_slack = 3
+weight_slack = 2
 order = (
-    "a00 a01 f00 a02 f01 q0 f02 q1 a10 q2 a11 c f10 a12 f11 "
-    "d10 f12 d11 b10 d12 D1 G1 b11 zd1 k10 b12 zl1 k11 d00 zh1 k12 d01 z P1 d02 za1 G0 z D0 b00 zl0 b01 zh0 k00 b02 zd0 k01 k02 "
-    "P0 za0"
+    "a00", "a01", "f00", "a02", "f01", "q0", "f02", "q1", "a10", "q2", "a11", "c", "f10", "a12", "f11", "d10",
+    "f12", "d11", "b10", "d12", "D1", "zd1", "G1", "b11", "z", "k10", "b12", "zl1", "k11", "d00", "zh1",
+    "k12", "d01", "z", "P1", "d02", "za1", "D0", "zd0", "G0", "b00", "zl0", "b01", "zh0", "k00", "b02", "z",
+    "k01", "k02", "z", "P0", "za0",
 )
 
 

time: 928 us -> 876 us (0.944)
  starting transfers between devices: 224 us -> 207 us
  waiting for transfers between devices: 293 us -> 276 us
  local copies, waits for them, and re-layouts: 90.7 us -> 78.9 us
    ppermute x24, waiting for transfers between devices: 110 us -> 87 us  [ctx_steps(): got = lax.ppermute(value, 'ctx', route)]
    ppermute x72, waiting for transfers between devices: 170 us -> 156 us  [step(): return lax.ppermute(block, ('section', axis), route)]
    ppermute x12, waiting for transfers between devices: 10.7 us -> 23.4 us  [direct(): return lax.ppermute(block, axis, [(i, i ^ mask) for i in range(size)])]
    ppermute x37, starting transfers between devices: 77.5 us -> 67.3 us  [other(): return lax.ppermute(block, 'section', [(0, 1), (1, 0)])]
    unnamed x574 -> x546, local copies, waits for them, and re-layouts: 65.2 us -> 57.2 us
  transfers between devices with their start and end apart: 145 -> 145, of which waited for: 44 -> 47; matrix products, arithmetic and copies ran while one was open for 8% -> 7% of each run, Pallas kernels for 25% -> 27%
where the time goes in v3:
time: 876 us; the launch traced here: 865 us
  waiting for transfers between devices  276 us (32%)
  Pallas kernels  250 us (29%)
  starting transfers between devices  207 us (24%)
  local copies, waits for them, and re-layouts  78.9 us (9%)
  other arithmetic  47.6 us (5%)
    pallas_call x47, Pallas kernels, call(): pl.pallas_call(kernel, out_shape=outs, grid=grid or (), in_specs=specs, o...  250 us
    ppermute x72, waiting for transfers between devices, step(): return lax.ppermute(block, ('section', axis), route)  156 us
    ppermute x24, waiting for transfers between devices, ctx_steps(): got = lax.ppermute(value, 'ctx', route)  87 us
    ppermute x72, starting transfers between devices, step(): return lax.ppermute(block, ('section', axis), route)  83.6 us
    ppermute x37, starting transfers between devices, other(): return lax.ppermute(block, 'section', [(0, 1), (1, 0)])  67.3 us
    unnamed x546, local copies, waits for them, and re-layouts  57.2 us
    ppermute x24, starting transfers between devices, ctx_steps(): got = lax.ppermute(value, 'ctx', route)  44.3 us
    ppermute x12, waiting for transfers between devices, direct(): return lax.ppermute(block, axis, [(i, i ^ mask) for i in range(size)])  23.4 us
  transfers between devices with their start and end apart: 145, of which 47 were waited for; matrix products, arithmetic and copies ran while one was open for 7% of the time, Pallas kernels for 27%

profile of v3, /device:TPU:1, one launch (start us, length us, event | category | flops | bytes accessed | tf_op | source)
XLA Modules:
  0.0 864.6 jit_solution(8316046624705316719)
XLA Ops:
  23.5 8.9 %collective-permute-done.2.refs_1_ = bf16[224,2176]{1,0:T(8,128)(2,1)S(1)} collective-permute-done((bf16[224,2176]{1,0:T(8,128)(2,1)S(1)}, bf16[224,2176]{1,0:T(8,128)(2,1)S(1)}, u32[]{:S(2)}, u32[]{:S(2)}) %collective-permute-start.2) | collective-permute-done | bytes 974880 | tf_op jit(solution)/shard_map/ppermute | solution.py:44
  66.0 12.9 %collective-permute-done.6 = bf16[2,384,256]{2,1,0:T(8,128)(2,1)S(1)} collective-permute-done((bf16[2,384,256]{2,1,0:T(8,128)(2,1)S(1)}, bf16[2,384,256]{2,1,0:T(8,128)(2,1)S(1)}, u32[]{:S(2)}, u32[]{:S(2)}) %collective-permute-start.6) | collective-permute-done | bytes 393248 | tf_op jit(solution)/shard_map/ppermute | solution.py:44
  86.1 5.5 collective-permute-done.10.refs_2_
  92.3 4.1 collective-permute-start.22
  96.7 6.8 shard_map.258
  117.7 6.6 shard_map.259
  130.9 7.3 collective-permute-done.17.refs_2_
  139.4 5.2 collective-permute-done.14.upper_ref.refs_1_
  144.6 6.7 shard_map.261
  151.5 6.8 shard_map.262
  180.5 7.1 shard_map.263
  195.9 7.3 shard_map.266
  212.6 5.6 shard_map.268
  223.2 4.0 collective-permute-start.43
  228.3 5.8 shard_map.270
  244.0 4.1 collective-permute-done.59
  253.2 6.0 shard_map.272
  259.3 5.6 shard_map.273
  265.8 8.0 collective-permute-done.52.upper_ref.refs_3_
  274.8 6.0 shard_map.274
  280.8 9.2 %shard_map.275 = (bf16[256,896]{1,0:T(8,128)(2,1)S(1)}, bf16[256,896]{1,0:T(8,128)(2,1)S(1)}, bf16[512,1280]{1,0:T(8,128)(2,1)S(1)}, bf16[512,1280]{1,0:T(8,128)(2,1)S(1)}) custom-call(bf16[2,3,128,896]{3,2,1,0:T(8,128)(2,1)S(1)} %constant_dynamic-update-slice_fusion.15.lower_ref.refs_3_.refs_5_.refs_7_, ...), custom_call_target="tpu_custom_call" | custom-call | flops 3523215360 | bytes 13959168 | tf_op jit(solution)/shard_map/pallas_call | solution.py:142
  291.6 6.4 shard_map.276
  298.7 9.2 %shard_map.277 = (bf16[256,896]{1,0:T(8,128)(2,1)S(1)}, bf16[256,896]{1,0:T(8,128)(2,1)S(1)}, bf16[512,1280]{1,0:T(8,128)(2,1)S(1)}, bf16[512,1280]{1,0:T(8,128)(2,1)S(1)}) custom-call(bf16[2,3,128,896]{3,2,1,0:T(8,128)(2,1)S(1)} %constant_dynamic-update-slice_fusion.15.lower_ref.refs_3_.refs_5_.refs_7_, ...), custom_call_target="tpu_custom_call" | custom-call | flops 3523215360 | bytes 13959168 | tf_op jit(solution)/shard_map/pallas_call | solution.py:142
  309.6 7.7 shard_map.278
  317.3 5.5 collective-permute-start.66
  322.8 9.4 %shard_map.279 = (bf16[256,896]{1,0:T(8,128)(2,1)S(1)}, bf16[256,896]{1,0:T(8,128)(2,1)S(1)}, bf16[512,1280]{1,0:T(8,128)(2,1)S(1)}, bf16[512,1280]{1,0:T(8,128)(2,1)S(1)}) custom-call(bf16[2,3,128,896]{3,2,1,0:T(8,128)(2,1)S(1)} %constant_dynamic-update-slice_fusion.15.lower_ref.refs_3_.refs_5_.refs_7_, ...), custom_call_target="tpu_custom_call" | custom-call | flops 3523215360 | bytes 13959168 | tf_op jit(solution)/shard_map/pallas_call | solution.py:142
  334.8 6.5 collective-permute-done.67
  341.3 4.8 shard_map.280
  351.0 11.0 %shard_map.281 = (bf16[4,2,112,1280]{3,2,1,0:T(8,128)(2,1)S(1)}, bf16[4,2,112,1280]{3,2,1,0:T(8,128)(2,1)S(1)}) custom-call(s32[10]{0:T(128)S(1)} %stack.193.info_ref, bf16[256,896]{1,0:T(8,128)(2,1)S(1)} %constant_dynamic-update-slice_fusion.9.lower_ref.refs_0_, bf16[256,896]{1,0:T(8,128)(2,1)S(1)} %copy-done.103, ...), custom_call_target="tpu_custom_call" | custom-call | flops 7046430720 | bytes 15204392 | tf_op jit(solution)/shard_map/pallas_call | solution.py:142
  366.5 7.6 collective-permute-done.61
  375.9 7.7 shard_map.282
  394.5 17.8 %collective-permute-done.73 = bf16[608,896]{1,0:T(8,128)(2,1)S(1)} collective-permute-done((bf16[608,896]{1,0:T(8,128)(2,1)S(1)}, bf16[608,896]{1,0:T(8,128)(2,1)S(1)}, u32[]{:S(2)}, u32[]{:S(2)}) %collective-permute-start.73) | collective-permute-done | bytes 1089568 | tf_op jit(solution)/shard_map/ppermute | solution.py:1106
  414.2 6.5 collective-permute-done.75
  423.3 6.0 collective-permute-start.91
  430.4 7.7 shard_map.284
  442.3 10.5 %collective-permute-start.86 = (bf16[256,256]{1,0:T(8,128)(2,1)S(1)}, bf16[256,256]{1,0:T(8,128)(2,1)S(1)}, u32[]{:S(2)}, u32[]{:S(2)}) collective-permute-start(bf16[256,256]{1,0:T(8,128)(2,1)S(1)} %slice.635), channel_id=1, source_target_pairs={{0,8},{4,12},{8,0},{12,4},{16,24},{20,28},{24,16},{28,20},{1,9},{5... | collective-permute-start | bytes 393224 | tf_op jit(solution)/shard_map/ppermute | solution.py:44
  455.0 5.4 collective-permute-start.97
  467.3 9.1 %shard_map.286 = (bf16[256,896]{1,0:T(8,128)(2,1)S(1)}, bf16[256,896]{1,0:T(8,128)(2,1)S(1)}, bf16[512,1280]{1,0:T(8,128)(2,1)S(1)}, bf16[512,1280]{1,0:T(8,128)(2,1)S(1)}) custom-call(bf16[256,896]{1,0:T(8,128)(2,1)S(1)} %constant_dynamic-update-slice_fusion.17.lower_ref.refs_3_, bf16[256,896]{1,0:T(8,128)(2,1)S(1)} %collective-permute-done.76.upper_ref.refs_4_, ...), custom_call_target="tpu_custom_call" | custom-call | flops 3523215360 | bytes 13959168 | tf_op jit(solution)/shard_map/pallas_call | solution.py:142
  476.5 9.1 %collective-permute-done.89.got_ref = bf16[128,256]{1,0:T(8,128)(2,1)S(1)} collective-permute-done((bf16[128,256]{1,0:T(8,128)(2,1)S(1)}, bf16[128,256]{1,0:T(8,128)(2,1)S(1)}, u32[]{:S(2)}, u32[]{:S(2)}) %collective-permute-start.89) | collective-permute-done | bytes 65568 | tf_op jit(solution)/shard_map/ppermute | solution.py:44
  490.3 8.2 collective-permute-done.87
  508.0 10.3 %shard_map.288 = (bf16[256,896]{1,0:T(8,128)(2,1)S(1)}, bf16[256,896]{1,0:T(8,128)(2,1)S(1)}, bf16[512,1280]{1,0:T(8,128)(2,1)S(1)}, bf16[512,1280]{1,0:T(8,128)(2,1)S(1)}) custom-call(bf16[256,896]{1,0:T(8,128)(2,1)} %constant_dynamic-update-slice_fusion.21.lower_ref.refs_5_, bf16[256,896]{1,0:T(8,128)(2,1)} %collective-permute-done.95.upper_ref.refs_6_, ...), custom_call_target="tpu_custom_call" | custom-call | flops 3523215360 | bytes 13959168 | tf_op jit(solution)/shard_map/pallas_call | solution.py:142
  522.2 6.5 collective-permute-start.102
  535.0 4.6 collective-permute-done.98
  542.3 10.2 %collective-permute-done.103 = bf16[224,2176]{1,0:T(8,128)(2,1)S(1)} collective-permute-done((bf16[224,2176]{1,0:T(8,128)(2,1)S(1)}, bf16[224,2176]{1,0:T(8,128)(2,1)S(1)}, u32[]{:S(2)}, u32[]{:S(2)}) %collective-permute-start.103) | collective-permute-done | bytes 974880 | tf_op jit(solution)/shard_map/ppermute | solution.py:44
  558.7 9.1 %shard_map.290 = (bf16[256,896]{1,0:T(8,128)(2,1)S(1)}, bf16[256,896]{1,0:T(8,128)(2,1)S(1)}, bf16[512,1280]{1,0:T(8,128)(2,1)S(1)}, bf16[512,1280]{1,0:T(8,128)(2,1)S(1)}) custom-call(bf16[256,896]{1,0:T(8,128)(2,1)S(1)} %constant_dynamic-update-slice_fusion.19.lower_ref.refs_7_, bf16[256,896]{1,0:T(8,128)(2,1)S(1)} %collective-permute-done.94.upper_ref.refs_8_, ...), custom_call_target="tpu_custom_call" | custom-call | flops 3523215360 | bytes 13959168 | tf_op jit(solution)/shard_map/pallas_call | solution.py:142
  568.7 11.4 %collective-permute-done.99 = bf16[2,2,112,1280]{3,2,1,0:T(8,128)(2,1)S(1)} collective-permute-done((bf16[2,2,112,1280]{3,2,1,0:T(8,128)(2,1)S(1)}, bf16[2,2,112,1280]{3,2,1,0:T(8,128)(2,1)S(1)}, u32[]{:S(2)}, u32[]{:S(2)}) %collective-permute-start.99) | collective-permute-done | bytes 1146912 | tf_op jit(solution)/shard_map/ppermute | solution.py:1106
  581.5 5.6 shard_map.291
  591.2 13.4 %collective-permute-done.101 = bf16[2,2,112,1280]{3,2,1,0:T(8,128)(2,1)S(1)} collective-permute-done((bf16[2,2,112,1280]{3,2,1,0:T(8,128)(2,1)S(1)}, bf16[2,2,112,1280]{3,2,1,0:T(8,128)(2,1)S(1)}, u32[]{:S(2)}, u32[]{:S(2)}) %collective-permute-start.101) | collective-permute-done | bytes 1146912 | tf_op jit(solution)/shard_map/ppermute | solution.py:1106
  605.7 12.2 %shard_map.292 = (bf16[4,2,112,1280]{3,2,1,0:T(8,128)(2,1)S(1)}, bf16[4,2,112,1280]{3,2,1,0:T(8,128)(2,1)S(1)}) custom-call(s32[10]{0:T(128)S(1)} %stack.193.info_ref, bf16[256,896]{1,0:T(8,128)(2,1)S(1)} %copy-done.71, bf16[256,896]{1,0:T(8,128)(2,1)S(1)} %copy-done.99, bf16[256,896]{1,0:T(8,128)(2,1)} %constant_dynamic-update-slice_fusion.5.lower_ref.refs_2_, ...), custom_call_target="tpu_custom_call" | custom-call | flops 7046430720 | bytes 15204392 | tf_op jit(solution)/shard_map/pallas_call | solution.py:142
  622.8 8.6 shard_map.293
  634.4 11.5 %collective-permute-done.113 = bf16[608,896]{1,0:T(8,128)(2,1)S(1)} collective-permute-done((bf16[608,896]{1,0:T(8,128)(2,1)S(1)}, bf16[608,896]{1,0:T(8,128)(2,1)S(1)}, u32[]{:S(2)}, u32[]{:S(2)}) %collective-permute-start.113) | collective-permute-done | bytes 1089568 | tf_op jit(solution)/shard_map/ppermute | solution.py:1106
  655.8 10.3 %collective-permute-done.118 = bf16[2,112,1280]{2,1,0:T(8,128)(2,1)S(1)} collective-permute-done((bf16[2,112,1280]{2,1,0:T(8,128)(2,1)S(1)}, bf16[2,112,1280]{2,1,0:T(8,128)(2,1)S(1)}, u32[]{:S(2)}, u32[]{:S(2)}) %collective-permute-start.118) | collective-permute-done | bytes 573472 | tf_op jit(solution)/shard_map/ppermute | solution.py:75
  668.7 8.7 %shard_map.294 = (bf16[128,896]{1,0:T(8,128)(2,1)S(1)}, bf16[512,256]{1,0:T(8,128)(2,1)S(1)}, bf16[512,256]{1,0:T(8,128)(2,1)S(1)}, f32[128,896]{1,0:T(8,128)S(1...) custom-call(bf16[3,128,896]{2,1,0:T(8,128)(2,1)S(1)} %bitcast.256, bf16[4,3,128,256]{3,2,1,0:T(8,128)(2,1)S(1)} %copy-done.30, ...), custom_call_target="tpu_custom_call" | custom-call | flops 3728736256 | bytes 6067456 | tf_op jit(solution)/shard_map/pallas_call | solution.py:142
  687.8 4.5 collective-permute-done.121
  702.9 8.7 %shard_map.296 = (bf16[128,896]{1,0:T(8,128)(2,1)S(1)}, bf16[512,256]{1,0:T(8,128)(2,1)S(1)}, bf16[512,256]{1,0:T(8,128)(2,1)S(1)}, f32[128,896]{1,0:T(8,128)S(1...) custom-call(bf16[3,128,896]{2,1,0:T(8,128)(2,1)S(1)} %bitcast.257, bf16[4,3,128,256]{3,2,1,0:T(8,128)(2,1)S(1)} %copy-done.30, ...), custom_call_target="tpu_custom_call" | custom-call | flops 3728736256 | bytes 6067456 | tf_op jit(solution)/shard_map/pallas_call | solution.py:142
  719.0 4.0 collective-permute-start.129
  725.7 28.5 %collective-permute-done.129 = bf16[256,256]{1,0:T(8,128)(2,1)S(1)} collective-permute-done((bf16[256,256]{1,0:T(8,128)(2,1)S(1)}, bf16[256,256]{1,0:T(8,128)(2,1)S(1)}, u32[]{:S(2)}, u32[]{:S(2)}) %collective-permute-start.129) | collective-permute-done | bytes 131104 | tf_op jit(solution)/shard_map/ppermute | solution.py:44
  772.1 4.1 shard_map.299
  776.3 4.7 collective-permute-start.134
  793.5 6.1 collective-permute-done.135
  814.3 5.0 collective-permute-done.137
  820.2 11.1 %collective-permute-done.141 = bf16[2,2,112,1280]{3,2,1,0:T(8,128)(2,1)S(1)} collective-permute-done((bf16[2,2,112,1280]{3,2,1,0:T(8,128)(2,1)S(1)}, bf16[2,2,112,1280]{3,2,1,0:T(8,128)(2,1)S(1)}, u32[]{:S(2)}, u32[]{:S(2)}) %collective-permute-start.141) | collective-permute-done | bytes 1146912 | tf_op jit(solution)/shard_map/ppermute | solution.py:1106
  837.5 10.7 %collective-permute-done.139 = bf16[112,2176]{1,0:T(8,128)(2,1)S(1)} collective-permute-done((bf16[112,2176]{1,0:T(8,128)(2,1)S(1)}, bf16[112,2176]{1,0:T(8,128)(2,1)S(1)}, u32[]{:S(2)}, u32[]{:S(2)}) %collective-permute-start.139) | collective-permute-done | bytes 487456 | tf_op jit(solution)/shard_map/ppermute | solution.py:1106
  854.5 6.3 shard_map.300
  (1040 shorter events, 347.8 us)
Async XLA Ops:
  12.7 97.4 %collective-permute-start.23 = (bf16[1216,896]{1,0:T(8,128)(2,1)}, bf16[1216,896]{1,0:T(8,128)(2,1)}, u32[]{:S(2)}, u32[]{:S(2)}) collective-permute-start(bf16[1216,896]{1,0:T(8,128)(2,1)} %bitcast.282), channel_id=1, source_target_pairs={{0,16},{16,0},{1,17},{17,1},{2,18},{18,2},{3,19},{19,3},{4,20},{20... | collective-permute-start | bytes 6537224 | tf_op jit(solution)/shard_map/ppermute | solution.py:79
  19.0 35.0 %collective-permute-start.8 = (bf16[4,2,112,1216]{3,2,1,0:T(8,128)(2,1)}, bf16[4,2,112,1216]{3,2,1,0:T(8,128)(2,1)}, u32[]{:S(2)}, u32[]{:S(2)}) collective-permute-start(bf16[4,2,112,1216]{3,2,1,0:T(8,128)(2,1)} %get-tuple-element.264), channel_id=1, source_target_pairs={{0,16},{16,0},{1,17},{17,1},{2,18},{18,2},{3,19},{19,3},{4,20},{20... | collective-permute-start | bytes 6537224 | tf_op jit(solution)/shard_map/ppermute | solution.py:79
  57.4 23.5 %collective-permute-start.12 = (bf16[112,2176]{1,0:T(8,128)(2,1)S(1)}, bf16[112,2176]{1,0:T(8,128)(2,1)S(1)}, u32[]{:S(2)}, u32[]{:S(2)}) collective-permute-start(bf16[112,2176]{1,0:T(8,128)(2,1)S(1)} %copy-done.236), channel_id=1, source_target_pairs={{0,1},{1,0},{2,3},{3,2},{16,18},{17,19},{18,16},{19,17},{4,5},{5,4... | collective-permute-start | bytes 1462280 | tf_op jit(solution)/shard_map/ppermute | solution.py:44
  59.3 19.6 %collective-permute-start.6 = (bf16[2,384,256]{2,1,0:T(8,128)(2,1)S(1)}, bf16[2,384,256]{2,1,0:T(8,128)(2,1)S(1)}, u32[]{:S(2)}, u32[]{:S(2)}) collective-permute-start(bf16[2,384,256]{2,1,0:T(8,128)(2,1)S(1)} %pad_maximum_fusion.11), channel_id=1, source_target_pairs={{0,8},{4,12},{8,0},{12,4},{16,24},{20,28},{24,16},{28,20},{1,9},{5... | collective-permute-start | bytes 1179656 | tf_op jit(solution)/shard_map/ppermute | solution.py:44
  62.8 20.7 %collective-permute-start.11 = (bf16[2,112,1216]{2,1,0:T(8,128)(2,1)S(1)}, bf16[2,112,1216]{2,1,0:T(8,128)(2,1)}, u32[]{:S(2)}, u32[]{:S(2)}) collective-permute-start(bf16[2,112,1216]{2,1,0:T(8,128)(2,1)S(1)} %get-tuple-element.587), channel_id=1, source_target_pairs={{0,3},{1,2},{2,1},{3,0},{4,7},{5,6},{6,5},{7,4},{8,11},{9,10},{10,... | collective-permute-start | bytes 1634312 | tf_op jit(solution)/shard_map/ppermute | solution.py:75
  64.9 26.6 %collective-permute-start.10 = (bf16[2,112,1216]{2,1,0:T(8,128)(2,1)}, bf16[2,112,1216]{2,1,0:T(8,128)(2,1)}, u32[]{:S(2)}, u32[]{:S(2)}) collective-permute-start(bf16[2,112,1216]{2,1,0:T(8,128)(2,1)} %get-tuple-element.588), channel_id=1, source_target_pairs={{0,2},{1,3},{2,0},{3,1},{4,6},{5,7},{6,4},{7,5},{8,10},{9,11},{10,... | collective-permute-start | bytes 1634312 | tf_op jit(solution)/shard_map/ppermute | solution.py:75
  83.4 20.9 %collective-permute-start.15 = (bf16[224,2176]{1,0:T(8,128)(2,1)}, bf16[224,2176]{1,0:T(8,128)(2,1)}, u32[]{:S(2)}, u32[]{:S(2)}) collective-permute-start(bf16[224,2176]{1,0:T(8,128)(2,1)} %constant_dynamic-update-slice_fusion.3.refs_0_), channel_id=1, source_target_pairs={{0,2},{1,3},{2,0},{3,1},{16,17},{17,16},{18,19},{19,18},{4,6},{5,7... | collective-permute-start | bytes 2924552 | tf_op jit(solution)/shard_map/ppermute | solution.py:44
  91.6 20.7 %collective-permute-start.19 = (bf16[2,112,1216]{2,1,0:T(8,128)(2,1)S(1)}, bf16[2,112,1216]{2,1,0:T(8,128)(2,1)S(1)}, u32[]{:S(2)}, u32[]{:S(2)}) collective-permute-start(bf16[2,112,1216]{2,1,0:T(8,128)(2,1)S(1)} %get-tuple-element.275.refs_0_), channel_id=1, source_target_pairs={{0,16},{16,0},{1,17},{17,1},{2,18},{18,2},{3,19},{19,3},{4,20},{20... | collective-permute-start | bytes 1634312 | tf_op jit(solution)/shard_map/ppermute | solution.py:79
  92.3 20.1 %collective-permute-start.22 = (bf16[2,112,1216]{2,1,0:T(8,128)(2,1)}, bf16[2,112,1216]{2,1,0:T(8,128)(2,1)S(1)}, u32[]{:S(2)}, u32[]{:S(2)}) collective-permute-start(bf16[2,112,1216]{2,1,0:T(8,128)(2,1)} %collective-permute-done.11.refs_3_), channel_id=1, source_target_pairs={{0,16},{16,0},{1,17},{17,1},{2,18},{18,2},{3,19},{19,3},{4,20},{20... | collective-permute-start | bytes 1634312 | tf_op jit(solution)/shard_map/ppermute | solution.py:79
  110.0 19.0 %collective-permute-start.18 = (bf16[2,112,1216]{2,1,0:T(8,128)(2,1)S(1)}, bf16[2,112,1216]{2,1,0:T(8,128)(2,1)S(1)}, u32[]{:S(2)}, u32[]{:S(2)}) collective-permute-start(bf16[2,112,1216]{2,1,0:T(8,128)(2,1)S(1)} %get-tuple-element.583), channel_id=1, source_target_pairs={{0,3},{1,2},{2,1},{3,0},{4,7},{5,6},{6,5},{7,4},{8,11},{9,10},{10,... | collective-permute-start | bytes 1634312 | tf_op jit(solution)/shard_map/ppermute | solution.py:75
  112.2 26.0 %collective-permute-start.17 = (bf16[2,112,1216]{2,1,0:T(8,128)(2,1)S(1)}, bf16[2,112,1216]{2,1,0:T(8,128)(2,1)S(1)}, u32[]{:S(2)}, u32[]{:S(2)}) collective-permute-start(bf16[2,112,1216]{2,1,0:T(8,128)(2,1)S(1)} %get-tuple-element.584), channel_id=1, source_target_pairs={{0,2},{1,3},{2,0},{3,1},{4,6},{5,7},{6,4},{7,5},{8,10},{9,11},{10,... | collective-permute-start | bytes 1634312 | tf_op jit(solution)/shard_map/ppermute | solution.py:75
  112.5 27.0 %collective-permute-start.16 = (bf16[2,112,1216]{2,1,0:T(8,128)(2,1)S(1)}, bf16[2,112,1216]{2,1,0:T(8,128)(2,1)S(1)}, u32[]{:S(2)}, u32[]{:S(2)}) collective-permute-start(bf16[2,112,1216]{2,1,0:T(8,128)(2,1)S(1)} %get-tuple-element.585), channel_id=1, source_target_pairs={{0,1},{1,0},{2,3},{3,2},{4,5},{5,4},{6,7},{7,6},{8,9},{9,8},{10,11... | collective-permute-start | bytes 1634312 | tf_op jit(solution)/shard_map/ppermute | solution.py:75
  113.1 31.5 %collective-permute-start.14 = (bf16[256,896]{1,0:T(8,128)(2,1)S(1)}, bf16[256,896]{1,0:T(8,128)(2,1)S(1)}, u32[]{:S(2)}, u32[]{:S(2)}) collective-permute-start(bf16[256,896]{1,0:T(8,128)(2,1)S(1)} %constant_dynamic-update-slice_fusion.1.lower_ref.refs_0_), channel_id=1, source_target_pairs={{0,2},{1,3},{2,0},{3,1},{16,17},{17,16},{18,19},{19,18},{4,6},{5,7... | collective-permute-start | bytes 1376264 | tf_op jit(solution)/shard_map/ppermute | solution.py:44
  125.1 40.4 %collective-permute-start.32 = (bf16[224,2176]{1,0:T(8,128)(2,1)}, bf16[224,2176]{1,0:T(8,128)(2,1)S(1)}, u32[]{:S(2)}, u32[]{:S(2)}) collective-permute-start(bf16[224,2176]{1,0:T(8,128)(2,1)} %constant_dynamic-update-slice_fusion.3.refs_0_), channel_id=1, source_target_pairs={{0,16},{16,0},{1,17},{17,1},{2,18},{18,2},{3,19},{19,3},{4,20},{20... | collective-permute-start | bytes 2924552 | tf_op jit(solution)/shard_map/ppermute | solution.py:79
  129.1 36.4 %collective-permute-start.33 = (bf16[224,2176]{1,0:T(8,128)(2,1)}, bf16[224,2176]{1,0:T(8,128)(2,1)S(1)}, u32[]{:S(2)}, u32[]{:S(2)}) collective-permute-start(bf16[224,2176]{1,0:T(8,128)(2,1)} %collective-permute-done.15.refs_1_), channel_id=1, source_target_pairs={{0,16},{16,0},{1,17},{17,1},{2,18},{18,2},{3,19},{19,3},{4,20},{20... | collective-permute-start | bytes 2924552 | tf_op jit(solution)/shard_map/ppermute | solution.py:79
  164.2 31.6 %collective-permute-start.31 = (bf16[256,896]{1,0:T(8,128)(2,1)}, bf16[256,896]{1,0:T(8,128)(2,1)}, u32[]{:S(2)}, u32[]{:S(2)}) collective-permute-start(bf16[256,896]{1,0:T(8,128)(2,1)} %constant_dynamic-update-slice_fusion.7.lower_ref.refs_4_), channel_id=1, source_target_pairs={{0,2},{1,3},{2,0},{3,1},{16,17},{17,16},{18,19},{19,18},{4,6},{5,7... | collective-permute-start | bytes 1376264 | tf_op jit(solution)/shard_map/ppermute | solution.py:44
  248.2 32.6 %collective-permute-start.60 = (bf16[2,3,128,896]{3,2,1,0:T(8,128)(2,1)S(1)}, bf16[2,3,128,896]{3,2,1,0:T(8,128)(2,1)S(1)}, u32[]{:S(2)}, u32[]{:S(2)}) collective-permute-start(bf16[2,3,128,896]{3,2,1,0:T(8,128)(2,1)S(1)} %constant_dynamic-update-slice_fusion.15.lower_ref.refs_3_.refs_5_.refs_7_), channel_id=1, source_target_pairs={{0,2},{1,3},{2,0},{3,1},{16,17},{17,16},{18,19},{19,18},{4,6},{5,7... | collective-permute-start | bytes 4128776 | tf_op jit(solution)/shard_map/ppermute | solution.py:44
  252.4 21.4 %collective-permute-start.52 = (bf16[256,896]{1,0:T(8,128)(2,1)S(1)}, bf16[256,896]{1,0:T(8,128)(2,1)S(1)}, u32[]{:S(2)}, u32[]{:S(2)}) collective-permute-start(bf16[256,896]{1,0:T(8,128)(2,1)S(1)} %constant_dynamic-update-slice_fusion.11.lower_ref.refs_2_), channel_id=1, source_target_pairs={{0,2},{1,3},{2,0},{3,1},{16,17},{17,16},{18,19},{19,18},{4,6},{5,7... | collective-permute-start | bytes 1376264 | tf_op jit(solution)/shard_map/ppermute | solution.py:44
  308.9 25.9 %collective-permute-start.55 = (bf16[256,896]{1,0:T(8,128)(2,1)S(1)}, bf16[256,896]{1,0:T(8,128)(2,1)S(1)}, u32[]{:S(2)}, u32[]{:S(2)}) collective-permute-start(bf16[256,896]{1,0:T(8,128)(2,1)S(1)} %get-tuple-element.341), channel_id=1, source_target_pairs={{0,2},{1,3},{2,0},{3,1},{16,17},{17,16},{18,19},{19,18},{4,6},{5,7... | collective-permute-start | bytes 1376264 | tf_op jit(solution)/shard_map/ppermute | solution.py:44
  361.9 27.6 %collective-permute-start.80 = (bf16[4,2,112,1280]{3,2,1,0:T(8,128)(2,1)S(1)}, bf16[4,2,112,1280]{3,2,1,0:T(8,128)(2,1)S(1)}, u32[]{:S(2)}, u32[]{:S(2)}) collective-permute-start(bf16[4,2,112,1280]{3,2,1,0:T(8,128)(2,1)S(1)} %get-tuple-element.387), channel_id=1, source_target_pairs={{0,16},{16,0},{1,17},{17,1},{2,18},{18,2},{3,19},{19,3},{4,20},{20... | collective-permute-start | bytes 6881288 | tf_op jit(solution)/shard_map/ppermute | solution.py:79
  363.7 57.7 %collective-permute-start.50 = (bf16[128,896]{1,0:T(8,128)(2,1)S(1)}, bf16[128,896]{1,0:T(8,128)(2,1)S(1)}, u32[]{:S(2)}, u32[]{:S(2)}) collective-permute-start(bf16[128,896]{1,0:T(8,128)(2,1)S(1)} %slice.628), channel_id=1, source_target_pairs={{0,1},{1,0},{2,3},{3,2},{16,18},{17,19},{18,16},{19,17},{4,5},{5,4... | collective-permute-start | bytes 688136 | tf_op jit(solution)/shard_map/ppermute | solution.py:44
  365.8 19.6 %collective-permute-start.72 = (bf16[608,896]{1,0:T(8,128)(2,1)S(1)}, bf16[608,896]{1,0:T(8,128)(2,1)S(1)}, u32[]{:S(2)}, u32[]{:S(2)}) collective-permute-start(bf16[608,896]{1,0:T(8,128)(2,1)S(1)} %get-tuple-element.379), channel_id=1, source_target_pairs={{0,16},{16,0},{1,17},{17,1},{2,18},{18,2},{3,19},{19,3},{4,20},{20... | collective-permute-start | bytes 3268616 | tf_op jit(solution)/shard_map/ppermute | solution.py:79
  385.7 26.6 %collective-permute-start.73 = (bf16[608,896]{1,0:T(8,128)(2,1)S(1)}, bf16[608,896]{1,0:T(8,128)(2,1)S(1)}, u32[]{:S(2)}, u32[]{:S(2)}) collective-permute-start(bf16[608,896]{1,0:T(8,128)(2,1)S(1)} %add_convert_fusion.15), channel_id=1, source_target_pairs={{0,4},{12,8},{1,5},{13,9},{2,6},{14,10},{3,7},{15,11},{16,20},{28,... | collective-permute-start | bytes 3268616 | tf_op jit(solution)/shard_map/ppermute | solution.py:1106
  390.3 32.0 %collective-permute-start.83 = (bf16[2,112,1280]{2,1,0:T(8,128)(2,1)S(1)}, bf16[2,112,1280]{2,1,0:T(8,128)(2,1)S(1)}, u32[]{:S(2)}, u32[]{:S(2)}) collective-permute-start(bf16[2,112,1280]{2,1,0:T(8,128)(2,1)S(1)} %get-tuple-element.580), channel_id=1, source_target_pairs={{0,3},{1,2},{2,1},{3,0},{4,7},{5,6},{6,5},{7,4},{8,11},{9,10},{10,... | collective-permute-start | bytes 1720328 | tf_op jit(solution)/shard_map/ppermute | solution.py:75
  391.3 31.0 %collective-permute-start.82 = (bf16[2,112,1280]{2,1,0:T(8,128)(2,1)S(1)}, bf16[2,112,1280]{2,1,0:T(8,128)(2,1)S(1)}, u32[]{:S(2)}, u32[]{:S(2)}) collective-permute-start(bf16[2,112,1280]{2,1,0:T(8,128)(2,1)S(1)} %get-tuple-element.581), channel_id=1, source_target_pairs={{0,2},{1,3},{2,0},{3,1},{4,6},{5,7},{6,4},{7,5},{8,10},{9,11},{10,... | collective-permute-start | bytes 1720328 | tf_op jit(solution)/shard_map/ppermute | solution.py:75
  393.8 29.3 %collective-permute-start.81 = (bf16[2,112,1280]{2,1,0:T(8,128)(2,1)S(1)}, bf16[2,112,1280]{2,1,0:T(8,128)(2,1)S(1)}, u32[]{:S(2)}, u32[]{:S(2)}) collective-permute-start(bf16[2,112,1280]{2,1,0:T(8,128)(2,1)S(1)} %get-tuple-element.582), channel_id=1, source_target_pairs={{0,1},{1,0},{2,3},{3,2},{4,5},{5,4},{6,7},{7,6},{8,9},{9,8},{10,11... | collective-permute-start | bytes 1720328 | tf_op jit(solution)/shard_map/ppermute | solution.py:75
  420.7 34.3 %collective-permute-start.56 = (bf16[128,896]{1,0:T(8,128)(2,1)S(1)}, bf16[128,896]{1,0:T(8,128)(2,1)S(1)}, u32[]{:S(2)}, u32[]{:S(2)}) collective-permute-start(bf16[128,896]{1,0:T(8,128)(2,1)S(1)} %slice.627), channel_id=1, source_target_pairs={{0,1},{1,0},{2,3},{3,2},{16,18},{17,19},{18,16},{19,17},{4,5},{5,4... | collective-permute-start | bytes 688136 | tf_op jit(solution)/shard_map/ppermute | solution.py:44
  421.4 68.8 %collective-permute-start.62 = (bf16[128,896]{1,0:T(8,128)(2,1)S(1)}, bf16[128,896]{1,0:T(8,128)(2,1)S(1)}, u32[]{:S(2)}, u32[]{:S(2)}) collective-permute-start(bf16[128,896]{1,0:T(8,128)(2,1)S(1)} %slice.626), channel_id=1, source_target_pairs={{0,1},{1,0},{2,3},{3,2},{16,18},{17,19},{18,16},{19,17},{4,5},{5,4... | collective-permute-start | bytes 688136 | tf_op jit(solution)/shard_map/ppermute | solution.py:44
  423.3 38.5 %collective-permute-start.91 = (bf16[2,2,112,1280]{3,2,1,0:T(8,128)(2,1)S(1)}, bf16[2,2,112,1280]{3,2,1,0:T(8,128)(2,1)S(1)}, u32[]{:S(2)}, u32[]{:S(2)}) collective-permute-start(bf16[2,2,112,1280]{3,2,1,0:T(8,128)(2,1)S(1)} %pad_maximum_fusion.2), channel_id=1, source_target_pairs={{0,4},{12,8},{1,5},{13,9},{2,6},{14,10},{3,7},{15,11},{16,20},{28,... | collective-permute-start | bytes 3440648 | tf_op jit(solution)/shard_map/ppermute | solution.py:1106
  455.0 63.3 %collective-permute-start.97 = (bf16[2,2,112,1280]{3,2,1,0:T(8,128)(2,1)}, bf16[2,2,112,1280]{3,2,1,0:T(8,128)(2,1)}, u32[]{:S(2)}, u32[]{:S(2)}) collective-permute-start(bf16[2,2,112,1280]{3,2,1,0:T(8,128)(2,1)} %pad_maximum_fusion.3), channel_id=1, source_target_pairs={{0,4},{12,8},{1,5},{13,9},{2,6},{14,10},{3,7},{15,11},{16,20},{28,... | collective-permute-start | bytes 3440648 | tf_op jit(solution)/shard_map/ppermute | solution.py:1106
  460.4 26.1 %collective-permute-start.90 = (bf16[608,896]{1,0:T(8,128)(2,1)S(1)}, bf16[608,896]{1,0:T(8,128)(2,1)S(1)}, u32[]{:S(2)}, u32[]{:S(2)}) collective-permute-start(bf16[608,896]{1,0:T(8,128)(2,1)S(1)} %add_convert_fusion.13), channel_id=1, source_target_pairs={{4,0},{8,12},{5,1},{9,13},{6,2},{10,14},{7,3},{11,15},{20,16},{24,... | collective-permute-start | bytes 3268616 | tf_op jit(solution)/shard_map/ppermute | solution.py:1106
  461.8 23.8 %collective-permute-start.89 = (bf16[128,256]{1,0:T(8,128)(2,1)S(1)}, bf16[128,256]{1,0:T(8,128)(2,1)S(1)}, u32[]{:S(2)}, u32[]{:S(2)}) collective-permute-start(bf16[128,256]{1,0:T(8,128)(2,1)S(1)} %slice.641), channel_id=1, source_target_pairs={{0,4},{4,0},{8,12},{12,8},{16,20},{20,16},{24,28},{28,24},{1,5},{5... | collective-permute-start | bytes 196616 | tf_op jit(solution)/shard_map/ppermute | solution.py:44
  465.3 53.0 %collective-permute-start.96 = (bf16[2,2,112,1280]{3,2,1,0:T(8,128)(2,1)}, bf16[2,2,112,1280]{3,2,1,0:T(8,128)(2,1)}, u32[]{:S(2)}, u32[]{:S(2)}) collective-permute-start(bf16[2,2,112,1280]{3,2,1,0:T(8,128)(2,1)} %add_convert_fusion.9), channel_id=1, source_target_pairs={{4,8},{8,4},{5,9},{9,5},{6,10},{10,6},{7,11},{11,7},{20,24},{24,20... | collective-permute-start | bytes 3440648 | tf_op jit(solution)/shard_map/ppermute | solution.py:1106
  528.8 28.4 %collective-permute-start.88 = (bf16[128,896]{1,0:T(8,128)(2,1)S(1)}, bf16[128,896]{1,0:T(8,128)(2,1)S(1)}, u32[]{:S(2)}, u32[]{:S(2)}) collective-permute-start(bf16[128,896]{1,0:T(8,128)(2,1)S(1)} %slice.622), channel_id=1, source_target_pairs={{0,1},{1,0},{2,3},{3,2},{16,18},{17,19},{18,16},{19,17},{4,5},{5,4... | collective-permute-start | bytes 688136 | tf_op jit(solution)/shard_map/ppermute | solution.py:44
  531.2 23.0 %collective-permute-start.100 = (bf16[2,2,112,1280]{3,2,1,0:T(8,128)(2,1)S(1)}, bf16[2,2,112,1280]{3,2,1,0:T(8,128)(2,1)S(1)}, u32[]{:S(2)}, u32[]{:S(2)}) collective-permute-start(bf16[2,2,112,1280]{3,2,1,0:T(8,128)(2,1)S(1)} %add_convert_fusion.7), channel_id=1, source_target_pairs={{4,8},{8,4},{5,9},{9,5},{6,10},{10,6},{7,11},{11,7},{20,24},{24,20... | collective-permute-start | bytes 3440648 | tf_op jit(solution)/shard_map/ppermute | solution.py:1106
  533.3 19.2 %collective-permute-start.103 = (bf16[224,2176]{1,0:T(8,128)(2,1)S(1)}, bf16[224,2176]{1,0:T(8,128)(2,1)S(1)}, u32[]{:S(2)}, u32[]{:S(2)}) collective-permute-start(bf16[224,2176]{1,0:T(8,128)(2,1)S(1)} %bitcast.287), channel_id=1, source_target_pairs={{0,2},{1,3},{2,0},{3,1},{16,17},{17,16},{18,19},{19,18},{4,6},{5,7... | collective-permute-start | bytes 2924552 | tf_op jit(solution)/shard_map/ppermute | solution.py:44
  534.1 24.5 %collective-permute-start.94 = (bf16[256,896]{1,0:T(8,128)(2,1)S(1)}, bf16[256,896]{1,0:T(8,128)(2,1)S(1)}, u32[]{:S(2)}, u32[]{:S(2)}) collective-permute-start(bf16[256,896]{1,0:T(8,128)(2,1)S(1)} %constant_dynamic-update-slice_fusion.19.lower_ref.refs_7_), channel_id=1, source_target_pairs={{0,2},{1,3},{2,0},{3,1},{16,17},{17,16},{18,19},{19,18},{4,6},{5,7... | collective-permute-start | bytes 1376264 | tf_op jit(solution)/shard_map/ppermute | solution.py:44
  539.7 51.4 %collective-permute-start.106 = (bf16[128,896]{1,0:T(8,128)(2,1)S(1)}, bf16[128,896]{1,0:T(8,128)(2,1)S(1)}, u32[]{:S(2)}, u32[]{:S(2)}) collective-permute-start(bf16[128,896]{1,0:T(8,128)(2,1)S(1)} %slice.621), channel_id=1, source_target_pairs={{0,1},{1,0},{2,3},{3,2},{16,18},{17,19},{18,16},{19,17},{4,5},{5,4... | collective-permute-start | bytes 688136 | tf_op jit(solution)/shard_map/ppermute | solution.py:44
  552.5 27.5 %collective-permute-start.99 = (bf16[2,2,112,1280]{3,2,1,0:T(8,128)(2,1)S(1)}, bf16[2,2,112,1280]{3,2,1,0:T(8,128)(2,1)S(1)}, u32[]{:S(2)}, u32[]{:S(2)}) collective-permute-start(bf16[2,2,112,1280]{3,2,1,0:T(8,128)(2,1)S(1)} %add_convert_fusion.8), channel_id=1, source_target_pairs={{4,0},{8,12},{5,1},{9,13},{6,2},{10,14},{7,3},{11,15},{20,16},{24,... | collective-permute-start | bytes 3440648 | tf_op jit(solution)/shard_map/ppermute | solution.py:1106
  554.1 25.9 %collective-permute-start.104 = (bf16[112,2176]{1,0:T(8,128)(2,1)S(1)}, bf16[112,2176]{1,0:T(8,128)(2,1)S(1)}, u32[]{:S(2)}, u32[]{:S(2)}) collective-permute-start(bf16[112,2176]{1,0:T(8,128)(2,1)S(1)} %slice.619), channel_id=1, source_target_pairs={{0,1},{1,0},{2,3},{3,2},{16,18},{17,19},{18,16},{19,17},{4,5},{5,4... | collective-permute-start | bytes 1462280 | tf_op jit(solution)/shard_map/ppermute | solution.py:44
  557.1 47.5 %collective-permute-start.101 = (bf16[2,2,112,1280]{3,2,1,0:T(8,128)(2,1)S(1)}, bf16[2,2,112,1280]{3,2,1,0:T(8,128)(2,1)S(1)}, u32[]{:S(2)}, u32[]{:S(2)}) collective-permute-start(bf16[2,2,112,1280]{3,2,1,0:T(8,128)(2,1)S(1)} %add_convert_fusion.6), channel_id=1, source_target_pairs={{4,0},{8,12},{5,1},{9,13},{6,2},{10,14},{7,3},{11,15},{20,16},{24,... | collective-permute-start | bytes 3440648 | tf_op jit(solution)/shard_map/ppermute | solution.py:1106
  567.9 23.3 %collective-permute-start.107 = (bf16[256,896]{1,0:T(8,128)(2,1)S(1)}, bf16[256,896]{1,0:T(8,128)(2,1)S(1)}, u32[]{:S(2)}, u32[]{:S(2)}) collective-permute-start(bf16[256,896]{1,0:T(8,128)(2,1)S(1)} %get-tuple-element.437), channel_id=1, source_target_pairs={{0,2},{1,3},{2,0},{3,1},{16,17},{17,16},{18,19},{19,18},{4,6},{5,7... | collective-permute-start | bytes 1376264 | tf_op jit(solution)/shard_map/ppermute | solution.py:44
  580.1 24.5 %collective-permute-start.105 = (bf16[112,2176]{1,0:T(8,128)(2,1)S(1)}, bf16[112,2176]{1,0:T(8,128)(2,1)S(1)}, u32[]{:S(2)}, u32[]{:S(2)}) collective-permute-start(bf16[112,2176]{1,0:T(8,128)(2,1)S(1)} %fusion.4), channel_id=1, source_target_pairs={{0,4},{12,8},{1,5},{13,9},{2,6},{14,10},{3,7},{15,11},{16,20},{28,... | collective-permute-start | bytes 1462280 | tf_op jit(solution)/shard_map/ppermute | solution.py:1106
  587.2 33.8 %collective-permute-start.112 = (bf16[608,896]{1,0:T(8,128)(2,1)S(1)}, bf16[608,896]{1,0:T(8,128)(2,1)S(1)}, u32[]{:S(2)}, u32[]{:S(2)}) collective-permute-start(bf16[608,896]{1,0:T(8,128)(2,1)S(1)} %get-tuple-element.448), channel_id=1, source_target_pairs={{0,16},{16,0},{1,17},{17,1},{2,18},{18,2},{3,19},{19,3},{4,20},{20... | collective-permute-start | bytes 3268616 | tf_op jit(solution)/shard_map/ppermute | solution.py:79
  617.8 34.2 %collective-permute-start.117 = (bf16[4,2,112,1280]{3,2,1,0:T(8,128)(2,1)S(1)}, bf16[4,2,112,1280]{3,2,1,0:T(8,128)(2,1)S(1)}, u32[]{:S(2)}, u32[]{:S(2)}) collective-permute-start(bf16[4,2,112,1280]{3,2,1,0:T(8,128)(2,1)S(1)} %get-tuple-element.453), channel_id=1, source_target_pairs={{0,16},{16,0},{1,17},{17,1},{2,18},{18,2},{3,19},{19,3},{4,20},{20... | collective-permute-start | bytes 6881288 | tf_op jit(solution)/shard_map/ppermute | solution.py:79
  620.2 31.9 %collective-permute-start.114 = (bf16[128,896]{1,0:T(8,128)(2,1)S(1)}, bf16[128,896]{1,0:T(8,128)(2,1)S(1)}, u32[]{:S(2)}, u32[]{:S(2)}) collective-permute-start(bf16[128,896]{1,0:T(8,128)(2,1)S(1)} %slice.620), channel_id=1, source_target_pairs={{0,1},{1,0},{2,3},{3,2},{16,18},{17,19},{18,16},{19,17},{4,5},{5,4... | collective-permute-start | bytes 688136 | tf_op jit(solution)/shard_map/ppermute | solution.py:44
  621.2 24.7 %collective-permute-start.113 = (bf16[608,896]{1,0:T(8,128)(2,1)S(1)}, bf16[608,896]{1,0:T(8,128)(2,1)S(1)}, u32[]{:S(2)}, u32[]{:S(2)}) collective-permute-start(bf16[608,896]{1,0:T(8,128)(2,1)S(1)} %add_convert_fusion.12), channel_id=1, source_target_pairs={{0,4},{12,8},{1,5},{13,9},{2,6},{14,10},{3,7},{15,11},{16,20},{28,... | collective-permute-start | bytes 3268616 | tf_op jit(solution)/shard_map/ppermute | solution.py:1106
  632.1 20.0 %collective-permute-start.111 = (bf16[112,2176]{1,0:T(8,128)(2,1)S(1)}, bf16[112,2176]{1,0:T(8,128)(2,1)S(1)}, u32[]{:S(2)}, u32[]{:S(2)}) collective-permute-start(bf16[112,2176]{1,0:T(8,128)(2,1)S(1)} %add_convert_fusion.19), channel_id=1, source_target_pairs={{4,8},{8,4},{5,9},{9,5},{6,10},{10,6},{7,11},{11,7},{20,24},{24,20... | collective-permute-start | bytes 1462280 | tf_op jit(solution)/shard_map/ppermute | solution.py:1106
  646.2 31.2 %collective-permute-start.116 = (bf16[608,896]{1,0:T(8,128)(2,1)S(1)}, bf16[608,896]{1,0:T(8,128)(2,1)S(1)}, u32[]{:S(2)}, u32[]{:S(2)}) collective-permute-start(bf16[608,896]{1,0:T(8,128)(2,1)S(1)} %add_convert_fusion.11), channel_id=1, source_target_pairs={{4,8},{8,4},{5,9},{9,5},{6,10},{10,6},{7,11},{11,7},{20,24},{24,20... | collective-permute-start | bytes 3268616 | tf_op jit(solution)/shard_map/ppermute | solution.py:1106
  648.8 46.7 %collective-permute-start.110 = (bf16[128,256]{1,0:T(8,128)(2,1)S(1)}, bf16[128,256]{1,0:T(8,128)(2,1)S(1)}, u32[]{:S(2)}, u32[]{:S(2)}) collective-permute-start(bf16[128,256]{1,0:T(8,128)(2,1)S(1)} %slice.640), channel_id=1, source_target_pairs={{0,4},{4,0},{8,12},{12,8},{16,20},{20,16},{24,28},{28,24},{1,5},{5... | collective-permute-start | bytes 196616 | tf_op jit(solution)/shard_map/ppermute | solution.py:44
  653.5 30.3 %collective-permute-start.125 = (bf16[2,112,1280]{2,1,0:T(8,128)(2,1)S(1)}, bf16[2,112,1280]{2,1,0:T(8,128)(2,1)S(1)}, u32[]{:S(2)}, u32[]{:S(2)}) collective-permute-start(bf16[2,112,1280]{2,1,0:T(8,128)(2,1)S(1)} %get-tuple-element.575), channel_id=1, source_target_pairs={{0,2},{1,3},{2,0},{3,1},{4,6},{5,7},{6,4},{7,5},{8,10},{9,11},{10,... | collective-permute-start | bytes 1720328 | tf_op jit(solution)/shard_map/ppermute | solution.py:75
  654.2 30.9 %collective-permute-start.126 = (bf16[2,112,1280]{2,1,0:T(8,128)(2,1)S(1)}, bf16[2,112,1280]{2,1,0:T(8,128)(2,1)S(1)}, u32[]{:S(2)}, u32[]{:S(2)}) collective-permute-start(bf16[2,112,1280]{2,1,0:T(8,128)(2,1)S(1)} %get-tuple-element.576), channel_id=1, source_target_pairs={{0,3},{1,2},{2,1},{3,0},{4,7},{5,6},{6,5},{7,4},{8,11},{9,10},{10,... | collective-permute-start | bytes 1720328 | tf_op jit(solution)/shard_map/ppermute | solution.py:75
  666.2 33.2 %collective-permute-start.119 = (bf16[2,2,112,1280]{3,2,1,0:T(8,128)(2,1)S(1)}, bf16[2,2,112,1280]{3,2,1,0:T(8,128)(2,1)S(1)}, u32[]{:S(2)}, u32[]{:S(2)}) collective-permute-start(bf16[2,2,112,1280]{3,2,1,0:T(8,128)(2,1)S(1)} %pad_maximum_fusion.4), channel_id=1, source_target_pairs={{0,4},{12,8},{1,5},{13,9},{2,6},{14,10},{3,7},{15,11},{16,20},{28,... | collective-permute-start | bytes 3440648 | tf_op jit(solution)/shard_map/ppermute | solution.py:1106
  683.8 70.6 %collective-permute-start.123 = (bf16[608,896]{1,0:T(8,128)(2,1)S(1)}, bf16[608,896]{1,0:T(8,128)(2,1)S(1)}, u32[]{:S(2)}, u32[]{:S(2)}) collective-permute-start(bf16[608,896]{1,0:T(8,128)(2,1)S(1)} %add_convert_fusion.10), channel_id=1, source_target_pairs={{4,0},{8,12},{5,1},{9,13},{6,2},{10,14},{7,3},{11,15},{20,16},{24,... | collective-permute-start | bytes 3268616 | tf_op jit(solution)/shard_map/ppermute | solution.py:1106
  692.3 23.6 %collective-permute-start.127 = (bf16[2,2,112,1280]{3,2,1,0:T(8,128)(2,1)S(1)}, bf16[2,2,112,1280]{3,2,1,0:T(8,128)(2,1)S(1)}, u32[]{:S(2)}, u32[]{:S(2)}) collective-permute-start(bf16[2,2,112,1280]{3,2,1,0:T(8,128)(2,1)S(1)} %pad_maximum_fusion.5), channel_id=1, source_target_pairs={{0,4},{12,8},{1,5},{13,9},{2,6},{14,10},{3,7},{15,11},{16,20},{28,... | collective-permute-start | bytes 3440648 | tf_op jit(solution)/shard_map/ppermute | solution.py:1106
  695.6 58.8 %collective-permute-start.122 = (bf16[128,256]{1,0:T(8,128)(2,1)S(1)}, bf16[128,256]{1,0:T(8,128)(2,1)S(1)}, u32[]{:S(2)}, u32[]{:S(2)}) collective-permute-start(bf16[128,256]{1,0:T(8,128)(2,1)S(1)} %slice.639), channel_id=1, source_target_pairs={{0,4},{4,0},{8,12},{12,8},{16,20},{20,16},{24,28},{28,24},{1,5},{5... | collective-permute-start | bytes 196616 | tf_op jit(solution)/shard_map/ppermute | solution.py:44
  700.2 22.8 %collective-permute-start.124 = (bf16[2,2,112,1280]{3,2,1,0:T(8,128)(2,1)S(1)}, bf16[2,2,112,1280]{3,2,1,0:T(8,128)(2,1)S(1)}, u32[]{:S(2)}, u32[]{:S(2)}) collective-permute-start(bf16[2,2,112,1280]{3,2,1,0:T(8,128)(2,1)S(1)} %add_convert_fusion.5), channel_id=1, source_target_pairs={{4,8},{8,4},{5,9},{9,5},{6,10},{10,6},{7,11},{11,7},{20,24},{24,20... | collective-permute-start | bytes 3440648 | tf_op jit(solution)/shard_map/ppermute | solution.py:1106
  717.3 45.2 %collective-permute-start.133 = (bf16[2,2,112,1280]{3,2,1,0:T(8,128)(2,1)}, bf16[2,2,112,1280]{3,2,1,0:T(8,128)(2,1)}, u32[]{:S(2)}, u32[]{:S(2)}) collective-permute-start(bf16[2,2,112,1280]{3,2,1,0:T(8,128)(2,1)} %add_convert_fusion.3), channel_id=1, source_target_pairs={{4,8},{8,4},{5,9},{9,5},{6,10},{10,6},{7,11},{11,7},{20,24},{24,20... | collective-permute-start | bytes 3440648 | tf_op jit(solution)/shard_map/ppermute | solution.py:1106
  719.0 35.2 %collective-permute-start.129 = (bf16[256,256]{1,0:T(8,128)(2,1)S(1)}, bf16[256,256]{1,0:T(8,128)(2,1)S(1)}, u32[]{:S(2)}, u32[]{:S(2)}) collective-permute-start(bf16[256,256]{1,0:T(8,128)(2,1)S(1)} %slice.632), channel_id=1, source_target_pairs={{0,8},{4,12},{8,0},{12,4},{16,24},{20,28},{24,16},{28,20},{1,9},{5... | collective-permute-start | bytes 393224 | tf_op jit(solution)/shard_map/ppermute | solution.py:44
  724.5 38.0 %collective-permute-start.132 = (bf16[2,2,112,1280]{3,2,1,0:T(8,128)(2,1)}, bf16[2,2,112,1280]{3,2,1,0:T(8,128)(2,1)}, u32[]{:S(2)}, u32[]{:S(2)}) collective-permute-start(bf16[2,2,112,1280]{3,2,1,0:T(8,128)(2,1)} %add_convert_fusion.4), channel_id=1, source_target_pairs={{4,0},{8,12},{5,1},{9,13},{6,2},{10,14},{7,3},{11,15},{20,16},{24,... | collective-permute-start | bytes 3440648 | tf_op jit(solution)/shard_map/ppermute | solution.py:1106
  804.0 27.3 %collective-permute-start.141 = (bf16[2,2,112,1280]{3,2,1,0:T(8,128)(2,1)S(1)}, bf16[2,2,112,1280]{3,2,1,0:T(8,128)(2,1)S(1)}, u32[]{:S(2)}, u32[]{:S(2)}) collective-permute-start(bf16[2,2,112,1280]{3,2,1,0:T(8,128)(2,1)S(1)} %add_convert_fusion.2), channel_id=1, source_target_pairs={{4,0},{8,12},{5,1},{9,13},{6,2},{10,14},{7,3},{11,15},{20,16},{24,... | collective-permute-start | bytes 3440648 | tf_op jit(solution)/shard_map/ppermute | solution.py:1106
  811.4 38.6 %collective-permute-start.144 = (bf16[608,896]{1,0:T(8,128)(2,1)S(1)}, bf16[608,896]{1,0:T(8,128)(2,1)S(1)}, u32[]{:S(2)}, u32[]{:S(2)}) collective-permute-start(bf16[608,896]{1,0:T(8,128)(2,1)S(1)} %get-tuple-element.572), channel_id=1, source_target_pairs={{0,16},{16,0},{1,17},{17,1},{2,18},{18,2},{3,19},{19,3},{4,20},{20... | collective-permute-start | bytes 3268616 | tf_op jit(solution)/shard_map/ppermute | solution.py:79
  814.2 38.5 %collective-permute-start.131 = (f32[3,128,896]{2,1,0:T(8,128)S(1)}, f32[3,128,896]{2,1,0:T(8,128)S(1)}, u32[]{:S(2)}, u32[]{:S(2)}) collective-permute-start(f32[3,128,896]{2,1,0:T(8,128)S(1)} %get-tuple-element.598), channel_id=1, source_target_pairs={{0,16},{16,0},{1,17},{17,1},{2,18},{18,2},{3,19},{19,3},{4,20},{20... | collective-permute-start | bytes 4128776 | tf_op jit(solution)/shard_map/ppermute | solution.py:79
  831.6 22.9 %collective-permute-start.143 = (bf16[2,2,112,1280]{3,2,1,0:T(8,128)(2,1)S(1)}, bf16[2,2,112,1280]{3,2,1,0:T(8,128)(2,1)S(1)}, u32[]{:S(2)}, u32[]{:S(2)}) collective-permute-start(bf16[2,2,112,1280]{3,2,1,0:T(8,128)(2,1)S(1)} %get-tuple-element.565), channel_id=1, source_target_pairs={{0,16},{16,0},{1,17},{17,1},{2,18},{18,2},{3,19},{19,3},{4,20},{20... | collective-permute-start | bytes 3440648 | tf_op jit(solution)/shard_map/ppermute | solution.py:79
  (349 other events, 3975.4 us)

commit v4 on v3

--- a/solution.py
+++ b/solution.py
@@ -1,4 +1,5 @@
 import functools
+from types import SimpleNamespace
 
 import jax
 import jax.numpy as jnp
@@ -190,12 +191,12 @@
 
 def qkv_rows(x, p, cos_table, sin_table, kv_width):
     rows, width = x.shape
-    total = p["qkv"].shape[1]
+    total = p.qkv.shape[1]
     query_width = total - 2 * kv_width
     return call(
         qkv_kernel,
         [shape(rows, width, bf16), shape(rows, query_width, bf16), shape(rows, 2 * kv_width, bf16)],
-        [x, p["gain_one"], p["qkv"], p["bias"], cos_table, sin_table],
+        [x, p.gain_one, p.qkv, p.bias, cos_table, sin_table],
         flops=2 * rows * width * total,
     )
 
@@ -273,7 +274,7 @@
     return call(
         functools.partial(attend_kernel, group),
         [shape(rows, width, bf16), shape(*x.shape, f32), shape(*x.shape, bf16)],
-        [queries, kva, kvb, bias, x, p["out"], turn_of(p["gain_two"])],
+        [queries, kva, kvb, bias, x, p.out, turn_of(p.gain_two)],
         scratch=[pltpu.VMEM((total, lanes), bf16)] * 2,
         flops=flops,
     )
@@ -381,9 +382,9 @@
             mix_low,
             mix_got,
             residual,
-            p["gain_two"],
+            p.gain_two,
             upstream,
-            p["out"],
+            p.out,
             cos_table,
             sin_table,
         ],
@@ -434,7 +435,7 @@
 
 def qkv_back(dq, low, got, x, grad_residual, p, cos_table, sin_table):
     rows, width = x.shape
-    total = p["qkv"].shape[1]
+    total = p.qkv.shape[1]
     return call(
         qkv_back_kernel,
         [
@@ -444,7 +445,7 @@
             shape(1, width, f32),
             shape(1, total, f32),
         ],
-        [dq, low, got, cos_table, sin_table, p["qkv"], x, p["gain_one"], grad_residual],
+        [dq, low, got, cos_table, sin_table, p.qkv, x, p.gain_one, grad_residual],
         flops=2 * rows * width * total,
     )
 
@@ -479,17 +480,18 @@
 
 def ffn(lower, upper, p):
     half, width = lower.shape
-    wide = p["gate"].shape[1]
-    chunk = chunk_of(wide)
+    wide = p.gate.shape[1]
+    chunk = wide
     rows = half + upper.shape[0]
     whole = pl.BlockSpec((half, width), lambda n: (0, 0))
     columns = pl.BlockSpec((width, chunk), lambda n: (0, n))
     return call(
         ffn_kernel,
         [shape(half, width, bf16), shape(rows - half, width, bf16)] + [shape(rows, wide, bf16)] * 3,
-        [lower, upper, p["gate"], p["up"], p["down"]],
+        [lower, upper, p.gate, p.up, p.down],
         scratch=[pltpu.VMEM((rows, width), bf16), pltpu.VMEM((rows, width), f32)],
         flops=6 * rows * width * wide,
+        vmem=6,
         grid=(wide // chunk,),
         in_specs=[whole, whole, columns, columns, pl.BlockSpec((chunk, width), lambda n: (n, 0))],
         out_specs=[whole, whole] + [pl.BlockSpec((rows, chunk), lambda n: (0, n))] * 3,
@@ -526,8 +528,8 @@
 
 def ffn_back(lower, upper, gate, up, p):
     half, width = gate.shape[0] // 2, lower.shape[-1]
-    wide = p["gate"].shape[1]
-    chunk = chunk_of(wide)
+    wide = p.gate.shape[1]
+    chunk = wide
     rows = 2 * half
     whole = pl.BlockSpec((half, width), lambda n: (0, 0))
     columns = pl.BlockSpec((width, chunk), lambda n: (0, n))
@@ -535,9 +537,10 @@
     return call(
         ffn_back_kernel,
         [shape(half, width, bf16), shape(rows - half, width, bf16)] + [shape(rows, wide, bf16)] * 2,
-        [lower, upper, gate, up, p["gate"], p["up"], p["down"]],
+        [lower, upper, gate, up, p.gate, p.up, p.down],
         scratch=[pltpu.VMEM((rows, width), bf16), pltpu.VMEM((rows, width), f32)],
         flops=6 * rows * width * wide,
+        vmem=6,
         grid=(wide // chunk,),
         in_specs=[
             whole,
@@ -873,7 +876,7 @@
     down_other = other(w_down[0])
     downs = by_section(w_down[0], down_other), by_section(down_other, w_down[0])
 
-    params = [{}, {}]
+    params = [SimpleNamespace(), SimpleNamespace()]
     clock, flows, last, pins = [0], [], [], []
 
     class Flow:
@@ -917,19 +920,19 @@
             ((0, edge), (edge, edge + width), (edge + width, edge + width + lanes)),
         )
         rows = small.T
-        p["qkv"], p["out"] = qkv, out
-        p["gain_one"], p["gain_two"] = rows[0:1], rows[1:2]
+        p.qkv, p.out = qkv, out
+        p.gain_one, p.gain_two = rows[0:1], rows[1:2]
         key_bias, value_bias = [
             rows[n].reshape(spread, shard)[:, :per].reshape(1, -1) for n in (3, 4)
         ]
-        p["bias"] = jnp.concatenate([rows[2:3], key_bias, value_bias], axis=1)
+        p.bias = jnp.concatenate([rows[2:3], key_bias, value_bias], axis=1)
         blocks = [blocks[0]] + [direct(blocks[mask], "dp", mask) for mask in range(1, spread)]
         yield blocks
         yield blocks
         blocks = blocks + [other(block) for block in blocks]
         blocks, down = after((blocks, downs[layer]), list(last))
-        p["gate"], p["up"] = lay_gate_up(gate_up_at, blocks, wide)
-        p["down"] = jnp.pad(down, ((0, wide - slice_ff), (0, 0)))
+        p.gate, p.up = lay_gate_up(gate_up_at, blocks, wide)
+        p.down = jnp.pad(down, ((0, wide - slice_ff), (0, 0)))
 
     first = core * share
     place = lax.axis_index("ctx")
@@ -960,15 +963,15 @@
         for n in range(micro_count)
     ]
 
-    kept = [[{} for _ in range(micro_count)] for _ in layers]
+    kept = [[SimpleNamespace() for _ in range(micro_count)] for _ in layers]
     for n in range(micro_count):
-        kept[1][n]["above"] = Part(my_cotangent, 0, n)
+        kept[1][n].above = Part(my_cotangent, 0, n)
     def kv_steps(ks, kv):
         def give(*parts):
             whole = jnp.concatenate(parts)
             theirs = other(whole)
             for n, k in enumerate(ks):
-                k["kva"], k["kvb"] = [
+                k.kva, k.kvb = [
                     Part(part.reshape(-1, len(ks), share, 2 * kv_width), 1, n)
                     for part in (whole, theirs)
                 ]
@@ -977,124 +980,124 @@
 
     def run_q_all():
         flow = Flow(weights_steps(0, attn_halves[0], gate_up_halves[0]), weight_slack)
-        while "qkv" not in params[0]:
+        while not hasattr(params[0], "qkv"):
             flow.move()
-        kept[0][0]["weights"] = flow
+        kept[0][0].weights = flow
         tokens_in = turn_of(my_tokens.reshape(-1, width))
         rows = qkv_rows(tokens_in, params[0], cos_all, sin_all, kv_width)
         done(rows[0])
         normed, queries = [part.reshape(micro_count, share, -1) for part in rows[:2]]
         for n in range(micro_count):
             k = kept[0][n]
-            k["x"], k["normed"], k["queries"] = [
+            k.x, k.normed, k.queries = [
                 Part(part, 0, n) for part in (my_tokens, normed, queries)
             ]
         flow = Flow(kv_steps(kept[0], rows[2]), 1)
         for n in range(micro_count):
-            kept[0][n]["kv"] = flow
+            kept[0][n].kv = flow
         halves = after((attn_halves[1], gate_up_halves[1]), list(last))
-        kept[1][0]["weights"] = Flow(weights_steps(1, *halves), 1)
+        kept[1][0].weights = Flow(weights_steps(1, *halves), 1)
 
     def run_q(n):
         k = kept[1][n]
-        kept[0][n]["scatter"].finish()
-        while "qkv" not in params[1]:
-            kept[1][0]["weights"].move()
-        k["x"] = turn_of(kept[0][n]["result"])
-        k["normed"], k["queries"], kv = qkv_rows(k["x"], params[1], *context[n][1:], kv_width)
-        done(k["normed"])
-        k["kv"] = Flow(kv_steps([k], kv), 2)
+        kept[0][n].scatter.finish()
+        while not hasattr(params[1], "qkv"):
+            kept[1][0].weights.move()
+        k.x = turn_of(kept[0][n].result)
+        k.normed, k.queries, kv = qkv_rows(k.x, params[1], *context[n][1:], kv_width)
+        done(k.normed)
+        k.kv = Flow(kv_steps([k], kv), 2)
 
     def run_a(layer, n):
         k, p = kept[layer][n], params[layer]
-        k["kv"].finish()
-        k["attended"], k["residual"], mixing = attend(
-            k["queries"], k["kva"], k["kvb"], context[n][0], k["x"], p, turn_of
+        k.kv.finish()
+        k.attended, k.residual, mixing = attend(
+            k.queries, k.kva, k.kvb, context[n][0], k.x, p, turn_of
         )
         done(mixing)
-        k["gather"] = Flow(gather_steps(mixing, "dp", lambda *got: k.update(mixing=got)), 2)
+        k.gather = Flow(gather_steps(mixing, "dp", lambda *got: k.__dict__.update(mixing=got)), 2)
 
     def run_f(layer, n):
         k, p = kept[layer][n], params[layer]
-        k["gather"].finish()
-        kept[layer][0]["weights"].finish()
-        lower, upper = k["mixing"]
-        part_low, part_up, k["hidden"], k["gate"], k["up"] = ffn(lower, turn_of(upper), p)
-        done(k["gate"])
+        k.gather.finish()
+        kept[layer][0].weights.finish()
+        lower, upper = k.mixing
+        part_low, part_up, k.hidden, k.gate, k.up = ffn(lower, turn_of(upper), p)
+        done(k.gate)
 
         def give(low, got):
-            k["result"] = (k["residual"] + low + got.astype(f32)).astype(bf16)
-
-        k["scatter"] = Flow(scatter_steps(part_low, part_up, "dp", give), 2 if layer == 0 else 6)
+            k.result = (k.residual + low + got.astype(f32)).astype(bf16)
+
+        k.scatter = Flow(scatter_steps(part_low, part_up, "dp", give), 2 if layer == 0 else 6)
         if layer:
-            k["after"] = k["scatter"]
+            k.after = k.scatter
 
     def run_c():
         def give(*parts):
             for n in range(micro_count):
-                kept[1][n]["grad_ffn"] = [
+                kept[1][n].grad_ffn = [
                     Part(part.reshape(-1, micro_count, share, width), 1, n) for part in parts
                 ]
 
         rows = after(my_cotangent[None], last)
-        kept[1][0]["cotangent"] = Flow(gather_steps(rows, "dp", give), 4)
+        kept[1][0].cotangent = Flow(gather_steps(rows, "dp", give), 4)
 
     def run_d(layer, n):
         k, p = kept[layer][n], params[layer]
         if layer:
-            kept[1][0]["cotangent"].finish()
+            kept[1][0].cotangent.finish()
         else:
-            k["gather"].finish()
-        lower, upper = k["grad_ffn"]
-        part_low, part_up, k["grad_gate"], k["grad_up"] = ffn_back(
-            lower, upper, turn_of(k["gate"]), k["up"], p
+            k.gather.finish()
+        lower, upper = k.grad_ffn
+        part_low, part_up, k.grad_gate, k.grad_up = ffn_back(
+            lower, upper, turn_of(k.gate), k.up, p
         )
-        done(k["grad_gate"])
-        k["scatter"] = Flow(
-            scatter_steps(part_low, part_up, "dp", lambda *got: k.update(scattered=got)), 2
+        done(k.grad_gate)
+        k.scatter = Flow(
+            scatter_steps(part_low, part_up, "dp", lambda *got: k.__dict__.update(scattered=got)), 2
         )
 
     def run_b(layer, n):
         k, p = kept[layer][n], params[layer]
-        k["scatter"].finish()
+        k.scatter.finish()
         bias, cos_table, sin_table = context[n]
-        low, got = k["scattered"]
-        k["dq"], dkva, dkvb, k["grad_residual"], k["grad_attended"], k["gain_two"] = attend_back(
-            k["queries"],
-            k["kva"],
-            k["kvb"],
+        low, got = k.scattered
+        k.dq, dkva, dkvb, k.grad_residual, k.grad_attended, k.gain_two = attend_back(
+            k.queries,
+            k.kva,
+            k.kvb,
             bias,
             low,
             turn_of(got),
-            k["residual"],
-            k["above"],
+            k.residual,
+            k.above,
             p,
             cos_table,
             sin_table,
         )
-        done(k["dq"])
+        done(k.dq)
         pair = dkva.astype(f32) + other(dkvb).astype(f32)
         middle = pair.shape[0] // 2
-        k["scatter"] = Flow(
+        k.scatter = Flow(
             scatter_steps(
-                pair[:middle], pair[middle:], "ctx", lambda *got: k.update(grad_kv=got)
+                pair[:middle], pair[middle:], "ctx", lambda *got: k.__dict__.update(grad_kv=got)
             ),
             2,
         )
 
     def run_k(layer, n):
         k, p = kept[layer][n], params[layer]
-        k["scatter"].finish()
-        low, got = k["grad_kv"]
-        k["grad_qkv"], k["grad_in"], grad_low, k["gain_one"], k["bias"] = qkv_back(
-            k["dq"], low, turn_of(got), k["x"], k["grad_residual"], p, *context[n][1:]
+        k.scatter.finish()
+        low, got = k.grad_kv
+        k.grad_qkv, k.grad_in, grad_low, k.gain_one, k.bias = qkv_back(
+            k.dq, low, turn_of(got), k.x, k.grad_residual, p, *context[n][1:]
         )
-        done(k["grad_qkv"])
+        done(k.grad_qkv)
         if layer:
             below = kept[0][n]
-            below["above"] = k["grad_in"]
-            below["gather"] = Flow(
-                gather_steps(grad_low, "dp", lambda *got: below.update(grad_ffn=got)), 2
+            below.above = k.grad_in
+            below.gather = Flow(
+                gather_steps(grad_low, "dp", lambda *got: below.__dict__.update(grad_ffn=got)), 2
             )
 
     ends = (place == 0) | (place == 3)
@@ -1124,10 +1127,10 @@
             moving.append(Flow(ctx_steps(name, waiting.pop(name)), 1000))
 
     def column_of(layer, name):
-        return [k[name] for k in kept[layer]]
+        return [getattr(k, name) for k in kept[layer]]
 
     def parts_of(layer, name):
-        return [part for k in kept[layer] for part in k[name]]
+        return [part for k in kept[layer] for part in getattr(k, name)]
 
     def over_cores(keep, send):
         return keep.astype(f32) + other(send).astype(f32)
@@ -1147,7 +1150,7 @@
         )
         done(keep)
         blocks = over_cores(keep, send).astype(bf16)
-        before = kept[layer][micro_count - 1]["scatter"].value
+        before = kept[layer][micro_count - 1].scatter.value
 
         def steps():
             sent = after(blocks, before) if before is not None else blocks
@@ -1215,8 +1218,8 @@
     while moving:
         tick()
     for k in kept[1]:
-        if "result" not in k:
-            k["after"].finish()
+        if not hasattr(k, "result"):
+            k.after.finish()
 
     section_out = both_rows([jnp.stack(column_of(layer, "result")) for layer in layers])
     section_grad = both_rows([jnp.stack(column_of(layer, "grad_in")) for layer in layers])

time: 876 us -> 850 us (0.970)
  Pallas kernels: 250 us -> 213 us
  waiting for transfers between devices: 276 us -> 287 us
    pallas_call x47, Pallas kernels: 250 us -> 213 us  [call(): pl.pallas_call(kernel, out_shape=outs, grid=grid or (), in_specs=specs, o...]
    unnamed x546 -> x532, local copies, waits for them, and re-layouts: 57.2 us -> 57.7 us
  transfers between devices with their start and end apart: 145 -> 145, of which waited for: 47 -> 49; matrix products, arithmetic and copies ran while one was open for 7% -> 8% of each run, Pallas kernels for 27% -> 23%
where the time goes in v4:
time: 850 us; the launch traced here: 838 us
  waiting for transfers between devices  287 us (34%)
  Pallas kernels  213 us (25%)
  starting transfers between devices  203 us (24%)
  local copies, waits for them, and re-layouts  79.9 us (9%)
  other arithmetic  47.9 us (6%)
    pallas_call x47, Pallas kernels, call(): pl.pallas_call(kernel, out_shape=outs, grid=grid or (), in_specs=specs, o...  213 us
    ppermute x72, waiting for transfers between devices, step(): return lax.ppermute(block, ('section', axis), route)  165 us
    ppermute x24, waiting for transfers between devices, ctx_steps(): got = lax.ppermute(value, 'ctx', route)  90.7 us
    ppermute x72, starting transfers between devices, step(): return lax.ppermute(block, ('section', axis), route)  82.7 us
    ppermute x37, starting transfers between devices, other(): return lax.ppermute(block, 'section', [(0, 1), (1, 0)])  65.7 us
    unnamed x532, local copies, waits for them, and re-layouts  57.7 us
    ppermute x24, starting transfers between devices, ctx_steps(): got = lax.ppermute(value, 'ctx', route)  43.9 us
    ppermute x12, waiting for transfers between devices, direct(): return lax.ppermute(block, axis, [(i, i ^ mask) for i in range(size)])  22.9 us
  transfers between devices with their start and end apart: 145, of which 49 were waited for; matrix products, arithmetic and copies ran while one was open for 8% of the time, Pallas kernels for 23%

profile of v4, /device:TPU:1, one launch (start us, length us, event | category | flops | bytes accessed | tf_op | source)
XLA Modules:
  0.0 837.7 jit_solution(4373672528918852480)
XLA Ops:
  23.5 8.9 %collective-permute-done.2.refs_1_ = bf16[224,2176]{1,0:T(8,128)(2,1)S(1)} collective-permute-done((bf16[224,2176]{1,0:T(8,128)(2,1)S(1)}, bf16[224,2176]{1,0:T(8,128)(2,1)S(1)}, u32[]{:S(2)}, u32[]{:S(2)}) %collective-permute-start.2) | collective-permute-done | bytes 974880 | tf_op jit(solution)/shard_map/ppermute | solution.py:45
  66.0 12.9 %collective-permute-done.6 = bf16[2,384,256]{2,1,0:T(8,128)(2,1)S(1)} collective-permute-done((bf16[2,384,256]{2,1,0:T(8,128)(2,1)S(1)}, bf16[2,384,256]{2,1,0:T(8,128)(2,1)S(1)}, u32[]{:S(2)}, u32[]{:S(2)}) %collective-permute-start.6) | collective-permute-done | bytes 393248 | tf_op jit(solution)/shard_map/ppermute | solution.py:45
  86.1 5.5 collective-permute-done.10.refs_2_
  92.3 4.1 collective-permute-start.22
  96.7 6.7 shard_map.258
  117.7 6.5 shard_map.259
  130.7 7.6 collective-permute-done.17.refs_2_
  139.5 5.0 collective-permute-done.14.upper_ref.refs_1_
  144.5 5.2 shard_map.261
  149.7 6.9 shard_map.262
  178.9 5.6 shard_map.263
  193.7 5.6 shard_map.266
  208.9 5.6 shard_map.268
  219.5 3.9 collective-permute-start.43
  224.9 5.6 shard_map.270
  249.8 4.4 shard_map.272
  254.2 5.6 shard_map.273
  260.8 9.9 %collective-permute-done.52.upper_ref.refs_3_ = bf16[256,896]{1,0:T(8,128)(2,1)S(1)} collective-permute-done((bf16[256,896]{1,0:T(8,128)(2,1)S(1)}, bf16[256,896]{1,0:T(8,128)(2,1)S(1)}, u32[]{:S(2)}, u32[]{:S(2)}) %collective-permute-start.52) | collective-permute-done | bytes 458784 | tf_op jit(solution)/shard_map/ppermute | solution.py:45
  271.5 4.6 shard_map.274
  277.2 4.4 shard_map.275
  283.2 4.4 shard_map.276
  291.6 4.5 shard_map.277
  297.7 7.9 shard_map.278
  308.2 4.5 shard_map.279
  315.1 7.3 collective-permute-done.67
  322.5 5.2 shard_map.280
  329.9 10.9 %shard_map.281 = (bf16[4,2,112,1280]{3,2,1,0:T(8,128)(2,1)S(1)}, bf16[4,2,112,1280]{3,2,1,0:T(8,128)(2,1)S(1)}) custom-call(s32[10]{0:T(128)S(1)} %stack.193.info_ref, bf16[256,896]{1,0:T(8,128)(2,1)S(1)} %constant_dynamic-update-slice_fusion.9.lower_ref.refs_0_, bf16[256,896]{1,0:T(8,128)(2,1)S(1)} %collective-permute-done.40.upper_ref.refs_1_, ...), custom_call_target="tpu_custom_call" | custom-call | flops 7046430720 | bytes 15204392 | tf_op jit(solution)/shard_map/pallas_call | solution.py:143
  344.4 8.0 collective-permute-done.61
  354.3 7.7 shard_map.282
  372.6 18.0 %collective-permute-done.73 = bf16[608,896]{1,0:T(8,128)(2,1)S(1)} collective-permute-done((bf16[608,896]{1,0:T(8,128)(2,1)S(1)}, bf16[608,896]{1,0:T(8,128)(2,1)S(1)}, u32[]{:S(2)}, u32[]{:S(2)}) %collective-permute-start.73) | collective-permute-done | bytes 1089568 | tf_op jit(solution)/shard_map/ppermute | solution.py:1109
  392.4 6.5 collective-permute-done.75
  401.5 5.8 collective-permute-start.91
  408.5 7.7 shard_map.284
  420.2 10.7 %collective-permute-start.86 = (bf16[256,256]{1,0:T(8,128)(2,1)S(1)}, bf16[256,256]{1,0:T(8,128)(2,1)S(1)}, u32[]{:S(2)}, u32[]{:S(2)}) collective-permute-start(bf16[256,256]{1,0:T(8,128)(2,1)S(1)} %slice.635), channel_id=1, source_target_pairs={{0,8},{4,12},{8,0},{12,4},{16,24},{20,28},{24,16},{28,20},{1,9},{5... | collective-permute-start | bytes 393224 | tf_op jit(solution)/shard_map/ppermute | solution.py:45
  433.0 5.5 collective-permute-start.97
  445.6 4.5 shard_map.286
  450.2 13.4 %collective-permute-done.89.got_ref = bf16[128,256]{1,0:T(8,128)(2,1)S(1)} collective-permute-done((bf16[128,256]{1,0:T(8,128)(2,1)S(1)}, bf16[128,256]{1,0:T(8,128)(2,1)S(1)}, u32[]{:S(2)}, u32[]{:S(2)}) %collective-permute-start.89) | collective-permute-done | bytes 65568 | tf_op jit(solution)/shard_map/ppermute | solution.py:45
  468.2 8.2 collective-permute-done.87
  486.1 5.7 shard_map.288
  495.7 6.5 collective-permute-start.102
  508.8 4.4 collective-permute-done.98
  516.1 10.0 %collective-permute-done.103 = bf16[224,2176]{1,0:T(8,128)(2,1)S(1)} collective-permute-done((bf16[224,2176]{1,0:T(8,128)(2,1)S(1)}, bf16[224,2176]{1,0:T(8,128)(2,1)S(1)}, u32[]{:S(2)}, u32[]{:S(2)}) %collective-permute-start.103) | collective-permute-done | bytes 974880 | tf_op jit(solution)/shard_map/ppermute | solution.py:45
  532.2 4.3 shard_map.290
  537.3 16.2 %collective-permute-done.99 = bf16[2,2,112,1280]{3,2,1,0:T(8,128)(2,1)S(1)} collective-permute-done((bf16[2,2,112,1280]{3,2,1,0:T(8,128)(2,1)S(1)}, bf16[2,2,112,1280]{3,2,1,0:T(8,128)(2,1)S(1)}, u32[]{:S(2)}, u32[]{:S(2)}) %collective-permute-start.99) | collective-permute-done | bytes 1146912 | tf_op jit(solution)/shard_map/ppermute | solution.py:1109
  556.0 5.6 shard_map.291
  561.6 4.2 collective-permute-start.112
  565.9 12.1 %collective-permute-done.101 = bf16[2,2,112,1280]{3,2,1,0:T(8,128)(2,1)S(1)} collective-permute-done((bf16[2,2,112,1280]{3,2,1,0:T(8,128)(2,1)S(1)}, bf16[2,2,112,1280]{3,2,1,0:T(8,128)(2,1)S(1)}, u32[]{:S(2)}, u32[]{:S(2)}) %collective-permute-start.101) | collective-permute-done | bytes 1146912 | tf_op jit(solution)/shard_map/ppermute | solution.py:1109
  578.1 12.3 %shard_map.292 = (bf16[4,2,112,1280]{3,2,1,0:T(8,128)(2,1)S(1)}, bf16[4,2,112,1280]{3,2,1,0:T(8,128)(2,1)S(1)}) custom-call(s32[10]{0:T(128)S(1)} %stack.193.info_ref, bf16[256,896]{1,0:T(8,128)(2,1)S(1)} %copy-done.64, bf16[256,896]{1,0:T(8,128)(2,1)S(1)} %copy-done.92, bf16[256,896]{1,0:T(8,128)(2,1)} %constant_dynamic-update-slice_fusion.5.lower_ref.refs_2_, ...), custom_call_target="tpu_custom_call" | custom-call | flops 7046430720 | bytes 15204392 | tf_op jit(solution)/shard_map/pallas_call | solution.py:143
  595.5 8.6 %shard_map.293 = (bf16[128,896]{1,0:T(8,128)(2,1)S(1)}, bf16[512,256]{1,0:T(8,128)(2,1)S(1)}, bf16[512,256]{1,0:T(8,128)(2,1)S(1)}, f32[128,896]{1,0:T(8,128)S(1...) custom-call(bf16[3,128,896]{2,1,0:T(8,128)(2,1)S(1)} %bitcast.255, bf16[4,3,128,256]{3,2,1,0:T(8,128)(2,1)S(1)} %copy-done.29, ...), custom_call_target="tpu_custom_call" | custom-call | flops 3728736256 | bytes 6067456 | tf_op jit(solution)/shard_map/pallas_call | solution.py:143
  607.3 11.3 %collective-permute-done.113 = bf16[608,896]{1,0:T(8,128)(2,1)S(1)} collective-permute-done((bf16[608,896]{1,0:T(8,128)(2,1)S(1)}, bf16[608,896]{1,0:T(8,128)(2,1)S(1)}, u32[]{:S(2)}, u32[]{:S(2)}) %collective-permute-start.113) | collective-permute-done | bytes 1089568 | tf_op jit(solution)/shard_map/ppermute | solution.py:1109
  628.0 9.5 %collective-permute-done.118 = bf16[2,112,1280]{2,1,0:T(8,128)(2,1)S(1)} collective-permute-done((bf16[2,112,1280]{2,1,0:T(8,128)(2,1)S(1)}, bf16[2,112,1280]{2,1,0:T(8,128)(2,1)S(1)}, u32[]{:S(2)}, u32[]{:S(2)}) %collective-permute-start.118) | collective-permute-done | bytes 573472 | tf_op jit(solution)/shard_map/ppermute | solution.py:76
  640.4 8.7 %shard_map.294 = (bf16[128,896]{1,0:T(8,128)(2,1)S(1)}, bf16[512,256]{1,0:T(8,128)(2,1)S(1)}, bf16[512,256]{1,0:T(8,128)(2,1)S(1)}, f32[128,896]{1,0:T(8,128)S(1...) custom-call(bf16[3,128,896]{2,1,0:T(8,128)(2,1)S(1)} %bitcast.256, bf16[4,3,128,256]{3,2,1,0:T(8,128)(2,1)S(1)} %copy-done.29, ...), custom_call_target="tpu_custom_call" | custom-call | flops 3728736256 | bytes 6067456 | tf_op jit(solution)/shard_map/pallas_call | solution.py:143
  649.0 5.4 collective-permute-start.120
  661.8 4.2 collective-permute-done.121
  676.1 8.7 %shard_map.296 = (bf16[128,896]{1,0:T(8,128)(2,1)S(1)}, bf16[512,256]{1,0:T(8,128)(2,1)S(1)}, bf16[512,256]{1,0:T(8,128)(2,1)S(1)}, f32[128,896]{1,0:T(8,128)S(1...) custom-call(bf16[3,128,896]{2,1,0:T(8,128)(2,1)S(1)} %bitcast.257, bf16[4,3,128,256]{3,2,1,0:T(8,128)(2,1)S(1)} %copy-done.29, ...), custom_call_target="tpu_custom_call" | custom-call | flops 3728736256 | bytes 6067456 | tf_op jit(solution)/shard_map/pallas_call | solution.py:143
  699.4 29.2 %collective-permute-done.129 = bf16[256,256]{1,0:T(8,128)(2,1)S(1)} collective-permute-done((bf16[256,256]{1,0:T(8,128)(2,1)S(1)}, bf16[256,256]{1,0:T(8,128)(2,1)S(1)}, u32[]{:S(2)}, u32[]{:S(2)}) %collective-permute-start.129) | collective-permute-done | bytes 131104 | tf_op jit(solution)/shard_map/ppermute | solution.py:45
  745.5 3.9 shard_map.299
  749.5 4.5 collective-permute-start.134
  766.2 6.3 collective-permute-done.135
  778.1 4.0 collective-permute-done.136
  787.2 5.0 collective-permute-done.137
  793.1 11.0 %collective-permute-done.141 = bf16[2,2,112,1280]{3,2,1,0:T(8,128)(2,1)S(1)} collective-permute-done((bf16[2,2,112,1280]{3,2,1,0:T(8,128)(2,1)S(1)}, bf16[2,2,112,1280]{3,2,1,0:T(8,128)(2,1)S(1)}, u32[]{:S(2)}, u32[]{:S(2)}) %collective-permute-start.141) | collective-permute-done | bytes 1146912 | tf_op jit(solution)/shard_map/ppermute | solution.py:1109
  810.2 10.5 %collective-permute-done.139 = bf16[112,2176]{1,0:T(8,128)(2,1)S(1)} collective-permute-done((bf16[112,2176]{1,0:T(8,128)(2,1)S(1)}, bf16[112,2176]{1,0:T(8,128)(2,1)S(1)}, u32[]{:S(2)}, u32[]{:S(2)}) %collective-permute-start.139) | collective-permute-done | bytes 487456 | tf_op jit(solution)/shard_map/ppermute | solution.py:1109
  827.2 6.3 shard_map.300
  (1026 shorter events, 348.4 us)
Async XLA Ops:
  12.7 97.3 %collective-permute-start.23 = (bf16[1216,896]{1,0:T(8,128)(2,1)}, bf16[1216,896]{1,0:T(8,128)(2,1)}, u32[]{:S(2)}, u32[]{:S(2)}) collective-permute-start(bf16[1216,896]{1,0:T(8,128)(2,1)} %bitcast.282), channel_id=1, source_target_pairs={{0,16},{16,0},{1,17},{17,1},{2,18},{18,2},{3,19},{19,3},{4,20},{20... | collective-permute-start | bytes 6537224 | tf_op jit(solution)/shard_map/ppermute | solution.py:80
  19.0 35.0 %collective-permute-start.8 = (bf16[4,2,112,1216]{3,2,1,0:T(8,128)(2,1)}, bf16[4,2,112,1216]{3,2,1,0:T(8,128)(2,1)}, u32[]{:S(2)}, u32[]{:S(2)}) collective-permute-start(bf16[4,2,112,1216]{3,2,1,0:T(8,128)(2,1)} %get-tuple-element.264), channel_id=1, source_target_pairs={{0,16},{16,0},{1,17},{17,1},{2,18},{18,2},{3,19},{19,3},{4,20},{20... | collective-permute-start | bytes 6537224 | tf_op jit(solution)/shard_map/ppermute | solution.py:80
  57.4 23.5 %collective-permute-start.12 = (bf16[112,2176]{1,0:T(8,128)(2,1)S(1)}, bf16[112,2176]{1,0:T(8,128)(2,1)S(1)}, u32[]{:S(2)}, u32[]{:S(2)}) collective-permute-start(bf16[112,2176]{1,0:T(8,128)(2,1)S(1)} %copy-done.231), channel_id=1, source_target_pairs={{0,1},{1,0},{2,3},{3,2},{16,18},{17,19},{18,16},{19,17},{4,5},{5,4... | collective-permute-start | bytes 1462280 | tf_op jit(solution)/shard_map/ppermute | solution.py:45
  59.3 19.6 %collective-permute-start.6 = (bf16[2,384,256]{2,1,0:T(8,128)(2,1)S(1)}, bf16[2,384,256]{2,1,0:T(8,128)(2,1)S(1)}, u32[]{:S(2)}, u32[]{:S(2)}) collective-permute-start(bf16[2,384,256]{2,1,0:T(8,128)(2,1)S(1)} %pad_maximum_fusion.11), channel_id=1, source_target_pairs={{0,8},{4,12},{8,0},{12,4},{16,24},{20,28},{24,16},{28,20},{1,9},{5... | collective-permute-start | bytes 1179656 | tf_op jit(solution)/shard_map/ppermute | solution.py:45
  62.8 20.7 %collective-permute-start.11 = (bf16[2,112,1216]{2,1,0:T(8,128)(2,1)S(1)}, bf16[2,112,1216]{2,1,0:T(8,128)(2,1)}, u32[]{:S(2)}, u32[]{:S(2)}) collective-permute-start(bf16[2,112,1216]{2,1,0:T(8,128)(2,1)S(1)} %get-tuple-element.587), channel_id=1, source_target_pairs={{0,3},{1,2},{2,1},{3,0},{4,7},{5,6},{6,5},{7,4},{8,11},{9,10},{10,... | collective-permute-start | bytes 1634312 | tf_op jit(solution)/shard_map/ppermute | solution.py:76
  64.9 26.6 %collective-permute-start.10 = (bf16[2,112,1216]{2,1,0:T(8,128)(2,1)}, bf16[2,112,1216]{2,1,0:T(8,128)(2,1)}, u32[]{:S(2)}, u32[]{:S(2)}) collective-permute-start(bf16[2,112,1216]{2,1,0:T(8,128)(2,1)} %get-tuple-element.588), channel_id=1, source_target_pairs={{0,2},{1,3},{2,0},{3,1},{4,6},{5,7},{6,4},{7,5},{8,10},{9,11},{10,... | collective-permute-start | bytes 1634312 | tf_op jit(solution)/shard_map/ppermute | solution.py:76
  83.5 20.9 %collective-permute-start.15 = (bf16[224,2176]{1,0:T(8,128)(2,1)}, bf16[224,2176]{1,0:T(8,128)(2,1)}, u32[]{:S(2)}, u32[]{:S(2)}) collective-permute-start(bf16[224,2176]{1,0:T(8,128)(2,1)} %constant_dynamic-update-slice_fusion.3.refs_0_), channel_id=1, source_target_pairs={{0,2},{1,3},{2,0},{3,1},{16,17},{17,16},{18,19},{19,18},{4,6},{5,7... | collective-permute-start | bytes 2924552 | tf_op jit(solution)/shard_map/ppermute | solution.py:45
  91.6 20.6 %collective-permute-start.19 = (bf16[2,112,1216]{2,1,0:T(8,128)(2,1)S(1)}, bf16[2,112,1216]{2,1,0:T(8,128)(2,1)S(1)}, u32[]{:S(2)}, u32[]{:S(2)}) collective-permute-start(bf16[2,112,1216]{2,1,0:T(8,128)(2,1)S(1)} %get-tuple-element.275.refs_0_), channel_id=1, source_target_pairs={{0,16},{16,0},{1,17},{17,1},{2,18},{18,2},{3,19},{19,3},{4,20},{20... | collective-permute-start | bytes 1634312 | tf_op jit(solution)/shard_map/ppermute | solution.py:80
  92.3 20.1 %collective-permute-start.22 = (bf16[2,112,1216]{2,1,0:T(8,128)(2,1)}, bf16[2,112,1216]{2,1,0:T(8,128)(2,1)S(1)}, u32[]{:S(2)}, u32[]{:S(2)}) collective-permute-start(bf16[2,112,1216]{2,1,0:T(8,128)(2,1)} %collective-permute-done.11.refs_3_), channel_id=1, source_target_pairs={{0,16},{16,0},{1,17},{17,1},{2,18},{18,2},{3,19},{19,3},{4,20},{20... | collective-permute-start | bytes 1634312 | tf_op jit(solution)/shard_map/ppermute | solution.py:80
  110.0 19.0 %collective-permute-start.18 = (bf16[2,112,1216]{2,1,0:T(8,128)(2,1)S(1)}, bf16[2,112,1216]{2,1,0:T(8,128)(2,1)}, u32[]{:S(2)}, u32[]{:S(2)}) collective-permute-start(bf16[2,112,1216]{2,1,0:T(8,128)(2,1)S(1)} %get-tuple-element.583), channel_id=1, source_target_pairs={{0,3},{1,2},{2,1},{3,0},{4,7},{5,6},{6,5},{7,4},{8,11},{9,10},{10,... | collective-permute-start | bytes 1634312 | tf_op jit(solution)/shard_map/ppermute | solution.py:76
  112.2 26.1 %collective-permute-start.17 = (bf16[2,112,1216]{2,1,0:T(8,128)(2,1)S(1)}, bf16[2,112,1216]{2,1,0:T(8,128)(2,1)}, u32[]{:S(2)}, u32[]{:S(2)}) collective-permute-start(bf16[2,112,1216]{2,1,0:T(8,128)(2,1)S(1)} %get-tuple-element.584), channel_id=1, source_target_pairs={{0,2},{1,3},{2,0},{3,1},{4,6},{5,7},{6,4},{7,5},{8,10},{9,11},{10,... | collective-permute-start | bytes 1634312 | tf_op jit(solution)/shard_map/ppermute | solution.py:76
  112.5 27.1 %collective-permute-start.16 = (bf16[2,112,1216]{2,1,0:T(8,128)(2,1)S(1)}, bf16[2,112,1216]{2,1,0:T(8,128)(2,1)}, u32[]{:S(2)}, u32[]{:S(2)}) collective-permute-start(bf16[2,112,1216]{2,1,0:T(8,128)(2,1)S(1)} %get-tuple-element.585), channel_id=1, source_target_pairs={{0,1},{1,0},{2,3},{3,2},{4,5},{5,4},{6,7},{7,6},{8,9},{9,8},{10,11... | collective-permute-start | bytes 1634312 | tf_op jit(solution)/shard_map/ppermute | solution.py:76
  113.1 31.4 %collective-permute-start.14 = (bf16[256,896]{1,0:T(8,128)(2,1)S(1)}, bf16[256,896]{1,0:T(8,128)(2,1)S(1)}, u32[]{:S(2)}, u32[]{:S(2)}) collective-permute-start(bf16[256,896]{1,0:T(8,128)(2,1)S(1)} %constant_dynamic-update-slice_fusion.1.lower_ref.refs_0_), channel_id=1, source_target_pairs={{0,2},{1,3},{2,0},{3,1},{16,17},{17,16},{18,19},{19,18},{4,6},{5,7... | collective-permute-start | bytes 1376264 | tf_op jit(solution)/shard_map/ppermute | solution.py:45
  125.0 38.9 %collective-permute-start.32 = (bf16[224,2176]{1,0:T(8,128)(2,1)}, bf16[224,2176]{1,0:T(8,128)(2,1)S(1)}, u32[]{:S(2)}, u32[]{:S(2)}) collective-permute-start(bf16[224,2176]{1,0:T(8,128)(2,1)} %constant_dynamic-update-slice_fusion.3.refs_0_), channel_id=1, source_target_pairs={{0,16},{16,0},{1,17},{17,1},{2,18},{18,2},{3,19},{19,3},{4,20},{20... | collective-permute-start | bytes 2924552 | tf_op jit(solution)/shard_map/ppermute | solution.py:80
  129.0 34.9 %collective-permute-start.33 = (bf16[224,2176]{1,0:T(8,128)(2,1)}, bf16[224,2176]{1,0:T(8,128)(2,1)S(1)}, u32[]{:S(2)}, u32[]{:S(2)}) collective-permute-start(bf16[224,2176]{1,0:T(8,128)(2,1)} %collective-permute-done.15.refs_1_), channel_id=1, source_target_pairs={{0,16},{16,0},{1,17},{17,1},{2,18},{18,2},{3,19},{19,3},{4,20},{20... | collective-permute-start | bytes 2924552 | tf_op jit(solution)/shard_map/ppermute | solution.py:80
  162.6 31.1 %collective-permute-start.31 = (bf16[256,896]{1,0:T(8,128)(2,1)}, bf16[256,896]{1,0:T(8,128)(2,1)}, u32[]{:S(2)}, u32[]{:S(2)}) collective-permute-start(bf16[256,896]{1,0:T(8,128)(2,1)} %constant_dynamic-update-slice_fusion.7.lower_ref.refs_4_), channel_id=1, source_target_pairs={{0,2},{1,3},{2,0},{3,1},{16,17},{17,16},{18,19},{19,18},{4,6},{5,7... | collective-permute-start | bytes 1376264 | tf_op jit(solution)/shard_map/ppermute | solution.py:45
  243.0 34.1 %collective-permute-start.60 = (bf16[2,3,128,896]{3,2,1,0:T(8,128)(2,1)S(1)}, bf16[2,3,128,896]{3,2,1,0:T(8,128)(2,1)S(1)}, u32[]{:S(2)}, u32[]{:S(2)}) collective-permute-start(bf16[2,3,128,896]{3,2,1,0:T(8,128)(2,1)S(1)} %constant_dynamic-update-slice_fusion.15.lower_ref.refs_3_.refs_5_.refs_7_), channel_id=1, source_target_pairs={{0,2},{1,3},{2,0},{3,1},{16,17},{17,16},{18,19},{19,18},{4,6},{5,7... | collective-permute-start | bytes 4128776 | tf_op jit(solution)/shard_map/ppermute | solution.py:45
  248.9 21.7 %collective-permute-start.52 = (bf16[256,896]{1,0:T(8,128)(2,1)S(1)}, bf16[256,896]{1,0:T(8,128)(2,1)S(1)}, u32[]{:S(2)}, u32[]{:S(2)}) collective-permute-start(bf16[256,896]{1,0:T(8,128)(2,1)S(1)} %constant_dynamic-update-slice_fusion.11.lower_ref.refs_2_), channel_id=1, source_target_pairs={{0,2},{1,3},{2,0},{3,1},{16,17},{17,16},{18,19},{19,18},{4,6},{5,7... | collective-permute-start | bytes 1376264 | tf_op jit(solution)/shard_map/ppermute | solution.py:45
  340.9 26.9 %collective-permute-start.80 = (bf16[4,2,112,1280]{3,2,1,0:T(8,128)(2,1)S(1)}, bf16[4,2,112,1280]{3,2,1,0:T(8,128)(2,1)S(1)}, u32[]{:S(2)}, u32[]{:S(2)}) collective-permute-start(bf16[4,2,112,1280]{3,2,1,0:T(8,128)(2,1)S(1)} %get-tuple-element.387), channel_id=1, source_target_pairs={{0,16},{16,0},{1,17},{17,1},{2,18},{18,2},{3,19},{19,3},{4,20},{20... | collective-permute-start | bytes 6881288 | tf_op jit(solution)/shard_map/ppermute | solution.py:80
  342.1 57.5 %collective-permute-start.50 = (bf16[128,896]{1,0:T(8,128)(2,1)S(1)}, bf16[128,896]{1,0:T(8,128)(2,1)S(1)}, u32[]{:S(2)}, u32[]{:S(2)}) collective-permute-start(bf16[128,896]{1,0:T(8,128)(2,1)S(1)} %slice.628), channel_id=1, source_target_pairs={{0,1},{1,0},{2,3},{3,2},{16,18},{17,19},{18,16},{19,17},{4,5},{5,4... | collective-permute-start | bytes 688136 | tf_op jit(solution)/shard_map/ppermute | solution.py:45
  343.8 19.9 %collective-permute-start.72 = (bf16[608,896]{1,0:T(8,128)(2,1)S(1)}, bf16[608,896]{1,0:T(8,128)(2,1)S(1)}, u32[]{:S(2)}, u32[]{:S(2)}) collective-permute-start(bf16[608,896]{1,0:T(8,128)(2,1)S(1)} %get-tuple-element.379), channel_id=1, source_target_pairs={{0,16},{16,0},{1,17},{17,1},{2,18},{18,2},{3,19},{19,3},{4,20},{20... | collective-permute-start | bytes 3268616 | tf_op jit(solution)/shard_map/ppermute | solution.py:80
  364.0 26.5 %collective-permute-start.73 = (bf16[608,896]{1,0:T(8,128)(2,1)S(1)}, bf16[608,896]{1,0:T(8,128)(2,1)S(1)}, u32[]{:S(2)}, u32[]{:S(2)}) collective-permute-start(bf16[608,896]{1,0:T(8,128)(2,1)S(1)} %add_convert_fusion.15), channel_id=1, source_target_pairs={{0,4},{12,8},{1,5},{13,9},{2,6},{14,10},{3,7},{15,11},{16,20},{28,... | collective-permute-start | bytes 3268616 | tf_op jit(solution)/shard_map/ppermute | solution.py:1109
  368.6 32.0 %collective-permute-start.83 = (bf16[2,112,1280]{2,1,0:T(8,128)(2,1)S(1)}, bf16[2,112,1280]{2,1,0:T(8,128)(2,1)S(1)}, u32[]{:S(2)}, u32[]{:S(2)}) collective-permute-start(bf16[2,112,1280]{2,1,0:T(8,128)(2,1)S(1)} %get-tuple-element.580), channel_id=1, source_target_pairs={{0,3},{1,2},{2,1},{3,0},{4,7},{5,6},{6,5},{7,4},{8,11},{9,10},{10,... | collective-permute-start | bytes 1720328 | tf_op jit(solution)/shard_map/ppermute | solution.py:76
  369.7 30.9 %collective-permute-start.82 = (bf16[2,112,1280]{2,1,0:T(8,128)(2,1)S(1)}, bf16[2,112,1280]{2,1,0:T(8,128)(2,1)S(1)}, u32[]{:S(2)}, u32[]{:S(2)}) collective-permute-start(bf16[2,112,1280]{2,1,0:T(8,128)(2,1)S(1)} %get-tuple-element.581), channel_id=1, source_target_pairs={{0,2},{1,3},{2,0},{3,1},{4,6},{5,7},{6,4},{7,5},{8,10},{9,11},{10,... | collective-permute-start | bytes 1720328 | tf_op jit(solution)/shard_map/ppermute | solution.py:76
  372.0 29.3 %collective-permute-start.81 = (bf16[2,112,1280]{2,1,0:T(8,128)(2,1)S(1)}, bf16[2,112,1280]{2,1,0:T(8,128)(2,1)S(1)}, u32[]{:S(2)}, u32[]{:S(2)}) collective-permute-start(bf16[2,112,1280]{2,1,0:T(8,128)(2,1)S(1)} %get-tuple-element.582), channel_id=1, source_target_pairs={{0,1},{1,0},{2,3},{3,2},{4,5},{5,4},{6,7},{7,6},{8,9},{9,8},{10,11... | collective-permute-start | bytes 1720328 | tf_op jit(solution)/shard_map/ppermute | solution.py:76
  399.0 34.0 %collective-permute-start.56 = (bf16[128,896]{1,0:T(8,128)(2,1)S(1)}, bf16[128,896]{1,0:T(8,128)(2,1)S(1)}, u32[]{:S(2)}, u32[]{:S(2)}) collective-permute-start(bf16[128,896]{1,0:T(8,128)(2,1)S(1)} %slice.627), channel_id=1, source_target_pairs={{0,1},{1,0},{2,3},{3,2},{16,18},{17,19},{18,16},{19,17},{4,5},{5,4... | collective-permute-start | bytes 688136 | tf_op jit(solution)/shard_map/ppermute | solution.py:45
  399.6 68.6 %collective-permute-start.62 = (bf16[128,896]{1,0:T(8,128)(2,1)S(1)}, bf16[128,896]{1,0:T(8,128)(2,1)S(1)}, u32[]{:S(2)}, u32[]{:S(2)}) collective-permute-start(bf16[128,896]{1,0:T(8,128)(2,1)S(1)} %slice.626), channel_id=1, source_target_pairs={{0,1},{1,0},{2,3},{3,2},{16,18},{17,19},{18,16},{19,17},{4,5},{5,4... | collective-permute-start | bytes 688136 | tf_op jit(solution)/shard_map/ppermute | solution.py:45
  401.5 38.4 %collective-permute-start.91 = (bf16[2,2,112,1280]{3,2,1,0:T(8,128)(2,1)S(1)}, bf16[2,2,112,1280]{3,2,1,0:T(8,128)(2,1)S(1)}, u32[]{:S(2)}, u32[]{:S(2)}) collective-permute-start(bf16[2,2,112,1280]{3,2,1,0:T(8,128)(2,1)S(1)} %pad_maximum_fusion.2), channel_id=1, source_target_pairs={{0,4},{12,8},{1,5},{13,9},{2,6},{14,10},{3,7},{15,11},{16,20},{28,... | collective-permute-start | bytes 3440648 | tf_op jit(solution)/shard_map/ppermute | solution.py:1109
  420.2 18.3 %collective-permute-start.86 = (bf16[256,256]{1,0:T(8,128)(2,1)S(1)}, bf16[256,256]{1,0:T(8,128)(2,1)S(1)}, u32[]{:S(2)}, u32[]{:S(2)}) collective-permute-start(bf16[256,256]{1,0:T(8,128)(2,1)S(1)} %slice.635), channel_id=1, source_target_pairs={{0,8},{4,12},{8,0},{12,4},{16,24},{20,28},{24,16},{28,20},{1,9},{5... | collective-permute-start | bytes 393224 | tf_op jit(solution)/shard_map/ppermute | solution.py:45
  433.0 58.8 %collective-permute-start.97 = (bf16[2,2,112,1280]{3,2,1,0:T(8,128)(2,1)}, bf16[2,2,112,1280]{3,2,1,0:T(8,128)(2,1)}, u32[]{:S(2)}, u32[]{:S(2)}) collective-permute-start(bf16[2,2,112,1280]{3,2,1,0:T(8,128)(2,1)} %pad_maximum_fusion.3), channel_id=1, source_target_pairs={{0,4},{12,8},{1,5},{13,9},{2,6},{14,10},{3,7},{15,11},{16,20},{28,... | collective-permute-start | bytes 3440648 | tf_op jit(solution)/shard_map/ppermute | solution.py:1109
  438.5 26.3 %collective-permute-start.90 = (bf16[608,896]{1,0:T(8,128)(2,1)S(1)}, bf16[608,896]{1,0:T(8,128)(2,1)S(1)}, u32[]{:S(2)}, u32[]{:S(2)}) collective-permute-start(bf16[608,896]{1,0:T(8,128)(2,1)S(1)} %add_convert_fusion.13), channel_id=1, source_target_pairs={{4,0},{8,12},{5,1},{9,13},{6,2},{10,14},{7,3},{11,15},{20,16},{24,... | collective-permute-start | bytes 3268616 | tf_op jit(solution)/shard_map/ppermute | solution.py:1109
  439.9 23.7 %collective-permute-start.89 = (bf16[128,256]{1,0:T(8,128)(2,1)S(1)}, bf16[128,256]{1,0:T(8,128)(2,1)S(1)}, u32[]{:S(2)}, u32[]{:S(2)}) collective-permute-start(bf16[128,256]{1,0:T(8,128)(2,1)S(1)} %slice.641), channel_id=1, source_target_pairs={{0,4},{4,0},{8,12},{12,8},{16,20},{20,16},{24,28},{28,24},{1,5},{5... | collective-permute-start | bytes 196616 | tf_op jit(solution)/shard_map/ppermute | solution.py:45
  443.5 48.4 %collective-permute-start.96 = (bf16[2,2,112,1280]{3,2,1,0:T(8,128)(2,1)}, bf16[2,2,112,1280]{3,2,1,0:T(8,128)(2,1)}, u32[]{:S(2)}, u32[]{:S(2)}) collective-permute-start(bf16[2,2,112,1280]{3,2,1,0:T(8,128)(2,1)} %add_convert_fusion.9), channel_id=1, source_target_pairs={{4,8},{8,4},{5,9},{9,5},{6,10},{10,6},{7,11},{11,7},{20,24},{24,20... | collective-permute-start | bytes 3440648 | tf_op jit(solution)/shard_map/ppermute | solution.py:1109
  502.4 28.5 %collective-permute-start.88 = (bf16[128,896]{1,0:T(8,128)(2,1)S(1)}, bf16[128,896]{1,0:T(8,128)(2,1)S(1)}, u32[]{:S(2)}, u32[]{:S(2)}) collective-permute-start(bf16[128,896]{1,0:T(8,128)(2,1)S(1)} %slice.622), channel_id=1, source_target_pairs={{0,1},{1,0},{2,3},{3,2},{16,18},{17,19},{18,16},{19,17},{4,5},{5,4... | collective-permute-start | bytes 688136 | tf_op jit(solution)/shard_map/ppermute | solution.py:45
  504.6 23.1 %collective-permute-start.100 = (bf16[2,2,112,1280]{3,2,1,0:T(8,128)(2,1)S(1)}, bf16[2,2,112,1280]{3,2,1,0:T(8,128)(2,1)S(1)}, u32[]{:S(2)}, u32[]{:S(2)}) collective-permute-start(bf16[2,2,112,1280]{3,2,1,0:T(8,128)(2,1)S(1)} %add_convert_fusion.7), channel_id=1, source_target_pairs={{4,8},{8,4},{5,9},{9,5},{6,10},{10,6},{7,11},{11,7},{20,24},{24,20... | collective-permute-start | bytes 3440648 | tf_op jit(solution)/shard_map/ppermute | solution.py:1109
  507.2 18.9 %collective-permute-start.103 = (bf16[224,2176]{1,0:T(8,128)(2,1)S(1)}, bf16[224,2176]{1,0:T(8,128)(2,1)S(1)}, u32[]{:S(2)}, u32[]{:S(2)}) collective-permute-start(bf16[224,2176]{1,0:T(8,128)(2,1)S(1)} %bitcast.287), channel_id=1, source_target_pairs={{0,2},{1,3},{2,0},{3,1},{16,17},{17,16},{18,19},{19,18},{4,6},{5,7... | collective-permute-start | bytes 2924552 | tf_op jit(solution)/shard_map/ppermute | solution.py:45
  507.8 24.4 %collective-permute-start.94 = (bf16[256,896]{1,0:T(8,128)(2,1)S(1)}, bf16[256,896]{1,0:T(8,128)(2,1)S(1)}, u32[]{:S(2)}, u32[]{:S(2)}) collective-permute-start(bf16[256,896]{1,0:T(8,128)(2,1)S(1)} %constant_dynamic-update-slice_fusion.19.lower_ref.refs_7_), channel_id=1, source_target_pairs={{0,2},{1,3},{2,0},{3,1},{16,17},{17,16},{18,19},{19,18},{4,6},{5,7... | collective-permute-start | bytes 1376264 | tf_op jit(solution)/shard_map/ppermute | solution.py:45
  513.3 52.6 %collective-permute-start.106 = (bf16[128,896]{1,0:T(8,128)(2,1)S(1)}, bf16[128,896]{1,0:T(8,128)(2,1)S(1)}, u32[]{:S(2)}, u32[]{:S(2)}) collective-permute-start(bf16[128,896]{1,0:T(8,128)(2,1)S(1)} %slice.621), channel_id=1, source_target_pairs={{0,1},{1,0},{2,3},{3,2},{16,18},{17,19},{18,16},{19,17},{4,5},{5,4... | collective-permute-start | bytes 688136 | tf_op jit(solution)/shard_map/ppermute | solution.py:45
  526.1 27.4 %collective-permute-start.99 = (bf16[2,2,112,1280]{3,2,1,0:T(8,128)(2,1)S(1)}, bf16[2,2,112,1280]{3,2,1,0:T(8,128)(2,1)S(1)}, u32[]{:S(2)}, u32[]{:S(2)}) collective-permute-start(bf16[2,2,112,1280]{3,2,1,0:T(8,128)(2,1)S(1)} %add_convert_fusion.8), channel_id=1, source_target_pairs={{4,0},{8,12},{5,1},{9,13},{6,2},{10,14},{7,3},{11,15},{20,16},{24,... | collective-permute-start | bytes 3440648 | tf_op jit(solution)/shard_map/ppermute | solution.py:1109
  527.7 26.8 %collective-permute-start.104 = (bf16[112,2176]{1,0:T(8,128)(2,1)S(1)}, bf16[112,2176]{1,0:T(8,128)(2,1)S(1)}, u32[]{:S(2)}, u32[]{:S(2)}) collective-permute-start(bf16[112,2176]{1,0:T(8,128)(2,1)S(1)} %slice.619), channel_id=1, source_target_pairs={{0,1},{1,0},{2,3},{3,2},{16,18},{17,19},{18,16},{19,17},{4,5},{5,4... | collective-permute-start | bytes 1462280 | tf_op jit(solution)/shard_map/ppermute | solution.py:45
  530.9 47.2 %collective-permute-start.101 = (bf16[2,2,112,1280]{3,2,1,0:T(8,128)(2,1)S(1)}, bf16[2,2,112,1280]{3,2,1,0:T(8,128)(2,1)S(1)}, u32[]{:S(2)}, u32[]{:S(2)}) collective-permute-start(bf16[2,2,112,1280]{3,2,1,0:T(8,128)(2,1)S(1)} %add_convert_fusion.6), channel_id=1, source_target_pairs={{4,0},{8,12},{5,1},{9,13},{6,2},{10,14},{7,3},{11,15},{20,16},{24,... | collective-permute-start | bytes 3440648 | tf_op jit(solution)/shard_map/ppermute | solution.py:1109
  536.6 29.3 %collective-permute-start.107 = (bf16[256,896]{1,0:T(8,128)(2,1)S(1)}, bf16[256,896]{1,0:T(8,128)(2,1)S(1)}, u32[]{:S(2)}, u32[]{:S(2)}) collective-permute-start(bf16[256,896]{1,0:T(8,128)(2,1)S(1)} %get-tuple-element.437), channel_id=1, source_target_pairs={{0,2},{1,3},{2,0},{3,1},{16,17},{17,16},{18,19},{19,18},{4,6},{5,7... | collective-permute-start | bytes 1376264 | tf_op jit(solution)/shard_map/ppermute | solution.py:45
  554.6 23.5 %collective-permute-start.105 = (bf16[112,2176]{1,0:T(8,128)(2,1)S(1)}, bf16[112,2176]{1,0:T(8,128)(2,1)S(1)}, u32[]{:S(2)}, u32[]{:S(2)}) collective-permute-start(bf16[112,2176]{1,0:T(8,128)(2,1)S(1)} %fusion.4), channel_id=1, source_target_pairs={{0,4},{12,8},{1,5},{13,9},{2,6},{14,10},{3,7},{15,11},{16,20},{28,... | collective-permute-start | bytes 1462280 | tf_op jit(solution)/shard_map/ppermute | solution.py:1109
  561.6 32.1 %collective-permute-start.112 = (bf16[608,896]{1,0:T(8,128)(2,1)S(1)}, bf16[608,896]{1,0:T(8,128)(2,1)S(1)}, u32[]{:S(2)}, u32[]{:S(2)}) collective-permute-start(bf16[608,896]{1,0:T(8,128)(2,1)S(1)} %get-tuple-element.448), channel_id=1, source_target_pairs={{0,16},{16,0},{1,17},{17,1},{2,18},{18,2},{3,19},{19,3},{4,20},{20... | collective-permute-start | bytes 3268616 | tf_op jit(solution)/shard_map/ppermute | solution.py:80
  590.4 33.9 %collective-permute-start.117 = (bf16[4,2,112,1280]{3,2,1,0:T(8,128)(2,1)S(1)}, bf16[4,2,112,1280]{3,2,1,0:T(8,128)(2,1)S(1)}, u32[]{:S(2)}, u32[]{:S(2)}) collective-permute-start(bf16[4,2,112,1280]{3,2,1,0:T(8,128)(2,1)S(1)} %get-tuple-element.453), channel_id=1, source_target_pairs={{0,16},{16,0},{1,17},{17,1},{2,18},{18,2},{3,19},{19,3},{4,20},{20... | collective-permute-start | bytes 6881288 | tf_op jit(solution)/shard_map/ppermute | solution.py:80
  592.9 31.4 %collective-permute-start.114 = (bf16[128,896]{1,0:T(8,128)(2,1)S(1)}, bf16[128,896]{1,0:T(8,128)(2,1)S(1)}, u32[]{:S(2)}, u32[]{:S(2)}) collective-permute-start(bf16[128,896]{1,0:T(8,128)(2,1)S(1)} %slice.620), channel_id=1, source_target_pairs={{0,1},{1,0},{2,3},{3,2},{16,18},{17,19},{18,16},{19,17},{4,5},{5,4... | collective-permute-start | bytes 688136 | tf_op jit(solution)/shard_map/ppermute | solution.py:45
  594.1 24.4 %collective-permute-start.113 = (bf16[608,896]{1,0:T(8,128)(2,1)S(1)}, bf16[608,896]{1,0:T(8,128)(2,1)S(1)}, u32[]{:S(2)}, u32[]{:S(2)}) collective-permute-start(bf16[608,896]{1,0:T(8,128)(2,1)S(1)} %add_convert_fusion.12), channel_id=1, source_target_pairs={{0,4},{12,8},{1,5},{13,9},{2,6},{14,10},{3,7},{15,11},{16,20},{28,... | collective-permute-start | bytes 3268616 | tf_op jit(solution)/shard_map/ppermute | solution.py:1109
  604.9 19.3 %collective-permute-start.111 = (bf16[112,2176]{1,0:T(8,128)(2,1)S(1)}, bf16[112,2176]{1,0:T(8,128)(2,1)S(1)}, u32[]{:S(2)}, u32[]{:S(2)}) collective-permute-start(bf16[112,2176]{1,0:T(8,128)(2,1)S(1)} %add_convert_fusion.19), channel_id=1, source_target_pairs={{4,8},{8,4},{5,9},{9,5},{6,10},{10,6},{7,11},{11,7},{20,24},{24,20... | collective-permute-start | bytes 1462280 | tf_op jit(solution)/shard_map/ppermute | solution.py:1109
  618.8 30.2 %collective-permute-start.116 = (bf16[608,896]{1,0:T(8,128)(2,1)S(1)}, bf16[608,896]{1,0:T(8,128)(2,1)S(1)}, u32[]{:S(2)}, u32[]{:S(2)}) collective-permute-start(bf16[608,896]{1,0:T(8,128)(2,1)S(1)} %add_convert_fusion.11), channel_id=1, source_target_pairs={{4,8},{8,4},{5,9},{9,5},{6,10},{10,6},{7,11},{11,7},{20,24},{24,20... | collective-permute-start | bytes 3268616 | tf_op jit(solution)/shard_map/ppermute | solution.py:1109
  621.4 47.3 %collective-permute-start.110 = (bf16[128,256]{1,0:T(8,128)(2,1)S(1)}, bf16[128,256]{1,0:T(8,128)(2,1)S(1)}, u32[]{:S(2)}, u32[]{:S(2)}) collective-permute-start(bf16[128,256]{1,0:T(8,128)(2,1)S(1)} %slice.640), channel_id=1, source_target_pairs={{0,4},{4,0},{8,12},{12,8},{16,20},{20,16},{24,28},{28,24},{1,5},{5... | collective-permute-start | bytes 196616 | tf_op jit(solution)/shard_map/ppermute | solution.py:45
  626.4 30.5 %collective-permute-start.125 = (bf16[2,112,1280]{2,1,0:T(8,128)(2,1)S(1)}, bf16[2,112,1280]{2,1,0:T(8,128)(2,1)S(1)}, u32[]{:S(2)}, u32[]{:S(2)}) collective-permute-start(bf16[2,112,1280]{2,1,0:T(8,128)(2,1)S(1)} %get-tuple-element.575), channel_id=1, source_target_pairs={{0,2},{1,3},{2,0},{3,1},{4,6},{5,7},{6,4},{7,5},{8,10},{9,11},{10,... | collective-permute-start | bytes 1720328 | tf_op jit(solution)/shard_map/ppermute | solution.py:76
  627.2 31.1 %collective-permute-start.126 = (bf16[2,112,1280]{2,1,0:T(8,128)(2,1)S(1)}, bf16[2,112,1280]{2,1,0:T(8,128)(2,1)S(1)}, u32[]{:S(2)}, u32[]{:S(2)}) collective-permute-start(bf16[2,112,1280]{2,1,0:T(8,128)(2,1)S(1)} %get-tuple-element.576), channel_id=1, source_target_pairs={{0,3},{1,2},{2,1},{3,0},{4,7},{5,6},{6,5},{7,4},{8,11},{9,10},{10,... | collective-permute-start | bytes 1720328 | tf_op jit(solution)/shard_map/ppermute | solution.py:76
  637.6 35.0 %collective-permute-start.119 = (bf16[2,2,112,1280]{3,2,1,0:T(8,128)(2,1)S(1)}, bf16[2,2,112,1280]{3,2,1,0:T(8,128)(2,1)S(1)}, u32[]{:S(2)}, u32[]{:S(2)}) collective-permute-start(bf16[2,2,112,1280]{3,2,1,0:T(8,128)(2,1)S(1)} %pad_maximum_fusion.4), channel_id=1, source_target_pairs={{0,4},{12,8},{1,5},{13,9},{2,6},{14,10},{3,7},{15,11},{16,20},{28,... | collective-permute-start | bytes 3440648 | tf_op jit(solution)/shard_map/ppermute | solution.py:1109
  657.0 71.8 %collective-permute-start.123 = (bf16[608,896]{1,0:T(8,128)(2,1)S(1)}, bf16[608,896]{1,0:T(8,128)(2,1)S(1)}, u32[]{:S(2)}, u32[]{:S(2)}) collective-permute-start(bf16[608,896]{1,0:T(8,128)(2,1)S(1)} %add_convert_fusion.10), channel_id=1, source_target_pairs={{4,0},{8,12},{5,1},{9,13},{6,2},{10,14},{7,3},{11,15},{20,16},{24,... | collective-permute-start | bytes 3268616 | tf_op jit(solution)/shard_map/ppermute | solution.py:1109
  666.0 23.6 %collective-permute-start.127 = (bf16[2,2,112,1280]{3,2,1,0:T(8,128)(2,1)S(1)}, bf16[2,2,112,1280]{3,2,1,0:T(8,128)(2,1)S(1)}, u32[]{:S(2)}, u32[]{:S(2)}) collective-permute-start(bf16[2,2,112,1280]{3,2,1,0:T(8,128)(2,1)S(1)} %pad_maximum_fusion.5), channel_id=1, source_target_pairs={{0,4},{12,8},{1,5},{13,9},{2,6},{14,10},{3,7},{15,11},{16,20},{28,... | collective-permute-start | bytes 3440648 | tf_op jit(solution)/shard_map/ppermute | solution.py:1109
  668.8 59.9 %collective-permute-start.122 = (bf16[128,256]{1,0:T(8,128)(2,1)S(1)}, bf16[128,256]{1,0:T(8,128)(2,1)S(1)}, u32[]{:S(2)}, u32[]{:S(2)}) collective-permute-start(bf16[128,256]{1,0:T(8,128)(2,1)S(1)} %slice.639), channel_id=1, source_target_pairs={{0,4},{4,0},{8,12},{12,8},{16,20},{20,16},{24,28},{28,24},{1,5},{5... | collective-permute-start | bytes 196616 | tf_op jit(solution)/shard_map/ppermute | solution.py:45
  673.4 23.3 %collective-permute-start.124 = (bf16[2,2,112,1280]{3,2,1,0:T(8,128)(2,1)S(1)}, bf16[2,2,112,1280]{3,2,1,0:T(8,128)(2,1)S(1)}, u32[]{:S(2)}, u32[]{:S(2)}) collective-permute-start(bf16[2,2,112,1280]{3,2,1,0:T(8,128)(2,1)S(1)} %add_convert_fusion.5), channel_id=1, source_target_pairs={{4,8},{8,4},{5,9},{9,5},{6,10},{10,6},{7,11},{11,7},{20,24},{24,20... | collective-permute-start | bytes 3440648 | tf_op jit(solution)/shard_map/ppermute | solution.py:1109
  691.1 44.8 %collective-permute-start.133 = (bf16[2,2,112,1280]{3,2,1,0:T(8,128)(2,1)}, bf16[2,2,112,1280]{3,2,1,0:T(8,128)(2,1)}, u32[]{:S(2)}, u32[]{:S(2)}) collective-permute-start(bf16[2,2,112,1280]{3,2,1,0:T(8,128)(2,1)} %add_convert_fusion.3), channel_id=1, source_target_pairs={{4,8},{8,4},{5,9},{9,5},{6,10},{10,6},{7,11},{11,7},{20,24},{24,20... | collective-permute-start | bytes 3440648 | tf_op jit(solution)/shard_map/ppermute | solution.py:1109
  692.8 35.7 %collective-permute-start.129 = (bf16[256,256]{1,0:T(8,128)(2,1)S(1)}, bf16[256,256]{1,0:T(8,128)(2,1)S(1)}, u32[]{:S(2)}, u32[]{:S(2)}) collective-permute-start(bf16[256,256]{1,0:T(8,128)(2,1)S(1)} %slice.632), channel_id=1, source_target_pairs={{0,8},{4,12},{8,0},{12,4},{16,24},{20,28},{24,16},{28,20},{1,9},{5... | collective-permute-start | bytes 393224 | tf_op jit(solution)/shard_map/ppermute | solution.py:45
  698.1 37.8 %collective-permute-start.132 = (bf16[2,2,112,1280]{3,2,1,0:T(8,128)(2,1)}, bf16[2,2,112,1280]{3,2,1,0:T(8,128)(2,1)}, u32[]{:S(2)}, u32[]{:S(2)}) collective-permute-start(bf16[2,2,112,1280]{3,2,1,0:T(8,128)(2,1)} %add_convert_fusion.4), channel_id=1, source_target_pairs={{4,0},{8,12},{5,1},{9,13},{6,2},{10,14},{7,3},{11,15},{20,16},{24,... | collective-permute-start | bytes 3440648 | tf_op jit(solution)/shard_map/ppermute | solution.py:1109
  776.7 27.4 %collective-permute-start.141 = (bf16[2,2,112,1280]{3,2,1,0:T(8,128)(2,1)S(1)}, bf16[2,2,112,1280]{3,2,1,0:T(8,128)(2,1)S(1)}, u32[]{:S(2)}, u32[]{:S(2)}) collective-permute-start(bf16[2,2,112,1280]{3,2,1,0:T(8,128)(2,1)S(1)} %add_convert_fusion.2), channel_id=1, source_target_pairs={{4,0},{8,12},{5,1},{9,13},{6,2},{10,14},{7,3},{11,15},{20,16},{24,... | collective-permute-start | bytes 3440648 | tf_op jit(solution)/shard_map/ppermute | solution.py:1109
  784.4 38.4 %collective-permute-start.144 = (bf16[608,896]{1,0:T(8,128)(2,1)S(1)}, bf16[608,896]{1,0:T(8,128)(2,1)S(1)}, u32[]{:S(2)}, u32[]{:S(2)}) collective-permute-start(bf16[608,896]{1,0:T(8,128)(2,1)S(1)} %get-tuple-element.572), channel_id=1, source_target_pairs={{0,16},{16,0},{1,17},{17,1},{2,18},{18,2},{3,19},{19,3},{4,20},{20... | collective-permute-start | bytes 3268616 | tf_op jit(solution)/shard_map/ppermute | solution.py:80
  787.1 38.3 %collective-permute-start.131 = (f32[3,128,896]{2,1,0:T(8,128)S(1)}, f32[3,128,896]{2,1,0:T(8,128)S(1)}, u32[]{:S(2)}, u32[]{:S(2)}) collective-permute-start(f32[3,128,896]{2,1,0:T(8,128)S(1)} %get-tuple-element.598), channel_id=1, source_target_pairs={{0,16},{16,0},{1,17},{17,1},{2,18},{18,2},{3,19},{19,3},{4,20},{20... | collective-permute-start | bytes 4128776 | tf_op jit(solution)/shard_map/ppermute | solution.py:80
  804.4 22.8 %collective-permute-start.143 = (bf16[2,2,112,1280]{3,2,1,0:T(8,128)(2,1)S(1)}, bf16[2,2,112,1280]{3,2,1,0:T(8,128)(2,1)S(1)}, u32[]{:S(2)}, u32[]{:S(2)}) collective-permute-start(bf16[2,2,112,1280]{3,2,1,0:T(8,128)(2,1)S(1)} %get-tuple-element.565), channel_id=1, source_target_pairs={{0,16},{16,0},{1,17},{17,1},{2,18},{18,2},{3,19},{19,3},{4,20},{20... | collective-permute-start | bytes 3440648 | tf_op jit(solution)/shard_map/ppermute | solution.py:80
  (342 other events, 3690.0 us)

commit v5 on v4

--- a/solution.py
+++ b/solution.py
@@ -1259,8 +1259,8 @@
 order = (
     "a00", "a01", "f00", "a02", "f01", "q0", "f02", "q1", "a10", "q2", "a11", "c", "f10", "a12", "f11", "d10",
     "f12", "d11", "b10", "d12", "D1", "zd1", "G1", "b11", "z", "k10", "b12", "zl1", "k11", "d00", "zh1",
-    "k12", "d01", "z", "P1", "d02", "za1", "D0", "zd0", "G0", "b00", "zl0", "b01", "zh0", "k00", "b02", "z",
-    "k01", "k02", "z", "P0", "za0",
+    "k12", "d01", "z", "P1", "d02", "D0", "zd0a1", "G0", "b00", "zl0", "b01", "zh0", "k00", "b02", "z", "k01",
+    "k02", "z", "P0", "za0",
 )
 
 

time: 850 us -> 870 us (1.024)
  waiting for transfers between devices: 287 us -> 312 us
    ppermute x72, waiting for transfers between devices: 165 us -> 203 us  [step(): return lax.ppermute(block, ('section', axis), route)]
    ppermute x37, starting transfers between devices: 65.7 us -> 53.8 us  [other(): return lax.ppermute(block, 'section', [(0, 1), (1, 0)])]
    ppermute x12, waiting for transfers between devices: 22.9 us -> 13.3 us  [direct(): return lax.ppermute(block, axis, [(i, i ^ mask) for i in range(size)])]
    unnamed x532 -> x546, local copies, waits for them, and re-layouts: 57.7 us -> 60.6 us
  transfers between devices with their start and end apart: 145 -> 145, of which waited for: 49 -> 48; matrix products, arithmetic and copies ran while one was open for 8% -> 7% of each run, Pallas kernels for 23% -> 20%
where the time goes in v5:
time: 870 us; the launch traced here: 858 us
  waiting for transfers between devices  312 us (36%)
  Pallas kernels  213 us (24%)
  starting transfers between devices  196 us (23%)
  local copies, waits for them, and re-layouts  82.7 us (10%)
  other arithmetic  48.1 us (6%)
    pallas_call x47, Pallas kernels, call(): pl.pallas_call(kernel, out_shape=outs, grid=grid or (), in_specs=specs, o...  213 us
    ppermute x72, waiting for transfers between devices, step(): return lax.ppermute(block, ('section', axis), route)  203 us
    ppermute x24, waiting for transfers between devices, ctx_steps(): got = lax.ppermute(value, 'ctx', route)  88.9 us
    ppermute x72, starting transfers between devices, step(): return lax.ppermute(block, ('section', axis), route)  88.3 us
    unnamed x546, local copies, waits for them, and re-layouts  60.6 us
    ppermute x37, starting transfers between devices, other(): return lax.ppermute(block, 'section', [(0, 1), (1, 0)])  53.8 us
    ppermute x24, starting transfers between devices, ctx_steps(): got = lax.ppermute(value, 'ctx', route)  42.1 us
  transfers between devices with their start and end apart: 145, of which 48 were waited for; matrix products, arithmetic and copies ran while one was open for 7% of the time, Pallas kernels for 20%

profile of v5, /device:TPU:1, one launch (start us, length us, event | category | flops | bytes accessed | tf_op | source)
XLA Modules:
  0.0 857.6 jit_solution(14527648320354455387)
XLA Ops:
  23.5 8.9 %collective-permute-done.2.refs_1_ = bf16[224,2176]{1,0:T(8,128)(2,1)S(1)} collective-permute-done((bf16[224,2176]{1,0:T(8,128)(2,1)S(1)}, bf16[224,2176]{1,0:T(8,128)(2,1)S(1)}, u32[]{:S(2)}, u32[]{:S(2)}) %collective-permute-start.2) | collective-permute-done | bytes 974880 | tf_op jit(solution)/shard_map/ppermute | solution.py:45
  66.0 12.9 %collective-permute-done.6 = bf16[2,384,256]{2,1,0:T(8,128)(2,1)S(1)} collective-permute-done((bf16[2,384,256]{2,1,0:T(8,128)(2,1)S(1)}, bf16[2,384,256]{2,1,0:T(8,128)(2,1)S(1)}, u32[]{:S(2)}, u32[]{:S(2)}) %collective-permute-start.6) | collective-permute-done | bytes 393248 | tf_op jit(solution)/shard_map/ppermute | solution.py:45
  86.2 5.5 collective-permute-done.10.refs_2_
  92.4 4.1 collective-permute-start.22
  96.7 6.7 shard_map.258
  117.7 6.5 shard_map.259
  130.8 7.5 collective-permute-done.17.refs_2_
  139.5 5.0 collective-permute-done.14.upper_ref.refs_1_
  144.5 5.1 shard_map.261
  149.7 6.9 shard_map.262
  169.1 3.9 collective-permute-done.24
  178.9 5.6 shard_map.263
  193.7 5.6 shard_map.266
  208.9 5.6 shard_map.268
  219.5 3.8 collective-permute-start.43
  224.9 5.6 shard_map.270
  249.7 4.4 shard_map.272
  254.1 5.6 shard_map.273
  260.6 10.0 %collective-permute-done.52.upper_ref.refs_3_ = bf16[256,896]{1,0:T(8,128)(2,1)S(1)} collective-permute-done((bf16[256,896]{1,0:T(8,128)(2,1)S(1)}, bf16[256,896]{1,0:T(8,128)(2,1)S(1)}, u32[]{:S(2)}, u32[]{:S(2)}) %collective-permute-start.52) | collective-permute-done | bytes 458784 | tf_op jit(solution)/shard_map/ppermute | solution.py:45
  271.5 4.6 shard_map.274
  277.1 4.4 shard_map.275
  283.1 4.4 shard_map.276
  291.5 4.5 shard_map.277
  297.7 7.9 shard_map.278
  308.2 4.5 shard_map.279
  315.1 7.2 collective-permute-done.67
  322.4 5.2 shard_map.280
  329.8 10.9 %shard_map.281 = (bf16[4,2,112,1280]{3,2,1,0:T(8,128)(2,1)S(1)}, bf16[4,2,112,1280]{3,2,1,0:T(8,128)(2,1)S(1)}) custom-call(s32[10]{0:T(128)S(1)} %stack.193.info_ref, bf16[256,896]{1,0:T(8,128)(2,1)S(1)} %constant_dynamic-update-slice_fusion.9.lower_ref.refs_0_, bf16[256,896]{1,0:T(8,128)(2,1)S(1)} %collective-permute-done.40.upper_ref.refs_1_, ...), custom_call_target="tpu_custom_call" | custom-call | flops 7046430720 | bytes 15204392 | tf_op jit(solution)/shard_map/pallas_call | solution.py:143
  344.5 8.0 collective-permute-done.61
  354.2 7.7 shard_map.282
  372.6 18.0 %collective-permute-done.73 = bf16[608,896]{1,0:T(8,128)(2,1)S(1)} collective-permute-done((bf16[608,896]{1,0:T(8,128)(2,1)S(1)}, bf16[608,896]{1,0:T(8,128)(2,1)S(1)}, u32[]{:S(2)}, u32[]{:S(2)}) %collective-permute-start.73) | collective-permute-done | bytes 1089568 | tf_op jit(solution)/shard_map/ppermute | solution.py:1109
  392.3 6.6 collective-permute-done.75
  401.4 5.9 collective-permute-start.91
  408.5 7.7 shard_map.284
  420.2 10.7 %collective-permute-start.86 = (bf16[256,256]{1,0:T(8,128)(2,1)S(1)}, bf16[256,256]{1,0:T(8,128)(2,1)S(1)}, u32[]{:S(2)}, u32[]{:S(2)}) collective-permute-start(bf16[256,256]{1,0:T(8,128)(2,1)S(1)} %slice.635), channel_id=1, source_target_pairs={{0,8},{4,12},{8,0},{12,4},{16,24},{20,28},{24,16},{28,20},{1,9},{5... | collective-permute-start | bytes 393224 | tf_op jit(solution)/shard_map/ppermute | solution.py:45
  433.0 5.4 collective-permute-start.97
  445.6 4.5 shard_map.286
  450.2 13.4 %collective-permute-done.89.got_ref = bf16[128,256]{1,0:T(8,128)(2,1)S(1)} collective-permute-done((bf16[128,256]{1,0:T(8,128)(2,1)S(1)}, bf16[128,256]{1,0:T(8,128)(2,1)S(1)}, u32[]{:S(2)}, u32[]{:S(2)}) %collective-permute-start.89) | collective-permute-done | bytes 65568 | tf_op jit(solution)/shard_map/ppermute | solution.py:45
  468.3 8.2 collective-permute-done.87
  486.2 5.7 shard_map.288
  495.8 6.4 collective-permute-start.99
  518.2 4.3 shard_map.290
  524.4 4.3 collective-permute-done.100
  529.8 5.6 shard_map.291
  535.9 4.9 collective-permute-done.101
  541.9 12.0 %shard_map.292 = (bf16[4,2,112,1280]{3,2,1,0:T(8,128)(2,1)S(1)}, bf16[4,2,112,1280]{3,2,1,0:T(8,128)(2,1)S(1)}) custom-call(s32[10]{0:T(128)S(1)} %stack.193.info_ref, bf16[256,896]{1,0:T(8,128)(2,1)S(1)} %copy-done.64, bf16[256,896]{1,0:T(8,128)(2,1)S(1)} %copy-done.92, bf16[256,896]{1,0:T(8,128)(2,1)} %constant_dynamic-update-slice_fusion.5.lower_ref.refs_2_, ...), custom_call_target="tpu_custom_call" | custom-call | flops 7046430720 | bytes 15204392 | tf_op jit(solution)/shard_map/pallas_call | solution.py:143
  554.1 8.8 %shard_map.293 = (bf16[128,896]{1,0:T(8,128)(2,1)S(1)}, bf16[512,256]{1,0:T(8,128)(2,1)S(1)}, bf16[512,256]{1,0:T(8,128)(2,1)S(1)}, f32[128,896]{1,0:T(8,128)S(1...) custom-call(bf16[3,128,896]{2,1,0:T(8,128)(2,1)S(1)} %bitcast.255, bf16[4,3,128,256]{3,2,1,0:T(8,128)(2,1)S(1)} %copy-done.29, ...), custom_call_target="tpu_custom_call" | custom-call | flops 3728736256 | bytes 6067456 | tf_op jit(solution)/shard_map/pallas_call | solution.py:143
  580.3 5.8 collective-permute-done.112
  587.0 13.0 %collective-permute-done.108 = bf16[2,2,112,1280]{3,2,1,0:T(8,128)(2,1)S(1)} collective-permute-done((bf16[2,2,112,1280]{3,2,1,0:T(8,128)(2,1)S(1)}, bf16[2,2,112,1280]{3,2,1,0:T(8,128)(2,1)S(1)}, u32[]{:S(2)}, u32[]{:S(2)}) %collective-permute-start.108) | collective-permute-done | bytes 1146912 | tf_op jit(solution)/shard_map/ppermute | solution.py:1109
  600.0 9.5 %collective-permute-done.110 = bf16[608,896]{1,0:T(8,128)(2,1)S(1)} collective-permute-done((bf16[608,896]{1,0:T(8,128)(2,1)S(1)}, bf16[608,896]{1,0:T(8,128)(2,1)S(1)}, u32[]{:S(2)}, u32[]{:S(2)}) %collective-permute-start.110) | collective-permute-done | bytes 1089568 | tf_op jit(solution)/shard_map/ppermute | solution.py:1109
  611.3 8.6 %shard_map.294 = (bf16[128,896]{1,0:T(8,128)(2,1)S(1)}, bf16[512,256]{1,0:T(8,128)(2,1)S(1)}, bf16[512,256]{1,0:T(8,128)(2,1)S(1)}, f32[128,896]{1,0:T(8,128)S(1...) custom-call(bf16[3,128,896]{2,1,0:T(8,128)(2,1)S(1)} %bitcast.256, bf16[4,3,128,256]{3,2,1,0:T(8,128)(2,1)S(1)} %copy-done.29, ...), custom_call_target="tpu_custom_call" | custom-call | flops 3728736256 | bytes 6067456 | tf_op jit(solution)/shard_map/pallas_call | solution.py:143
  624.3 4.6 collective-permute-start.120
  630.6 25.6 %collective-permute-done.120 = bf16[256,256]{1,0:T(8,128)(2,1)S(1)} collective-permute-done((bf16[256,256]{1,0:T(8,128)(2,1)S(1)}, bf16[256,256]{1,0:T(8,128)(2,1)S(1)}, u32[]{:S(2)}, u32[]{:S(2)}) %collective-permute-start.120) | collective-permute-done | bytes 131104 | tf_op jit(solution)/shard_map/ppermute | solution.py:45
  666.6 8.8 %shard_map.296 = (bf16[128,896]{1,0:T(8,128)(2,1)S(1)}, bf16[512,256]{1,0:T(8,128)(2,1)S(1)}, bf16[512,256]{1,0:T(8,128)(2,1)S(1)}, f32[128,896]{1,0:T(8,128)S(1...) custom-call(bf16[3,128,896]{2,1,0:T(8,128)(2,1)S(1)} %bitcast.257, bf16[4,3,128,256]{3,2,1,0:T(8,128)(2,1)S(1)} %copy-done.29, ...), custom_call_target="tpu_custom_call" | custom-call | flops 3728736256 | bytes 6067456 | tf_op jit(solution)/shard_map/pallas_call | solution.py:143
  675.4 10.5 %collective-permute-done.127 = bf16[2,2,112,1280]{3,2,1,0:T(8,128)(2,1)S(1)} collective-permute-done((bf16[2,2,112,1280]{3,2,1,0:T(8,128)(2,1)S(1)}, bf16[2,2,112,1280]{3,2,1,0:T(8,128)(2,1)S(1)}, u32[]{:S(2)}, u32[]{:S(2)}) %collective-permute-start.127) | collective-permute-done | bytes 1146912 | tf_op jit(solution)/shard_map/ppermute | solution.py:1109
  696.0 29.4 %collective-permute-done.129 = bf16[256,256]{1,0:T(8,128)(2,1)S(1)} collective-permute-done((bf16[256,256]{1,0:T(8,128)(2,1)S(1)}, bf16[256,256]{1,0:T(8,128)(2,1)S(1)}, u32[]{:S(2)}, u32[]{:S(2)}) %collective-permute-start.129) | collective-permute-done | bytes 131104 | tf_op jit(solution)/shard_map/ppermute | solution.py:45
  731.6 23.1 %collective-permute-done.130.got_ref = bf16[128,256]{1,0:T(8,128)(2,1)S(1)} collective-permute-done((bf16[128,256]{1,0:T(8,128)(2,1)S(1)}, bf16[128,256]{1,0:T(8,128)(2,1)S(1)}, u32[]{:S(2)}, u32[]{:S(2)}) %collective-permute-start.130) | collective-permute-done | bytes 65568 | tf_op jit(solution)/shard_map/ppermute | solution.py:45
  767.9 3.9 shard_map.299
  786.1 6.2 collective-permute-done.135
  798.0 3.9 collective-permute-done.136
  806.6 5.3 collective-permute-done.137
  812.7 11.0 %collective-permute-done.141 = bf16[2,2,112,1280]{3,2,1,0:T(8,128)(2,1)S(1)} collective-permute-done((bf16[2,2,112,1280]{3,2,1,0:T(8,128)(2,1)S(1)}, bf16[2,2,112,1280]{3,2,1,0:T(8,128)(2,1)S(1)}, u32[]{:S(2)}, u32[]{:S(2)}) %collective-permute-start.141) | collective-permute-done | bytes 1146912 | tf_op jit(solution)/shard_map/ppermute | solution.py:1109
  830.2 10.8 %collective-permute-done.139 = bf16[112,2176]{1,0:T(8,128)(2,1)S(1)} collective-permute-done((bf16[112,2176]{1,0:T(8,128)(2,1)S(1)}, bf16[112,2176]{1,0:T(8,128)(2,1)S(1)}, u32[]{:S(2)}, u32[]{:S(2)}) %collective-permute-start.139) | collective-permute-done | bytes 487456 | tf_op jit(solution)/shard_map/ppermute | solution.py:1109
  847.2 6.3 shard_map.300
  (1041 shorter events, 344.5 us)
Async XLA Ops:
  12.7 97.4 %collective-permute-start.23 = (bf16[1216,896]{1,0:T(8,128)(2,1)}, bf16[1216,896]{1,0:T(8,128)(2,1)}, u32[]{:S(2)}, u32[]{:S(2)}) collective-permute-start(bf16[1216,896]{1,0:T(8,128)(2,1)} %bitcast.282), channel_id=1, source_target_pairs={{0,16},{16,0},{1,17},{17,1},{2,18},{18,2},{3,19},{19,3},{4,20},{20... | collective-permute-start | bytes 6537224 | tf_op jit(solution)/shard_map/ppermute | solution.py:80
  19.0 35.0 %collective-permute-start.8 = (bf16[4,2,112,1216]{3,2,1,0:T(8,128)(2,1)}, bf16[4,2,112,1216]{3,2,1,0:T(8,128)(2,1)}, u32[]{:S(2)}, u32[]{:S(2)}) collective-permute-start(bf16[4,2,112,1216]{3,2,1,0:T(8,128)(2,1)} %get-tuple-element.264), channel_id=1, source_target_pairs={{0,16},{16,0},{1,17},{17,1},{2,18},{18,2},{3,19},{19,3},{4,20},{20... | collective-permute-start | bytes 6537224 | tf_op jit(solution)/shard_map/ppermute | solution.py:80
  57.4 23.5 %collective-permute-start.12 = (bf16[112,2176]{1,0:T(8,128)(2,1)S(1)}, bf16[112,2176]{1,0:T(8,128)(2,1)S(1)}, u32[]{:S(2)}, u32[]{:S(2)}) collective-permute-start(bf16[112,2176]{1,0:T(8,128)(2,1)S(1)} %copy-done.232), channel_id=1, source_target_pairs={{0,1},{1,0},{2,3},{3,2},{16,18},{17,19},{18,16},{19,17},{4,5},{5,4... | collective-permute-start | bytes 1462280 | tf_op jit(solution)/shard_map/ppermute | solution.py:45
  59.3 19.6 %collective-permute-start.6 = (bf16[2,384,256]{2,1,0:T(8,128)(2,1)S(1)}, bf16[2,384,256]{2,1,0:T(8,128)(2,1)S(1)}, u32[]{:S(2)}, u32[]{:S(2)}) collective-permute-start(bf16[2,384,256]{2,1,0:T(8,128)(2,1)S(1)} %pad_maximum_fusion.11), channel_id=1, source_target_pairs={{0,8},{4,12},{8,0},{12,4},{16,24},{20,28},{24,16},{28,20},{1,9},{5... | collective-permute-start | bytes 1179656 | tf_op jit(solution)/shard_map/ppermute | solution.py:45
  62.8 20.7 %collective-permute-start.11 = (bf16[2,112,1216]{2,1,0:T(8,128)(2,1)S(1)}, bf16[2,112,1216]{2,1,0:T(8,128)(2,1)}, u32[]{:S(2)}, u32[]{:S(2)}) collective-permute-start(bf16[2,112,1216]{2,1,0:T(8,128)(2,1)S(1)} %get-tuple-element.587), channel_id=1, source_target_pairs={{0,3},{1,2},{2,1},{3,0},{4,7},{5,6},{6,5},{7,4},{8,11},{9,10},{10,... | collective-permute-start | bytes 1634312 | tf_op jit(solution)/shard_map/ppermute | solution.py:76
  65.0 26.6 %collective-permute-start.10 = (bf16[2,112,1216]{2,1,0:T(8,128)(2,1)}, bf16[2,112,1216]{2,1,0:T(8,128)(2,1)}, u32[]{:S(2)}, u32[]{:S(2)}) collective-permute-start(bf16[2,112,1216]{2,1,0:T(8,128)(2,1)} %get-tuple-element.588), channel_id=1, source_target_pairs={{0,2},{1,3},{2,0},{3,1},{4,6},{5,7},{6,4},{7,5},{8,10},{9,11},{10,... | collective-permute-start | bytes 1634312 | tf_op jit(solution)/shard_map/ppermute | solution.py:76
  83.5 20.9 %collective-permute-start.15 = (bf16[224,2176]{1,0:T(8,128)(2,1)}, bf16[224,2176]{1,0:T(8,128)(2,1)}, u32[]{:S(2)}, u32[]{:S(2)}) collective-permute-start(bf16[224,2176]{1,0:T(8,128)(2,1)} %constant_dynamic-update-slice_fusion.3.refs_0_), channel_id=1, source_target_pairs={{0,2},{1,3},{2,0},{3,1},{16,17},{17,16},{18,19},{19,18},{4,6},{5,7... | collective-permute-start | bytes 2924552 | tf_op jit(solution)/shard_map/ppermute | solution.py:45
  91.6 20.6 %collective-permute-start.19 = (bf16[2,112,1216]{2,1,0:T(8,128)(2,1)S(1)}, bf16[2,112,1216]{2,1,0:T(8,128)(2,1)S(1)}, u32[]{:S(2)}, u32[]{:S(2)}) collective-permute-start(bf16[2,112,1216]{2,1,0:T(8,128)(2,1)S(1)} %get-tuple-element.275.refs_0_), channel_id=1, source_target_pairs={{0,16},{16,0},{1,17},{17,1},{2,18},{18,2},{3,19},{19,3},{4,20},{20... | collective-permute-start | bytes 1634312 | tf_op jit(solution)/shard_map/ppermute | solution.py:80
  92.4 20.1 %collective-permute-start.22 = (bf16[2,112,1216]{2,1,0:T(8,128)(2,1)}, bf16[2,112,1216]{2,1,0:T(8,128)(2,1)S(1)}, u32[]{:S(2)}, u32[]{:S(2)}) collective-permute-start(bf16[2,112,1216]{2,1,0:T(8,128)(2,1)} %collective-permute-done.11.refs_3_), channel_id=1, source_target_pairs={{0,16},{16,0},{1,17},{17,1},{2,18},{18,2},{3,19},{19,3},{4,20},{20... | collective-permute-start | bytes 1634312 | tf_op jit(solution)/shard_map/ppermute | solution.py:80
  96.6 16.5 %collective-permute-start.21 = (bf16[2,112,1216]{2,1,0:T(8,128)(2,1)}, bf16[2,112,1216]{2,1,0:T(8,128)(2,1)S(1)}, u32[]{:S(2)}, u32[]{:S(2)}) collective-permute-start(bf16[2,112,1216]{2,1,0:T(8,128)(2,1)} %collective-permute-done.10.refs_2_), channel_id=1, source_target_pairs={{0,16},{16,0},{1,17},{17,1},{2,18},{18,2},{3,19},{19,3},{4,20},{20... | collective-permute-start | bytes 1634312 | tf_op jit(solution)/shard_map/ppermute | solution.py:80
  110.0 19.0 %collective-permute-start.18 = (bf16[2,112,1216]{2,1,0:T(8,128)(2,1)S(1)}, bf16[2,112,1216]{2,1,0:T(8,128)(2,1)}, u32[]{:S(2)}, u32[]{:S(2)}) collective-permute-start(bf16[2,112,1216]{2,1,0:T(8,128)(2,1)S(1)} %get-tuple-element.583), channel_id=1, source_target_pairs={{0,3},{1,2},{2,1},{3,0},{4,7},{5,6},{6,5},{7,4},{8,11},{9,10},{10,... | collective-permute-start | bytes 1634312 | tf_op jit(solution)/shard_map/ppermute | solution.py:76
  112.2 26.1 %collective-permute-start.17 = (bf16[2,112,1216]{2,1,0:T(8,128)(2,1)S(1)}, bf16[2,112,1216]{2,1,0:T(8,128)(2,1)}, u32[]{:S(2)}, u32[]{:S(2)}) collective-permute-start(bf16[2,112,1216]{2,1,0:T(8,128)(2,1)S(1)} %get-tuple-element.584), channel_id=1, source_target_pairs={{0,2},{1,3},{2,0},{3,1},{4,6},{5,7},{6,4},{7,5},{8,10},{9,11},{10,... | collective-permute-start | bytes 1634312 | tf_op jit(solution)/shard_map/ppermute | solution.py:76
  112.5 27.1 %collective-permute-start.16 = (bf16[2,112,1216]{2,1,0:T(8,128)(2,1)S(1)}, bf16[2,112,1216]{2,1,0:T(8,128)(2,1)}, u32[]{:S(2)}, u32[]{:S(2)}) collective-permute-start(bf16[2,112,1216]{2,1,0:T(8,128)(2,1)S(1)} %get-tuple-element.585), channel_id=1, source_target_pairs={{0,1},{1,0},{2,3},{3,2},{4,5},{5,4},{6,7},{7,6},{8,9},{9,8},{10,11... | collective-permute-start | bytes 1634312 | tf_op jit(solution)/shard_map/ppermute | solution.py:76
  113.1 31.4 %collective-permute-start.14 = (bf16[256,896]{1,0:T(8,128)(2,1)S(1)}, bf16[256,896]{1,0:T(8,128)(2,1)S(1)}, u32[]{:S(2)}, u32[]{:S(2)}) collective-permute-start(bf16[256,896]{1,0:T(8,128)(2,1)S(1)} %constant_dynamic-update-slice_fusion.1.lower_ref.refs_0_), channel_id=1, source_target_pairs={{0,2},{1,3},{2,0},{3,1},{16,17},{17,16},{18,19},{19,18},{4,6},{5,7... | collective-permute-start | bytes 1376264 | tf_op jit(solution)/shard_map/ppermute | solution.py:45
  125.0 38.9 %collective-permute-start.32 = (bf16[224,2176]{1,0:T(8,128)(2,1)}, bf16[224,2176]{1,0:T(8,128)(2,1)S(1)}, u32[]{:S(2)}, u32[]{:S(2)}) collective-permute-start(bf16[224,2176]{1,0:T(8,128)(2,1)} %constant_dynamic-update-slice_fusion.3.refs_0_), channel_id=1, source_target_pairs={{0,16},{16,0},{1,17},{17,1},{2,18},{18,2},{3,19},{19,3},{4,20},{20... | collective-permute-start | bytes 2924552 | tf_op jit(solution)/shard_map/ppermute | solution.py:80
  129.0 34.9 %collective-permute-start.33 = (bf16[224,2176]{1,0:T(8,128)(2,1)}, bf16[224,2176]{1,0:T(8,128)(2,1)S(1)}, u32[]{:S(2)}, u32[]{:S(2)}) collective-permute-start(bf16[224,2176]{1,0:T(8,128)(2,1)} %collective-permute-done.15.refs_1_), channel_id=1, source_target_pairs={{0,16},{16,0},{1,17},{17,1},{2,18},{18,2},{3,19},{19,3},{4,20},{20... | collective-permute-start | bytes 2924552 | tf_op jit(solution)/shard_map/ppermute | solution.py:80
  157.6 18.0 %collective-permute-start.27 = (bf16[256,896]{1,0:T(8,128)(2,1)}, bf16[256,896]{1,0:T(8,128)(2,1)}, u32[]{:S(2)}, u32[]{:S(2)}) collective-permute-start(bf16[256,896]{1,0:T(8,128)(2,1)} %constant_dynamic-update-slice_fusion.5.lower_ref.refs_2_), channel_id=1, source_target_pairs={{0,2},{1,3},{2,0},{3,1},{16,17},{17,16},{18,19},{19,18},{4,6},{5,7... | collective-permute-start | bytes 1376264 | tf_op jit(solution)/shard_map/ppermute | solution.py:45
  162.7 31.0 %collective-permute-start.31 = (bf16[256,896]{1,0:T(8,128)(2,1)}, bf16[256,896]{1,0:T(8,128)(2,1)}, u32[]{:S(2)}, u32[]{:S(2)}) collective-permute-start(bf16[256,896]{1,0:T(8,128)(2,1)} %constant_dynamic-update-slice_fusion.7.lower_ref.refs_4_), channel_id=1, source_target_pairs={{0,2},{1,3},{2,0},{3,1},{16,17},{17,16},{18,19},{19,18},{4,6},{5,7... | collective-permute-start | bytes 1376264 | tf_op jit(solution)/shard_map/ppermute | solution.py:45
  242.9 34.2 %collective-permute-start.60 = (bf16[2,3,128,896]{3,2,1,0:T(8,128)(2,1)S(1)}, bf16[2,3,128,896]{3,2,1,0:T(8,128)(2,1)S(1)}, u32[]{:S(2)}, u32[]{:S(2)}) collective-permute-start(bf16[2,3,128,896]{3,2,1,0:T(8,128)(2,1)S(1)} %constant_dynamic-update-slice_fusion.15.lower_ref.refs_3_.refs_5_.refs_7_), channel_id=1, source_target_pairs={{0,2},{1,3},{2,0},{3,1},{16,17},{17,16},{18,19},{19,18},{4,6},{5,7... | collective-permute-start | bytes 4128776 | tf_op jit(solution)/shard_map/ppermute | solution.py:45
  248.9 21.7 %collective-permute-start.52 = (bf16[256,896]{1,0:T(8,128)(2,1)S(1)}, bf16[256,896]{1,0:T(8,128)(2,1)S(1)}, u32[]{:S(2)}, u32[]{:S(2)}) collective-permute-start(bf16[256,896]{1,0:T(8,128)(2,1)S(1)} %constant_dynamic-update-slice_fusion.11.lower_ref.refs_2_), channel_id=1, source_target_pairs={{0,2},{1,3},{2,0},{3,1},{16,17},{17,16},{18,19},{19,18},{4,6},{5,7... | collective-permute-start | bytes 1376264 | tf_op jit(solution)/shard_map/ppermute | solution.py:45
  296.9 18.1 %collective-permute-start.55 = (bf16[256,896]{1,0:T(8,128)(2,1)S(1)}, bf16[256,896]{1,0:T(8,128)(2,1)S(1)}, u32[]{:S(2)}, u32[]{:S(2)}) collective-permute-start(bf16[256,896]{1,0:T(8,128)(2,1)S(1)} %get-tuple-element.341), channel_id=1, source_target_pairs={{0,2},{1,3},{2,0},{3,1},{16,17},{17,16},{18,19},{19,18},{4,6},{5,7... | collective-permute-start | bytes 1376264 | tf_op jit(solution)/shard_map/ppermute | solution.py:45
  340.8 26.9 %collective-permute-start.80 = (bf16[4,2,112,1280]{3,2,1,0:T(8,128)(2,1)S(1)}, bf16[4,2,112,1280]{3,2,1,0:T(8,128)(2,1)S(1)}, u32[]{:S(2)}, u32[]{:S(2)}) collective-permute-start(bf16[4,2,112,1280]{3,2,1,0:T(8,128)(2,1)S(1)} %get-tuple-element.387), channel_id=1, source_target_pairs={{0,16},{16,0},{1,17},{17,1},{2,18},{18,2},{3,19},{19,3},{4,20},{20... | collective-permute-start | bytes 6881288 | tf_op jit(solution)/shard_map/ppermute | solution.py:80
  342.1 57.5 %collective-permute-start.50 = (bf16[128,896]{1,0:T(8,128)(2,1)S(1)}, bf16[128,896]{1,0:T(8,128)(2,1)S(1)}, u32[]{:S(2)}, u32[]{:S(2)}) collective-permute-start(bf16[128,896]{1,0:T(8,128)(2,1)S(1)} %slice.628), channel_id=1, source_target_pairs={{0,1},{1,0},{2,3},{3,2},{16,18},{17,19},{18,16},{19,17},{4,5},{5,4... | collective-permute-start | bytes 688136 | tf_op jit(solution)/shard_map/ppermute | solution.py:45
  343.8 19.9 %collective-permute-start.72 = (bf16[608,896]{1,0:T(8,128)(2,1)S(1)}, bf16[608,896]{1,0:T(8,128)(2,1)S(1)}, u32[]{:S(2)}, u32[]{:S(2)}) collective-permute-start(bf16[608,896]{1,0:T(8,128)(2,1)S(1)} %get-tuple-element.379), channel_id=1, source_target_pairs={{0,16},{16,0},{1,17},{17,1},{2,18},{18,2},{3,19},{19,3},{4,20},{20... | collective-permute-start | bytes 3268616 | tf_op jit(solution)/shard_map/ppermute | solution.py:80
  364.0 26.5 %collective-permute-start.73 = (bf16[608,896]{1,0:T(8,128)(2,1)S(1)}, bf16[608,896]{1,0:T(8,128)(2,1)S(1)}, u32[]{:S(2)}, u32[]{:S(2)}) collective-permute-start(bf16[608,896]{1,0:T(8,128)(2,1)S(1)} %add_convert_fusion.15), channel_id=1, source_target_pairs={{0,4},{12,8},{1,5},{13,9},{2,6},{14,10},{3,7},{15,11},{16,20},{28,... | collective-permute-start | bytes 3268616 | tf_op jit(solution)/shard_map/ppermute | solution.py:1109
  368.5 32.0 %collective-permute-start.83 = (bf16[2,112,1280]{2,1,0:T(8,128)(2,1)S(1)}, bf16[2,112,1280]{2,1,0:T(8,128)(2,1)S(1)}, u32[]{:S(2)}, u32[]{:S(2)}) collective-permute-start(bf16[2,112,1280]{2,1,0:T(8,128)(2,1)S(1)} %get-tuple-element.580), channel_id=1, source_target_pairs={{0,3},{1,2},{2,1},{3,0},{4,7},{5,6},{6,5},{7,4},{8,11},{9,10},{10,... | collective-permute-start | bytes 1720328 | tf_op jit(solution)/shard_map/ppermute | solution.py:76
  369.7 30.8 %collective-permute-start.82 = (bf16[2,112,1280]{2,1,0:T(8,128)(2,1)S(1)}, bf16[2,112,1280]{2,1,0:T(8,128)(2,1)S(1)}, u32[]{:S(2)}, u32[]{:S(2)}) collective-permute-start(bf16[2,112,1280]{2,1,0:T(8,128)(2,1)S(1)} %get-tuple-element.581), channel_id=1, source_target_pairs={{0,2},{1,3},{2,0},{3,1},{4,6},{5,7},{6,4},{7,5},{8,10},{9,11},{10,... | collective-permute-start | bytes 1720328 | tf_op jit(solution)/shard_map/ppermute | solution.py:76
  371.9 29.3 %collective-permute-start.81 = (bf16[2,112,1280]{2,1,0:T(8,128)(2,1)S(1)}, bf16[2,112,1280]{2,1,0:T(8,128)(2,1)S(1)}, u32[]{:S(2)}, u32[]{:S(2)}) collective-permute-start(bf16[2,112,1280]{2,1,0:T(8,128)(2,1)S(1)} %get-tuple-element.582), channel_id=1, source_target_pairs={{0,1},{1,0},{2,3},{3,2},{4,5},{5,4},{6,7},{7,6},{8,9},{9,8},{10,11... | collective-permute-start | bytes 1720328 | tf_op jit(solution)/shard_map/ppermute | solution.py:76
  398.9 34.1 %collective-permute-start.56 = (bf16[128,896]{1,0:T(8,128)(2,1)S(1)}, bf16[128,896]{1,0:T(8,128)(2,1)S(1)}, u32[]{:S(2)}, u32[]{:S(2)}) collective-permute-start(bf16[128,896]{1,0:T(8,128)(2,1)S(1)} %slice.627), channel_id=1, source_target_pairs={{0,1},{1,0},{2,3},{3,2},{16,18},{17,19},{18,16},{19,17},{4,5},{5,4... | collective-permute-start | bytes 688136 | tf_op jit(solution)/shard_map/ppermute | solution.py:45
  399.6 68.7 %collective-permute-start.62 = (bf16[128,896]{1,0:T(8,128)(2,1)S(1)}, bf16[128,896]{1,0:T(8,128)(2,1)S(1)}, u32[]{:S(2)}, u32[]{:S(2)}) collective-permute-start(bf16[128,896]{1,0:T(8,128)(2,1)S(1)} %slice.626), channel_id=1, source_target_pairs={{0,1},{1,0},{2,3},{3,2},{16,18},{17,19},{18,16},{19,17},{4,5},{5,4... | collective-permute-start | bytes 688136 | tf_op jit(solution)/shard_map/ppermute | solution.py:45
  400.5 15.7 %collective-permute-start.79 = (bf16[128,256]{1,0:T(8,128)(2,1)S(1)}, bf16[128,256]{1,0:T(8,128)(2,1)S(1)}, u32[]{:S(2)}, u32[]{:S(2)}) collective-permute-start(bf16[128,256]{1,0:T(8,128)(2,1)S(1)} %slice.642), channel_id=1, source_target_pairs={{0,4},{4,0},{8,12},{12,8},{16,20},{20,16},{24,28},{28,24},{1,5},{5... | collective-permute-start | bytes 196616 | tf_op jit(solution)/shard_map/ppermute | solution.py:45
  400.5 17.6 %collective-permute-start.84 = (bf16[608,896]{1,0:T(8,128)(2,1)S(1)}, bf16[608,896]{1,0:T(8,128)(2,1)S(1)}, u32[]{:S(2)}, u32[]{:S(2)}) collective-permute-start(bf16[608,896]{1,0:T(8,128)(2,1)S(1)} %add_convert_fusion.14), channel_id=1, source_target_pairs={{4,8},{8,4},{5,9},{9,5},{6,10},{10,6},{7,11},{11,7},{20,24},{24,20... | collective-permute-start | bytes 3268616 | tf_op jit(solution)/shard_map/ppermute | solution.py:1109
  401.4 38.4 %collective-permute-start.91 = (bf16[2,2,112,1280]{3,2,1,0:T(8,128)(2,1)S(1)}, bf16[2,2,112,1280]{3,2,1,0:T(8,128)(2,1)S(1)}, u32[]{:S(2)}, u32[]{:S(2)}) collective-permute-start(bf16[2,2,112,1280]{3,2,1,0:T(8,128)(2,1)S(1)} %pad_maximum_fusion.2), channel_id=1, source_target_pairs={{0,4},{12,8},{1,5},{13,9},{2,6},{14,10},{3,7},{15,11},{16,20},{28,... | collective-permute-start | bytes 3440648 | tf_op jit(solution)/shard_map/ppermute | solution.py:1109
  420.2 18.3 %collective-permute-start.86 = (bf16[256,256]{1,0:T(8,128)(2,1)S(1)}, bf16[256,256]{1,0:T(8,128)(2,1)S(1)}, u32[]{:S(2)}, u32[]{:S(2)}) collective-permute-start(bf16[256,256]{1,0:T(8,128)(2,1)S(1)} %slice.635), channel_id=1, source_target_pairs={{0,8},{4,12},{8,0},{12,4},{16,24},{20,28},{24,16},{28,20},{1,9},{5... | collective-permute-start | bytes 393224 | tf_op jit(solution)/shard_map/ppermute | solution.py:45
  433.0 58.9 %collective-permute-start.97 = (bf16[2,2,112,1280]{3,2,1,0:T(8,128)(2,1)}, bf16[2,2,112,1280]{3,2,1,0:T(8,128)(2,1)}, u32[]{:S(2)}, u32[]{:S(2)}) collective-permute-start(bf16[2,2,112,1280]{3,2,1,0:T(8,128)(2,1)} %pad_maximum_fusion.3), channel_id=1, source_target_pairs={{0,4},{12,8},{1,5},{13,9},{2,6},{14,10},{3,7},{15,11},{16,20},{28,... | collective-permute-start | bytes 3440648 | tf_op jit(solution)/shard_map/ppermute | solution.py:1109
  438.5 26.1 %collective-permute-start.90 = (bf16[608,896]{1,0:T(8,128)(2,1)S(1)}, bf16[608,896]{1,0:T(8,128)(2,1)S(1)}, u32[]{:S(2)}, u32[]{:S(2)}) collective-permute-start(bf16[608,896]{1,0:T(8,128)(2,1)S(1)} %add_convert_fusion.13), channel_id=1, source_target_pairs={{4,0},{8,12},{5,1},{9,13},{6,2},{10,14},{7,3},{11,15},{20,16},{24,... | collective-permute-start | bytes 3268616 | tf_op jit(solution)/shard_map/ppermute | solution.py:1109
  439.9 23.7 %collective-permute-start.89 = (bf16[128,256]{1,0:T(8,128)(2,1)S(1)}, bf16[128,256]{1,0:T(8,128)(2,1)S(1)}, u32[]{:S(2)}, u32[]{:S(2)}) collective-permute-start(bf16[128,256]{1,0:T(8,128)(2,1)S(1)} %slice.641), channel_id=1, source_target_pairs={{0,4},{4,0},{8,12},{12,8},{16,20},{20,16},{24,28},{28,24},{1,5},{5... | collective-permute-start | bytes 196616 | tf_op jit(solution)/shard_map/ppermute | solution.py:45
  443.4 48.5 %collective-permute-start.96 = (bf16[2,2,112,1280]{3,2,1,0:T(8,128)(2,1)}, bf16[2,2,112,1280]{3,2,1,0:T(8,128)(2,1)}, u32[]{:S(2)}, u32[]{:S(2)}) collective-permute-start(bf16[2,2,112,1280]{3,2,1,0:T(8,128)(2,1)} %add_convert_fusion.9), channel_id=1, source_target_pairs={{4,8},{8,4},{5,9},{9,5},{6,10},{10,6},{7,11},{11,7},{20,24},{24,20... | collective-permute-start | bytes 3440648 | tf_op jit(solution)/shard_map/ppermute | solution.py:1109
  504.6 30.8 %collective-permute-start.102 = (bf16[2,2,112,1280]{3,2,1,0:T(8,128)(2,1)S(1)}, bf16[2,2,112,1280]{3,2,1,0:T(8,128)(2,1)S(1)}, u32[]{:S(2)}, u32[]{:S(2)}) collective-permute-start(bf16[2,2,112,1280]{3,2,1,0:T(8,128)(2,1)S(1)} %add_convert_fusion.7), channel_id=1, source_target_pairs={{4,8},{8,4},{5,9},{9,5},{6,10},{10,6},{7,11},{11,7},{20,24},{24,20... | collective-permute-start | bytes 3440648 | tf_op jit(solution)/shard_map/ppermute | solution.py:1109
  507.9 20.8 %collective-permute-start.100 = (bf16[224,2176]{1,0:T(8,128)(2,1)S(1)}, bf16[224,2176]{1,0:T(8,128)(2,1)S(1)}, u32[]{:S(2)}, u32[]{:S(2)}) collective-permute-start(bf16[224,2176]{1,0:T(8,128)(2,1)S(1)} %bitcast.287), channel_id=1, source_target_pairs={{0,2},{1,3},{2,0},{3,1},{16,17},{17,16},{18,19},{19,18},{4,6},{5,7... | collective-permute-start | bytes 2924552 | tf_op jit(solution)/shard_map/ppermute | solution.py:45
  513.1 27.7 %collective-permute-start.101 = (bf16[2,2,112,1280]{3,2,1,0:T(8,128)(2,1)S(1)}, bf16[2,2,112,1280]{3,2,1,0:T(8,128)(2,1)S(1)}, u32[]{:S(2)}, u32[]{:S(2)}) collective-permute-start(bf16[2,2,112,1280]{3,2,1,0:T(8,128)(2,1)S(1)} %add_convert_fusion.8), channel_id=1, source_target_pairs={{4,0},{8,12},{5,1},{9,13},{6,2},{10,14},{7,3},{11,15},{20,16},{24,... | collective-permute-start | bytes 3440648 | tf_op jit(solution)/shard_map/ppermute | solution.py:1109
  568.4 31.6 %collective-permute-start.108 = (bf16[2,2,112,1280]{3,2,1,0:T(8,128)(2,1)S(1)}, bf16[2,2,112,1280]{3,2,1,0:T(8,128)(2,1)S(1)}, u32[]{:S(2)}, u32[]{:S(2)}) collective-permute-start(bf16[2,2,112,1280]{3,2,1,0:T(8,128)(2,1)S(1)} %add_convert_fusion.6), channel_id=1, source_target_pairs={{4,0},{8,12},{5,1},{9,13},{6,2},{10,14},{7,3},{11,15},{20,16},{24,... | collective-permute-start | bytes 3440648 | tf_op jit(solution)/shard_map/ppermute | solution.py:1109
  569.7 39.8 %collective-permute-start.116 = (bf16[4,2,112,1280]{3,2,1,0:T(8,128)(2,1)S(1)}, bf16[4,2,112,1280]{3,2,1,0:T(8,128)(2,1)S(1)}, u32[]{:S(2)}, u32[]{:S(2)}) collective-permute-start(bf16[4,2,112,1280]{3,2,1,0:T(8,128)(2,1)S(1)} %get-tuple-element.453), channel_id=1, source_target_pairs={{0,16},{16,0},{1,17},{17,1},{2,18},{18,2},{3,19},{19,3},{4,20},{20... | collective-permute-start | bytes 6881288 | tf_op jit(solution)/shard_map/ppermute | solution.py:80
  574.9 34.6 %collective-permute-start.110 = (bf16[608,896]{1,0:T(8,128)(2,1)S(1)}, bf16[608,896]{1,0:T(8,128)(2,1)S(1)}, u32[]{:S(2)}, u32[]{:S(2)}) collective-permute-start(bf16[608,896]{1,0:T(8,128)(2,1)S(1)} %add_convert_fusion.12), channel_id=1, source_target_pairs={{0,4},{12,8},{1,5},{13,9},{2,6},{14,10},{3,7},{15,11},{16,20},{28,... | collective-permute-start | bytes 3268616 | tf_op jit(solution)/shard_map/ppermute | solution.py:1109
  586.3 42.7 %collective-permute-start.115 = (bf16[112,2176]{1,0:T(8,128)(2,1)S(1)}, bf16[112,2176]{1,0:T(8,128)(2,1)S(1)}, u32[]{:S(2)}, u32[]{:S(2)}) collective-permute-start(bf16[112,2176]{1,0:T(8,128)(2,1)S(1)} %add_convert_fusion.19), channel_id=1, source_target_pairs={{4,8},{8,4},{5,9},{9,5},{6,10},{10,6},{7,11},{11,7},{20,24},{24,20... | collective-permute-start | bytes 1462280 | tf_op jit(solution)/shard_map/ppermute | solution.py:1109
  621.4 38.5 %collective-permute-start.114 = (bf16[608,896]{1,0:T(8,128)(2,1)S(1)}, bf16[608,896]{1,0:T(8,128)(2,1)S(1)}, u32[]{:S(2)}, u32[]{:S(2)}) collective-permute-start(bf16[608,896]{1,0:T(8,128)(2,1)S(1)} %add_convert_fusion.11), channel_id=1, source_target_pairs={{4,8},{8,4},{5,9},{9,5},{6,10},{10,6},{7,11},{11,7},{20,24},{24,20... | collective-permute-start | bytes 3268616 | tf_op jit(solution)/shard_map/ppermute | solution.py:1109
  622.1 34.1 %collective-permute-start.125 = (bf16[2,112,1280]{2,1,0:T(8,128)(2,1)S(1)}, bf16[2,112,1280]{2,1,0:T(8,128)(2,1)S(1)}, u32[]{:S(2)}, u32[]{:S(2)}) collective-permute-start(bf16[2,112,1280]{2,1,0:T(8,128)(2,1)S(1)} %get-tuple-element.575), channel_id=1, source_target_pairs={{0,2},{1,3},{2,0},{3,1},{4,6},{5,7},{6,4},{7,5},{8,10},{9,11},{10,... | collective-permute-start | bytes 1720328 | tf_op jit(solution)/shard_map/ppermute | solution.py:76
  622.9 34.6 %collective-permute-start.126 = (bf16[2,112,1280]{2,1,0:T(8,128)(2,1)S(1)}, bf16[2,112,1280]{2,1,0:T(8,128)(2,1)S(1)}, u32[]{:S(2)}, u32[]{:S(2)}) collective-permute-start(bf16[2,112,1280]{2,1,0:T(8,128)(2,1)S(1)} %get-tuple-element.576), channel_id=1, source_target_pairs={{0,3},{1,2},{2,1},{3,0},{4,7},{5,6},{6,5},{7,4},{8,11},{9,10},{10,... | collective-permute-start | bytes 1720328 | tf_op jit(solution)/shard_map/ppermute | solution.py:76
  624.3 31.8 %collective-permute-start.120 = (bf16[256,256]{1,0:T(8,128)(2,1)S(1)}, bf16[256,256]{1,0:T(8,128)(2,1)S(1)}, u32[]{:S(2)}, u32[]{:S(2)}) collective-permute-start(bf16[256,256]{1,0:T(8,128)(2,1)S(1)} %slice.633), channel_id=1, source_target_pairs={{0,8},{4,12},{8,0},{12,4},{16,24},{20,28},{24,16},{28,20},{1,9},{5... | collective-permute-start | bytes 393224 | tf_op jit(solution)/shard_map/ppermute | solution.py:45
  629.0 34.4 %collective-permute-start.118 = (bf16[2,2,112,1280]{3,2,1,0:T(8,128)(2,1)S(1)}, bf16[2,2,112,1280]{3,2,1,0:T(8,128)(2,1)S(1)}, u32[]{:S(2)}, u32[]{:S(2)}) collective-permute-start(bf16[2,2,112,1280]{3,2,1,0:T(8,128)(2,1)S(1)} %pad_maximum_fusion.4), channel_id=1, source_target_pairs={{0,4},{12,8},{1,5},{13,9},{2,6},{14,10},{3,7},{15,11},{16,20},{28,... | collective-permute-start | bytes 3440648 | tf_op jit(solution)/shard_map/ppermute | solution.py:1109
  656.2 70.5 %collective-permute-start.123 = (bf16[112,2176]{1,0:T(8,128)(2,1)S(1)}, bf16[112,2176]{1,0:T(8,128)(2,1)S(1)}, u32[]{:S(2)}, u32[]{:S(2)}) collective-permute-start(bf16[112,2176]{1,0:T(8,128)(2,1)S(1)} %add_convert_fusion.18), channel_id=1, source_target_pairs={{4,0},{8,12},{5,1},{9,13},{6,2},{10,14},{7,3},{11,15},{20,16},{24,... | collective-permute-start | bytes 1462280 | tf_op jit(solution)/shard_map/ppermute | solution.py:1109
  657.5 72.4 %collective-permute-start.121 = (bf16[128,256]{1,0:T(8,128)(2,1)S(1)}, bf16[128,256]{1,0:T(8,128)(2,1)S(1)}, u32[]{:S(2)}, u32[]{:S(2)}) collective-permute-start(bf16[128,256]{1,0:T(8,128)(2,1)S(1)} %slice.639), channel_id=1, source_target_pairs={{0,4},{4,0},{8,12},{12,8},{16,20},{20,16},{24,28},{28,24},{1,5},{5... | collective-permute-start | bytes 196616 | tf_op jit(solution)/shard_map/ppermute | solution.py:45
  659.8 26.1 %collective-permute-start.127 = (bf16[2,2,112,1280]{3,2,1,0:T(8,128)(2,1)S(1)}, bf16[2,2,112,1280]{3,2,1,0:T(8,128)(2,1)S(1)}, u32[]{:S(2)}, u32[]{:S(2)}) collective-permute-start(bf16[2,2,112,1280]{3,2,1,0:T(8,128)(2,1)S(1)} %pad_maximum_fusion.5), channel_id=1, source_target_pairs={{0,4},{12,8},{1,5},{13,9},{2,6},{14,10},{3,7},{15,11},{16,20},{28,... | collective-permute-start | bytes 3440648 | tf_op jit(solution)/shard_map/ppermute | solution.py:1109
  662.1 67.8 %collective-permute-start.122 = (bf16[608,896]{1,0:T(8,128)(2,1)S(1)}, bf16[608,896]{1,0:T(8,128)(2,1)S(1)}, u32[]{:S(2)}, u32[]{:S(2)}) collective-permute-start(bf16[608,896]{1,0:T(8,128)(2,1)S(1)} %add_convert_fusion.10), channel_id=1, source_target_pairs={{4,0},{8,12},{5,1},{9,13},{6,2},{10,14},{7,3},{11,15},{20,16},{24,... | collective-permute-start | bytes 3268616 | tf_op jit(solution)/shard_map/ppermute | solution.py:1109
  663.7 27.1 %collective-permute-start.124 = (bf16[2,2,112,1280]{3,2,1,0:T(8,128)(2,1)S(1)}, bf16[2,2,112,1280]{3,2,1,0:T(8,128)(2,1)S(1)}, u32[]{:S(2)}, u32[]{:S(2)}) collective-permute-start(bf16[2,2,112,1280]{3,2,1,0:T(8,128)(2,1)S(1)} %add_convert_fusion.5), channel_id=1, source_target_pairs={{4,8},{8,4},{5,9},{9,5},{6,10},{10,6},{7,11},{11,7},{20,24},{24,20... | collective-permute-start | bytes 3440648 | tf_op jit(solution)/shard_map/ppermute | solution.py:1109
  689.1 69.2 %collective-permute-start.133 = (bf16[2,2,112,1280]{3,2,1,0:T(8,128)(2,1)}, bf16[2,2,112,1280]{3,2,1,0:T(8,128)(2,1)}, u32[]{:S(2)}, u32[]{:S(2)}) collective-permute-start(bf16[2,2,112,1280]{3,2,1,0:T(8,128)(2,1)} %add_convert_fusion.3), channel_id=1, source_target_pairs={{4,8},{8,4},{5,9},{9,5},{6,10},{10,6},{7,11},{11,7},{20,24},{24,20... | collective-permute-start | bytes 3440648 | tf_op jit(solution)/shard_map/ppermute | solution.py:1109
  690.9 34.5 %collective-permute-start.129 = (bf16[256,256]{1,0:T(8,128)(2,1)S(1)}, bf16[256,256]{1,0:T(8,128)(2,1)S(1)}, u32[]{:S(2)}, u32[]{:S(2)}) collective-permute-start(bf16[256,256]{1,0:T(8,128)(2,1)S(1)} %slice.632), channel_id=1, source_target_pairs={{0,8},{4,12},{8,0},{12,4},{16,24},{20,28},{24,16},{28,20},{1,9},{5... | collective-permute-start | bytes 393224 | tf_op jit(solution)/shard_map/ppermute | solution.py:45
  725.3 32.9 %collective-permute-start.132 = (bf16[2,2,112,1280]{3,2,1,0:T(8,128)(2,1)}, bf16[2,2,112,1280]{3,2,1,0:T(8,128)(2,1)}, u32[]{:S(2)}, u32[]{:S(2)}) collective-permute-start(bf16[2,2,112,1280]{3,2,1,0:T(8,128)(2,1)} %add_convert_fusion.4), channel_id=1, source_target_pairs={{4,0},{8,12},{5,1},{9,13},{6,2},{10,14},{7,3},{11,15},{20,16},{24,... | collective-permute-start | bytes 3440648 | tf_op jit(solution)/shard_map/ppermute | solution.py:1109
  726.7 28.0 %collective-permute-start.130 = (bf16[128,256]{1,0:T(8,128)(2,1)S(1)}, bf16[128,256]{1,0:T(8,128)(2,1)S(1)}, u32[]{:S(2)}, u32[]{:S(2)}) collective-permute-start(bf16[128,256]{1,0:T(8,128)(2,1)S(1)} %slice.638), channel_id=1, source_target_pairs={{0,4},{4,0},{8,12},{12,8},{16,20},{20,16},{24,28},{28,24},{1,5},{5... | collective-permute-start | bytes 196616 | tf_op jit(solution)/shard_map/ppermute | solution.py:45
  796.6 27.2 %collective-permute-start.141 = (bf16[2,2,112,1280]{3,2,1,0:T(8,128)(2,1)S(1)}, bf16[2,2,112,1280]{3,2,1,0:T(8,128)(2,1)S(1)}, u32[]{:S(2)}, u32[]{:S(2)}) collective-permute-start(bf16[2,2,112,1280]{3,2,1,0:T(8,128)(2,1)S(1)} %add_convert_fusion.2), channel_id=1, source_target_pairs={{4,0},{8,12},{5,1},{9,13},{6,2},{10,14},{7,3},{11,15},{20,16},{24,... | collective-permute-start | bytes 3440648 | tf_op jit(solution)/shard_map/ppermute | solution.py:1109
  803.9 38.8 %collective-permute-start.144 = (bf16[608,896]{1,0:T(8,128)(2,1)S(1)}, bf16[608,896]{1,0:T(8,128)(2,1)S(1)}, u32[]{:S(2)}, u32[]{:S(2)}) collective-permute-start(bf16[608,896]{1,0:T(8,128)(2,1)S(1)} %get-tuple-element.572), channel_id=1, source_target_pairs={{0,16},{16,0},{1,17},{17,1},{2,18},{18,2},{3,19},{19,3},{4,20},{20... | collective-permute-start | bytes 3268616 | tf_op jit(solution)/shard_map/ppermute | solution.py:80
  806.5 38.8 %collective-permute-start.131 = (f32[3,128,896]{2,1,0:T(8,128)S(1)}, f32[3,128,896]{2,1,0:T(8,128)S(1)}, u32[]{:S(2)}, u32[]{:S(2)}) collective-permute-start(f32[3,128,896]{2,1,0:T(8,128)S(1)} %get-tuple-element.598), channel_id=1, source_target_pairs={{0,16},{16,0},{1,17},{17,1},{2,18},{18,2},{3,19},{19,3},{4,20},{20... | collective-permute-start | bytes 4128776 | tf_op jit(solution)/shard_map/ppermute | solution.py:80
  824.1 23.0 %collective-permute-start.143 = (bf16[2,2,112,1280]{3,2,1,0:T(8,128)(2,1)S(1)}, bf16[2,2,112,1280]{3,2,1,0:T(8,128)(2,1)S(1)}, u32[]{:S(2)}, u32[]{:S(2)}) collective-permute-start(bf16[2,2,112,1280]{3,2,1,0:T(8,128)(2,1)S(1)} %get-tuple-element.565), channel_id=1, source_target_pairs={{0,16},{16,0},{1,17},{17,1},{2,18},{18,2},{3,19},{19,3},{4,20},{20... | collective-permute-start | bytes 3440648 | tf_op jit(solution)/shard_map/ppermute | solution.py:80
  830.1 17.1 %collective-permute-start.142 = (bf16[2,2,112,1280]{3,2,1,0:T(8,128)(2,1)S(1)}, bf16[2,2,112,1280]{3,2,1,0:T(8,128)(2,1)S(1)}, u32[]{:S(2)}, u32[]{:S(2)}) collective-permute-start(bf16[2,2,112,1280]{3,2,1,0:T(8,128)(2,1)S(1)} %get-tuple-element.567), channel_id=1, source_target_pairs={{0,16},{16,0},{1,17},{17,1},{2,18},{18,2},{3,19},{19,3},{4,20},{20... | collective-permute-start | bytes 3440648 | tf_op jit(solution)/shard_map/ppermute | solution.py:80
  (350 other events, 3634.9 us)
